TPU v7x, 32 devices: a whole 2x2x4 slice. The times are simulated.
32 devices in a mesh: group: 2 (over x), ep: 16 (over z, y, core).
Axes of the slice: x: 2, y: 2, z: 4, core: 2. Of those that a mesh axis runs over, the one named last changes fastest.
Arguments:
- hidden: bfloat16 [512, 7168], P(('group', 'ep')), parts along dimension 0, may hold values from -6 to 6
- ffn_gain: float32 [7168], replicated, may hold values from 0.25 to 1.75
- attn_gain: float32 [7168], replicated, may hold values from 0.25 to 1.75
- latent_norm_gain: float32 [512], replicated, may hold values from 0.25 to 1.75
- routes: int32 [512, 2], P(('group', 'ep')), parts along dimension 0, may hold values from 0 to 3, all different within a row; in each aligned block of 16 rows (0 to 15, 16 to 31, ...) at most 9 rows name the same one
- gate_weights: float32 [512, 2], P(('group', 'ep')), parts along dimension 0, may hold values from 0.2 to 1
- expert_in: bfloat16 [16, 7168, 1024], P('ep'), may hold values from -0.0625 to 0.0625
- expert_down: bfloat16 [16, 512, 7168], P('ep'), may hold values from -0.125 to 0.125
- kv_down: bfloat16 [7168, 576], P('ep'), may hold values from -0.0625 to 0.0625
- parents: int32 [32, 16], P(('group', 'ep')), parts along dimension 0, may hold values from -1 to 14, as said below
- lengths: int32 [32], P(('group', 'ep')), parts along dimension 0, may hold values from 128 to 1024, as said below
- queries: bfloat16 [512, 128, 576], P(('group', 'ep')), parts along dimension 0
- cache: bfloat16 [32, 1024, 576], P(('group', 'ep')), parts along dimension 0
Outputs:
- residual_after_expert: bfloat16 [512, 7168], P(('group', 'ep')), parts along dimension 0
- draft_latent_entries: bfloat16 [512, 576], P(('group', 'ep')), parts along dimension 0
- attention_output: bfloat16 [512, 128, 512], P(('group', 'ep')), parts along dimension 0
There are 2 independent parts, one for each index of `group`. A program takes and returns all parts, laid end to end along the dimension named above; an argument that names none is the same for every part. Nothing has to cross between parts.
Inputs may be any that keep to these rules, and one draw needn't show every extreme that they name: `parents`: node 0 of each request is its root, with parent -1; every other node's parent is an earlier node of the same request. `lengths`: cache slots at or past a request's length are not used.
All inputs are finite; a program needn't handle non-finite values.
Results may differ from a plain program's by a relative error of at most 0.008.
Values may be sent and summed in bfloat16 or wider, within the bound.
No kernel may reach another device: no remote copies, remote signals or barrier semaphores. Data moves between devices by JAX's collectives and lax.ppermute only.
A program may use at most 128 MiB of HBM per device.

v0:
```python
import jax
import jax.numpy as jnp
from jax import lax
from jax.sharding import PartitionSpec as P

KEY_VALUE_RANK = 512
NODES = 16
TOPK = 2
EXPERTS = 4
CAP = 9


softmax_scale = 192.0 ** (-0.5)


def normalized_rows(values, gain):
    return values * lax.rsqrt(jnp.mean(values * values, axis=-1, keepdims=True) + 1e-06) * gain


def ancestors(parents):
    count = parents.shape[1]
    link = (parents[:, :, None] == jnp.arange(count, dtype=jnp.int32)[None, None, :]).astype(
        jnp.float32
    )
    reach = jnp.eye(count, dtype=jnp.float32)[None] + link
    for _ in range(max(1, (count - 1).bit_length())):
        reach = jnp.minimum(
            jnp.einsum("rij,rjk->rik", reach, reach, precision=lax.Precision.HIGHEST), 1.0
        )
    return reach


def apply_rotation(part, token_position):
    half = part.shape[-1] // 2
    index = jnp.arange(half, dtype=jnp.float32)
    inverse = 10000.0 ** (-2.0 * index / part.shape[-1])
    angle = token_position[:, None] * inverse[None, :]
    first = part[:, :half]
    second = part[:, half:]
    return jnp.concatenate(
        [
            first * jnp.cos(angle) - second * jnp.sin(angle),
            first * jnp.sin(angle) + second * jnp.cos(angle),
        ],
        axis=-1,
    )


def local(
    hidden,
    ffn_gain,
    attn_gain,
    latent_norm_gain,
    routes,
    gate_weights,
    expert_in,
    expert_down,
    kv_down,
    parents,
    lengths,
    queries,
    cache,
):
    token_total = hidden.shape[0]
    width = hidden.shape[1]
    split = lax.axis_size("ep") // EXPERTS
    hid_units = expert_down.shape[1]
    w_in = expert_in[0]
    w_out = expert_down[0]
    source = hidden.astype(jnp.float32)
    units = normalized_rows(source, ffn_gain).astype(jnp.bfloat16)
    flat = routes.reshape(-1)
    hits = (flat[:, None] == jnp.arange(EXPERTS, dtype=jnp.int32)[None, :]).astype(jnp.float32)
    ranks = jnp.cumsum(hits, axis=0) - hits
    placed = hits[:, :, None] * (
        ranks[:, :, None] == jnp.arange(CAP, dtype=jnp.float32)[None, None, :]
    ).astype(jnp.float32)
    placed = placed.reshape(token_total, TOPK, EXPERTS * CAP)
    combine = jnp.einsum("tk,tks->ts", gate_weights, placed)
    all_units, all_routes = (
        lax.all_gather(units, "ep", axis=0, tiled=True),
        lax.all_gather(routes, "ep", axis=0, tiled=True),
    )
    mine = lax.axis_index("ep") // split
    route_blocks = all_routes.reshape(-1, token_total * TOPK)
    senders = route_blocks.shape[0]
    mine_hits = (route_blocks == mine).astype(jnp.float32)
    mine_ranks = jnp.cumsum(mine_hits, axis=1) - mine_hits
    picks = mine_hits[:, :, None] * (
        mine_ranks[:, :, None] == jnp.arange(CAP, dtype=jnp.float32)[None, None, :]
    ).astype(jnp.float32)
    picks = jnp.sum(picks.reshape(senders, token_total, TOPK, CAP), axis=2).astype(jnp.bfloat16)
    received = jnp.einsum(
        "stc,std->scd",
        picks,
        all_units.reshape(senders, token_total, width),
        preferred_element_type=jnp.float32,
    ).astype(jnp.bfloat16)
    senders = received.shape[0]
    count = received.shape[1]
    rows = received.reshape(senders * count, width)
    proj = jnp.dot(rows, w_in, preferred_element_type=jnp.float32)
    act = (jax.nn.silu(proj[:, :hid_units]) * proj[:, hid_units:]).astype(jnp.bfloat16)
    partial_value = jnp.dot(act, w_out, preferred_element_type=jnp.float32).astype(jnp.bfloat16)
    returned = lax.all_to_all(
        partial_value.reshape(senders, count, width), "ep", split_axis=0, concat_axis=0, tiled=True
    )
    summed = jnp.sum(
        returned.reshape(EXPERTS, split, CAP, width).astype(jnp.float32), axis=1
    ).reshape(EXPERTS * CAP, width)
    moe = jnp.dot(combine, summed, precision=lax.Precision.HIGHEST)
    mixed = source + moe
    residual_after_expert = mixed.astype(jnp.bfloat16)
    normed = normalized_rows(mixed, attn_gain).astype(jnp.bfloat16)
    lat_width = kv_down.shape[1]
    compressed_rows = jnp.dot(
        normed,
        lax.all_gather(kv_down, "ep", axis=0, tiled=True),
        preferred_element_type=jnp.float32,
    )
    reach = ancestors(parents)
    depth = jnp.sum(reach, axis=-1) - 1.0
    token_position = (lengths[:, None].astype(jnp.float32) + depth).reshape(token_total)
    latent_rows = normalized_rows(compressed_rows[:, :KEY_VALUE_RANK], latent_norm_gain)
    draft_latent_entries = jnp.concatenate(
        [latent_rows, apply_rotation(compressed_rows[:, KEY_VALUE_RANK:], token_position)], axis=-1
    ).astype(jnp.bfloat16)
    req_count = cache.shape[0]
    ctx_slots = cache.shape[1]
    head_rows = queries.shape[1]
    query_blocks = queries.reshape(req_count, NODES * head_rows, lat_width)
    draft_node_keys = draft_latent_entries.reshape(req_count, NODES, lat_width)
    ctx_scores = (
        jnp.einsum("rqc,rkc->rqk", query_blocks, cache, preferred_element_type=jnp.float32)
        * softmax_scale
    )
    valid = jnp.arange(ctx_slots, dtype=jnp.int32)[None, None, :] < lengths[:, None, None]
    ctx_scores = jnp.where(valid, ctx_scores, -jnp.inf)
    own_scores = (
        jnp.einsum(
            "rqc,rkc->rqk", query_blocks, draft_node_keys, preferred_element_type=jnp.float32
        )
        * softmax_scale
    )
    allowed = jnp.repeat(reach, head_rows, axis=1) > 0.5
    own_scores = jnp.where(allowed, own_scores, -jnp.inf)
    top = jnp.maximum(
        jnp.max(ctx_scores, axis=-1, keepdims=True), jnp.max(own_scores, axis=-1, keepdims=True)
    )
    ctx_exp = jnp.exp(ctx_scores - top)
    own_exp = jnp.exp(own_scores - top)
    total = jnp.sum(ctx_exp, axis=-1, keepdims=True) + jnp.sum(own_exp, axis=-1, keepdims=True)
    context_probabilities = (ctx_exp / total).astype(jnp.bfloat16)
    self_probabilities = (own_exp / total).astype(jnp.bfloat16)
    final_result = jnp.einsum(
        "swd,sdn->swn",
        context_probabilities,
        cache[:, :, :KEY_VALUE_RANK],
        preferred_element_type=jnp.float32,
    )
    final_result = final_result + jnp.einsum(
        "swd,sdn->swn",
        self_probabilities,
        draft_node_keys[:, :, :KEY_VALUE_RANK],
        preferred_element_type=jnp.float32,
    )
    attention_output = final_result.astype(jnp.bfloat16).reshape(
        token_total, head_rows, KEY_VALUE_RANK
    )
    return (residual_after_expert, draft_latent_entries, attention_output)


def solution(mesh):
    placed = (
        P(("group", "ep"), None),
        P(),
        P(),
        P(),
        P(("group", "ep"), None),
        P(("group", "ep"), None),
        P("ep", None, None),
        P("ep", None, None),
        P("ep", None),
        P(("group", "ep"), None),
        P(("group", "ep")),
        P(("group", "ep"), None, None),
        P(("group", "ep"), None, None),
    )
    return jax.shard_map(
        local,
        mesh=mesh,
        in_specs=placed,
        out_specs=(
            P(("group", "ep"), None),
            P(("group", "ep"), None),
            P(("group", "ep"), None, None),
        ),
        check_vma=False,
    )
```

profile of v0, /device:TPU:15, one launch (start us, length us, event | category | flops | bytes accessed | tf_op | source)
XLA Modules:
  0.0 238.2 jit_solution(1739094594569856654)
XLA Ops:
  7.2 1.3 fusion.24
  8.5 1.8 fusion.26
  10.3 0.7 all-gather.6.cloned.1.call-update
  11.0 15.8 %all-gather = s32[16,16,2]{1,2,0:T(2,128)S(1)} all-gather(s32[1,16,2]{1,2,0:T(2,128)} %bitcast.87), channel_id=1, replica_groups=mesh['group'=2,'ep'=16] {'ep'}, dimensions={0}, use_global_device_ids=true | all-gather | bytes 2176 | tf_op jit(solution)/shard_map/all_gather | solution.py:82
  27.0 0.3 copy.47
  27.2 1.9 fusion.58
  29.1 0.1 reduce.10
  29.4 30.2 %all-gather.4.cloned.1.call-done = bf16[256,7168]{1,0:T(8,128)(2,1)} async-done(((bf16[16,7168]{1,0:T(8,128)(2,1)}), bf16[256,7168]{1,0:T(8,128)(2,1)}) %all-gather.4.cloned.1.call-update) | async-done | bytes 3670032 | tf_op jit(solution)/shard_map/all_gather | solution.py:81
  59.6 5.0 %convolution_convert_fusion = bf16[16,9,7168]{2,1,0:T(8,128)(2,1)} fusion(bf16[16,16,7168]{2,1,0:T(8,128)(2,1)} %bitcast.80, bf16[16,16,9]{1,0,2:T(8,128)(2,1)S(1)} %select_reduce_fusion), kind=kOutput, calls=%fused_computation.2 | convolution fusion | flops 34062336 | bytes 5739008 | tf_op jit(solution)/shard_map/stc,std->scd/dot_general | solution.py:93
  64.6 3.5 %reshape.466 = bf16[144,7168]{1,0:T(8,128)(2,1)} reshape(bf16[16,9,7168]{2,1,0:T(8,128)(2,1)} %convolution_convert_fusion) | data formatting | bytes 4128768 | tf_op jit(solution)/shard_map/reshape | solution.py:101
  68.1 8.6 %fusion = f32[144,1024]{1,0:T(8,128)S(1)} fusion(bf16[144,7168]{1,0:T(8,128)(2,1)} %reshape.466, bf16[1,7168,1024]{2,1,0:T(8,128)(2,1)} %param.19), kind=kOutput, calls=%fused_computation | convolution fusion | flops 2113929216 | bytes 17334272 | tf_op jit(solution)/shard_map/dot_general | solution.py:102
  76.7 5.7 %convolution_convert_fusion.1 = bf16[144,7168]{1,0:T(8,128)(2,1)} fusion(bf16[1,512,7168]{2,1,0:T(8,128)(2,1)} %param.20, f32[144,1024]{1,0:T(8,128)S(1)} %fusion), kind=kOutput, calls=%fused_computation.3 | convolution fusion | flops 1058439168 | bytes 9994240 | tf_op jit(solution)/shard_map/dot_general | solution.py:104
  82.4 3.5 %reshape.467 = bf16[16,9,7168]{2,1,0:T(8,128)(2,1)} reshape(bf16[144,7168]{1,0:T(8,128)(2,1)} %convolution_convert_fusion.1) | data formatting | bytes 4128768 | tf_op jit(solution)/shard_map/reshape | solution.py:106
  85.9 5.1 %all-to-all-start = ((bf16[16,9,7168]{2,1,0:T(8,128)(2,1)}), bf16[16,9,7168]{2,1,0:T(8,128)(2,1)}, u32[]{:S(2)}, u32[]{:S(2)}) async-start(bf16[16,9,7168]{2,1,0:T(8,128)(2,1)} %reshape.467), calls=%async_computation | async-start | bytes 7340032 | tf_op jit(solution)/shard_map/all_to_all | solution.py:105
  92.7 0.1 convolution_minimum_fusion.3
  92.8 0.1 convolution_minimum_fusion.2
  93.0 0.1 convolution_minimum_fusion.1
  93.1 0.3 fusion.56
  93.5 0.5 multiply_power_fusion
  94.0 0.6 add_add_fusion
  94.6 0.1 fusion.39
  94.7 7.1 %fusion.2 = (f32[2048]{0:T(1024)S(1)}, f32[2048,1024]{0,1:T(8,128)}) fusion(pred[1024]{0:T(1024)(128)(4,1)S(1)} %iota_compare_fusion.2, bf16[1,1024,576]{1,2,0:T(8,128)(2,1)} %param.25, bf16[16,128,576]{1,2,0:T(8,128)(2,1)S(1)} %copy-done), kind=kOutput, calls=%fused_computation.8 | convolution fusion | flops 2422208512 | bytes 11936768 | tf_op jit(solution)/shard_map/rqc,rkc->rqk/dot_general | solution.py:134
  101.8 107.2 %all-to-all-done = bf16[16,9,7168]{2,1,0:T(8,128)(2,1)} async-done(((bf16[16,9,7168]{2,1,0:T(8,128)(2,1)}), bf16[16,9,7168]{2,1,0:T(8,128)(2,1)}, u32[]{:S(2)}, u32[]{:S(2)}) %all-to-all-start) | async-done | bytes 2064416 | tf_op jit(solution)/shard_map/all_to_all | solution.py:105
  209.0 4.1 %convert_reduce_fusion = f32[4,9,7168]{2,1,0:T(8,128)} fusion(bf16[16,9,7168]{2,1,0:T(8,128)(2,1)} %all-to-all-done), kind=kLoop, calls=%fused_computation.9 | loop fusion | flops 1806336 | bytes 3096576 | tf_op jit(solution)/shard_map/reduce_sum | solution.py:108
  213.2 1.6 reshape.468
  214.8 2.6 %multiply_reduce_fusion = (f32[16]{0:T(128)S(1)}, bf16[16,7168]{1,0:T(8,128)(2,1)}, f32[16,7168]{1,0:T(8,128)}) fusion(f32[16,36]{1,0:T(8,128)S(1)} %bitcast.86, f32[36,7168]{1,0:T(8,128)S(1)} %reshape.468, bf16[16,7168]{1,0:T(8,128)(2,1)} %param.13), kind=kOutput, calls=%fused_computation.36 | convolution fusion | flops 50118640 | bytes 1952064 | tf_op jit(solution)/shard_map/dot_general | solution.py:111
  217.5 5.2 %fusion.28 = f32[16,576]{1,0:T(8,128)S(1)} fusion(bf16[7168,576]{1,0:T(8,128)(2,1)} %all-gather.6.cloned.1.call-done, f32[16,7168]{1,0:T(8,128)} %get-tuple-element.7, f32[7168]{0:T(1024)S(1)} %copy-done.1, f32[16]{0:T(128)S(1)} %add_rsqrt_fusion.1), kind=kOutput, calls=%fused_computation.39 | convolution fusion | flops 132464640 | bytes 8781888 | tf_op jit(solution)/shard_map/dot_general | solution.py:116
  222.7 0.1 multiply_reduce_fusion.1
  223.3 0.5 fusion.57
  223.8 2.5 %fusion.4 = f32[2048]{0:T(1024)S(1)} fusion(f32[2048,1024]{0,1:T(8,128)S(1)} %bitcast.79, f32[2048]{0:T(1024)S(1)} %max.8, pred[1024]{0:T(1024)(128)(4,1)S(1)} %copy-done.6), kind=kLoop, calls=%fused_computation.11 | loop fusion | flops 8386560 | bytes 8406016 | tf_op jit(solution)/shard_map/reduce_sum | solution.py:152
  226.4 2.9 %fusion.5 = f32[2048,512]{1,0:T(8,128)S(1)} fusion(f32[2048,1024]{0,1:T(8,128)S(1)} %bitcast.79, f32[2048]{0:T(1024)S(1)} %add.107, f32[2048]{0:T(1024)S(1)} %max.8, pred[1024]{0:T(1024)(128)(4,1)S(1)} %copy-done.6, bf16[1,1024,576]{1,2,0:T(8,128)(2,1)S(1)} %copy-done.11), kind=kOutput, calls=%fused_computation.13 | convolution fusion | flops 2157969408 | bytes 13648896 | tf_op jit(solution)/shard_map/swd,sdn->swn/dot_general | solution.py:155
  229.3 2.1 add_convert_fusion
  (64 shorter events, 2.0 us)
Async XLA Ops:
  7.2 87.6 %copy-start = (bf16[16,128,576]{1,2,0:T(8,128)(2,1)S(1)}, bf16[16,128,576]{1,2,0:T(8,128)(2,1)}, u32[]{:S(2)}) copy-start(bf16[16,128,576]{1,2,0:T(8,128)(2,1)} %param.24) | copy-start | bytes 7077892
  7.2 52.4 %all-gather.4.cloned.1.call-start = ((), (), s32[]{:S(2)}) async-start(), calls=%async_computation.1 | async-start | bytes 3899392 | tf_op jit(solution)/shard_map/all_gather | solution.py:81
  10.3 207.1 %all-gather.6.cloned.1.call-start = ((), (), s32[]{:S(2)}) async-start(), calls=%async_computation.2 | async-start | bytes 9748480 | tf_op jit(solution)/shard_map/all_gather | solution.py:118
  85.9 5.1 %copy-start.3 = (s32[16,2]{0,1:T(2,128)S(1)}, s32[16,2]{0,1:T(2,128)}, u32[]{:S(2)}) copy-start(s32[16,2]{0,1:T(2,128)} %param.17) | copy-start | bytes 388
  85.9 5.2 %copy-start.7 = (f32[16,2]{0,1:T(2,128)S(1)}, f32[16,2]{0,1:T(2,128)}, u32[]{:S(2)}) copy-start(f32[16,2]{0,1:T(2,128)} %param.18) | copy-start | bytes 388
  85.9 6.7 %copy-start.8 = (s32[1,16]{1,0:T(1,128)S(1)}, s32[1,16]{1,0:T(1,128)}, u32[]{:S(2)}) copy-start(s32[1,16]{1,0:T(1,128)} %param.22) | copy-start | bytes 196
  85.9 123.1 %all-to-all-start = ((bf16[16,9,7168]{2,1,0:T(8,128)(2,1)}), bf16[16,9,7168]{2,1,0:T(8,128)(2,1)}, u32[]{:S(2)}, u32[]{:S(2)}) async-start(bf16[16,9,7168]{2,1,0:T(8,128)(2,1)} %reshape.467), calls=%async_computation | async-start | bytes 7340032 | tf_op jit(solution)/shard_map/all_to_all | solution.py:105
  94.0 7.8 %copy-start.5 = (pred[1024]{0:T(1024)(128)(4,1)}, pred[1024]{0:T(1024)(128)(4,1)S(1)}, u32[]{:S(2)}) copy-start(pred[1024]{0:T(1024)(128)(4,1)S(1)} %iota_compare_fusion.2) | copy-start | bytes 3076
  101.8 115.6 %copy-start.1 = (f32[7168]{0:T(1024)S(1)}, f32[7168]{0:T(1024)}, u32[]{:S(2)}) copy-start(f32[7168]{0:T(1024)} %param.15) | copy-start | bytes 86020
  217.4 6.3 %slice-start = ((s8[8388608]{0:T(1024)(128)(4,1)}), s8[4194304]{0:T(1024)(128)(4,1)S(1)}, s32[]{:S(2)}) async-start(s8[8388608]{0:T(1024)(128)(4,1)} %bitcast.78), calls=%async_computation.3 | async-start | bytes 8388608
  217.4 5.4 %copy-start.9 = (f32[32]{0:T(128)S(1)}, f32[32]{0:T(128)}, u32[]{:S(2)}) copy-start(f32[32]{0:T(128)} %multiply_power_fusion) | copy-start | bytes 388
  217.5 5.4 %copy-start.10 = (f32[16]{0:T(128)S(1)}, f32[16]{0:T(128)}, u32[]{:S(2)}) copy-start(f32[16]{0:T(128)} %add_add_fusion) | copy-start | bytes 196
  217.5 5.5 %copy-start.4 = (f32[512]{0:T(512)S(1)}, f32[512]{0:T(512)}, u32[]{:S(2)}) copy-start(f32[512]{0:T(512)} %param.16) | copy-start | bytes 6148
  217.5 6.3 %slice-start.1 = ((s8[8388608]{0:T(1024)(128)(4,1)}), s8[4194304]{0:T(1024)(128)(4,1)S(1)}, s32[]{:S(2)}) async-start(s8[8388608]{0:T(1024)(128)(4,1)} %bitcast.78), calls=%async_computation.4 | async-start | bytes 8388608
  217.5 6.3 %copy-start.6 = (pred[1024]{0:T(1024)(128)(4,1)S(1)}, pred[1024]{0:T(1024)(128)(4,1)}, u32[]{:S(2)}) copy-start(pred[1024]{0:T(1024)(128)(4,1)} %copy-done.5) | copy-start | bytes 3076
  223.2 3.1 %copy-start.2 = (bf16[16,576]{1,0:T(8,128)(2,1)}, bf16[16,576]{1,0:T(8,128)(2,1)S(1)}, u32[]{:S(2)}) copy-start(bf16[16,576]{1,0:T(8,128)(2,1)S(1)} %pad_maximum_fusion) | copy-start | bytes 55300
  223.8 2.6 %copy-start.11 = (bf16[1,1024,576]{1,2,0:T(8,128)(2,1)S(1)}, bf16[1,1024,576]{1,2,0:T(8,128)(2,1)}, u32[]{:S(2)}) copy-start(bf16[1,1024,576]{1,2,0:T(8,128)(2,1)} %param.25) | copy-start | bytes 3538948
Sparse Core Ops, SparseCore 0:
  10.9 48.6 all-gather.3
  61.9 129.2 all-gather.5
where the time goes:
time: 239 us; the launch traced here: 238 us
  waiting for transfers between devices  138 us (58%)
  matrix products  40.4 us (17%)
  blocking collectives  15.8 us (7%)
  between operations  15 us (6%)
  other arithmetic  13.6 us (6%)
  local copies, waits for them, and re-layouts  10.1 us (4%)
  starting transfers between devices  5.15 us (2%)
    all_to_all x1, waiting for transfers between devices, local(): lax.all_to_all(partial_value.reshape(senders, count, width), 'ep', split_...  107 us
    all_gather x1, waiting for transfers between devices, local(): lax.all_gather(units, 'ep', axis=0, tiled=True)  30.2 us
    all_gather x1, blocking collectives, local(): lax.all_gather(routes, 'ep', axis=0, tiled=True)  15.8 us
    dot_general x1, matrix products, local(): proj = jnp.dot(rows, w_in, preferred_element_type=jnp.float32)  8.58 us
    dot_general x1, matrix products, local(): jnp.einsum('rqc,rkc->rqk', query_blocks, cache, preferred_element_type=jn...  7.07 us
    dot_general x1, matrix products, local(): jnp.dot(act, w_out, preferred_element_type=jnp.float32).astype(jnp.bfloat16)  5.68 us
    dot_general x1, matrix products, local(): jnp.dot(normed, lax.all_gather(kv_down, 'ep', axis=0, tiled=True), prefer...  5.22 us
    all_to_all x1, starting transfers between devices, local(): lax.all_to_all(partial_value.reshape(senders, count, width), 'ep', split_...  5.07 us
  transfers between devices with their start and end apart: 3, of which 2 were waited for; matrix products, arithmetic and copies ran while one was open for 20% of the time, Pallas kernels for 0%

commit v1 on v0

v1 whole, which is shorter than its diff:
```python
import functools

import jax
import jax.numpy as jnp
from jax import lax
from jax.experimental import pallas as pl
from jax.experimental.pallas import tpu as pltpu
from jax.sharding import PartitionSpec as P

KEY_VALUE_RANK = 512
NODES = 16
EXPERTS = 4
CAP = 9
TAIL = 128
ROWS = 40
BF = jnp.bfloat16
F32 = jnp.float32
softmax_scale = 192.0 ** (-0.5)
VMEM = 48 * 1024 * 1024


def iota(shape, dim):
    return lax.broadcasted_iota(jnp.int32, shape, dim)


def dot(a, b):
    return jnp.dot(a, b, preferred_element_type=F32)


def dot_t(a, b):
    return lax.dot_general(a, b, (((1,), (1,)), ((), ())), preferred_element_type=F32)


def params(semantics=None):
    return pltpu.CompilerParams(vmem_limit_bytes=VMEM, dimension_semantics=semantics)


def whole(shape):
    zeros = (0,) * len(shape)
    return pl.BlockSpec(shape, lambda *_: zeros)


def pack_kernel(e_ref, hidden_ref, gain_ref, routes_ref, gates_ref, *outs):
    chunks, parts = outs[:EXPERTS], outs[EXPERTS:]
    tokens, width = hidden_ref.shape
    piece = width // 8
    quarter = width // EXPERTS
    x = hidden_ref[...].astype(F32)
    scale = lax.rsqrt(jnp.mean(x * x, axis=-1, keepdims=True) + 1e-06)
    units = (x * scale * gain_ref[...]).astype(BF)
    first = jnp.broadcast_to(routes_ref[0:1, :], (8, tokens))
    second = jnp.broadcast_to(routes_ref[1:2, :], (8, tokens))
    row = iota((8, tokens), 0)
    before = (iota((tokens, tokens), 0) < iota((tokens, tokens), 1)).astype(BF)
    main, ninth = [], []
    for k in range(EXPERTS):
        expert = e_ref[0] ^ k
        hit = jnp.where((first == expert) | (second == expert), 1.0, 0.0)
        rank = dot(hit.astype(BF), before)
        main.append(jnp.where(rank == row.astype(F32), hit, 0.0))
        ninth.append(jnp.where(rank == 8.0, hit, 0.0))
    main = jnp.concatenate(main, axis=0).astype(BF)
    ninth = jnp.concatenate(ninth, axis=0)
    rows = iota(ninth.shape, 0) % 8
    picked = dot(main, units).astype(BF)
    cut = jnp.zeros((8 * EXPERTS, piece), F32)
    for j in range(8):
        cut = cut + dot(
            jnp.where(rows == j, ninth, 0.0).astype(BF), units[:, j * piece : (j + 1) * piece]
        )
    cut = cut.astype(BF)
    info = jnp.where(row == 0, first.astype(F32), second.astype(F32))
    for choice in range(2):
        gate = jnp.broadcast_to(gates_ref[choice : choice + 1, :], (8, tokens))
        for part in range(3):
            rounded = gate.astype(BF).astype(F32)
            info = jnp.where(row == 2 + 3 * choice + part, rounded, info)
            gate = gate - rounded
    spread = (iota((tokens, TAIL), 0) == iota((tokens, TAIL), 1)).astype(BF)
    tail = dot(info.astype(BF), spread).astype(BF)
    for k in range(EXPERTS):
        expert = e_ref[0] ^ k
        chunks[k][:, :width] = picked[8 * k : 8 * k + 8]
        chunks[k][:, width : width + piece] = cut[8 * k : 8 * k + 8]
        chunks[k][:, width + piece :] = tail
        start = pl.multiple_of(expert * quarter, 128)
        parts[k][...] = hidden_ref[:, pl.ds(start, quarter)]


def pack(e, hidden, gain, routes_t, gates_t):
    tokens, width = hidden.shape
    chunk = jax.ShapeDtypeStruct((8, width + width // 8 + TAIL), BF)
    part = jax.ShapeDtypeStruct((tokens, width // EXPERTS), BF)
    return pl.pallas_call(
        pack_kernel,
        out_shape=[chunk] * EXPERTS + [part] * EXPERTS,
        grid_spec=pltpu.PrefetchScalarGridSpec(
            num_scalar_prefetch=1,
            grid=(1,),
            in_specs=[
                whole(hidden.shape),
                whole(gain.shape),
                whole(routes_t.shape),
                whole(gates_t.shape),
            ],
            out_specs=[whole(chunk.shape)] * EXPERTS + [whole(part.shape)] * EXPERTS,
        ),
        compiler_params=params(),
        name="pack",
    )(e, hidden, gain, routes_t, gates_t)


def expert_kernel(split, steps, piece, hid, e_ref, *refs):
    groups = refs[:split]
    w_in, w_out, keep, send, acc, act = refs[split:]
    t = pl.program_id(0)
    width = piece * steps
    main_rows, last_rows = 32 * split, 8 * split

    @pl.when(t < steps)
    def _():
        start = pl.multiple_of(t * piece, 128)
        ext = jnp.concatenate([g[:, width : width + piece] for g in groups], axis=0)
        r = iota((last_rows, main_rows), 0)
        col = iota((last_rows, main_rows), 1)
        want = 32 * (r // 8) + 8 * (r % 8) + t
        pick = jnp.where((r % 8 < 4) & (col == want), 1.0, 0.0).astype(BF)
        last = dot(pick, ext).astype(BF)
        rows = jnp.concatenate([g[:, pl.ds(start, piece)] for g in groups] + [last], axis=0)
        term = dot(rows, w_in[0])

        @pl.when(t == 0)
        def _():
            acc[...] = term

        @pl.when(t > 0)
        def _():
            acc[...] += term

    @pl.when(t >= steps)
    def _():
        @pl.when(t == steps)
        def _():
            gate, up = acc[:, :hid], acc[:, hid:]
            act[...] = (gate / (1.0 + jnp.exp(-gate)) * up).astype(BF)

        out = dot(act[...], w_out[0])
        for r in range(split):
            mine = jnp.concatenate(
                [out[32 * r : 32 * r + 32], out[main_rows + 8 * r : main_rows + 8 * r + 8]], axis=0
            ).astype(BF)
            (send if r % 2 else keep)[r // 2, 0] = mine


def expert_slice(e, groups, w_in, w_out):
    split = len(groups)
    width, hid2 = w_in.shape[1:]
    hid = hid2 // 2
    steps = 8
    piece = width // steps
    quarter = width // EXPERTS
    out = jax.ShapeDtypeStruct((split // 2, EXPERTS, ROWS, quarter), BF)
    out_spec = pl.BlockSpec(
        (split // 2, 1, ROWS, quarter), lambda t, e: (0, jnp.maximum(t - steps, 0), 0, 0)
    )
    rows = ROWS * split
    return pl.pallas_call(
        functools.partial(expert_kernel, split, steps, piece, hid),
        out_shape=[out, out],
        grid_spec=pltpu.PrefetchScalarGridSpec(
            num_scalar_prefetch=1,
            grid=(steps + EXPERTS,),
            in_specs=[whole(g.shape) for g in groups]
            + [
                pl.BlockSpec((1, piece, hid2), lambda t, e: (0, jnp.minimum(t, steps - 1), 0)),
                pl.BlockSpec(
                    (1, hid, quarter), lambda t, e: (0, 0, e[0] ^ jnp.maximum(t - steps, 0))
                ),
            ],
            out_specs=[out_spec, out_spec],
            scratch_shapes=[pltpu.VMEM((rows, hid2), F32), pltpu.VMEM((rows, hid), BF)],
        ),
        compiler_params=params(("arbitrary",)),
        cost_estimate=pl.CostEstimate(
            flops=6 * rows * width * hid, bytes_accessed=6 * width * hid, transcendentals=rows * hid
        ),
        name="experts",
    )(e, *groups, w_in, w_out)


def combine_kernel(split, tokens, e_ref, *refs):
    outs_e, hid = refs[:EXPERTS], refs[EXPERTS : 2 * EXPERTS]
    info_ref, gain_ref = refs[2 * EXPERTS : 2 * EXPERTS + 2]
    kvs = refs[2 * EXPERTS + 2 : 2 * EXPERTS + 2 + split]
    rest = refs[2 * EXPERTS + 2 + split :]
    sums, residuals = rest[:EXPERTS], rest[EXPERTS : 2 * EXPERTS]
    kv_ref, sem = rest[2 * EXPERTS :]
    part = kvs[0].shape[0]
    lat = kvs[0].shape[1]
    copies = []
    for r in range(split):
        place = pl.multiple_of((e_ref[1] ^ r) * part, 16)
        copies.append(
            pltpu.make_async_copy(kvs[r], kv_ref.at[pl.ds(place, part), :], sem.at[r])
        )
        copies[-1].start()
    one = (iota((tokens, TAIL), 0) == iota((tokens, TAIL), 1)).astype(BF)
    info = dot_t(one, info_ref[...])
    earlier = (iota((tokens, tokens), 1) < iota((tokens, tokens), 0)).astype(BF)
    lane = iota((tokens, ROWS), 1).astype(F32)
    hits = []
    for k in range(EXPERTS):
        expert = (e_ref[0] ^ k).astype(F32)
        hits.append(jnp.where(info == expert, 1.0, 0.0))
    moe = None
    for k in range(EXPERTS):
        blocks = [[], [], []]
        for s in range(EXPERTS):
            h0 = hits[k][:, 8 * s : 8 * s + 1]
            h1 = hits[k][:, 8 * s + 1 : 8 * s + 2]
            hit = jnp.broadcast_to(h0 + h1, (tokens, ROWS))
            rank = dot(earlier, hit.astype(BF))
            line = s ^ k
            want = jnp.where(rank < 8.0, rank + 8.0 * line, 32.0 + line)
            chosen = (lane == want) & (hit > 0.5)
            for p in range(3):
                g0 = info[:, 8 * s + 2 + p : 8 * s + 3 + p]
                g1 = info[:, 8 * s + 5 + p : 8 * s + 6 + p]
                gate = jnp.broadcast_to(h0 * g0 + h1 * g1, (tokens, ROWS))
                blocks[p].append(jnp.where(chosen, gate, 0.0))
        weights = jnp.concatenate(blocks[0] + blocks[1] + blocks[2], axis=0).astype(BF)
        term = dot(weights, outs_e[k][...])
        moe = term if moe is None else moe + term
    total = EXPERTS * tokens
    moe = moe[:total] + moe[total : 2 * total] + moe[2 * total :]
    mixed = jnp.concatenate([h[...].astype(F32) for h in hid], axis=0) + moe
    for s in range(EXPERTS):
        residuals[s][...] = mixed[s * tokens : (s + 1) * tokens].astype(BF)
    square = jnp.sum(mixed * mixed, axis=-1, keepdims=True)
    scaled = (mixed * gain_ref[...]).astype(BF)
    for c in copies:
        c.wait()
    rows = dot(scaled, kv_ref[...])
    for s in range(EXPERTS):
        sums[s][:, :lat] = rows[s * tokens : (s + 1) * tokens]
        sums[s][:, lat:] = jnp.broadcast_to(
            square[s * tokens : (s + 1) * tokens], (tokens, sums[s].shape[1] - lat)
        )


def combine(place, outs_e, hid, line, gain, kvs):
    split = len(kvs)
    tokens, quarter = hid[0].shape
    part, lat = kvs[0].shape
    padded = (lat // 128 + 1) * 128
    tail_block = line.shape[1] // TAIL - 1
    sums = jax.ShapeDtypeStruct((tokens, padded), F32)
    residual = jax.ShapeDtypeStruct((tokens, quarter), BF)
    return pl.pallas_call(
        functools.partial(combine_kernel, split, tokens),
        out_shape=[sums] * EXPERTS + [residual] * EXPERTS,
        grid_spec=pltpu.PrefetchScalarGridSpec(
            num_scalar_prefetch=1,
            grid=(1,),
            in_specs=[whole(o.shape) for o in outs_e]
            + [whole(h.shape) for h in hid]
            + [
                pl.BlockSpec((line.shape[0], TAIL), lambda t, e: (0, tail_block)),
                pl.BlockSpec((1, quarter), lambda t, e: (0, e[0])),
            ]
            + [pl.BlockSpec(memory_space=pl.ANY)] * split,
            out_specs=[whole(sums.shape)] * EXPERTS + [whole(residual.shape)] * EXPERTS,
            scratch_shapes=[
                pltpu.VMEM((split * part, lat), BF),
                pltpu.SemaphoreType.DMA((split,)),
            ],
        ),
        compiler_params=params(),
        name="combine",
    )(place, *outs_e, *hid, line, gain, *kvs)


def cached_kernel(length_ref, q_ref, cache_ref, out_ref, top_ref, sum_ref, keys_ref):
    nodes, lat, heads = q_ref.shape
    ctx = cache_ref.shape[2]

    @pl.when(pl.program_id(0) == 0)
    def _():
        keys_ref[...] = cache_ref[0].T

    q = jnp.concatenate([q_ref[i] for i in range(nodes)], axis=1)
    scores = dot(keys_ref[...], q) * softmax_scale
    valid = iota((ctx, nodes * heads), 0) < length_ref[0]
    scores = jnp.where(valid, scores, -jnp.inf)
    top = jnp.max(scores, axis=0, keepdims=True)
    weight = jnp.exp(scores - top)
    total = jnp.sum(weight, axis=0, keepdims=True)
    out = dot(cache_ref[0, :KEY_VALUE_RANK, :], weight.astype(BF)) * (1.0 / total)
    for i in range(nodes):
        span = slice(i * heads, (i + 1) * heads)
        out_ref[i] = out[:, span].T.astype(out_ref.dtype)
        top_ref[i] = top[:, span]
        sum_ref[i] = total[:, span]


def cached_attention(lengths, q_t, cache_t, first, count, per=2):
    tokens, lat, heads = q_t.shape
    ctx = cache_t.shape[2]
    row = jax.ShapeDtypeStruct((count, 1, heads), F32)
    begin = first // per
    return pl.pallas_call(
        cached_kernel,
        out_shape=[jax.ShapeDtypeStruct((count, heads, KEY_VALUE_RANK), BF), row, row],
        grid_spec=pltpu.PrefetchScalarGridSpec(
            num_scalar_prefetch=1,
            grid=(count // per,),
            in_specs=[
                pl.BlockSpec((per, lat, heads), lambda t, n: (t + begin, 0, 0)),
                whole(cache_t.shape),
            ],
            out_specs=[
                pl.BlockSpec((per, heads, KEY_VALUE_RANK), lambda t, n: (t, 0, 0)),
                pl.BlockSpec((per, 1, heads), lambda t, n: (t, 0, 0)),
                pl.BlockSpec((per, 1, heads), lambda t, n: (t, 0, 0)),
            ],
            scratch_shapes=[pltpu.VMEM((ctx, lat), BF)],
        ),
        compiler_params=params(("arbitrary",)),
        cost_estimate=pl.CostEstimate(
            flops=2 * count * heads * ctx * (lat + KEY_VALUE_RANK),
            bytes_accessed=2 * count * heads * (lat + KEY_VALUE_RANK),
            transcendentals=count * heads * ctx,
        ),
        name="cached",
    )(lengths, q_t, cache_t)


def final_kernel(width, *refs):
    sums = refs[:EXPERTS]
    gain_ref, turn_ref, allow_ref, q_ref, ctx_ref, top_ref, sum_ref = refs[EXPERTS : EXPERTS + 7]
    entry_ref, out_ref, keys_ref = refs[EXPERTS + 7 :]
    nodes, lat, heads = q_ref.shape

    @pl.when(pl.program_id(0) == 0)
    def _():
        raw = sums[0][...] + sums[1][...] + sums[2][...] + sums[3][...]
        scale = lax.rsqrt(raw[:, lat : lat + 1] / width + 1e-06)
        raw = raw * scale
        head = raw[:, :KEY_VALUE_RANK]
        head = head * lax.rsqrt(jnp.mean(head * head, axis=-1, keepdims=True) + 1e-06)
        head = head * gain_ref[...]
        tail = raw[:, KEY_VALUE_RANK:]
        half = (lat - KEY_VALUE_RANK) // 2
        lanes = tail.shape[1]
        tail = (
            tail * turn_ref[0]
            + pltpu.roll(tail, lanes - half, 1) * turn_ref[1]
            + pltpu.roll(tail, half, 1) * turn_ref[2]
        )
        entries = jnp.concatenate([head, tail], axis=1).astype(BF)[:, :lat]
        entry_ref[...] = entries
        keys_ref[...] = entries

    keys = keys_ref[...]
    count = keys.shape[0]
    for i in range(nodes):
        scores = dot(keys, q_ref[i]) * softmax_scale
        scores = jnp.where(allow_ref[i] > 0.5, scores, -jnp.inf)
        old = top_ref[i]
        top = jnp.maximum(old, jnp.max(scores, axis=0, keepdims=True))
        weight = jnp.exp(scores - top)
        share = sum_ref[i] * jnp.exp(old - top)
        scale = 1.0 / (share + jnp.sum(weight, axis=0, keepdims=True))
        both = jnp.concatenate(
            [weight * scale, jnp.broadcast_to(share * scale, (8, heads))], axis=0
        ).T
        out = ctx_ref[i].astype(F32) * both[:, count : count + 1]
        out = out + dot(both[:, :count].astype(BF), keys[:, :KEY_VALUE_RANK])
        out_ref[i] = out.astype(BF)


def final_attention(width, sums, gain, turn, allow, q_t, ctx_out, top, total, per=4):
    tokens, lat, heads = q_t.shape
    row = pl.BlockSpec((per, 1, heads), lambda t: (t, 0, 0))
    wide = pl.BlockSpec((per, heads, KEY_VALUE_RANK), lambda t: (t, 0, 0))
    return pl.pallas_call(
        functools.partial(final_kernel, width),
        out_shape=[
            jax.ShapeDtypeStruct((tokens, lat), BF),
            jax.ShapeDtypeStruct((tokens, heads, KEY_VALUE_RANK), BF),
        ],
        grid=(tokens // per,),
        in_specs=[whole(s.shape) for s in sums]
        + [
            whole(gain.shape),
            whole(turn.shape),
            pl.BlockSpec((per, NODES, heads), lambda t: (t, 0, 0)),
            pl.BlockSpec((per, lat, heads), lambda t: (t, 0, 0)),
            wide,
            row,
            row,
        ],
        out_specs=[whole((tokens, lat)), wide],
        scratch_shapes=[pltpu.VMEM((tokens, lat), BF)],
        compiler_params=params(("arbitrary",)),
        name="final",
    )(*sums, gain, turn, allow, q_t, ctx_out, top, total)


def place_kernel(e_ref, *refs):
    out_ref = refs[EXPERTS]
    quarter = refs[0].shape[1]
    for k in range(EXPERTS):
        start = pl.multiple_of((e_ref[0] ^ k) * quarter, 128)
        out_ref[:, pl.ds(start, quarter)] = refs[k][...]


def place_quarters(place, parts):
    tokens, quarter = parts[0].shape
    return pl.pallas_call(
        place_kernel,
        out_shape=jax.ShapeDtypeStruct((tokens, EXPERTS * quarter), BF),
        grid_spec=pltpu.PrefetchScalarGridSpec(
            num_scalar_prefetch=1,
            grid=(1,),
            in_specs=[whole(p.shape) for p in parts],
            out_specs=whole((tokens, EXPERTS * quarter)),
        ),
        compiler_params=params(),
        name="place",
    )(place, *parts)


def tree(parents, lengths, rank, lat):
    count = parents.shape[1]
    link = (parents[0][:, None] == jnp.arange(count, dtype=jnp.int32)[None, :]).astype(F32)
    reach = jnp.eye(count, dtype=F32) + link
    for _ in range(max(1, (count - 1).bit_length())):
        reach = jnp.minimum(jnp.dot(reach, reach, precision=lax.Precision.HIGHEST), 1.0)
    depth = jnp.sum(reach, axis=-1) - 1.0
    position = lengths.astype(F32) + depth
    half = (lat - rank) // 2
    index = jnp.arange(half, dtype=F32)
    inverse = 10000.0 ** (-2.0 * index / (2 * half))
    angle = position[:, None] * inverse[None, :]
    c, s = jnp.cos(angle), jnp.sin(angle)
    gap = jnp.zeros((count, 128 - 2 * half), F32)
    none = jnp.zeros_like(s)
    turn = jnp.stack(
        [
            jnp.concatenate([c, c, gap], axis=1),
            jnp.concatenate([-s, none, gap], axis=1),
            jnp.concatenate([none, s, gap], axis=1),
        ]
    )
    return reach, turn


def local(
    hidden,
    ffn_gain,
    attn_gain,
    latent_norm_gain,
    routes,
    gate_weights,
    expert_in,
    expert_down,
    kv_down,
    parents,
    lengths,
    queries,
    cache,
):
    size = lax.axis_size("ep")
    split = size // EXPERTS
    bits = [1 << b for b in range(split.bit_length() - 1)]
    width = hidden.shape[1]
    lat = kv_down.shape[1]
    heads = queries.shape[1]
    index = lax.axis_index("ep")
    place = jnp.stack([index // split, index % split]).astype(jnp.int32)

    def swap(x, bit):
        return lax.ppermute(x, "ep", [(i, i ^ bit) for i in range(size)])

    packed = pack(place, hidden, ffn_gain[None], routes.T, gate_weights.T)
    chunks, quarters = packed[:EXPERTS], packed[EXPERTS:]
    line = [chunks[0]] + [swap(chunks[k], k * split) for k in range(1, EXPERTS)]
    line = jnp.concatenate(line, axis=0)
    groups = {0: line}
    for bit in reversed(bits):
        for r in sorted(groups):
            groups[r ^ bit] = swap(groups[r], bit)
    groups = [groups[r] for r in range(split)]
    kvs = {0: kv_down}
    for bit in reversed(bits):
        for r in sorted(kvs):
            kvs[r ^ bit] = swap(kvs[r], bit)
    kvs = [kvs[r] for r in range(split)]
    own_quarters = [quarters[0]] + [swap(quarters[k], k * split) for k in range(1, EXPERTS)]

    q_t = jnp.transpose(queries, (0, 2, 1))
    cache_t = jnp.transpose(cache, (0, 2, 1))
    ctx_out, top, total = cached_attention(lengths, q_t, cache_t, 0, queries.shape[0])
    reach, turn = tree(parents, lengths, KEY_VALUE_RANK, lat)
    allow = jnp.broadcast_to(reach[:, :, None], reach.shape + (heads,))

    keep, send = expert_slice(place, groups, expert_in, expert_down)
    terms = [keep, swap(send, bits[0])]
    for bit in bits[1:]:
        out = sum(t[1::2].astype(F32) for t in terms).astype(BF)
        terms = [t[0::2] for t in terms] + [swap(out, bit)]
    sums = [
        sum(t[0, k].astype(F32) for t in terms).astype(BF) for k in range(EXPERTS)
    ]
    outs_e = [sums[0]] + [swap(sums[k], k * split) for k in range(1, EXPERTS)]

    mixed = combine(place, outs_e, own_quarters, line, attn_gain[None], kvs)
    rows, residuals = mixed[:EXPERTS], mixed[EXPERTS:]
    rows = [rows[0]] + [swap(rows[k], k * split) for k in range(1, EXPERTS)]
    residuals = [residuals[0]] + [swap(residuals[k], k * split) for k in range(1, EXPERTS)]
    entries, attention = final_attention(
        width, rows, latent_norm_gain[None], turn, allow, q_t, ctx_out, top, total
    )
    return (place_quarters(place, residuals), entries, attention)


def solution(mesh):
    placed = (
        P(("group", "ep"), None),
        P(),
        P(),
        P(),
        P(("group", "ep"), None),
        P(("group", "ep"), None),
        P("ep", None, None),
        P("ep", None, None),
        P("ep", None),
        P(("group", "ep"), None),
        P(("group", "ep")),
        P(("group", "ep"), None, None),
        P(("group", "ep"), None, None),
    )
    return jax.shard_map(
        local,
        mesh=mesh,
        in_specs=placed,
        out_specs=(
            P(("group", "ep"), None),
            P(("group", "ep"), None),
            P(("group", "ep"), None, None),
        ),
        check_vma=False,
    )
```

time: 239 us -> 121 us (0.51)
  the two profiles are of different devices: /device:TPU:15 before, /device:TPU:0 now
where the time goes in v1:
time: 121 us
  Pallas kernels  41 us (34%)
  waiting for transfers between devices  39.9 us (33%)
  starting transfers between devices  32.3 us (27%)
  local copies, waits for them, and re-layouts  4.94 us (4%)
  between operations  1.54 us (1%)
    ppermute x23, waiting for transfers between devices, swap(): return lax.ppermute(x, 'ep', [(i, i ^ bit) for i in range(size)])  39.9 us
    ppermute x23, starting transfers between devices, swap(): return lax.ppermute(x, 'ep', [(i, i ^ bit) for i in range(size)])  32.3 us
    pallas_call x1, Pallas kernels, expert_slice(): pl.pallas_call(functools.partial(expert_kernel, split, steps, piece, hid)...  15.2 us
    pallas_call x1, Pallas kernels, cached_attention(): pl.pallas_call(cached_kernel, out_shape=[jax.ShapeDtypeStruct((count, hea...  14.2 us
    pallas_call x1, Pallas kernels, final_attention(): pl.pallas_call(functools.partial(final_kernel, width), out_shape=[jax.Sha...  6.07 us
    unnamed x27, local copies, waits for them, and re-layouts  4.7 us
    pallas_call x1, Pallas kernels, combine(): pl.pallas_call(functools.partial(combine_kernel, split, tokens), out_shap...  3.22 us
  transfers between devices with their start and end apart: 23, of which 8 were waited for; matrix products, arithmetic and copies ran while one was open for 1% of the time, Pallas kernels for 17%

profile of v1, /device:TPU:0, one launch (start us, length us, event | category | flops | bytes accessed | tf_op | source)
XLA Modules:
  0.0 121.0 jit_solution(11643196142887127704)
XLA Ops:
  0.7 0.9 copy-done.4
  1.7 0.7 copy-done.6
  2.4 0.7 copy-done.8
  3.8 1.1 pack.1
  4.9 3.1 %collective-permute-start = (bf16[8,8192]{1,0:T(8,128)(2,1)S(1)}, bf16[8,8192]{1,0:T(8,128)(2,1)S(1)}, u32[]{:S(2)}, u32[]{:S(2)}) collective-permute-start(bf16[8,8192]{1,0:T(8,128)(2,1)S(1)} %get-tuple-element.27), channel_id=1, source_target_pairs={{0,4},{1,5},{2,6},{3,7},{4,0},{5,1},{6,2},{7,3},{8,12},{9,13},{10,... | collective-permute-start | bytes 393224 | tf_op jit(solution)/shard_map/ppermute | solution.py:484
  8.0 2.6 %collective-permute-start.1 = (bf16[8,8192]{1,0:T(8,128)(2,1)S(1)}, bf16[8,8192]{1,0:T(8,128)(2,1)S(1)}, u32[]{:S(2)}, u32[]{:S(2)}) collective-permute-start(bf16[8,8192]{1,0:T(8,128)(2,1)S(1)} %get-tuple-element.28), channel_id=1, source_target_pairs={{0,8},{1,9},{2,10},{3,11},{4,12},{5,13},{6,14},{7,15},{8,0},{9,1},... | collective-permute-start | bytes 393224 | tf_op jit(solution)/shard_map/ppermute | solution.py:484
  10.6 2.4 %collective-permute-done = bf16[8,8192]{1,0:T(8,128)(2,1)S(1)} collective-permute-done((bf16[8,8192]{1,0:T(8,128)(2,1)S(1)}, bf16[8,8192]{1,0:T(8,128)(2,1)S(1)}, u32[]{:S(2)}, u32[]{:S(2)}) %collective-permute-start) | collective-permute-done | bytes 131104 | tf_op jit(solution)/shard_map/ppermute | solution.py:484
  13.0 7.9 %collective-permute-done.1 = bf16[8,8192]{1,0:T(8,128)(2,1)S(1)} collective-permute-done((bf16[8,8192]{1,0:T(8,128)(2,1)S(1)}, bf16[8,8192]{1,0:T(8,128)(2,1)S(1)}, u32[]{:S(2)}, u32[]{:S(2)}) %collective-permute-start.1) | collective-permute-done | bytes 131104 | tf_op jit(solution)/shard_map/ppermute | solution.py:484
  20.9 1.6 %collective-permute-start.4 = (bf16[32,8192]{1,0:T(8,128)(2,1)S(1)}, bf16[32,8192]{1,0:T(8,128)(2,1)S(1)}, u32[]{:S(2)}, u32[]{:S(2)}) collective-permute-start(bf16[32,8192]{1,0:T(8,128)(2,1)S(1)} %constant_dynamic-update-slice_fusion.refs_0_.refs_8_), channel_id=1, source_target_pairs={{0,2},{1,3},{2,0},{3,1},{4,6},{5,7},{6,4},{7,5},{8,10},{9,11},{10,... | collective-permute-start | bytes 1572872 | tf_op jit(solution)/shard_map/ppermute | solution.py:484
  22.5 9.7 %collective-permute-done.4.refs_2_ = bf16[32,8192]{1,0:T(8,128)(2,1)S(1)} collective-permute-done((bf16[32,8192]{1,0:T(8,128)(2,1)S(1)}, bf16[32,8192]{1,0:T(8,128)(2,1)S(1)}, u32[]{:S(2)}, u32[]{:S(2)}) %collective-permute-start.4) | collective-permute-done | bytes 524320 | tf_op jit(solution)/shard_map/ppermute | solution.py:484
  32.2 1.9 %collective-permute-done.5.refs_3_ = bf16[32,8192]{1,0:T(8,128)(2,1)S(1)} collective-permute-done((bf16[32,8192]{1,0:T(8,128)(2,1)S(1)}, bf16[32,8192]{1,0:T(8,128)(2,1)S(1)}, u32[]{:S(2)}, u32[]{:S(2)}) %collective-permute-start.5) | collective-permute-done | bytes 524320 | tf_op jit(solution)/shard_map/ppermute | solution.py:484
  34.1 15.2 %experts.1 = (bf16[2,4,40,1792]{3,2,1,0:T(8,128)(2,1)S(1)}, bf16[2,4,40,1792]{3,2,1,0:T(8,128)(2,1)S(1)}) custom-call(s32[2]{0:T(128)S(1)} %pad_add_fusion.e_ref, bf16[32,8192]{1,0:T(8,128)(2,1)S(1)} %constant_dynamic-update-slice_fusion.refs_0_.refs_8_, bf16[32,8192]{1,0:T(8,128)(2,1)S(1)} %collective-permute-done.3.refs_1_, ...), custom_call_target="tpu_custom_call" | custom-call | flops 3523215360 | bytes 22020096 | tf_op jit(solution)/shard_map/experts/pallas_call | solution.py:167
  49.9 1.5 %collective-permute-start.15 = (bf16[448,576]{1,0:T(8,128)(2,1)S(1)}, bf16[448,576]{1,0:T(8,128)(2,1)S(1)}, u32[]{:S(2)}, u32[]{:S(2)}) collective-permute-start(bf16[448,576]{1,0:T(8,128)(2,1)S(1)} %copy-done.3), channel_id=1, source_target_pairs={{0,2},{1,3},{2,0},{3,1},{4,6},{5,7},{6,4},{7,5},{8,10},{9,11},{10,... | collective-permute-start | bytes 1548296 | tf_op jit(solution)/shard_map/ppermute | solution.py:484
  51.5 3.0 %collective-permute-start.11 = (bf16[16,1792]{1,0:T(8,128)(2,1)S(1)}, bf16[16,1792]{1,0:T(8,128)(2,1)S(1)}, u32[]{:S(2)}, u32[]{:S(2)}) collective-permute-start(bf16[16,1792]{1,0:T(8,128)(2,1)S(1)} %get-tuple-element.33), channel_id=1, source_target_pairs={{0,4},{1,5},{2,6},{3,7},{4,0},{5,1},{6,2},{7,3},{8,12},{9,13},{10,... | collective-permute-start | bytes 172040 | tf_op jit(solution)/shard_map/ppermute | solution.py:484
  54.4 1.5 %collective-permute-start.12 = (bf16[16,1792]{1,0:T(8,128)(2,1)S(1)}, bf16[16,1792]{1,0:T(8,128)(2,1)S(1)}, u32[]{:S(2)}, u32[]{:S(2)}) collective-permute-start(bf16[16,1792]{1,0:T(8,128)(2,1)S(1)} %get-tuple-element.34), channel_id=1, source_target_pairs={{0,8},{1,9},{2,10},{3,11},{4,12},{5,13},{6,14},{7,15},{8,0},{9,1},... | collective-permute-start | bytes 172040 | tf_op jit(solution)/shard_map/ppermute | solution.py:484
  58.1 14.2 %cached.1 = (bf16[16,128,512]{2,1,0:T(8,128)(2,1)S(1)}, f32[16,1,128]{2,1,0:T(1,128)S(1)}, f32[16,1,128]{2,1,0:T(1,128)S(1)}) custom-call(s32[1]{0:T(128)S(6)} %copy.20.length_ref, bf16[16,576,128]{2,1,0:T(8,128)(2,1)S(1)} %bitcast.31, bf16[1,576,1024]{2,1,0:T(8,128)(2,1)S(1)} %bitcast.38), custom_call_target="tpu_custom_call" | custom-call | flops 4563402752 | bytes 4456448 | tf_op jit(solution)/shard_map/cached/pallas_call | solution.py:311
  72.4 1.5 %collective-permute-start.13 = (bf16[16,1792]{1,0:T(8,128)(2,1)S(1)}, bf16[16,1792]{1,0:T(8,128)(2,1)S(1)}, u32[]{:S(2)}, u32[]{:S(2)}) collective-permute-start(bf16[16,1792]{1,0:T(8,128)(2,1)S(1)} %get-tuple-element.35), channel_id=1, source_target_pairs={{0,12},{1,13},{2,14},{3,15},{4,8},{5,9},{6,10},{7,11},{8,4},{9,5},... | collective-permute-start | bytes 172040 | tf_op jit(solution)/shard_map/ppermute | solution.py:484
  73.9 3.3 %collective-permute-done.7 = bf16[1,4,40,1792]{3,2,1,0:T(8,128)(2,1)S(1)} collective-permute-done((bf16[1,4,40,1792]{3,2,1,0:T(8,128)(2,1)S(1)}, bf16[1,4,40,1792]{3,2,1,0:T(8,128)(2,1)S(1)}, u32[]{:S(2)}, u32[]{:S(2)}) %collective-permute-start.7) | collective-permute-done | bytes 573472 | tf_op jit(solution)/shard_map/ppermute | solution.py:484
  77.5 3.0 %collective-permute-start.8 = (bf16[40,1792]{1,0:T(8,128)(2,1)S(1)}, bf16[40,1792]{1,0:T(8,128)(2,1)S(1)}, u32[]{:S(2)}, u32[]{:S(2)}) collective-permute-start(bf16[40,1792]{1,0:T(8,128)(2,1)S(1)} %get-tuple-element.51), channel_id=1, source_target_pairs={{0,4},{1,5},{2,6},{3,7},{4,0},{5,1},{6,2},{7,3},{8,12},{9,13},{10,... | collective-permute-start | bytes 430088 | tf_op jit(solution)/shard_map/ppermute | solution.py:484
  80.6 1.6 %collective-permute-start.9 = (bf16[40,1792]{1,0:T(8,128)(2,1)S(1)}, bf16[40,1792]{1,0:T(8,128)(2,1)S(1)}, u32[]{:S(2)}, u32[]{:S(2)}) collective-permute-start(bf16[40,1792]{1,0:T(8,128)(2,1)S(1)} %get-tuple-element.50), channel_id=1, source_target_pairs={{0,8},{1,9},{2,10},{3,11},{4,12},{5,13},{6,14},{7,15},{8,0},{9,1},... | collective-permute-start | bytes 430088 | tf_op jit(solution)/shard_map/ppermute | solution.py:484
  82.1 1.4 %collective-permute-start.10 = (bf16[40,1792]{1,0:T(8,128)(2,1)S(1)}, bf16[40,1792]{1,0:T(8,128)(2,1)S(1)}, u32[]{:S(2)}, u32[]{:S(2)}) collective-permute-start(bf16[40,1792]{1,0:T(8,128)(2,1)S(1)} %get-tuple-element.49), channel_id=1, source_target_pairs={{0,12},{1,13},{2,14},{3,15},{4,8},{5,9},{6,10},{7,11},{8,4},{9,5},... | collective-permute-start | bytes 430088 | tf_op jit(solution)/shard_map/ppermute | solution.py:484
  83.7 4.0 %collective-permute-done.8.refs_1_ = bf16[40,1792]{1,0:T(8,128)(2,1)S(1)} collective-permute-done((bf16[40,1792]{1,0:T(8,128)(2,1)S(1)}, bf16[40,1792]{1,0:T(8,128)(2,1)S(1)}, u32[]{:S(2)}, u32[]{:S(2)}) %collective-permute-start.8) | collective-permute-done | bytes 143392 | tf_op jit(solution)/shard_map/ppermute | solution.py:484
  87.8 6.5 %collective-permute-done.9.refs_2_ = bf16[40,1792]{1,0:T(8,128)(2,1)S(1)} collective-permute-done((bf16[40,1792]{1,0:T(8,128)(2,1)S(1)}, bf16[40,1792]{1,0:T(8,128)(2,1)S(1)}, u32[]{:S(2)}, u32[]{:S(2)}) %collective-permute-start.9) | collective-permute-done | bytes 143392 | tf_op jit(solution)/shard_map/ppermute | solution.py:484
  94.3 3.2 %combine.1 = (f32[16,640]{1,0:T(8,128)S(1)}, f32[16,640]{1,0:T(8,128)S(1)}, f32[16,640]{1,0:T(8,128)S(1)}, f32[16,640]{1,0:T(8,128)S(1)}, bf16[16,1792]{1,0:T(8,...) custom-call(s32[2]{0:T(128)S(1)} %pad_add_fusion.e_ref, ...), custom_call_target="tpu_custom_call" | custom-call | tf_op jit(solution)/shard_map/combine/pallas_call | solution.py:259
  97.5 3.0 %collective-permute-start.20 = (f32[16,640]{1,0:T(8,128)S(1)}, f32[16,640]{1,0:T(8,128)S(1)}, u32[]{:S(2)}, u32[]{:S(2)}) collective-permute-start(f32[16,640]{1,0:T(8,128)S(1)} %get-tuple-element.41), channel_id=1, source_target_pairs={{0,4},{1,5},{2,6},{3,7},{4,0},{5,1},{6,2},{7,3},{8,12},{9,13},{10,... | collective-permute-start | bytes 122888 | tf_op jit(solution)/shard_map/ppermute | solution.py:484
  100.6 3.4 %collective-permute-start.18 = (bf16[16,1792]{1,0:T(8,128)(2,1)S(1)}, bf16[16,1792]{1,0:T(8,128)(2,1)S(1)}, u32[]{:S(2)}, u32[]{:S(2)}) collective-permute-start(bf16[16,1792]{1,0:T(8,128)(2,1)S(1)} %get-tuple-element.38), channel_id=1, source_target_pairs={{0,8},{1,9},{2,10},{3,11},{4,12},{5,13},{6,14},{7,15},{8,0},{9,1},... | collective-permute-start | bytes 172040 | tf_op jit(solution)/shard_map/ppermute | solution.py:484
  104.0 0.9 collective-permute-start.19
  105.6 2.3 %collective-permute-start.22 = (f32[16,640]{1,0:T(8,128)S(1)}, f32[16,640]{1,0:T(8,128)S(1)}, u32[]{:S(2)}, u32[]{:S(2)}) collective-permute-start(f32[16,640]{1,0:T(8,128)S(1)} %get-tuple-element.43), channel_id=1, source_target_pairs={{0,12},{1,13},{2,14},{3,15},{4,8},{5,9},{6,10},{7,11},{8,4},{9,5},... | collective-permute-start | bytes 122888 | tf_op jit(solution)/shard_map/ppermute | solution.py:484
  107.9 4.1 %collective-permute-done.21.refs_2_ = f32[16,640]{1,0:T(8,128)S(1)} collective-permute-done((f32[16,640]{1,0:T(8,128)S(1)}, f32[16,640]{1,0:T(8,128)S(1)}, u32[]{:S(2)}, u32[]{:S(2)}) %collective-permute-start.21) | collective-permute-done | bytes 40992 | tf_op jit(solution)/shard_map/ppermute | solution.py:484
  112.1 1.6 %copy-done.2 = bf16[16,128,512]{2,1,0:T(8,128)(2,1)S(1)} copy-done((bf16[16,128,512]{2,1,0:T(8,128)(2,1)S(1)}, bf16[16,128,512]{2,1,0:T(8,128)(2,1)}, u32[]{:S(2)}) %copy-start.2) | copy-done | bytes 2097176
  113.7 6.1 %final.1 = (bf16[16,576]{1,0:T(8,128)(2,1)}, bf16[16,128,512]{2,1,0:T(8,128)(2,1)}) custom-call(f32[16,640]{1,0:T(8,128)S(1)} %get-tuple-element.40.refs_0_, f32[16,640]{1,0:T(8,128)S(1)} %collective-permute-done.20.refs_1_, f32[16,640]{1,0:T(8,128)S(1)} %collective-permute-done.21.refs_2_, f32[16,640]{1,0:T(8,128)S(1)} %collective-permute-done.22.refs_3_, ...), custom_call_target="tpu_custom_call" | custom-call | tf_op jit(solution)/shard_map/final/pallas_call | solution.py:386
  119.8 1.2 %place.1 = bf16[16,7168]{1,0:T(8,128)(2,1)} custom-call(s32[2]{0:T(128)S(1)} %pad_add_fusion.e_ref, bf16[16,1792]{1,0:T(8,128)(2,1)S(1)} %get-tuple-element.36.refs_0_, bf16[16,1792]{1,0:T(8,128)(2,1)S(1)} %collective-permute-done.17.refs_1_, bf16[16,1792]{1,0:T(8,128)(2,1)S(1)} %collective-permute-done.18.refs_2_, ...), custom_call_target="tpu_custom_call" | custom-call | tf_op jit(solution)/shard_map/place/pallas_call | solution.py:420
  (65 shorter events, 4.2 us)
Async XLA Ops:
  0.7 0.9 copy-start.4
  4.9 8.1 %collective-permute-start = (bf16[8,8192]{1,0:T(8,128)(2,1)S(1)}, bf16[8,8192]{1,0:T(8,128)(2,1)S(1)}, u32[]{:S(2)}, u32[]{:S(2)}) collective-permute-start(bf16[8,8192]{1,0:T(8,128)(2,1)S(1)} %get-tuple-element.27), channel_id=1, source_target_pairs={{0,4},{1,5},{2,6},{3,7},{4,0},{5,1},{6,2},{7,3},{8,12},{9,13},{10,... | collective-permute-start | bytes 393224 | tf_op jit(solution)/shard_map/ppermute | solution.py:484
  8.0 12.9 %collective-permute-start.1 = (bf16[8,8192]{1,0:T(8,128)(2,1)S(1)}, bf16[8,8192]{1,0:T(8,128)(2,1)S(1)}, u32[]{:S(2)}, u32[]{:S(2)}) collective-permute-start(bf16[8,8192]{1,0:T(8,128)(2,1)S(1)} %get-tuple-element.28), channel_id=1, source_target_pairs={{0,8},{1,9},{2,10},{3,11},{4,12},{5,13},{6,14},{7,15},{8,0},{9,1},... | collective-permute-start | bytes 393224 | tf_op jit(solution)/shard_map/ppermute | solution.py:484
  10.5 10.4 %collective-permute-start.2 = (bf16[8,8192]{1,0:T(8,128)(2,1)S(1)}, bf16[8,8192]{1,0:T(8,128)(2,1)S(1)}, u32[]{:S(2)}, u32[]{:S(2)}) collective-permute-start(bf16[8,8192]{1,0:T(8,128)(2,1)S(1)} %get-tuple-element.29), channel_id=1, source_target_pairs={{0,12},{1,13},{2,14},{3,15},{4,8},{5,9},{6,10},{7,11},{8,4},{9,5},... | collective-permute-start | bytes 393224 | tf_op jit(solution)/shard_map/ppermute | solution.py:484
  20.9 28.6 %copy-start.3 = (bf16[448,576]{1,0:T(8,128)(2,1)S(1)}, bf16[448,576]{1,0:T(8,128)(2,1)}, u32[]{:S(2)}) copy-start(bf16[448,576]{1,0:T(8,128)(2,1)} %refs_10_.1) | copy-start | bytes 1548292
  20.9 35.6 %copy-start.11 = (s32[1,16]{1,0:T(1,128)S(1)}, s32[1,16]{1,0:T(1,128)}, u32[]{:S(2)}) copy-start(s32[1,16]{1,0:T(1,128)} %param.22) | copy-start | bytes 196
  20.9 11.3 %collective-permute-start.4 = (bf16[32,8192]{1,0:T(8,128)(2,1)S(1)}, bf16[32,8192]{1,0:T(8,128)(2,1)S(1)}, u32[]{:S(2)}, u32[]{:S(2)}) collective-permute-start(bf16[32,8192]{1,0:T(8,128)(2,1)S(1)} %constant_dynamic-update-slice_fusion.refs_0_.refs_8_), channel_id=1, source_target_pairs={{0,2},{1,3},{2,0},{3,1},{4,6},{5,7},{6,4},{7,5},{8,10},{9,11},{10,... | collective-permute-start | bytes 1572872 | tf_op jit(solution)/shard_map/ppermute | solution.py:484
  22.5 9.7 %collective-permute-start.3 = (bf16[32,8192]{1,0:T(8,128)(2,1)S(1)}, bf16[32,8192]{1,0:T(8,128)(2,1)S(1)}, u32[]{:S(2)}, u32[]{:S(2)}) collective-permute-start(bf16[32,8192]{1,0:T(8,128)(2,1)S(1)} %constant_dynamic-update-slice_fusion.refs_0_.refs_8_), channel_id=1, source_target_pairs={{0,1},{1,0},{2,3},{3,2},{4,5},{5,4},{6,7},{7,6},{8,9},{9,8},{10,11... | collective-permute-start | bytes 1572872 | tf_op jit(solution)/shard_map/ppermute | solution.py:484
  32.2 1.9 %collective-permute-start.5 = (bf16[32,8192]{1,0:T(8,128)(2,1)S(1)}, bf16[32,8192]{1,0:T(8,128)(2,1)S(1)}, u32[]{:S(2)}, u32[]{:S(2)}) collective-permute-start(bf16[32,8192]{1,0:T(8,128)(2,1)S(1)} %collective-permute-done.4.refs_2_), channel_id=1, source_target_pairs={{0,1},{1,0},{2,3},{3,2},{4,5},{5,4},{6,7},{7,6},{8,9},{9,8},{10,11... | collective-permute-start | bytes 1572872 | tf_op jit(solution)/shard_map/ppermute | solution.py:484
  34.1 24.0 %copy-start = (bf16[16,128,576]{1,2,0:T(8,128)(2,1)S(1)}, bf16[16,128,576]{1,2,0:T(8,128)(2,1)}, u32[]{:S(2)}) copy-start(bf16[16,128,576]{1,2,0:T(8,128)(2,1)} %param.24) | copy-start | bytes 7077892
  49.3 8.8 %copy-start.10 = (bf16[1,1024,576]{1,2,0:T(8,128)(2,1)S(1)}, bf16[1,1024,576]{1,2,0:T(8,128)(2,1)}, u32[]{:S(2)}) copy-start(bf16[1,1024,576]{1,2,0:T(8,128)(2,1)} %param.25) | copy-start | bytes 3538948
  49.3 8.0 %collective-permute-start.6 = (bf16[2,4,40,1792]{3,2,1,0:T(8,128)(2,1)S(1)}, bf16[2,4,40,1792]{3,2,1,0:T(8,128)(2,1)S(1)}, u32[]{:S(2)}, u32[]{:S(2)}) collective-permute-start(bf16[2,4,40,1792]{3,2,1,0:T(8,128)(2,1)S(1)} %get-tuple-element.31), channel_id=1, source_target_pairs={{0,1},{1,0},{2,3},{3,2},{4,5},{5,4},{6,7},{7,6},{8,9},{9,8},{10,11... | collective-permute-start | bytes 3440648 | tf_op jit(solution)/shard_map/ppermute | solution.py:484
  49.6 34.1 %collective-permute-start.14 = (bf16[448,576]{1,0:T(8,128)(2,1)S(1)}, bf16[448,576]{1,0:T(8,128)(2,1)S(1)}, u32[]{:S(2)}, u32[]{:S(2)}) collective-permute-start(bf16[448,576]{1,0:T(8,128)(2,1)S(1)} %copy-done.3), channel_id=1, source_target_pairs={{0,1},{1,0},{2,3},{3,2},{4,5},{5,4},{6,7},{7,6},{8,9},{9,8},{10,11... | collective-permute-start | bytes 1548296 | tf_op jit(solution)/shard_map/ppermute | solution.py:484
  49.9 22.4 %collective-permute-start.15 = (bf16[448,576]{1,0:T(8,128)(2,1)S(1)}, bf16[448,576]{1,0:T(8,128)(2,1)S(1)}, u32[]{:S(2)}, u32[]{:S(2)}) collective-permute-start(bf16[448,576]{1,0:T(8,128)(2,1)S(1)} %copy-done.3), channel_id=1, source_target_pairs={{0,2},{1,3},{2,0},{3,1},{4,6},{5,7},{6,4},{7,5},{8,10},{9,11},{10,... | collective-permute-start | bytes 1548296 | tf_op jit(solution)/shard_map/ppermute | solution.py:484
  51.5 26.0 %collective-permute-start.11 = (bf16[16,1792]{1,0:T(8,128)(2,1)S(1)}, bf16[16,1792]{1,0:T(8,128)(2,1)S(1)}, u32[]{:S(2)}, u32[]{:S(2)}) collective-permute-start(bf16[16,1792]{1,0:T(8,128)(2,1)S(1)} %get-tuple-element.33), channel_id=1, source_target_pairs={{0,4},{1,5},{2,6},{3,7},{4,0},{5,1},{6,2},{7,3},{8,12},{9,13},{10,... | collective-permute-start | bytes 172040 | tf_op jit(solution)/shard_map/ppermute | solution.py:484
  54.4 26.1 %collective-permute-start.12 = (bf16[16,1792]{1,0:T(8,128)(2,1)S(1)}, bf16[16,1792]{1,0:T(8,128)(2,1)S(1)}, u32[]{:S(2)}, u32[]{:S(2)}) collective-permute-start(bf16[16,1792]{1,0:T(8,128)(2,1)S(1)} %get-tuple-element.34), channel_id=1, source_target_pairs={{0,8},{1,9},{2,10},{3,11},{4,12},{5,13},{6,14},{7,15},{8,0},{9,1},... | collective-permute-start | bytes 172040 | tf_op jit(solution)/shard_map/ppermute | solution.py:484
  57.5 19.8 %collective-permute-start.7 = (bf16[1,4,40,1792]{3,2,1,0:T(8,128)(2,1)S(1)}, bf16[1,4,40,1792]{3,2,1,0:T(8,128)(2,1)S(1)}, u32[]{:S(2)}, u32[]{:S(2)}) collective-permute-start(bf16[1,4,40,1792]{3,2,1,0:T(8,128)(2,1)S(1)} %add_convert_fusion), channel_id=1, source_target_pairs={{0,2},{1,3},{2,0},{3,1},{4,6},{5,7},{6,4},{7,5},{8,10},{9,11},{10,... | collective-permute-start | bytes 1720328 | tf_op jit(solution)/shard_map/ppermute | solution.py:484
  72.3 5.2 %copy-start.1 = (bf16[16,128,512]{2,1,0:T(8,128)(2,1)}, bf16[16,128,512]{2,1,0:T(8,128)(2,1)S(1)}, u32[]{:S(2)}) copy-start(bf16[16,128,512]{2,1,0:T(8,128)(2,1)S(1)} %get-tuple-element.44.refs_8_) | copy-start | bytes 6291460
  72.4 21.9 %copy-start.5 = (f32[7168]{0:T(1024)S(1)}, f32[7168]{0:T(1024)}, u32[]{:S(2)}) copy-start(f32[7168]{0:T(1024)} %param.15) | copy-start | bytes 86020
  72.4 9.8 %collective-permute-start.13 = (bf16[16,1792]{1,0:T(8,128)(2,1)S(1)}, bf16[16,1792]{1,0:T(8,128)(2,1)S(1)}, u32[]{:S(2)}, u32[]{:S(2)}) collective-permute-start(bf16[16,1792]{1,0:T(8,128)(2,1)S(1)} %get-tuple-element.35), channel_id=1, source_target_pairs={{0,12},{1,13},{2,14},{3,15},{4,8},{5,9},{6,10},{7,11},{8,4},{9,5},... | collective-permute-start | bytes 172040 | tf_op jit(solution)/shard_map/ppermute | solution.py:484
  77.2 6.5 %collective-permute-start.16 = (bf16[448,576]{1,0:T(8,128)(2,1)S(1)}, bf16[448,576]{1,0:T(8,128)(2,1)S(1)}, u32[]{:S(2)}, u32[]{:S(2)}) collective-permute-start(bf16[448,576]{1,0:T(8,128)(2,1)S(1)} %collective-permute-done.15.refs_12_), channel_id=1, source_target_pairs={{0,1},{1,0},{2,3},{3,2},{4,5},{5,4},{6,7},{7,6},{8,9},{9,8},{10,11... | collective-permute-start | bytes 1548296 | tf_op jit(solution)/shard_map/ppermute | solution.py:484
  77.5 10.3 %collective-permute-start.8 = (bf16[40,1792]{1,0:T(8,128)(2,1)S(1)}, bf16[40,1792]{1,0:T(8,128)(2,1)S(1)}, u32[]{:S(2)}, u32[]{:S(2)}) collective-permute-start(bf16[40,1792]{1,0:T(8,128)(2,1)S(1)} %get-tuple-element.51), channel_id=1, source_target_pairs={{0,4},{1,5},{2,6},{3,7},{4,0},{5,1},{6,2},{7,3},{8,12},{9,13},{10,... | collective-permute-start | bytes 430088 | tf_op jit(solution)/shard_map/ppermute | solution.py:484
  80.6 13.7 %collective-permute-start.9 = (bf16[40,1792]{1,0:T(8,128)(2,1)S(1)}, bf16[40,1792]{1,0:T(8,128)(2,1)S(1)}, u32[]{:S(2)}, u32[]{:S(2)}) collective-permute-start(bf16[40,1792]{1,0:T(8,128)(2,1)S(1)} %get-tuple-element.50), channel_id=1, source_target_pairs={{0,8},{1,9},{2,10},{3,11},{4,12},{5,13},{6,14},{7,15},{8,0},{9,1},... | collective-permute-start | bytes 430088 | tf_op jit(solution)/shard_map/ppermute | solution.py:484
  82.1 12.1 %collective-permute-start.10 = (bf16[40,1792]{1,0:T(8,128)(2,1)S(1)}, bf16[40,1792]{1,0:T(8,128)(2,1)S(1)}, u32[]{:S(2)}, u32[]{:S(2)}) collective-permute-start(bf16[40,1792]{1,0:T(8,128)(2,1)S(1)} %get-tuple-element.49), channel_id=1, source_target_pairs={{0,12},{1,13},{2,14},{3,15},{4,8},{5,9},{6,10},{7,11},{8,4},{9,5},... | collective-permute-start | bytes 430088 | tf_op jit(solution)/shard_map/ppermute | solution.py:484
  94.2 17.9 %copy-start.7 = (f32[512]{0:T(512)S(1)}, f32[512]{0:T(512)}, u32[]{:S(2)}) copy-start(f32[512]{0:T(512)} %param.16) | copy-start | bytes 6148
  97.5 8.1 %collective-permute-start.20 = (f32[16,640]{1,0:T(8,128)S(1)}, f32[16,640]{1,0:T(8,128)S(1)}, u32[]{:S(2)}, u32[]{:S(2)}) collective-permute-start(f32[16,640]{1,0:T(8,128)S(1)} %get-tuple-element.41), channel_id=1, source_target_pairs={{0,4},{1,5},{2,6},{3,7},{4,0},{5,1},{6,2},{7,3},{8,12},{9,13},{10,... | collective-permute-start | bytes 122888 | tf_op jit(solution)/shard_map/ppermute | solution.py:484
  100.5 19.2 %collective-permute-start.17 = (bf16[16,1792]{1,0:T(8,128)(2,1)S(1)}, bf16[16,1792]{1,0:T(8,128)(2,1)S(1)}, u32[]{:S(2)}, u32[]{:S(2)}) collective-permute-start(bf16[16,1792]{1,0:T(8,128)(2,1)S(1)} %get-tuple-element.37), channel_id=1, source_target_pairs={{0,4},{1,5},{2,6},{3,7},{4,0},{5,1},{6,2},{7,3},{8,12},{9,13},{10,... | collective-permute-start | bytes 172040 | tf_op jit(solution)/shard_map/ppermute | solution.py:484
  100.6 19.2 %collective-permute-start.18 = (bf16[16,1792]{1,0:T(8,128)(2,1)S(1)}, bf16[16,1792]{1,0:T(8,128)(2,1)S(1)}, u32[]{:S(2)}, u32[]{:S(2)}) collective-permute-start(bf16[16,1792]{1,0:T(8,128)(2,1)S(1)} %get-tuple-element.38), channel_id=1, source_target_pairs={{0,8},{1,9},{2,10},{3,11},{4,12},{5,13},{6,14},{7,15},{8,0},{9,1},... | collective-permute-start | bytes 172040 | tf_op jit(solution)/shard_map/ppermute | solution.py:484
  104.0 15.8 %collective-permute-start.19 = (bf16[16,1792]{1,0:T(8,128)(2,1)S(1)}, bf16[16,1792]{1,0:T(8,128)(2,1)S(1)}, u32[]{:S(2)}, u32[]{:S(2)}) collective-permute-start(bf16[16,1792]{1,0:T(8,128)(2,1)S(1)} %get-tuple-element.39), channel_id=1, source_target_pairs={{0,12},{1,13},{2,14},{3,15},{4,8},{5,9},{6,10},{7,11},{8,4},{9,5},... | collective-permute-start | bytes 172040 | tf_op jit(solution)/shard_map/ppermute | solution.py:484
  104.9 7.1 %collective-permute-start.21 = (f32[16,640]{1,0:T(8,128)S(1)}, f32[16,640]{1,0:T(8,128)S(1)}, u32[]{:S(2)}, u32[]{:S(2)}) collective-permute-start(f32[16,640]{1,0:T(8,128)S(1)} %get-tuple-element.42), channel_id=1, source_target_pairs={{0,8},{1,9},{2,10},{3,11},{4,12},{5,13},{6,14},{7,15},{8,0},{9,1},... | collective-permute-start | bytes 122888 | tf_op jit(solution)/shard_map/ppermute | solution.py:484
  105.6 6.4 %collective-permute-start.22 = (f32[16,640]{1,0:T(8,128)S(1)}, f32[16,640]{1,0:T(8,128)S(1)}, u32[]{:S(2)}, u32[]{:S(2)}) collective-permute-start(f32[16,640]{1,0:T(8,128)S(1)} %get-tuple-element.43), channel_id=1, source_target_pairs={{0,12},{1,13},{2,14},{3,15},{4,8},{5,9},{6,10},{7,11},{8,4},{9,5},... | collective-permute-start | bytes 122888 | tf_op jit(solution)/shard_map/ppermute | solution.py:484
  112.1 1.6 %copy-start.2 = (bf16[16,128,512]{2,1,0:T(8,128)(2,1)S(1)}, bf16[16,128,512]{2,1,0:T(8,128)(2,1)}, u32[]{:S(2)}) copy-start(bf16[16,128,512]{2,1,0:T(8,128)(2,1)} %copy-done.1) | copy-start | bytes 6291460
  (3 other events, 2.1 us)

commit v2 on v1

v2 whole, which is shorter than its diff:
```python
import functools

import jax
import jax.numpy as jnp
from jax import lax
from jax.experimental import pallas as pl
from jax.experimental.pallas import tpu as pltpu
from jax.sharding import PartitionSpec as P

KEY_VALUE_RANK = 512
NODES = 16
EXPERTS = 4
CAP = 9
TAIL = 128
ROWS = 40
BF = jnp.bfloat16
F32 = jnp.float32
softmax_scale = 192.0 ** (-0.5)
MIB = 1024 * 1024
COST = pl.CostEstimate(flops=1024, bytes_accessed=1024, transcendentals=0)
LOG2E = 1.4426950408889634


def iota(shape, dim):
    return lax.broadcasted_iota(jnp.int32, shape, dim)


def dot(a, b):
    return jnp.dot(a, b, preferred_element_type=F32)


def dot_t(a, b):
    return lax.dot_general(a, b, (((1,), (1,)), ((), ())), preferred_element_type=F32)


def params(mib, semantics=None):
    return pltpu.CompilerParams(vmem_limit_bytes=mib * MIB, dimension_semantics=semantics)


def after(x, *others):
    return lax.optimization_barrier((x, others))[0]


def whole(shape):
    zeros = (0,) * len(shape)
    return pl.BlockSpec(shape, lambda *_: zeros)


def pack_kernel(e_ref, *refs):
    ins, outs = refs[:4], refs[4 : 4 + 2 * EXPERTS]
    held, sem = refs[4 + 2 * EXPERTS : -1], refs[-1]
    copies = [pltpu.make_async_copy(a, b, sem.at[i]) for i, (a, b) in enumerate(zip(ins, held))]
    for c in copies:
        c.start()
    for c in copies:
        c.wait()
    hidden_ref, gain_ref, routes_ref, gates_ref = held
    chunks, parts = outs[:EXPERTS], outs[EXPERTS:]
    tokens, width = hidden_ref.shape
    piece = width // 8
    quarter = width // EXPERTS
    x = hidden_ref[...].astype(F32)
    scale = lax.rsqrt(jnp.mean(x * x, axis=-1, keepdims=True) + 1e-06)
    units = (x * scale * gain_ref[...]).astype(BF)
    first = jnp.broadcast_to(routes_ref[0:1, :], (8, tokens))
    second = jnp.broadcast_to(routes_ref[1:2, :], (8, tokens))
    row = iota((8, tokens), 0)
    before = (iota((tokens, tokens), 0) < iota((tokens, tokens), 1)).astype(BF)
    main, ninth = [], []
    for k in range(EXPERTS):
        expert = e_ref[0] ^ k
        hit = jnp.where((first == expert) | (second == expert), 1.0, 0.0)
        rank = dot(hit.astype(BF), before)
        main.append(jnp.where(rank == row.astype(F32), hit, 0.0))
        ninth.append(jnp.where(rank == 8.0, hit, 0.0))
    main = jnp.concatenate(main, axis=0).astype(BF)
    ninth = jnp.concatenate(ninth, axis=0)
    rows = iota(ninth.shape, 0) % 8
    picked = dot(main, units).astype(BF)
    cut = jnp.zeros((8 * EXPERTS, piece), F32)
    for j in range(8):
        cut = cut + dot(
            jnp.where(rows == j, ninth, 0.0).astype(BF), units[:, j * piece : (j + 1) * piece]
        )
    cut = cut.astype(BF)
    info = jnp.where(row == 0, first.astype(F32), second.astype(F32))
    for choice in range(2):
        gate = jnp.broadcast_to(gates_ref[choice : choice + 1, :], (8, tokens))
        for part in range(3):
            rounded = gate.astype(BF).astype(F32)
            info = jnp.where(row == 2 + 3 * choice + part, rounded, info)
            gate = gate - rounded
    spread = (iota((tokens, TAIL), 0) == iota((tokens, TAIL), 1)).astype(BF)
    tail = dot(info.astype(BF), spread).astype(BF)
    for k in range(EXPERTS):
        expert = e_ref[0] ^ k
        chunks[k][:, :width] = picked[8 * k : 8 * k + 8]
        chunks[k][:, width : width + piece] = cut[8 * k : 8 * k + 8]
        chunks[k][:, width + piece :] = tail
        start = pl.multiple_of(expert * quarter, 128)
        parts[k][...] = hidden_ref[:, pl.ds(start, quarter)]


def pack(e, hidden, gain, routes_t, gates_t):
    tokens, width = hidden.shape
    chunk = jax.ShapeDtypeStruct((8, width + width // 8 + TAIL), BF)
    part = jax.ShapeDtypeStruct((tokens, width // EXPERTS), BF)
    hbm = pl.BlockSpec(memory_space=pltpu.HBM)
    vmem = pl.BlockSpec(memory_space=pltpu.VMEM)
    given = [hidden, gain, routes_t, gates_t]
    placed = [pltpu.with_memory_space_constraint(a, pltpu.HBM) for a in given]
    return pl.pallas_call(
        pack_kernel,
        out_shape=[chunk] * EXPERTS + [part] * EXPERTS,
        in_specs=[pl.BlockSpec(memory_space=pltpu.SMEM)] + [hbm] * 4,
        out_specs=[vmem] * (2 * EXPERTS),
        scratch_shapes=[pltpu.VMEM(a.shape, a.dtype) for a in given]
        + [pltpu.SemaphoreType.DMA((4,))],
        compiler_params=params(8),
        cost_estimate=COST,
        name="pack",
    )(e, *placed)


def down(split, e_ref, act, w_out, keep, send, first):
    quarter = keep.shape[3]
    step = quarter // 2
    main_rows = 32 * split
    for k in range(keep.shape[1]):
        start = (e_ref[0] ^ (first + k)) * quarter
        for h in range(2):
            columns = pl.ds(pl.multiple_of(start + h * step, 128), step)
            out = dot(act[...], w_out[0, :, columns])
            for r in range(split):
                lower = out[32 * r : 32 * r + 32]
                upper = out[main_rows + 8 * r : main_rows + 8 * r + 8]
                mine = jnp.concatenate([lower, upper], axis=0).astype(BF)
                (send if r % 2 else keep)[r // 2, k, :, h * step : (h + 1) * step] = mine


def expert_kernel(split, e_ref, *refs):
    groups = refs[:split]
    w_in, w_out, act, keep, send, x = refs[split:]
    width = w_in.shape[1]
    hid = act.shape[1]
    piece = width // 8
    main_rows, last_rows = 32 * split, 8 * split
    for r in range(split):
        x[32 * r : 32 * r + 32, :] = groups[r][:, :width]
    ext = jnp.concatenate([g[:, width : width + piece] for g in groups], axis=0)
    row = iota((8 * last_rows, main_rows), 0)
    col = iota((8 * last_rows, main_rows), 1)
    place = row % last_rows
    want = 32 * (place // 8) + 8 * (place % 8) + row // last_rows
    pick = jnp.where((place % 8 < 4) & (col == want), 1.0, 0.0).astype(BF)
    last = dot(pick, ext).astype(BF)
    for j in range(8):
        x[main_rows:, j * piece : (j + 1) * piece] = last[j * last_rows : (j + 1) * last_rows]
    step = min(256, hid)
    for i in range(hid // step):
        gate = dot(x[...], w_in[0, :, i * step : (i + 1) * step])
        up = dot(x[...], w_in[0, :, hid + i * step : hid + (i + 1) * step])
        act[:, i * step : (i + 1) * step] = (gate / (1.0 + jnp.exp(-gate)) * up).astype(BF)
    down(split, e_ref, act, w_out, keep, send, 2)


def expert_rest_kernel(split, e_ref, act, w_out, keep, send):
    down(split, e_ref, act, w_out, keep, send, 0)


def expert_slice(e, groups, w_in, w_out):
    split = len(groups)
    width, hid2 = w_in.shape[1:]
    hid = hid2 // 2
    quarter = width // EXPERTS
    half = jax.ShapeDtypeStruct((split // 2, EXPERTS // 2, ROWS, quarter), BF)
    rows = ROWS * split
    act = jax.ShapeDtypeStruct((rows, hid), BF)
    vmem = pl.BlockSpec(memory_space=pltpu.VMEM)
    smem = pl.BlockSpec(memory_space=pltpu.SMEM)
    act, keep_a, send_a = pl.pallas_call(
        functools.partial(expert_kernel, split),
        out_shape=[act, half, half],
        in_specs=[smem] + [vmem] * (split + 2),
        out_specs=[vmem] * 3,
        scratch_shapes=[pltpu.VMEM((rows, width), BF)],
        compiler_params=params(10),
        cost_estimate=COST,
        name="experts",
    )(e, *groups, w_in, w_out)
    keep_b, send_b = pl.pallas_call(
        functools.partial(expert_rest_kernel, split),
        out_shape=[half, half],
        in_specs=[smem] + [vmem] * 2,
        out_specs=[vmem] * 2,
        compiler_params=params(6),
        cost_estimate=COST,
        name="experts_rest",
    )(e, act, w_out)
    return keep_a, send_a, keep_b, send_b


def combine_kernel(split, tokens, e_ref, *refs):
    outs_e, hid = refs[:EXPERTS], refs[EXPERTS : 2 * EXPERTS]
    info_ref, gain_ref = refs[2 * EXPERTS : 2 * EXPERTS + 2]
    kvs = refs[2 * EXPERTS + 2 : 2 * EXPERTS + 2 + split]
    rest = refs[2 * EXPERTS + 2 + split :]
    own_sum, own_part = rest[:2]
    sent = rest[2 : 1 + EXPERTS]
    kv_ref, sem = rest[1 + EXPERTS :]
    part = kvs[0].shape[0]
    lat = kvs[0].shape[1]
    copies = []
    for r in range(split):
        place = pl.multiple_of((e_ref[1] ^ r) * part, 16)
        copies.append(
            pltpu.make_async_copy(kvs[r], kv_ref.at[pl.ds(place, part), :], sem.at[r])
        )
        copies[-1].start()
    one = (iota((tokens, TAIL), 0) == iota((tokens, TAIL), 1)).astype(BF)
    info = dot_t(one, info_ref[...])
    earlier = (iota((tokens, tokens), 1) < iota((tokens, tokens), 0)).astype(BF)
    lane = iota((tokens, ROWS), 1).astype(F32)
    hits = []
    for k in range(EXPERTS):
        expert = (e_ref[0] ^ k).astype(F32)
        hits.append(jnp.where(info == expert, 1.0, 0.0))
    moe = None
    for k in range(EXPERTS):
        blocks = [[], [], []]
        for s in range(EXPERTS):
            h0 = hits[k][:, 8 * s : 8 * s + 1]
            h1 = hits[k][:, 8 * s + 1 : 8 * s + 2]
            hit = jnp.broadcast_to(h0 + h1, (tokens, ROWS))
            rank = dot(earlier, hit.astype(BF))
            line = s ^ k
            want = jnp.where(rank < 8.0, rank + 8.0 * line, 32.0 + line)
            chosen = (lane == want) & (hit > 0.5)
            for p in range(3):
                g0 = info[:, 8 * s + 2 + p : 8 * s + 3 + p]
                g1 = info[:, 8 * s + 5 + p : 8 * s + 6 + p]
                gate = jnp.broadcast_to(h0 * g0 + h1 * g1, (tokens, ROWS))
                blocks[p].append(jnp.where(chosen, gate, 0.0))
        weights = jnp.concatenate(blocks[0] + blocks[1] + blocks[2], axis=0).astype(BF)
        term = dot(weights, outs_e[k][...])
        moe = term if moe is None else moe + term
    total = EXPERTS * tokens
    moe = moe[:total] + moe[total : 2 * total] + moe[2 * total :]
    mixed = jnp.concatenate([h[...].astype(F32) for h in hid], axis=0) + moe
    square = jnp.sum(mixed * mixed, axis=-1, keepdims=True)
    scaled = (mixed * gain_ref[...]).astype(BF)
    for c in copies:
        c.wait()
    rows = dot(scaled, kv_ref[...])
    padded = own_sum.shape[1]
    for s in range(EXPERTS):
        span = slice(s * tokens, (s + 1) * tokens)
        rest = jnp.broadcast_to(square[span], (tokens, padded - lat))
        first = iota(rest.shape, 1) == 0
        if s:
            high = rest.astype(BF).astype(F32)
            sent[s - 1][:, :lat] = rows[span].astype(BF)
            sent[s - 1][:, lat:padded] = jnp.where(first, high, rest - high).astype(BF)
            sent[s - 1][:, padded:] = mixed[span].astype(BF)
        else:
            own_sum[:, :lat] = rows[span]
            own_sum[:, lat:] = jnp.where(first, rest, 0.0)
            own_part[...] = mixed[span].astype(BF)


def combine(place, outs_e, hid, info, gain, kvs):
    split = len(kvs)
    tokens, quarter = hid[0].shape
    part, lat = kvs[0].shape
    padded = (lat // 128 + 1) * 128
    outs = [pltpu.VMEM((tokens, padded), F32), pltpu.VMEM((tokens, quarter), BF)]
    outs += [pltpu.VMEM((tokens, padded + quarter), BF)] * (EXPERTS - 1)
    return pl.pallas_call(
        functools.partial(combine_kernel, split, tokens),
        out_shape=outs,
        grid_spec=pltpu.PrefetchScalarGridSpec(
            num_scalar_prefetch=1,
            grid=(1,),
            in_specs=[whole(o.shape) for o in outs_e]
            + [whole(h.shape) for h in hid]
            + [
                whole(info.shape),
                pl.BlockSpec((1, quarter), lambda t, e: (0, e[0])),
            ]
            + [pl.BlockSpec(memory_space=pl.ANY)] * split,
            out_specs=[whole(o.shape) for o in outs],
            scratch_shapes=[
                pltpu.VMEM((split * part, lat), BF),
                pltpu.SemaphoreType.DMA((split,)),
            ],
        ),
        compiler_params=params(8),
        cost_estimate=COST,
        name="combine",
    )(place, *outs_e, *hid, info, gain, *kvs)


def cached_kernel(begin, per, length_ref, *refs):
    q_hbm, cache_hbm, w_hbm, out_ref, stat_ref, w_ref, q_ref, cache_ref, keys_ref, sem = refs
    nodes, lat, heads = q_ref.shape
    ctx = cache_ref.shape[2]
    spare = keys_ref.shape[1] - lat
    copies = [
        pltpu.make_async_copy(cache_hbm, cache_ref, sem.at[0]),
        pltpu.make_async_copy(q_hbm.at[pl.ds(begin, nodes)], q_ref, sem.at[1]),
        pltpu.make_async_copy(w_hbm, w_ref, sem.at[2]),
    ]
    for c in copies:
        c.start()
    unused = (iota((ctx, spare), 0) >= length_ref[0]) & (iota((ctx, spare), 1) == 0)
    keys_ref[:, lat:] = jnp.where(unused, -jnp.inf, 0.0).astype(BF)
    one = (iota((spare, per * heads), 0) == 0).astype(BF)
    factor = softmax_scale * LOG2E
    copies[0].wait()
    keys_ref[:, :lat] = cache_ref[0].T
    copies[1].wait()

    for g in range(nodes // per):
        q = jnp.concatenate([q_ref[g * per + i] for i in range(per)], axis=1)
        q = jnp.concatenate([q, one], axis=0)
        scores = dot(keys_ref[...], q)
        top = jnp.max(scores, axis=0, keepdims=True) * factor
        weight = jnp.exp2(scores * factor - top)
        total = jnp.sum(weight, axis=0, keepdims=True)
        out = dot(cache_ref[0, :KEY_VALUE_RANK, :], weight.astype(BF)) * (1.0 / total)
        for i in range(per):
            span = slice(i * heads, (i + 1) * heads)
            out_ref[g * per + i] = out[:, span].T.astype(out_ref.dtype)
            stat_ref[g * per + i] = jnp.concatenate([top[:, span], total[:, span]], axis=0)
    copies[2].wait()


def cached_attention(lengths, q_t, cache_t, weight, first, count, per=4):
    tokens, lat, heads = q_t.shape
    ctx = cache_t.shape[2]
    hbm = pl.BlockSpec(memory_space=pltpu.HBM)
    vmem = pl.BlockSpec(memory_space=pltpu.VMEM)
    given = [pltpu.with_memory_space_constraint(a, pltpu.HBM) for a in (q_t, cache_t, weight)]
    return pl.pallas_call(
        functools.partial(cached_kernel, first, per),
        out_shape=[
            pltpu.VMEM((count, heads, KEY_VALUE_RANK), BF),
            pltpu.VMEM((count, 2, heads), F32),
            pltpu.VMEM(weight.shape, weight.dtype),
        ],
        in_specs=[pl.BlockSpec(memory_space=pltpu.SMEM), hbm, hbm, hbm],
        out_specs=[vmem, vmem, vmem],
        scratch_shapes=[
            pltpu.VMEM((count, lat, heads), BF),
            pltpu.VMEM(cache_t.shape, BF),
            pltpu.VMEM((ctx, (lat // 128 + 1) * 128), BF),
            pltpu.SemaphoreType.DMA((3,)),
        ],
        compiler_params=params(16),
        cost_estimate=pl.CostEstimate(
            flops=4 * count * heads * ctx * (lat + KEY_VALUE_RANK),
            bytes_accessed=2 * weight.size,
            transcendentals=count * heads * ctx,
        ),
        name="cached",
    )(lengths, *given)


def final_kernel(width, per, e_ref, *refs):
    own_sum, own_part = refs[:2]
    got = refs[2 : 1 + EXPERTS]
    gain_ref, turn_ref, allow_ref, q_ref = refs[1 + EXPERTS : 5 + EXPERTS]
    halves = refs[5 + EXPERTS : 7 + EXPERTS], refs[7 + EXPERTS : 9 + EXPERTS]
    part_ref, entry_ref, out_hbm, out_ref, sem = refs[9 + EXPERTS :]
    nodes, lat, heads = q_ref.shape
    padded = own_sum.shape[1]
    quarter = own_part.shape[1]
    raw = own_sum[...]
    for g in got:
        raw = raw + g[:, :padded].astype(F32)
    square = raw[:, lat : lat + 1] + raw[:, lat + 1 : lat + 2]
    raw = raw * lax.rsqrt(square / width + 1e-06)
    head = raw[:, :KEY_VALUE_RANK]
    head = head * lax.rsqrt(jnp.mean(head * head, axis=-1, keepdims=True) + 1e-06)
    head = head * gain_ref[...]
    tail = raw[:, KEY_VALUE_RANK:]
    half = (lat - KEY_VALUE_RANK) // 2
    lanes = tail.shape[1]
    tail = (
        tail * turn_ref[0]
        + pltpu.roll(tail, lanes - half, 1) * turn_ref[1]
        + pltpu.roll(tail, half, 1) * turn_ref[2]
    )
    keys = jnp.concatenate([head, tail], axis=1).astype(BF)[:, :lat]
    entry_ref[...] = keys
    count = keys.shape[0]
    in_half = halves[0][0].shape[0]
    copies = []
    for g in range(nodes // per):
        span = range(g * per, (g + 1) * per)

        def side(ref):
            return jnp.concatenate([ref[i] for i in span], axis=1)

        ctx_ref, stat_ref = halves[g * per // in_half]
        begin = g * per % in_half
        scores = dot(keys, side(q_ref)) * (softmax_scale * LOG2E)
        scores = jnp.where(side(allow_ref) > 0.5, scores, -jnp.inf)
        stats = jnp.concatenate([stat_ref[begin + i] for i in range(per)], axis=1)
        old = stats[0:1]
        top = jnp.maximum(old, jnp.max(scores, axis=0, keepdims=True))
        weight = jnp.exp2(scores - top)
        share = stats[1:2] * jnp.exp2(old - top)
        scale = 1.0 / (share + jnp.sum(weight, axis=0, keepdims=True))
        share = jnp.broadcast_to(share * scale, (8, per * heads))
        both = jnp.concatenate([weight * scale, share], axis=0).T
        for i in range(per):
            mine = both[i * heads : (i + 1) * heads]
            out = ctx_ref[begin + i].astype(F32) * mine[:, count : count + 1]
            out = out + dot(mine[:, :count].astype(BF), keys[:, :KEY_VALUE_RANK])
            out_ref[g * per + i] = out.astype(BF)
        here = pl.ds(g * per, per)
        copies.append(pltpu.make_async_copy(out_ref.at[here], out_hbm.at[here], sem.at[g]))
        copies[-1].start()
    for k in range(EXPERTS):
        start = pl.multiple_of((e_ref[0] ^ k) * quarter, 128)
        part_ref[:, pl.ds(start, quarter)] = got[k - 1][:, padded:] if k else own_part[...]
    for c in copies:
        c.wait()


def final_attention(place, width, rows, gain, turn, allow, q_t, first, second, per=4):
    tokens, lat, heads = q_t.shape
    vmem = pl.BlockSpec(memory_space=pltpu.VMEM)
    given = [*rows, gain, turn, allow, q_t, *first, *second]
    given = [pltpu.with_memory_space_constraint(x, pltpu.VMEM) for x in given]
    out = jax.ShapeDtypeStruct((tokens, heads, KEY_VALUE_RANK), BF)
    return pl.pallas_call(
        functools.partial(final_kernel, width, per),
        out_shape=[
            jax.ShapeDtypeStruct((tokens, width), BF),
            jax.ShapeDtypeStruct((tokens, lat), BF),
            out,
        ],
        in_specs=[pl.BlockSpec(memory_space=pltpu.SMEM)] + [vmem] * len(given),
        out_specs=[vmem, vmem, pl.BlockSpec(memory_space=pltpu.HBM)],
        scratch_shapes=[
            pltpu.VMEM(out.shape, BF),
            pltpu.SemaphoreType.DMA((tokens // per,)),
        ],
        compiler_params=params(12),
        cost_estimate=COST,
        name="final",
    )(place, *given)


def tree(parents, lengths, rank, lat):
    count = parents.shape[1]
    link = (parents[0][:, None] == jnp.arange(count, dtype=jnp.int32)[None, :]).astype(F32)
    reach = jnp.eye(count, dtype=F32) + link
    for _ in range(max(1, (count - 1).bit_length())):
        reach = jnp.minimum(jnp.dot(reach, reach, precision=lax.Precision.HIGHEST), 1.0)
    depth = jnp.sum(reach, axis=-1) - 1.0
    position = lengths.astype(F32) + depth
    half = (lat - rank) // 2
    index = jnp.arange(half, dtype=F32)
    inverse = 10000.0 ** (-2.0 * index / (2 * half))
    angle = position[:, None] * inverse[None, :]
    c, s = jnp.cos(angle), jnp.sin(angle)
    gap = jnp.zeros((count, 128 - 2 * half), F32)
    none = jnp.zeros_like(s)
    turn = jnp.stack(
        [
            jnp.concatenate([c, c, gap], axis=1),
            jnp.concatenate([-s, none, gap], axis=1),
            jnp.concatenate([none, s, gap], axis=1),
        ]
    )
    return reach, turn


def local(
    hidden,
    ffn_gain,
    attn_gain,
    latent_norm_gain,
    routes,
    gate_weights,
    expert_in,
    expert_down,
    kv_down,
    parents,
    lengths,
    queries,
    cache,
):
    size = lax.axis_size("ep")
    split = size // EXPERTS
    bits = [1 << b for b in range(split.bit_length() - 1)]
    width = hidden.shape[1]
    lat = kv_down.shape[1]
    heads = queries.shape[1]
    index = lax.axis_index("ep")
    place = jnp.stack([index // split, index % split]).astype(jnp.int32)

    def swap(x, bit):
        return lax.ppermute(x, "ep", [(i, i ^ bit) for i in range(size)])

    def spread(have, some):
        for bit in some:
            for r in sorted(have):
                have = have | {r ^ bit: swap(have[r], bit)}
        return have

    def to_line(xs):
        return [xs[0]] + [swap(xs[k], k * split) for k in range(1, EXPERTS)]

    q_t = jnp.transpose(queries, (0, 2, 1))
    cache_t = jnp.transpose(cache, (0, 2, 1))
    half = queries.shape[0] // 2
    reach, turn = tree(parents, lengths, KEY_VALUE_RANK, lat)
    allow = jnp.broadcast_to(reach[:, :, None], reach.shape + (heads,))

    packed = pack(place, hidden, ffn_gain[None], routes.T, gate_weights.T)
    near = to_line(packed[:EXPERTS])
    kv_far = swap(kv_down, bits[-1])
    first = cached_attention(lengths, after(q_t, packed[0]), cache_t, expert_in, 0, half)
    near, kv_far, first = lax.optimization_barrier((near, kv_far, first))
    *first, w_in = first
    line = jnp.concatenate(near, axis=0)
    info = jnp.concatenate([c[:, -TAIL:] for c in near], axis=0)
    groups = spread({0: line}, bits[:0:-1])
    own_quarters = to_line(after(packed[EXPERTS:], near[0]))
    second = cached_attention(lengths, after(q_t, line), cache_t, expert_down, half, half)
    groups, own_quarters, info, allow, turn, second = lax.optimization_barrier(
        (groups, own_quarters, info, allow, turn, second)
    )
    *second, w_out = second
    groups = spread(groups, bits[:1])
    kvs = spread({0: kv_down, bits[-1]: kv_far}, bits[-2::-1])
    groups, kvs = lax.optimization_barrier((groups, kvs))
    groups = [groups[r] for r in range(split)]
    kvs = [kvs[r] for r in range(split)]
    keep_a, send_a, keep_b, send_b = expert_slice(place, groups, w_in, w_out)

    def gathered(keep, got):
        terms = [keep, got]
        for bit in bits[1:]:
            out = sum(t[1::2].astype(F32) for t in terms).astype(BF)
            terms = [t[0::2] for t in terms] + [swap(out, bit)]
        return [sum(t[0, k].astype(F32) for t in terms).astype(BF) for k in range(EXPERTS // 2)]

    far = gathered(keep_a, swap(send_a, bits[0]))
    close = gathered(keep_b, swap(send_b, bits[0]))
    outs_e = to_line(close + far)
    own_sum, own_part, *rows = combine(place, outs_e, own_quarters, info, attn_gain[None], kvs)
    rows = [own_sum, own_part] + [swap(r, (k + 1) * split) for k, r in enumerate(rows)]
    return final_attention(
        place, width, rows, latent_norm_gain[None], turn, allow, q_t, first, second
    )


def solution(mesh):
    placed = (
        P(("group", "ep"), None),
        P(),
        P(),
        P(),
        P(("group", "ep"), None),
        P(("group", "ep"), None),
        P("ep", None, None),
        P("ep", None, None),
        P("ep", None),
        P(("group", "ep"), None),
        P(("group", "ep")),
        P(("group", "ep"), None, None),
        P(("group", "ep"), None, None),
    )
    return jax.shard_map(
        local,
        mesh=mesh,
        in_specs=placed,
        out_specs=(
            P(("group", "ep"), None),
            P(("group", "ep"), None),
            P(("group", "ep"), None, None),
        ),
        check_vma=False,
    )
```

time: 121 us -> 96 us (0.79)
  Pallas kernels: 41 us -> 26.9 us
  starting transfers between devices: 32.3 us -> 24.6 us
  waiting for transfers between devices: 39.9 us -> 35 us
    pallas_call x4 -> x5, Pallas kernels: 36.7 us -> 21.6 us  [the longest x2 11.6 us: cached_attention(): pl.pallas_call(functools.partial(cached_kernel, first, per), out_shape=[p...]
    ppermute x23 -> x22, starting transfers between devices: 32.3 us -> 24.6 us  [swap(): return lax.ppermute(x, 'ep', [(i, i ^ bit) for i in range(size)])]
    ppermute x23 -> x22, waiting for transfers between devices: 39.9 us -> 35 us  [swap(): return lax.ppermute(x, 'ep', [(i, i ^ bit) for i in range(size)])]
    unnamed x27 -> x15, local copies, waits for them, and re-layouts: 4.7 us -> 5.23 us
  transfers between devices with their start and end apart: 23 -> 22, of which waited for: 8 -> 12; matrix products, arithmetic and copies ran while one was open for 1% -> 2% of each run, Pallas kernels for 17% -> 14%
where the time goes in v2:
time: 96 us; the launch traced here: 95.8 us
  waiting for transfers between devices  35 us (36%)
  Pallas kernels  26.9 us (28%)
  starting transfers between devices  24.6 us (26%)
  local copies, waits for them, and re-layouts  5.49 us (6%)
  between operations  1.73 us (2%)
  matrix products  1.43 us (1%)
    ppermute x22, waiting for transfers between devices, swap(): return lax.ppermute(x, 'ep', [(i, i ^ bit) for i in range(size)])  35 us
    ppermute x22, starting transfers between devices, swap(): return lax.ppermute(x, 'ep', [(i, i ^ bit) for i in range(size)])  24.6 us
    pallas_call x2, Pallas kernels, cached_attention(): pl.pallas_call(functools.partial(cached_kernel, first, per), out_shape=[p...  11.6 us
    unnamed x15, local copies, waits for them, and re-layouts  5.23 us
    pallas_call x1, Pallas kernels, final_attention(): pl.pallas_call(functools.partial(final_kernel, width, per), out_shape=[ja...  4.4 us
    pallas_call x1, Pallas kernels, expert_slice(): pl.pallas_call(functools.partial(expert_kernel, split), out_shape=[act, h...  4.05 us
    pallas_call x1, Pallas kernels, combine(): pl.pallas_call(functools.partial(combine_kernel, split, tokens), out_shap...  3.22 us
    pallas_call x1, Pallas kernels, pack(): pl.pallas_call(pack_kernel, out_shape=[chunk] * EXPERTS + [part] * EXPERT...  2.09 us
  transfers between devices with their start and end apart: 22, of which 12 were waited for; matrix products, arithmetic and copies ran while one was open for 2% of the time, Pallas kernels for 14%

profile of v2, /device:TPU:0, one launch (start us, length us, event | category | flops | bytes accessed | tf_op | source)
XLA Modules:
  0.0 95.8 jit_solution(673861155926460121)
XLA Ops:
  0.6 3.0 %collective-permute-start.3 = (bf16[448,576]{1,0:T(8,128)(2,1)}, bf16[448,576]{1,0:T(8,128)(2,1)S(1)}, u32[]{:S(2)}, u32[]{:S(2)}) collective-permute-start(bf16[448,576]{1,0:T(8,128)(2,1)} %refs_10_), channel_id=1, source_target_pairs={{0,2},{1,3},{2,0},{3,1},{4,6},{5,7},{6,4},{7,5},{8,10},{9,11},{10,... | collective-permute-start | bytes 1548296 | tf_op jit(solution)/shard_map/ppermute | solution.py:507
  3.7 2.1 %pack.1 = (bf16[8,8192]{1,0:T(8,128)(2,1)S(1)}, bf16[8,8192]{1,0:T(8,128)(2,1)S(1)}, bf16[8,8192]{1,0:T(8,128)(2,1)S(1)}, bf16[8,8192]{1,0:T(8,128)(2,1)S(1)}, b...) custom-call(s32[2]{0:T(128)S(1)} %pad_add_fusion.e_ref, ...), custom_call_target="tpu_custom_call" | custom-call | flops 1024 | bytes 1024 | tf_op jit(solution)/shard_map/pack/pallas_call | solution.py:112
  5.8 1.6 %collective-permute-start = (bf16[8,8192]{1,0:T(8,128)(2,1)S(1)}, bf16[8,8192]{1,0:T(8,128)(2,1)S(1)}, u32[]{:S(2)}, u32[]{:S(2)}) collective-permute-start(bf16[8,8192]{1,0:T(8,128)(2,1)S(1)} %get-tuple-element.62), channel_id=1, source_target_pairs={{0,4},{1,5},{2,6},{3,7},{4,0},{5,1},{6,2},{7,3},{8,12},{9,13},{10,... | collective-permute-start | bytes 393224 | tf_op jit(solution)/shard_map/ppermute | solution.py:507
  7.5 2.6 %collective-permute-start.1 = (bf16[8,8192]{1,0:T(8,128)(2,1)S(1)}, bf16[8,8192]{1,0:T(8,128)(2,1)S(1)}, u32[]{:S(2)}, u32[]{:S(2)}) collective-permute-start(bf16[8,8192]{1,0:T(8,128)(2,1)S(1)} %get-tuple-element.63), channel_id=1, source_target_pairs={{0,8},{1,9},{2,10},{3,11},{4,12},{5,13},{6,14},{7,15},{8,0},{9,1},... | collective-permute-start | bytes 393224 | tf_op jit(solution)/shard_map/ppermute | solution.py:507
  11.0 1.0 %convolution_minimum_fusion.3 = f32[16,16]{0,1:T(8,128)S(1)} fusion(s32[16]{0:T(128)} %bitcast.41), kind=kOutput, calls=%fused_computation.3 | convolution fusion | flops 50688 | bytes 1088 | tf_op jit(solution)/shard_map/dot_general | solution.py:462
  12.5 5.9 %cached.2 = (bf16[8,128,512]{2,1,0:T(8,128)(2,1)S(1)}, f32[8,2,128]{2,1,0:T(2,128)S(1)}, bf16[1,7168,1024]{2,1,0:T(8,128)(2,1)S(1)}) custom-call(s32[1]{0:T(128)S(6)} %copy.20.length_ref, bf16[16,576,128]{2,1,0:T(8,128)(2,1)} %bitcast.31, bf16[1,576,1024]{2,1,0:T(8,128)(2,1)} %bitcast.36, bf16[1,7168,1024]{2,1,0:T(8,128)(2,1)} %refs_2_.2), custom_call_target="tpu_custom_call" | custom-call | flops 4563402752 | bytes 14680064 | tf_op jit(solution)/shard_map/cached/pallas_call | solution.py:344
  18.4 5.2 %copy-done = bf16[1,7168,1024]{2,1,0:T(8,128)(2,1)} copy-done((bf16[1,7168,1024]{2,1,0:T(8,128)(2,1)}, bf16[1,7168,1024]{2,1,0:T(8,128)(2,1)S(1)}, u32[]{:S(2)}) %copy-start) | copy-done | bytes 14680088
  24.4 0.9 collective-permute-start.5
  25.3 3.5 %collective-permute-start.6 = (bf16[16,1792]{1,0:T(8,128)(2,1)S(1)}, bf16[16,1792]{1,0:T(8,128)(2,1)S(1)}, u32[]{:S(2)}, u32[]{:S(2)}) collective-permute-start(bf16[16,1792]{1,0:T(8,128)(2,1)S(1)} %get-tuple-element.79), channel_id=1, source_target_pairs={{0,8},{1,9},{2,10},{3,11},{4,12},{5,13},{6,14},{7,15},{8,0},{9,1},... | collective-permute-start | bytes 172040 | tf_op jit(solution)/shard_map/ppermute | solution.py:507
  28.8 5.6 %cached.3 = (bf16[8,128,512]{2,1,0:T(8,128)(2,1)S(1)}, f32[8,2,128]{2,1,0:T(2,128)S(1)}, bf16[1,512,7168]{2,1,0:T(8,128)(2,1)S(1)}) custom-call(s32[1]{0:T(128)S(6)} %copy.20.length_ref, bf16[16,576,128]{2,1,0:T(8,128)(2,1)} %bitcast.32, bf16[1,576,1024]{2,1,0:T(8,128)(2,1)} %bitcast.37, bf16[1,512,7168]{2,1,0:T(8,128)(2,1)} %refs_2_.3), custom_call_target="tpu_custom_call" | custom-call | flops 4563402752 | bytes 7340032 | tf_op jit(solution)/shard_map/cached/pallas_call | solution.py:344
  34.8 2.0 %collective-permute-done.4.refs_2_ = bf16[32,8192]{1,0:T(8,128)(2,1)S(1)} collective-permute-done((bf16[32,8192]{1,0:T(8,128)(2,1)S(1)}, bf16[32,8192]{1,0:T(8,128)(2,1)S(1)}, u32[]{:S(2)}, u32[]{:S(2)}) %collective-permute-start.4) | collective-permute-done | bytes 524320 | tf_op jit(solution)/shard_map/ppermute | solution.py:507
  36.9 0.5 collective-permute-start.9
  37.5 0.4 collective-permute-start.11
  37.9 2.5 %collective-permute-done.10.refs_11_ = bf16[448,576]{1,0:T(8,128)(2,1)S(1)} collective-permute-done((bf16[448,576]{1,0:T(8,128)(2,1)S(1)}, bf16[448,576]{1,0:T(8,128)(2,1)S(1)}, u32[]{:S(2)}, u32[]{:S(2)}) %collective-permute-start.10) | collective-permute-done | bytes 516128 | tf_op jit(solution)/shard_map/ppermute | solution.py:507
  40.3 0.8 collective-permute-done.11.refs_13_
  41.2 4.0 %experts.1 = (bf16[160,512]{1,0:T(8,128)(2,1)S(1)}, bf16[2,2,40,1792]{3,2,1,0:T(8,128)(2,1)S(1)}, bf16[2,2,40,1792]{3,2,1,0:T(8,128)(2,1)S(1)}) custom-call(s32[2]{0:T(128)S(1)} %pad_add_fusion.e_ref, bf16[32,8192]{1,0:T(8,128)(2,1)S(1)} %constant_dynamic-update-slice_fusion.refs_0_, bf16[32,8192]{1,0:T(8,128)(2,1)S(1)} %collective-permute-done.8.refs_1_, ...), custom_call_target="tpu_custom_call" | custom-call | flops 1024 | bytes 1024 | tf_op jit(solution)/shard_map/experts/pallas_call | solution.py:181
  45.3 1.6 %experts_rest.1 = (bf16[2,2,40,1792]{3,2,1,0:T(8,128)(2,1)S(1)}, bf16[2,2,40,1792]{3,2,1,0:T(8,128)(2,1)S(1)}) custom-call(s32[2]{0:T(128)S(1)} %pad_add_fusion.e_ref, bf16[160,512]{1,0:T(8,128)(2,1)S(1)} %get-tuple-element.94.act, bf16[1,512,7168]{2,1,0:T(8,128)(2,1)S(1)} %get-tuple-element.93.refs_5_.w_out), custom_call_target="tpu_custom_call" | custom-call | flops 1024 | bytes 1024 | tf_op jit(solution)/shard_map/experts_rest/pallas_call | solution.py:191
  47.5 1.5 %collective-permute-done.12 = bf16[2,2,40,1792]{3,2,1,0:T(8,128)(2,1)S(1)} collective-permute-done((bf16[2,2,40,1792]{3,2,1,0:T(8,128)(2,1)S(1)}, bf16[2,2,40,1792]{3,2,1,0:T(8,128)(2,1)S(1)}, u32[]{:S(2)}, u32[]{:S(2)}) %collective-permute-start.12) | collective-permute-done | bytes 573472 | tf_op jit(solution)/shard_map/ppermute | solution.py:507
  49.0 0.6 collective-permute-start.13
  49.8 1.4 %collective-permute-start.16 = (bf16[1,2,40,1792]{3,2,1,0:T(8,128)(2,1)S(1)}, bf16[1,2,40,1792]{3,2,1,0:T(8,128)(2,1)S(1)}, u32[]{:S(2)}, u32[]{:S(2)}) collective-permute-start(bf16[1,2,40,1792]{3,2,1,0:T(8,128)(2,1)S(1)} %add_convert_fusion), channel_id=1, source_target_pairs={{0,2},{1,3},{2,0},{3,1},{4,6},{5,7},{6,4},{7,5},{8,10},{9,11},{10,... | collective-permute-start | bytes 860168 | tf_op jit(solution)/shard_map/ppermute | solution.py:507
  51.3 7.5 %collective-permute-done.13 = bf16[1,2,40,1792]{3,2,1,0:T(8,128)(2,1)S(1)} collective-permute-done((bf16[1,2,40,1792]{3,2,1,0:T(8,128)(2,1)S(1)}, bf16[1,2,40,1792]{3,2,1,0:T(8,128)(2,1)S(1)}, u32[]{:S(2)}, u32[]{:S(2)}) %collective-permute-start.13) | collective-permute-done | bytes 286752 | tf_op jit(solution)/shard_map/ppermute | solution.py:507
  58.9 0.7 collective-permute-start.14
  59.6 4.5 %collective-permute-done.16 = bf16[1,2,40,1792]{3,2,1,0:T(8,128)(2,1)S(1)} collective-permute-done((bf16[1,2,40,1792]{3,2,1,0:T(8,128)(2,1)S(1)}, bf16[1,2,40,1792]{3,2,1,0:T(8,128)(2,1)S(1)}, u32[]{:S(2)}, u32[]{:S(2)}) %collective-permute-start.16) | collective-permute-done | bytes 286752 | tf_op jit(solution)/shard_map/ppermute | solution.py:507
  64.2 3.6 %collective-permute-start.18 = (bf16[40,1792]{1,0:T(8,128)(2,1)S(1)}, bf16[40,1792]{1,0:T(8,128)(2,1)S(1)}, u32[]{:S(2)}, u32[]{:S(2)}) collective-permute-start(bf16[40,1792]{1,0:T(8,128)(2,1)S(1)} %get-tuple-element.119), channel_id=1, source_target_pairs={{0,12},{1,13},{2,14},{3,15},{4,8},{5,9},{6,10},{7,11},{8,4},{9,5},... | collective-permute-start | bytes 430088 | tf_op jit(solution)/shard_map/ppermute | solution.py:507
  67.8 4.9 %collective-permute-done.18.refs_3_ = bf16[40,1792]{1,0:T(8,128)(2,1)S(1)} collective-permute-done((bf16[40,1792]{1,0:T(8,128)(2,1)S(1)}, bf16[40,1792]{1,0:T(8,128)(2,1)S(1)}, u32[]{:S(2)}, u32[]{:S(2)}) %collective-permute-start.18) | collective-permute-done | bytes 143392 | tf_op jit(solution)/shard_map/ppermute | solution.py:507
  72.7 6.0 %collective-permute-done.17.refs_2_ = bf16[40,1792]{1,0:T(8,128)(2,1)S(1)} collective-permute-done((bf16[40,1792]{1,0:T(8,128)(2,1)S(1)}, bf16[40,1792]{1,0:T(8,128)(2,1)S(1)}, u32[]{:S(2)}, u32[]{:S(2)}) %collective-permute-start.17) | collective-permute-done | bytes 143392 | tf_op jit(solution)/shard_map/ppermute | solution.py:507
  78.6 3.2 %combine.1 = (f32[16,640]{1,0:T(8,128)S(1)}, bf16[16,1792]{1,0:T(8,128)(2,1)S(1)}, bf16[16,2432]{1,0:T(8,128)(2,1)S(1)}, bf16[16,2432]{1,0:T(8,128)(2,1)S(1)}, bf16[16,2432]{1,0:T(8,128)(2,1)S(1)}) custom-call(s32[2]{0:T(128)S(1)} %pad_add_fusion.e_ref, bf16[40,1792]{1,0:T(8,128)(2,1)S(1)} %get-tuple-element.122.refs_0_, ...), custom_call_target="tpu_custom_call" | custom-call | flops 1024 | bytes 1024 | tf_op jit(solution)/shard_map/combine/pallas_call | solution.py:278
  82.0 3.0 %collective-permute-start.20 = (bf16[16,2432]{1,0:T(8,128)(2,1)S(1)}, bf16[16,2432]{1,0:T(8,128)(2,1)S(1)}, u32[]{:S(2)}, u32[]{:S(2)}) collective-permute-start(bf16[16,2432]{1,0:T(8,128)(2,1)S(1)} %get-tuple-element.111), channel_id=1, source_target_pairs={{0,8},{1,9},{2,10},{3,11},{4,12},{5,13},{6,14},{7,15},{8,0},{9,1},... | collective-permute-start | bytes 233480 | tf_op jit(solution)/shard_map/ppermute | solution.py:507
  85.0 1.3 %collective-permute-start.21 = (bf16[16,2432]{1,0:T(8,128)(2,1)S(1)}, bf16[16,2432]{1,0:T(8,128)(2,1)S(1)}, u32[]{:S(2)}, u32[]{:S(2)}) collective-permute-start(bf16[16,2432]{1,0:T(8,128)(2,1)S(1)} %get-tuple-element.112), channel_id=1, source_target_pairs={{0,12},{1,13},{2,14},{3,15},{4,8},{5,9},{6,10},{7,11},{8,4},{9,5},... | collective-permute-start | bytes 233480 | tf_op jit(solution)/shard_map/ppermute | solution.py:507
  86.3 3.2 %collective-permute-done.20.refs_3_ = bf16[16,2432]{1,0:T(8,128)(2,1)S(1)} collective-permute-done((bf16[16,2432]{1,0:T(8,128)(2,1)S(1)}, bf16[16,2432]{1,0:T(8,128)(2,1)S(1)}, u32[]{:S(2)}, u32[]{:S(2)}) %collective-permute-start.20) | collective-permute-done | bytes 77856 | tf_op jit(solution)/shard_map/ppermute | solution.py:507
  89.5 1.7 %collective-permute-done.21.refs_4_ = bf16[16,2432]{1,0:T(8,128)(2,1)S(1)} collective-permute-done((bf16[16,2432]{1,0:T(8,128)(2,1)S(1)}, bf16[16,2432]{1,0:T(8,128)(2,1)S(1)}, u32[]{:S(2)}, u32[]{:S(2)}) %collective-permute-start.21) | collective-permute-done | bytes 77856 | tf_op jit(solution)/shard_map/ppermute | solution.py:507
  91.2 4.4 %final.1 = (bf16[16,7168]{1,0:T(8,128)(2,1)}, bf16[16,576]{1,0:T(8,128)(2,1)}, bf16[16,128,512]{2,1,0:T(8,128)(2,1)}) custom-call(s32[2]{0:T(128)S(1)} %pad_add_fusion.e_ref, f32[16,640]{1,0:T(8,128)S(1)} %get-tuple-element.108.refs_0_, bf16[16,1792]{1,0:T(8,128)(2,1)S(1)} %get-tuple-element.109.refs_1_, ...), custom_call_target="tpu_custom_call" | custom-call | flops 1024 | bytes 1024 | tf_op jit(solution)/shard_map/final/pallas_call | solution.py:438
  (59 shorter events, 3.3 us)
Async XLA Ops:
  0.6 23.3 %collective-permute-start.3 = (bf16[448,576]{1,0:T(8,128)(2,1)}, bf16[448,576]{1,0:T(8,128)(2,1)S(1)}, u32[]{:S(2)}, u32[]{:S(2)}) collective-permute-start(bf16[448,576]{1,0:T(8,128)(2,1)} %refs_10_), channel_id=1, source_target_pairs={{0,2},{1,3},{2,0},{3,1},{4,6},{5,7},{6,4},{7,5},{8,10},{9,11},{10,... | collective-permute-start | bytes 1548296 | tf_op jit(solution)/shard_map/ppermute | solution.py:507
  5.8 18.1 %collective-permute-start = (bf16[8,8192]{1,0:T(8,128)(2,1)S(1)}, bf16[8,8192]{1,0:T(8,128)(2,1)S(1)}, u32[]{:S(2)}, u32[]{:S(2)}) collective-permute-start(bf16[8,8192]{1,0:T(8,128)(2,1)S(1)} %get-tuple-element.62), channel_id=1, source_target_pairs={{0,4},{1,5},{2,6},{3,7},{4,0},{5,1},{6,2},{7,3},{8,12},{9,13},{10,... | collective-permute-start | bytes 393224 | tf_op jit(solution)/shard_map/ppermute | solution.py:507
  7.5 16.4 %collective-permute-start.1 = (bf16[8,8192]{1,0:T(8,128)(2,1)S(1)}, bf16[8,8192]{1,0:T(8,128)(2,1)S(1)}, u32[]{:S(2)}, u32[]{:S(2)}) collective-permute-start(bf16[8,8192]{1,0:T(8,128)(2,1)S(1)} %get-tuple-element.63), channel_id=1, source_target_pairs={{0,8},{1,9},{2,10},{3,11},{4,12},{5,13},{6,14},{7,15},{8,0},{9,1},... | collective-permute-start | bytes 393224 | tf_op jit(solution)/shard_map/ppermute | solution.py:507
  10.1 13.8 %collective-permute-start.2 = (bf16[8,8192]{1,0:T(8,128)(2,1)S(1)}, bf16[8,8192]{1,0:T(8,128)(2,1)S(1)}, u32[]{:S(2)}, u32[]{:S(2)}) collective-permute-start(bf16[8,8192]{1,0:T(8,128)(2,1)S(1)} %get-tuple-element.64), channel_id=1, source_target_pairs={{0,12},{1,13},{2,14},{3,15},{4,8},{5,9},{6,10},{7,11},{8,4},{9,5},... | collective-permute-start | bytes 393224 | tf_op jit(solution)/shard_map/ppermute | solution.py:507
  18.4 5.2 %copy-start = (bf16[1,7168,1024]{2,1,0:T(8,128)(2,1)}, bf16[1,7168,1024]{2,1,0:T(8,128)(2,1)S(1)}, u32[]{:S(2)}) copy-start(bf16[1,7168,1024]{2,1,0:T(8,128)(2,1)S(1)} %get-tuple-element.92.refs_4_) | copy-start | bytes 44040196
  24.0 12.7 %collective-permute-start.4 = (bf16[32,8192]{1,0:T(8,128)(2,1)S(1)}, bf16[32,8192]{1,0:T(8,128)(2,1)S(1)}, u32[]{:S(2)}, u32[]{:S(2)}) collective-permute-start(bf16[32,8192]{1,0:T(8,128)(2,1)S(1)} %constant_dynamic-update-slice_fusion.refs_0_), channel_id=1, source_target_pairs={{0,2},{1,3},{2,0},{3,1},{4,6},{5,7},{6,4},{7,5},{8,10},{9,11},{10,... | collective-permute-start | bytes 1572872 | tf_op jit(solution)/shard_map/ppermute | solution.py:507
  24.4 13.0 %copy-start.3 = (bf16[448,576]{1,0:T(8,128)(2,1)S(1)}, bf16[448,576]{1,0:T(8,128)(2,1)}, u32[]{:S(2)}) copy-start(bf16[448,576]{1,0:T(8,128)(2,1)} %refs_10_) | copy-start | bytes 1548292
  24.4 16.8 %copy-start.1 = (bf16[1,7168,1024]{2,1,0:T(8,128)(2,1)S(1)}, bf16[1,7168,1024]{2,1,0:T(8,128)(2,1)}, u32[]{:S(2)}) copy-start(bf16[1,7168,1024]{2,1,0:T(8,128)(2,1)} %copy-done) | copy-start | bytes 44040196
  24.4 10.0 %collective-permute-start.5 = (bf16[16,1792]{1,0:T(8,128)(2,1)S(1)}, bf16[16,1792]{1,0:T(8,128)(2,1)S(1)}, u32[]{:S(2)}, u32[]{:S(2)}) collective-permute-start(bf16[16,1792]{1,0:T(8,128)(2,1)S(1)} %get-tuple-element.78), channel_id=1, source_target_pairs={{0,4},{1,5},{2,6},{3,7},{4,0},{5,1},{6,2},{7,3},{8,12},{9,13},{10,... | collective-permute-start | bytes 172040 | tf_op jit(solution)/shard_map/ppermute | solution.py:507
  25.3 9.2 %collective-permute-start.6 = (bf16[16,1792]{1,0:T(8,128)(2,1)S(1)}, bf16[16,1792]{1,0:T(8,128)(2,1)S(1)}, u32[]{:S(2)}, u32[]{:S(2)}) collective-permute-start(bf16[16,1792]{1,0:T(8,128)(2,1)S(1)} %get-tuple-element.79), channel_id=1, source_target_pairs={{0,8},{1,9},{2,10},{3,11},{4,12},{5,13},{6,14},{7,15},{8,0},{9,1},... | collective-permute-start | bytes 172040 | tf_op jit(solution)/shard_map/ppermute | solution.py:507
  28.8 6.0 %collective-permute-start.7 = (bf16[16,1792]{1,0:T(8,128)(2,1)S(1)}, bf16[16,1792]{1,0:T(8,128)(2,1)S(1)}, u32[]{:S(2)}, u32[]{:S(2)}) collective-permute-start(bf16[16,1792]{1,0:T(8,128)(2,1)S(1)} %get-tuple-element.80), channel_id=1, source_target_pairs={{0,12},{1,13},{2,14},{3,15},{4,8},{5,9},{6,10},{7,11},{8,4},{9,5},... | collective-permute-start | bytes 172040 | tf_op jit(solution)/shard_map/ppermute | solution.py:507
  36.8 4.4 %collective-permute-start.8 = (bf16[32,8192]{1,0:T(8,128)(2,1)S(1)}, bf16[32,8192]{1,0:T(8,128)(2,1)S(1)}, u32[]{:S(2)}, u32[]{:S(2)}) collective-permute-start(bf16[32,8192]{1,0:T(8,128)(2,1)S(1)} %constant_dynamic-update-slice_fusion.refs_0_), channel_id=1, source_target_pairs={{0,1},{1,0},{2,3},{3,2},{4,5},{5,4},{6,7},{7,6},{8,9},{9,8},{10,11... | collective-permute-start | bytes 1572872 | tf_op jit(solution)/shard_map/ppermute | solution.py:507
  36.9 4.3 %collective-permute-start.9 = (bf16[32,8192]{1,0:T(8,128)(2,1)S(1)}, bf16[32,8192]{1,0:T(8,128)(2,1)S(1)}, u32[]{:S(2)}, u32[]{:S(2)}) collective-permute-start(bf16[32,8192]{1,0:T(8,128)(2,1)S(1)} %collective-permute-done.4.refs_2_), channel_id=1, source_target_pairs={{0,1},{1,0},{2,3},{3,2},{4,5},{5,4},{6,7},{7,6},{8,9},{9,8},{10,11... | collective-permute-start | bytes 1572872 | tf_op jit(solution)/shard_map/ppermute | solution.py:507
  37.4 3.0 %collective-permute-start.10 = (bf16[448,576]{1,0:T(8,128)(2,1)S(1)}, bf16[448,576]{1,0:T(8,128)(2,1)S(1)}, u32[]{:S(2)}, u32[]{:S(2)}) collective-permute-start(bf16[448,576]{1,0:T(8,128)(2,1)S(1)} %copy-done.3), channel_id=1, source_target_pairs={{0,1},{1,0},{2,3},{3,2},{4,5},{5,4},{6,7},{7,6},{8,9},{9,8},{10,11... | collective-permute-start | bytes 1548296 | tf_op jit(solution)/shard_map/ppermute | solution.py:507
  37.5 3.7 %collective-permute-start.11 = (bf16[448,576]{1,0:T(8,128)(2,1)S(1)}, bf16[448,576]{1,0:T(8,128)(2,1)S(1)}, u32[]{:S(2)}, u32[]{:S(2)}) collective-permute-start(bf16[448,576]{1,0:T(8,128)(2,1)S(1)} %collective-permute-done.3.refs_12_), channel_id=1, source_target_pairs={{0,1},{1,0},{2,3},{3,2},{4,5},{5,4},{6,7},{7,6},{8,9},{9,8},{10,11... | collective-permute-start | bytes 1548296 | tf_op jit(solution)/shard_map/ppermute | solution.py:507
  45.2 33.4 %copy-start.4 = (f32[7168]{0:T(1024)S(1)}, f32[7168]{0:T(1024)}, u32[]{:S(2)}) copy-start(f32[7168]{0:T(1024)} %param.15) | copy-start | bytes 86020
  45.2 46.0 %copy-start.2 = (bf16[16,128,576]{1,2,0:T(8,128)(2,1)S(1)}, bf16[16,128,576]{1,2,0:T(8,128)(2,1)}, u32[]{:S(2)}) copy-start(bf16[16,128,576]{1,2,0:T(8,128)(2,1)} %param.24) | copy-start | bytes 7077892
  45.3 46.0 %copy-start.5 = (f32[512]{0:T(512)S(1)}, f32[512]{0:T(512)}, u32[]{:S(2)}) copy-start(f32[512]{0:T(512)} %param.16) | copy-start | bytes 6148
  46.9 2.0 %collective-permute-start.12 = (bf16[2,2,40,1792]{3,2,1,0:T(8,128)(2,1)S(1)}, bf16[2,2,40,1792]{3,2,1,0:T(8,128)(2,1)S(1)}, u32[]{:S(2)}, u32[]{:S(2)}) collective-permute-start(bf16[2,2,40,1792]{3,2,1,0:T(8,128)(2,1)S(1)} %get-tuple-element.96), channel_id=1, source_target_pairs={{0,1},{1,0},{2,3},{3,2},{4,5},{5,4},{6,7},{7,6},{8,9},{9,8},{10,11... | collective-permute-start | bytes 1720328 | tf_op jit(solution)/shard_map/ppermute | solution.py:507
  47.1 2.7 %collective-permute-start.15 = (bf16[2,2,40,1792]{3,2,1,0:T(8,128)(2,1)S(1)}, bf16[2,2,40,1792]{3,2,1,0:T(8,128)(2,1)S(1)}, u32[]{:S(2)}, u32[]{:S(2)}) collective-permute-start(bf16[2,2,40,1792]{3,2,1,0:T(8,128)(2,1)S(1)} %get-tuple-element.98), channel_id=1, source_target_pairs={{0,1},{1,0},{2,3},{3,2},{4,5},{5,4},{6,7},{7,6},{8,9},{9,8},{10,11... | collective-permute-start | bytes 1720328 | tf_op jit(solution)/shard_map/ppermute | solution.py:507
  49.0 9.7 %collective-permute-start.13 = (bf16[1,2,40,1792]{3,2,1,0:T(8,128)(2,1)S(1)}, bf16[1,2,40,1792]{3,2,1,0:T(8,128)(2,1)S(1)}, u32[]{:S(2)}, u32[]{:S(2)}) collective-permute-start(bf16[1,2,40,1792]{3,2,1,0:T(8,128)(2,1)S(1)} %add_convert_fusion.1), channel_id=1, source_target_pairs={{0,2},{1,3},{2,0},{3,1},{4,6},{5,7},{6,4},{7,5},{8,10},{9,11},{10,... | collective-permute-start | bytes 860168 | tf_op jit(solution)/shard_map/ppermute | solution.py:507
  49.8 14.3 %collective-permute-start.16 = (bf16[1,2,40,1792]{3,2,1,0:T(8,128)(2,1)S(1)}, bf16[1,2,40,1792]{3,2,1,0:T(8,128)(2,1)S(1)}, u32[]{:S(2)}, u32[]{:S(2)}) collective-permute-start(bf16[1,2,40,1792]{3,2,1,0:T(8,128)(2,1)S(1)} %add_convert_fusion), channel_id=1, source_target_pairs={{0,2},{1,3},{2,0},{3,1},{4,6},{5,7},{6,4},{7,5},{8,10},{9,11},{10,... | collective-permute-start | bytes 860168 | tf_op jit(solution)/shard_map/ppermute | solution.py:507
  58.9 8.9 %collective-permute-start.14 = (bf16[40,1792]{1,0:T(8,128)(2,1)S(1)}, bf16[40,1792]{1,0:T(8,128)(2,1)S(1)}, u32[]{:S(2)}, u32[]{:S(2)}) collective-permute-start(bf16[40,1792]{1,0:T(8,128)(2,1)S(1)} %get-tuple-element.121), channel_id=1, source_target_pairs={{0,4},{1,5},{2,6},{3,7},{4,0},{5,1},{6,2},{7,3},{8,12},{9,13},{10,... | collective-permute-start | bytes 430088 | tf_op jit(solution)/shard_map/ppermute | solution.py:507
  64.2 8.5 %collective-permute-start.18 = (bf16[40,1792]{1,0:T(8,128)(2,1)S(1)}, bf16[40,1792]{1,0:T(8,128)(2,1)S(1)}, u32[]{:S(2)}, u32[]{:S(2)}) collective-permute-start(bf16[40,1792]{1,0:T(8,128)(2,1)S(1)} %get-tuple-element.119), channel_id=1, source_target_pairs={{0,12},{1,13},{2,14},{3,15},{4,8},{5,9},{6,10},{7,11},{8,4},{9,5},... | collective-permute-start | bytes 430088 | tf_op jit(solution)/shard_map/ppermute | solution.py:507
  67.8 10.8 %collective-permute-start.17 = (bf16[40,1792]{1,0:T(8,128)(2,1)S(1)}, bf16[40,1792]{1,0:T(8,128)(2,1)S(1)}, u32[]{:S(2)}, u32[]{:S(2)}) collective-permute-start(bf16[40,1792]{1,0:T(8,128)(2,1)S(1)} %get-tuple-element.120), channel_id=1, source_target_pairs={{0,8},{1,9},{2,10},{3,11},{4,12},{5,13},{6,14},{7,15},{8,0},{9,1},... | collective-permute-start | bytes 430088 | tf_op jit(solution)/shard_map/ppermute | solution.py:507
  81.9 4.5 %collective-permute-start.19 = (bf16[16,2432]{1,0:T(8,128)(2,1)S(1)}, bf16[16,2432]{1,0:T(8,128)(2,1)S(1)}, u32[]{:S(2)}, u32[]{:S(2)}) collective-permute-start(bf16[16,2432]{1,0:T(8,128)(2,1)S(1)} %get-tuple-element.110), channel_id=1, source_target_pairs={{0,4},{1,5},{2,6},{3,7},{4,0},{5,1},{6,2},{7,3},{8,12},{9,13},{10,... | collective-permute-start | bytes 233480 | tf_op jit(solution)/shard_map/ppermute | solution.py:507
  82.0 7.6 %collective-permute-start.20 = (bf16[16,2432]{1,0:T(8,128)(2,1)S(1)}, bf16[16,2432]{1,0:T(8,128)(2,1)S(1)}, u32[]{:S(2)}, u32[]{:S(2)}) collective-permute-start(bf16[16,2432]{1,0:T(8,128)(2,1)S(1)} %get-tuple-element.111), channel_id=1, source_target_pairs={{0,8},{1,9},{2,10},{3,11},{4,12},{5,13},{6,14},{7,15},{8,0},{9,1},... | collective-permute-start | bytes 233480 | tf_op jit(solution)/shard_map/ppermute | solution.py:507
  85.0 6.2 %collective-permute-start.21 = (bf16[16,2432]{1,0:T(8,128)(2,1)S(1)}, bf16[16,2432]{1,0:T(8,128)(2,1)S(1)}, u32[]{:S(2)}, u32[]{:S(2)}) collective-permute-start(bf16[16,2432]{1,0:T(8,128)(2,1)S(1)} %get-tuple-element.112), channel_id=1, source_target_pairs={{0,12},{1,13},{2,14},{3,15},{4,8},{5,9},{6,10},{7,11},{8,4},{9,5},... | collective-permute-start | bytes 233480 | tf_op jit(solution)/shard_map/ppermute | solution.py:507

commit v3 on v2

--- a/solution.py
+++ b/solution.py
@@ -140,7 +140,7 @@
 
 def expert_kernel(split, e_ref, *refs):
     groups = refs[:split]
-    w_in, w_out, act, keep, send, x = refs[split:]
+    w_in, w_out, act, *pieces, x = refs[split:]
     width = w_in.shape[1]
     hid = act.shape[1]
     piece = width // 8
@@ -161,7 +161,8 @@
         gate = dot(x[...], w_in[0, :, i * step : (i + 1) * step])
         up = dot(x[...], w_in[0, :, hid + i * step : hid + (i + 1) * step])
         act[:, i * step : (i + 1) * step] = (gate / (1.0 + jnp.exp(-gate)) * up).astype(BF)
-    down(split, e_ref, act, w_out, keep, send, 2)
+    down(split, e_ref, act, w_out, pieces[0], pieces[1], 3)
+    down(split, e_ref, act, w_out, pieces[2], pieces[3], 2)
 
 
 def expert_rest_kernel(split, e_ref, act, w_out, keep, send):
@@ -174,21 +175,22 @@
     hid = hid2 // 2
     quarter = width // EXPERTS
     half = jax.ShapeDtypeStruct((split // 2, EXPERTS // 2, ROWS, quarter), BF)
+    single = jax.ShapeDtypeStruct((split // 2, 1, ROWS, quarter), BF)
     rows = ROWS * split
     act = jax.ShapeDtypeStruct((rows, hid), BF)
     vmem = pl.BlockSpec(memory_space=pltpu.VMEM)
     smem = pl.BlockSpec(memory_space=pltpu.SMEM)
-    act, keep_a, send_a = pl.pallas_call(
+    act, *single = pl.pallas_call(
         functools.partial(expert_kernel, split),
-        out_shape=[act, half, half],
+        out_shape=[act] + [single] * 4,
         in_specs=[smem] + [vmem] * (split + 2),
-        out_specs=[vmem] * 3,
+        out_specs=[vmem] * 5,
         scratch_shapes=[pltpu.VMEM((rows, width), BF)],
         compiler_params=params(10),
         cost_estimate=COST,
         name="experts",
     )(e, *groups, w_in, w_out)
-    keep_b, send_b = pl.pallas_call(
+    rest = pl.pallas_call(
         functools.partial(expert_rest_kernel, split),
         out_shape=[half, half],
         in_specs=[smem] + [vmem] * 2,
@@ -197,7 +199,7 @@
         cost_estimate=COST,
         name="experts_rest",
     )(e, act, w_out)
-    return keep_a, send_a, keep_b, send_b
+    return single[:2], single[2:], rest
 
 
 def combine_kernel(split, tokens, e_ref, *refs):
@@ -356,7 +358,7 @@
             pltpu.VMEM((ctx, (lat // 128 + 1) * 128), BF),
             pltpu.SemaphoreType.DMA((3,)),
         ],
-        compiler_params=params(16),
+        compiler_params=params(14),
         cost_estimate=pl.CostEstimate(
             flops=4 * count * heads * ctx * (lat + KEY_VALUE_RANK),
             bytes_accessed=2 * weight.size,
@@ -524,35 +526,33 @@
     packed = pack(place, hidden, ffn_gain[None], routes.T, gate_weights.T)
     near = to_line(packed[:EXPERTS])
     kv_far = swap(kv_down, bits[-1])
-    first = cached_attention(lengths, after(q_t, packed[0]), cache_t, expert_in, 0, half)
+    *first, w_out = cached_attention(lengths, after(q_t, packed[0]), cache_t, expert_down, 0, half)
     near, kv_far, first = lax.optimization_barrier((near, kv_far, first))
-    *first, w_in = first
     line = jnp.concatenate(near, axis=0)
     info = jnp.concatenate([c[:, -TAIL:] for c in near], axis=0)
     groups = spread({0: line}, bits[:0:-1])
     own_quarters = to_line(after(packed[EXPERTS:], near[0]))
-    second = cached_attention(lengths, after(q_t, line), cache_t, expert_down, half, half)
+    *second, w_in = cached_attention(lengths, after(q_t, line), cache_t, expert_in, half, half)
     groups, own_quarters, info, allow, turn, second = lax.optimization_barrier(
         (groups, own_quarters, info, allow, turn, second)
     )
-    *second, w_out = second
     groups = spread(groups, bits[:1])
-    kvs = spread({0: kv_down, bits[-1]: kv_far}, bits[-2::-1])
-    groups, kvs = lax.optimization_barrier((groups, kvs))
     groups = [groups[r] for r in range(split)]
+    pieces = expert_slice(place, groups, w_in, w_out)
+    kvs = {0: after(kv_down, pieces[0]), bits[-1]: kv_far}
+    kvs = spread(kvs, bits[-2::-1])
     kvs = [kvs[r] for r in range(split)]
-    keep_a, send_a, keep_b, send_b = expert_slice(place, groups, w_in, w_out)
-
-    def gathered(keep, got):
-        terms = [keep, got]
+
+    def gathered(keep, send):
+        terms = [keep, swap(send, bits[0])]
         for bit in bits[1:]:
             out = sum(t[1::2].astype(F32) for t in terms).astype(BF)
             terms = [t[0::2] for t in terms] + [swap(out, bit)]
-        return [sum(t[0, k].astype(F32) for t in terms).astype(BF) for k in range(EXPERTS // 2)]
-
-    far = gathered(keep_a, swap(send_a, bits[0]))
-    close = gathered(keep_b, swap(send_b, bits[0]))
-    outs_e = to_line(close + far)
+        return [sum(t[0, k].astype(F32) for t in terms).astype(BF) for k in range(keep.shape[1])]
+
+    far, middle, close = [gathered(*p) for p in pieces]
+    close = close + middle + far
+    outs_e = to_line(close)
     own_sum, own_part, *rows = combine(place, outs_e, own_quarters, info, attn_gain[None], kvs)
     rows = [own_sum, own_part] + [swap(r, (k + 1) * split) for k, r in enumerate(rows)]
     return final_attention(

time: 96 us -> 85.4 us (0.89)
  waiting for transfers between devices: 35 us -> 24.3 us
  starting transfers between devices: 24.6 us -> 27 us
  local copies, waits for them, and re-layouts: 5.49 us -> 3.2 us
    ppermute x22 -> x24, waiting for transfers between devices: 35 us -> 24.3 us  [swap(): return lax.ppermute(x, 'ep', [(i, i ^ bit) for i in range(size)])]
    ppermute x22 -> x24, starting transfers between devices: 24.6 us -> 27 us  [swap(): return lax.ppermute(x, 'ep', [(i, i ^ bit) for i in range(size)])]
    unnamed x15 -> x17, local copies, waits for them, and re-layouts: 5.23 us -> 2.95 us
  transfers between devices with their start and end apart: 22 -> 24, of which waited for: 12 -> 11; matrix products, arithmetic and copies ran while one was open for 2% -> 3% of each run, Pallas kernels for 14% -> 15%
where the time goes in v3:
time: 85.4 us; the launch traced here: 85.2 us
  starting transfers between devices  27 us (32%)
  Pallas kernels  26.7 us (31%)
  waiting for transfers between devices  24.3 us (28%)
  local copies, waits for them, and re-layouts  3.2 us (4%)
  between operations  1.79 us (2%)
  matrix products  1.43 us (2%)
    ppermute x24, starting transfers between devices, swap(): return lax.ppermute(x, 'ep', [(i, i ^ bit) for i in range(size)])  27 us
    ppermute x24, waiting for transfers between devices, swap(): return lax.ppermute(x, 'ep', [(i, i ^ bit) for i in range(size)])  24.3 us
    pallas_call x2, Pallas kernels, cached_attention(): pl.pallas_call(functools.partial(cached_kernel, first, per), out_shape=[p...  11.6 us
    pallas_call x1, Pallas kernels, final_attention(): pl.pallas_call(functools.partial(final_kernel, width, per), out_shape=[ja...  4.4 us
    pallas_call x1, Pallas kernels, expert_slice(): pl.pallas_call(functools.partial(expert_kernel, split), out_shape=[act] +...  4.05 us
    pallas_call x1, Pallas kernels, combine(): pl.pallas_call(functools.partial(combine_kernel, split, tokens), out_shap...  3.22 us
    unnamed x17, local copies, waits for them, and re-layouts  2.95 us
    pallas_call x1, Pallas kernels, pack(): pl.pallas_call(pack_kernel, out_shape=[chunk] * EXPERTS + [part] * EXPERT...  2.09 us
  transfers between devices with their start and end apart: 24, of which 11 were waited for; matrix products, arithmetic and copies ran while one was open for 3% of the time, Pallas kernels for 15%

profile of v3, /device:TPU:0, one launch (start us, length us, event | category | flops | bytes accessed | tf_op | source)
XLA Modules:
  0.0 85.2 jit_solution(6482539644917840135)
XLA Ops:
  0.7 2.1 %pack.1 = (bf16[8,8192]{1,0:T(8,128)(2,1)S(1)}, bf16[8,8192]{1,0:T(8,128)(2,1)S(1)}, bf16[8,8192]{1,0:T(8,128)(2,1)S(1)}, bf16[8,8192]{1,0:T(8,128)(2,1)S(1)}, b...) custom-call(s32[2]{0:T(128)S(1)} %pad_add_fusion.e_ref, ...), custom_call_target="tpu_custom_call" | custom-call | flops 1024 | bytes 1024 | tf_op jit(solution)/shard_map/pack/pallas_call | solution.py:112
  2.8 3.1 %collective-permute-start = (bf16[8,8192]{1,0:T(8,128)(2,1)S(1)}, bf16[8,8192]{1,0:T(8,128)(2,1)S(1)}, u32[]{:S(2)}, u32[]{:S(2)}) collective-permute-start(bf16[8,8192]{1,0:T(8,128)(2,1)S(1)} %get-tuple-element.55), channel_id=1, source_target_pairs={{0,4},{1,5},{2,6},{3,7},{4,0},{5,1},{6,2},{7,3},{8,12},{9,13},{10,... | collective-permute-start | bytes 393224 | tf_op jit(solution)/shard_map/ppermute | solution.py:509
  5.9 2.6 %collective-permute-start.1 = (bf16[8,8192]{1,0:T(8,128)(2,1)S(1)}, bf16[8,8192]{1,0:T(8,128)(2,1)S(1)}, u32[]{:S(2)}, u32[]{:S(2)}) collective-permute-start(bf16[8,8192]{1,0:T(8,128)(2,1)S(1)} %get-tuple-element.56), channel_id=1, source_target_pairs={{0,8},{1,9},{2,10},{3,11},{4,12},{5,13},{6,14},{7,15},{8,0},{9,1},... | collective-permute-start | bytes 393224 | tf_op jit(solution)/shard_map/ppermute | solution.py:509
  8.5 1.7 %collective-permute-start.3 = (bf16[448,576]{1,0:T(8,128)(2,1)}, bf16[448,576]{1,0:T(8,128)(2,1)S(1)}, u32[]{:S(2)}, u32[]{:S(2)}) collective-permute-start(bf16[448,576]{1,0:T(8,128)(2,1)} %refs_10_), channel_id=1, source_target_pairs={{0,2},{1,3},{2,0},{3,1},{4,6},{5,7},{6,4},{7,5},{8,10},{9,11},{10,... | collective-permute-start | bytes 1548296 | tf_op jit(solution)/shard_map/ppermute | solution.py:509
  10.9 1.0 %convolution_minimum_fusion.3 = f32[16,16]{0,1:T(8,128)S(1)} fusion(s32[16]{0:T(128)} %bitcast.43), kind=kOutput, calls=%fused_computation.3 | convolution fusion | flops 50688 | bytes 1088 | tf_op jit(solution)/shard_map/dot_general | solution.py:464
  12.4 5.6 %cached.2 = (bf16[8,128,512]{2,1,0:T(8,128)(2,1)S(1)}, f32[8,2,128]{2,1,0:T(2,128)S(1)}, bf16[1,512,7168]{2,1,0:T(8,128)(2,1)S(1)}) custom-call(s32[1]{0:T(128)S(6)} %copy.20.length_ref, bf16[16,576,128]{2,1,0:T(8,128)(2,1)} %bitcast.33, bf16[1,576,1024]{2,1,0:T(8,128)(2,1)} %bitcast.38, bf16[1,512,7168]{2,1,0:T(8,128)(2,1)} %refs_2_.2), custom_call_target="tpu_custom_call" | custom-call | flops 4563402752 | bytes 7340032 | tf_op jit(solution)/shard_map/cached/pallas_call | solution.py:346
  18.1 2.9 %copy-done = bf16[1,512,7168]{2,1,0:T(8,128)(2,1)} copy-done((bf16[1,512,7168]{2,1,0:T(8,128)(2,1)}, bf16[1,512,7168]{2,1,0:T(8,128)(2,1)S(1)}, u32[]{:S(2)}) %copy-start) | copy-done | bytes 7340056
  21.3 1.6 %collective-permute-done.3.refs_12_ = bf16[448,576]{1,0:T(8,128)(2,1)S(1)} collective-permute-done((bf16[448,576]{1,0:T(8,128)(2,1)}, bf16[448,576]{1,0:T(8,128)(2,1)S(1)}, u32[]{:S(2)}, u32[]{:S(2)}) %collective-permute-start.3) | collective-permute-done | bytes 516128 | tf_op jit(solution)/shard_map/ppermute | solution.py:509
  23.0 1.6 %collective-permute-start.4 = (bf16[32,8192]{1,0:T(8,128)(2,1)S(1)}, bf16[32,8192]{1,0:T(8,128)(2,1)S(1)}, u32[]{:S(2)}, u32[]{:S(2)}) collective-permute-start(bf16[32,8192]{1,0:T(8,128)(2,1)S(1)} %constant_dynamic-update-slice_fusion.refs_0_), channel_id=1, source_target_pairs={{0,2},{1,3},{2,0},{3,1},{4,6},{5,7},{6,4},{7,5},{8,10},{9,11},{10,... | collective-permute-start | bytes 1572872 | tf_op jit(solution)/shard_map/ppermute | solution.py:509
  24.6 0.6 collective-permute-start.5
  25.2 3.5 %collective-permute-start.6 = (bf16[16,1792]{1,0:T(8,128)(2,1)S(1)}, bf16[16,1792]{1,0:T(8,128)(2,1)S(1)}, u32[]{:S(2)}, u32[]{:S(2)}) collective-permute-start(bf16[16,1792]{1,0:T(8,128)(2,1)S(1)} %get-tuple-element.71), channel_id=1, source_target_pairs={{0,8},{1,9},{2,10},{3,11},{4,12},{5,13},{6,14},{7,15},{8,0},{9,1},... | collective-permute-start | bytes 172040 | tf_op jit(solution)/shard_map/ppermute | solution.py:509
  29.0 5.9 %cached.3 = (bf16[8,128,512]{2,1,0:T(8,128)(2,1)S(1)}, f32[8,2,128]{2,1,0:T(2,128)S(1)}, bf16[1,7168,1024]{2,1,0:T(8,128)(2,1)S(1)}) custom-call(s32[1]{0:T(128)S(6)} %copy.20.length_ref, bf16[16,576,128]{2,1,0:T(8,128)(2,1)} %bitcast.34, bf16[1,576,1024]{2,1,0:T(8,128)(2,1)} %bitcast.39, bf16[1,7168,1024]{2,1,0:T(8,128)(2,1)} %refs_2_.3), custom_call_target="tpu_custom_call" | custom-call | flops 4563402752 | bytes 14680064 | tf_op jit(solution)/shard_map/cached/pallas_call | solution.py:346
  35.4 0.5 collective-permute-start.9
  35.9 1.4 %collective-permute-done.8.refs_1_ = bf16[32,8192]{1,0:T(8,128)(2,1)S(1)} collective-permute-done((bf16[32,8192]{1,0:T(8,128)(2,1)S(1)}, bf16[32,8192]{1,0:T(8,128)(2,1)S(1)}, u32[]{:S(2)}, u32[]{:S(2)}) %collective-permute-start.8) | collective-permute-done | bytes 524320 | tf_op jit(solution)/shard_map/ppermute | solution.py:509
  37.3 0.7 collective-permute-done.9.refs_3_
  38.1 4.1 %experts.1 = (bf16[160,512]{1,0:T(8,128)(2,1)S(1)}, bf16[2,1,40,1792]{3,2,1,0:T(8,128)(2,1)S(1)}, bf16[2,1,40,1792]{3,2,1,0:T(8,128)(2,1)S(1)}, bf16[2,1,40,1792...) custom-call(s32[2]{0:T(128)S(1)} %pad_add_fusion.e_ref, bf16[32,8192]{1,0:T(8,128)(2,1)S(1)} %constant_dynamic-update-slice_fusion.refs_0_, ...), custom_call_target="tpu_custom_call" | custom-call | flops 1024 | bytes 1024 | tf_op jit(solution)/shard_map/experts/pallas_call | solution.py:183
  42.3 0.4 collective-permute-start.20
  43.2 1.4 %experts_rest.1 = (bf16[2,2,40,1792]{3,2,1,0:T(8,128)(2,1)S(1)}, bf16[2,2,40,1792]{3,2,1,0:T(8,128)(2,1)S(1)}) custom-call(s32[2]{0:T(128)S(1)} %pad_add_fusion.e_ref, bf16[160,512]{1,0:T(8,128)(2,1)S(1)} %get-tuple-element.80.act, bf16[1,512,7168]{2,1,0:T(8,128)(2,1)S(1)} %bitcast.32), custom_call_target="tpu_custom_call" | custom-call | flops 1024 | bytes 1024 | tf_op jit(solution)/shard_map/experts_rest/pallas_call | solution.py:193
  45.0 1.4 %collective-permute-start.17 = (bf16[1,1,40,1792]{3,2,1,0:T(8,128)(2,1)S(1)}, bf16[1,1,40,1792]{3,2,1,0:T(8,128)(2,1)S(1)}, u32[]{:S(2)}, u32[]{:S(2)}) collective-permute-start(bf16[1,1,40,1792]{3,2,1,0:T(8,128)(2,1)S(1)} %add_convert_fusion.2), channel_id=1, source_target_pairs={{0,2},{1,3},{2,0},{3,1},{4,6},{5,7},{6,4},{7,5},{8,10},{9,11},{10,... | collective-permute-start | bytes 430088 | tf_op jit(solution)/shard_map/ppermute | solution.py:509
  46.4 0.8 collective-permute-start.14
  47.2 4.4 %collective-permute-done.17 = bf16[1,1,40,1792]{3,2,1,0:T(8,128)(2,1)S(1)} collective-permute-done((bf16[1,1,40,1792]{3,2,1,0:T(8,128)(2,1)S(1)}, bf16[1,1,40,1792]{3,2,1,0:T(8,128)(2,1)S(1)}, u32[]{:S(2)}, u32[]{:S(2)}) %collective-permute-start.17) | collective-permute-done | bytes 143392 | tf_op jit(solution)/shard_map/ppermute | solution.py:509
  51.7 3.3 %collective-permute-start.18 = (bf16[40,1792]{1,0:T(8,128)(2,1)S(1)}, bf16[40,1792]{1,0:T(8,128)(2,1)S(1)}, u32[]{:S(2)}, u32[]{:S(2)}) collective-permute-start(bf16[40,1792]{1,0:T(8,128)(2,1)S(1)} %fusion.3), channel_id=1, source_target_pairs={{0,12},{1,13},{2,14},{3,15},{4,8},{5,9},{6,10},{7,11},{8,4},{9,5},... | collective-permute-start | bytes 430088 | tf_op jit(solution)/shard_map/ppermute | solution.py:509
  55.1 1.6 %collective-permute-start.11 = (bf16[1,2,40,1792]{3,2,1,0:T(8,128)(2,1)S(1)}, bf16[1,2,40,1792]{3,2,1,0:T(8,128)(2,1)S(1)}, u32[]{:S(2)}, u32[]{:S(2)}) collective-permute-start(bf16[1,2,40,1792]{3,2,1,0:T(8,128)(2,1)S(1)} %add_convert_fusion), channel_id=1, source_target_pairs={{0,2},{1,3},{2,0},{3,1},{4,6},{5,7},{6,4},{7,5},{8,10},{9,11},{10,... | collective-permute-start | bytes 860168 | tf_op jit(solution)/shard_map/ppermute | solution.py:509
  56.8 5.6 %collective-permute-done.11 = bf16[1,2,40,1792]{3,2,1,0:T(8,128)(2,1)S(1)} collective-permute-done((bf16[1,2,40,1792]{3,2,1,0:T(8,128)(2,1)S(1)}, bf16[1,2,40,1792]{3,2,1,0:T(8,128)(2,1)S(1)}, u32[]{:S(2)}, u32[]{:S(2)}) %collective-permute-start.11) | collective-permute-done | bytes 286752 | tf_op jit(solution)/shard_map/ppermute | solution.py:509
  62.7 3.2 %collective-permute-done.15.refs_2_ = bf16[40,1792]{1,0:T(8,128)(2,1)S(1)} collective-permute-done((bf16[40,1792]{1,0:T(8,128)(2,1)S(1)}, bf16[40,1792]{1,0:T(8,128)(2,1)S(1)}, u32[]{:S(2)}, u32[]{:S(2)}) %collective-permute-start.15) | collective-permute-done | bytes 143392 | tf_op jit(solution)/shard_map/ppermute | solution.py:509
  65.8 2.7 %collective-permute-done.12.refs_1_ = bf16[40,1792]{1,0:T(8,128)(2,1)S(1)} collective-permute-done((bf16[40,1792]{1,0:T(8,128)(2,1)S(1)}, bf16[40,1792]{1,0:T(8,128)(2,1)S(1)}, u32[]{:S(2)}, u32[]{:S(2)}) %collective-permute-start.12) | collective-permute-done | bytes 143392 | tf_op jit(solution)/shard_map/ppermute | solution.py:509
  68.5 3.2 %combine.1 = (f32[16,640]{1,0:T(8,128)S(1)}, bf16[16,1792]{1,0:T(8,128)(2,1)S(1)}, bf16[16,2432]{1,0:T(8,128)(2,1)S(1)}, bf16[16,2432]{1,0:T(8,128)(2,1)S(1)}, bf16[16,2432]{1,0:T(8,128)(2,1)S(1)}) custom-call(s32[2]{0:T(128)S(1)} %pad_add_fusion.e_ref, bf16[40,1792]{1,0:T(8,128)(2,1)S(1)} %get-tuple-element.106.refs_0_, ...), custom_call_target="tpu_custom_call" | custom-call | flops 1024 | bytes 1024 | tf_op jit(solution)/shard_map/combine/pallas_call | solution.py:280
  71.8 2.5 %collective-permute-start.22 = (bf16[16,2432]{1,0:T(8,128)(2,1)S(1)}, bf16[16,2432]{1,0:T(8,128)(2,1)S(1)}, u32[]{:S(2)}, u32[]{:S(2)}) collective-permute-start(bf16[16,2432]{1,0:T(8,128)(2,1)S(1)} %get-tuple-element.97), channel_id=1, source_target_pairs={{0,8},{1,9},{2,10},{3,11},{4,12},{5,13},{6,14},{7,15},{8,0},{9,1},... | collective-permute-start | bytes 233480 | tf_op jit(solution)/shard_map/ppermute | solution.py:509
  74.3 1.9 %collective-permute-start.23 = (bf16[16,2432]{1,0:T(8,128)(2,1)S(1)}, bf16[16,2432]{1,0:T(8,128)(2,1)S(1)}, u32[]{:S(2)}, u32[]{:S(2)}) collective-permute-start(bf16[16,2432]{1,0:T(8,128)(2,1)S(1)} %get-tuple-element.98), channel_id=1, source_target_pairs={{0,12},{1,13},{2,14},{3,15},{4,8},{5,9},{6,10},{7,11},{8,4},{9,5},... | collective-permute-start | bytes 233480 | tf_op jit(solution)/shard_map/ppermute | solution.py:509
  76.3 3.3 %collective-permute-done.22.refs_3_ = bf16[16,2432]{1,0:T(8,128)(2,1)S(1)} collective-permute-done((bf16[16,2432]{1,0:T(8,128)(2,1)S(1)}, bf16[16,2432]{1,0:T(8,128)(2,1)S(1)}, u32[]{:S(2)}, u32[]{:S(2)}) %collective-permute-start.22) | collective-permute-done | bytes 77856 | tf_op jit(solution)/shard_map/ppermute | solution.py:509
  79.7 0.9 %collective-permute-done.23.refs_4_ = bf16[16,2432]{1,0:T(8,128)(2,1)S(1)} collective-permute-done((bf16[16,2432]{1,0:T(8,128)(2,1)S(1)}, bf16[16,2432]{1,0:T(8,128)(2,1)S(1)}, u32[]{:S(2)}, u32[]{:S(2)}) %collective-permute-start.23) | collective-permute-done | bytes 77856 | tf_op jit(solution)/shard_map/ppermute | solution.py:509
  80.6 4.4 %final.1 = (bf16[16,7168]{1,0:T(8,128)(2,1)}, bf16[16,576]{1,0:T(8,128)(2,1)}, bf16[16,128,512]{2,1,0:T(8,128)(2,1)}) custom-call(s32[2]{0:T(128)S(1)} %pad_add_fusion.e_ref, f32[16,640]{1,0:T(8,128)S(1)} %get-tuple-element.94.refs_0_, bf16[16,1792]{1,0:T(8,128)(2,1)S(1)} %get-tuple-element.95.refs_1_, bf16[16,2432]{1,0:T(8,128)(2,1)S(1)} %collective-permute-done.21.refs_2_, ...), custom_call_target="tpu_custom_call" | custom-call | flops 1024 | bytes 1024 | tf_op jit(solution)/shard_map/final/pallas_call | solution.py:440
  (68 shorter events, 3.5 us)
Async XLA Ops:
  2.8 18.5 %collective-permute-start = (bf16[8,8192]{1,0:T(8,128)(2,1)S(1)}, bf16[8,8192]{1,0:T(8,128)(2,1)S(1)}, u32[]{:S(2)}, u32[]{:S(2)}) collective-permute-start(bf16[8,8192]{1,0:T(8,128)(2,1)S(1)} %get-tuple-element.55), channel_id=1, source_target_pairs={{0,4},{1,5},{2,6},{3,7},{4,0},{5,1},{6,2},{7,3},{8,12},{9,13},{10,... | collective-permute-start | bytes 393224 | tf_op jit(solution)/shard_map/ppermute | solution.py:509
  5.9 15.4 %collective-permute-start.1 = (bf16[8,8192]{1,0:T(8,128)(2,1)S(1)}, bf16[8,8192]{1,0:T(8,128)(2,1)S(1)}, u32[]{:S(2)}, u32[]{:S(2)}) collective-permute-start(bf16[8,8192]{1,0:T(8,128)(2,1)S(1)} %get-tuple-element.56), channel_id=1, source_target_pairs={{0,8},{1,9},{2,10},{3,11},{4,12},{5,13},{6,14},{7,15},{8,0},{9,1},... | collective-permute-start | bytes 393224 | tf_op jit(solution)/shard_map/ppermute | solution.py:509
  8.5 12.8 %collective-permute-start.2 = (bf16[8,8192]{1,0:T(8,128)(2,1)S(1)}, bf16[8,8192]{1,0:T(8,128)(2,1)S(1)}, u32[]{:S(2)}, u32[]{:S(2)}) collective-permute-start(bf16[8,8192]{1,0:T(8,128)(2,1)S(1)} %get-tuple-element.57), channel_id=1, source_target_pairs={{0,12},{1,13},{2,14},{3,15},{4,8},{5,9},{6,10},{7,11},{8,4},{9,5},... | collective-permute-start | bytes 393224 | tf_op jit(solution)/shard_map/ppermute | solution.py:509
  8.5 14.4 %collective-permute-start.3 = (bf16[448,576]{1,0:T(8,128)(2,1)}, bf16[448,576]{1,0:T(8,128)(2,1)S(1)}, u32[]{:S(2)}, u32[]{:S(2)}) collective-permute-start(bf16[448,576]{1,0:T(8,128)(2,1)} %refs_10_), channel_id=1, source_target_pairs={{0,2},{1,3},{2,0},{3,1},{4,6},{5,7},{6,4},{7,5},{8,10},{9,11},{10,... | collective-permute-start | bytes 1548296 | tf_op jit(solution)/shard_map/ppermute | solution.py:509
  18.1 2.9 %copy-start = (bf16[1,512,7168]{2,1,0:T(8,128)(2,1)}, bf16[1,512,7168]{2,1,0:T(8,128)(2,1)S(1)}, u32[]{:S(2)}) copy-start(bf16[1,512,7168]{2,1,0:T(8,128)(2,1)S(1)} %get-tuple-element.79.refs_5_.w_out) | copy-start | bytes 22020100
  23.0 12.2 %collective-permute-start.4 = (bf16[32,8192]{1,0:T(8,128)(2,1)S(1)}, bf16[32,8192]{1,0:T(8,128)(2,1)S(1)}, u32[]{:S(2)}, u32[]{:S(2)}) collective-permute-start(bf16[32,8192]{1,0:T(8,128)(2,1)S(1)} %constant_dynamic-update-slice_fusion.refs_0_), channel_id=1, source_target_pairs={{0,2},{1,3},{2,0},{3,1},{4,6},{5,7},{6,4},{7,5},{8,10},{9,11},{10,... | collective-permute-start | bytes 1572872 | tf_op jit(solution)/shard_map/ppermute | solution.py:509
  24.6 13.5 %slice-start = ((s8[7340032]{0:T(1024)(128)(4,1)}), s8[4194304]{0:T(1024)(128)(4,1)S(1)}, s32[]{:S(2)}) async-start(s8[7340032]{0:T(1024)(128)(4,1)} %bitcast.31), calls=%async_computation | async-start | bytes 8388608
  24.6 13.5 %slice-start.1 = ((s8[7340032]{0:T(1024)(128)(4,1)}), s8[3145728]{0:T(1024)(128)(4,1)S(1)}, s32[]{:S(2)}) async-start(s8[7340032]{0:T(1024)(128)(4,1)} %bitcast.31), calls=%async_computation.1 | async-start | bytes 6291456
  24.6 10.3 %collective-permute-start.5 = (bf16[16,1792]{1,0:T(8,128)(2,1)S(1)}, bf16[16,1792]{1,0:T(8,128)(2,1)S(1)}, u32[]{:S(2)}, u32[]{:S(2)}) collective-permute-start(bf16[16,1792]{1,0:T(8,128)(2,1)S(1)} %get-tuple-element.70), channel_id=1, source_target_pairs={{0,4},{1,5},{2,6},{3,7},{4,0},{5,1},{6,2},{7,3},{8,12},{9,13},{10,... | collective-permute-start | bytes 172040 | tf_op jit(solution)/shard_map/ppermute | solution.py:509
  25.2 9.7 %collective-permute-start.6 = (bf16[16,1792]{1,0:T(8,128)(2,1)S(1)}, bf16[16,1792]{1,0:T(8,128)(2,1)S(1)}, u32[]{:S(2)}, u32[]{:S(2)}) collective-permute-start(bf16[16,1792]{1,0:T(8,128)(2,1)S(1)} %get-tuple-element.71), channel_id=1, source_target_pairs={{0,8},{1,9},{2,10},{3,11},{4,12},{5,13},{6,14},{7,15},{8,0},{9,1},... | collective-permute-start | bytes 172040 | tf_op jit(solution)/shard_map/ppermute | solution.py:509
  28.7 6.3 %collective-permute-start.7 = (bf16[16,1792]{1,0:T(8,128)(2,1)S(1)}, bf16[16,1792]{1,0:T(8,128)(2,1)S(1)}, u32[]{:S(2)}, u32[]{:S(2)}) collective-permute-start(bf16[16,1792]{1,0:T(8,128)(2,1)S(1)} %get-tuple-element.72), channel_id=1, source_target_pairs={{0,12},{1,13},{2,14},{3,15},{4,8},{5,9},{6,10},{7,11},{8,4},{9,5},... | collective-permute-start | bytes 172040 | tf_op jit(solution)/shard_map/ppermute | solution.py:509
  35.3 2.0 %collective-permute-start.8 = (bf16[32,8192]{1,0:T(8,128)(2,1)S(1)}, bf16[32,8192]{1,0:T(8,128)(2,1)S(1)}, u32[]{:S(2)}, u32[]{:S(2)}) collective-permute-start(bf16[32,8192]{1,0:T(8,128)(2,1)S(1)} %constant_dynamic-update-slice_fusion.refs_0_), channel_id=1, source_target_pairs={{0,1},{1,0},{2,3},{3,2},{4,5},{5,4},{6,7},{7,6},{8,9},{9,8},{10,11... | collective-permute-start | bytes 1572872 | tf_op jit(solution)/shard_map/ppermute | solution.py:509
  35.4 2.6 %collective-permute-start.9 = (bf16[32,8192]{1,0:T(8,128)(2,1)S(1)}, bf16[32,8192]{1,0:T(8,128)(2,1)S(1)}, u32[]{:S(2)}, u32[]{:S(2)}) collective-permute-start(bf16[32,8192]{1,0:T(8,128)(2,1)S(1)} %collective-permute-done.4.refs_2_), channel_id=1, source_target_pairs={{0,1},{1,0},{2,3},{3,2},{4,5},{5,4},{6,7},{7,6},{8,9},{9,8},{10,11... | collective-permute-start | bytes 1572872 | tf_op jit(solution)/shard_map/ppermute | solution.py:509
  38.1 4.7 %copy-start.2 = (bf16[448,576]{1,0:T(8,128)(2,1)S(1)}, bf16[448,576]{1,0:T(8,128)(2,1)}, u32[]{:S(2)}) copy-start(bf16[448,576]{1,0:T(8,128)(2,1)} %refs_10_) | copy-start | bytes 1548292
  42.1 26.4 %copy-start.3 = (f32[7168]{0:T(1024)S(1)}, f32[7168]{0:T(1024)}, u32[]{:S(2)}) copy-start(f32[7168]{0:T(1024)} %param.15) | copy-start | bytes 86020
  42.1 2.8 %collective-permute-start.16 = (bf16[2,1,40,1792]{3,2,1,0:T(8,128)(2,1)S(1)}, bf16[2,1,40,1792]{3,2,1,0:T(8,128)(2,1)S(1)}, u32[]{:S(2)}, u32[]{:S(2)}) collective-permute-start(bf16[2,1,40,1792]{3,2,1,0:T(8,128)(2,1)S(1)} %get-tuple-element.86), channel_id=1, source_target_pairs={{0,1},{1,0},{2,3},{3,2},{4,5},{5,4},{6,7},{7,6},{8,9},{9,8},{10,11... | collective-permute-start | bytes 860168 | tf_op jit(solution)/shard_map/ppermute | solution.py:509
  42.3 20.3 %collective-permute-start.20 = (bf16[448,576]{1,0:T(8,128)(2,1)S(1)}, bf16[448,576]{1,0:T(8,128)(2,1)S(1)}, u32[]{:S(2)}, u32[]{:S(2)}) collective-permute-start(bf16[448,576]{1,0:T(8,128)(2,1)S(1)} %collective-permute-done.3.refs_12_), channel_id=1, source_target_pairs={{0,1},{1,0},{2,3},{3,2},{4,5},{5,4},{6,7},{7,6},{8,9},{9,8},{10,11... | collective-permute-start | bytes 1548296 | tf_op jit(solution)/shard_map/ppermute | solution.py:509
  42.7 37.9 %copy-start.1 = (bf16[16,128,576]{1,2,0:T(8,128)(2,1)S(1)}, bf16[16,128,576]{1,2,0:T(8,128)(2,1)}, u32[]{:S(2)}) copy-start(bf16[16,128,576]{1,2,0:T(8,128)(2,1)} %param.24) | copy-start | bytes 7077892
  42.7 37.9 %copy-start.4 = (f32[512]{0:T(512)S(1)}, f32[512]{0:T(512)}, u32[]{:S(2)}) copy-start(f32[512]{0:T(512)} %param.16) | copy-start | bytes 6148
  42.7 19.9 %collective-permute-start.19 = (bf16[448,576]{1,0:T(8,128)(2,1)S(1)}, bf16[448,576]{1,0:T(8,128)(2,1)S(1)}, u32[]{:S(2)}, u32[]{:S(2)}) collective-permute-start(bf16[448,576]{1,0:T(8,128)(2,1)S(1)} %copy-done.2), channel_id=1, source_target_pairs={{0,1},{1,0},{2,3},{3,2},{4,5},{5,4},{6,7},{7,6},{8,9},{9,8},{10,11... | collective-permute-start | bytes 1548296 | tf_op jit(solution)/shard_map/ppermute | solution.py:509
  42.8 3.5 %collective-permute-start.13 = (bf16[2,1,40,1792]{3,2,1,0:T(8,128)(2,1)S(1)}, bf16[2,1,40,1792]{3,2,1,0:T(8,128)(2,1)S(1)}, u32[]{:S(2)}, u32[]{:S(2)}) collective-permute-start(bf16[2,1,40,1792]{3,2,1,0:T(8,128)(2,1)S(1)} %get-tuple-element.84), channel_id=1, source_target_pairs={{0,1},{1,0},{2,3},{3,2},{4,5},{5,4},{6,7},{7,6},{8,9},{9,8},{10,11... | collective-permute-start | bytes 860168 | tf_op jit(solution)/shard_map/ppermute | solution.py:509
  44.6 10.4 %collective-permute-start.10 = (bf16[2,2,40,1792]{3,2,1,0:T(8,128)(2,1)S(1)}, bf16[2,2,40,1792]{3,2,1,0:T(8,128)(2,1)S(1)}, u32[]{:S(2)}, u32[]{:S(2)}) collective-permute-start(bf16[2,2,40,1792]{3,2,1,0:T(8,128)(2,1)S(1)} %get-tuple-element.82), channel_id=1, source_target_pairs={{0,1},{1,0},{2,3},{3,2},{4,5},{5,4},{6,7},{7,6},{8,9},{9,8},{10,11... | collective-permute-start | bytes 1720328 | tf_op jit(solution)/shard_map/ppermute | solution.py:509
  45.0 6.7 %collective-permute-start.17 = (bf16[1,1,40,1792]{3,2,1,0:T(8,128)(2,1)S(1)}, bf16[1,1,40,1792]{3,2,1,0:T(8,128)(2,1)S(1)}, u32[]{:S(2)}, u32[]{:S(2)}) collective-permute-start(bf16[1,1,40,1792]{3,2,1,0:T(8,128)(2,1)S(1)} %add_convert_fusion.2), channel_id=1, source_target_pairs={{0,2},{1,3},{2,0},{3,1},{4,6},{5,7},{6,4},{7,5},{8,10},{9,11},{10,... | collective-permute-start | bytes 430088 | tf_op jit(solution)/shard_map/ppermute | solution.py:509
  46.4 10.3 %collective-permute-start.14 = (bf16[1,1,40,1792]{3,2,1,0:T(8,128)(2,1)S(1)}, bf16[1,1,40,1792]{3,2,1,0:T(8,128)(2,1)S(1)}, u32[]{:S(2)}, u32[]{:S(2)}) collective-permute-start(bf16[1,1,40,1792]{3,2,1,0:T(8,128)(2,1)S(1)} %add_convert_fusion.4), channel_id=1, source_target_pairs={{0,2},{1,3},{2,0},{3,1},{4,6},{5,7},{6,4},{7,5},{8,10},{9,11},{10,... | collective-permute-start | bytes 430088 | tf_op jit(solution)/shard_map/ppermute | solution.py:509
  51.7 10.9 %collective-permute-start.18 = (bf16[40,1792]{1,0:T(8,128)(2,1)S(1)}, bf16[40,1792]{1,0:T(8,128)(2,1)S(1)}, u32[]{:S(2)}, u32[]{:S(2)}) collective-permute-start(bf16[40,1792]{1,0:T(8,128)(2,1)S(1)} %fusion.3), channel_id=1, source_target_pairs={{0,12},{1,13},{2,14},{3,15},{4,8},{5,9},{6,10},{7,11},{8,4},{9,5},... | collective-permute-start | bytes 430088 | tf_op jit(solution)/shard_map/ppermute | solution.py:509
  55.1 7.3 %collective-permute-start.11 = (bf16[1,2,40,1792]{3,2,1,0:T(8,128)(2,1)S(1)}, bf16[1,2,40,1792]{3,2,1,0:T(8,128)(2,1)S(1)}, u32[]{:S(2)}, u32[]{:S(2)}) collective-permute-start(bf16[1,2,40,1792]{3,2,1,0:T(8,128)(2,1)S(1)} %add_convert_fusion), channel_id=1, source_target_pairs={{0,2},{1,3},{2,0},{3,1},{4,6},{5,7},{6,4},{7,5},{8,10},{9,11},{10,... | collective-permute-start | bytes 860168 | tf_op jit(solution)/shard_map/ppermute | solution.py:509
  56.8 9.1 %collective-permute-start.15 = (bf16[40,1792]{1,0:T(8,128)(2,1)S(1)}, bf16[40,1792]{1,0:T(8,128)(2,1)S(1)}, u32[]{:S(2)}, u32[]{:S(2)}) collective-permute-start(bf16[40,1792]{1,0:T(8,128)(2,1)S(1)} %fusion.2), channel_id=1, source_target_pairs={{0,8},{1,9},{2,10},{3,11},{4,12},{5,13},{6,14},{7,15},{8,0},{9,1},... | collective-permute-start | bytes 430088 | tf_op jit(solution)/shard_map/ppermute | solution.py:509
  62.5 6.0 %collective-permute-start.12 = (bf16[40,1792]{1,0:T(8,128)(2,1)S(1)}, bf16[40,1792]{1,0:T(8,128)(2,1)S(1)}, u32[]{:S(2)}, u32[]{:S(2)}) collective-permute-start(bf16[40,1792]{1,0:T(8,128)(2,1)S(1)} %get-tuple-element.105), channel_id=1, source_target_pairs={{0,4},{1,5},{2,6},{3,7},{4,0},{5,1},{6,2},{7,3},{8,12},{9,13},{10,... | collective-permute-start | bytes 430088 | tf_op jit(solution)/shard_map/ppermute | solution.py:509
  71.7 4.6 %collective-permute-start.21 = (bf16[16,2432]{1,0:T(8,128)(2,1)S(1)}, bf16[16,2432]{1,0:T(8,128)(2,1)S(1)}, u32[]{:S(2)}, u32[]{:S(2)}) collective-permute-start(bf16[16,2432]{1,0:T(8,128)(2,1)S(1)} %get-tuple-element.96), channel_id=1, source_target_pairs={{0,4},{1,5},{2,6},{3,7},{4,0},{5,1},{6,2},{7,3},{8,12},{9,13},{10,... | collective-permute-start | bytes 233480 | tf_op jit(solution)/shard_map/ppermute | solution.py:509
  71.8 7.9 %collective-permute-start.22 = (bf16[16,2432]{1,0:T(8,128)(2,1)S(1)}, bf16[16,2432]{1,0:T(8,128)(2,1)S(1)}, u32[]{:S(2)}, u32[]{:S(2)}) collective-permute-start(bf16[16,2432]{1,0:T(8,128)(2,1)S(1)} %get-tuple-element.97), channel_id=1, source_target_pairs={{0,8},{1,9},{2,10},{3,11},{4,12},{5,13},{6,14},{7,15},{8,0},{9,1},... | collective-permute-start | bytes 233480 | tf_op jit(solution)/shard_map/ppermute | solution.py:509
  74.3 6.3 %collective-permute-start.23 = (bf16[16,2432]{1,0:T(8,128)(2,1)S(1)}, bf16[16,2432]{1,0:T(8,128)(2,1)S(1)}, u32[]{:S(2)}, u32[]{:S(2)}) collective-permute-start(bf16[16,2432]{1,0:T(8,128)(2,1)S(1)} %get-tuple-element.98), channel_id=1, source_target_pairs={{0,12},{1,13},{2,14},{3,15},{4,8},{5,9},{6,10},{7,11},{8,4},{9,5},... | collective-permute-start | bytes 233480 | tf_op jit(solution)/shard_map/ppermute | solution.py:509

commit v4 on v3

--- a/solution.py
+++ b/solution.py
@@ -17,6 +17,7 @@
 F32 = jnp.float32
 softmax_scale = 192.0 ** (-0.5)
 MIB = 1024 * 1024
+LONG = pl.CostEstimate(flops=1 << 34, bytes_accessed=1 << 24, transcendentals=0)
 COST = pl.CostEstimate(flops=1024, bytes_accessed=1024, transcendentals=0)
 LOG2E = 1.4426950408889634
 
@@ -139,14 +140,14 @@
 
 
 def expert_kernel(split, e_ref, *refs):
-    groups = refs[:split]
-    w_in, w_out, act, *pieces, x = refs[split:]
+    groups = refs[: 2 * split]
+    w_in, w_out, act, *pieces, x = refs[2 * split :]
     width = w_in.shape[1]
     hid = act.shape[1]
     piece = width // 8
     main_rows, last_rows = 32 * split, 8 * split
-    for r in range(split):
-        x[32 * r : 32 * r + 32, :] = groups[r][:, :width]
+    for r in range(2 * split):
+        x[16 * r : 16 * r + 16, :] = groups[r][:, :width]
     ext = jnp.concatenate([g[:, width : width + piece] for g in groups], axis=0)
     row = iota((8 * last_rows, main_rows), 0)
     col = iota((8 * last_rows, main_rows), 1)
@@ -170,7 +171,7 @@
 
 
 def expert_slice(e, groups, w_in, w_out):
-    split = len(groups)
+    split = len(groups) // 2
     width, hid2 = w_in.shape[1:]
     hid = hid2 // 2
     quarter = width // EXPERTS
@@ -183,7 +184,7 @@
     act, *single = pl.pallas_call(
         functools.partial(expert_kernel, split),
         out_shape=[act] + [single] * 4,
-        in_specs=[smem] + [vmem] * (split + 2),
+        in_specs=[smem] + [vmem] * (2 * split + 2),
         out_specs=[vmem] * 5,
         scratch_shapes=[pltpu.VMEM((rows, width), BF)],
         compiler_params=params(10),
@@ -202,32 +203,36 @@
     return single[:2], single[2:], rest
 
 
-def combine_kernel(split, tokens, e_ref, *refs):
-    outs_e, hid = refs[:EXPERTS], refs[EXPERTS : 2 * EXPERTS]
-    info_ref, gain_ref = refs[2 * EXPERTS : 2 * EXPERTS + 2]
-    kvs = refs[2 * EXPERTS + 2 : 2 * EXPERTS + 2 + split]
-    rest = refs[2 * EXPERTS + 2 + split :]
-    own_sum, own_part = rest[:2]
-    sent = rest[2 : 1 + EXPERTS]
-    kv_ref, sem = rest[1 + EXPERTS :]
-    part = kvs[0].shape[0]
-    lat = kvs[0].shape[1]
-    copies = []
-    for r in range(split):
-        place = pl.multiple_of((e_ref[1] ^ r) * part, 16)
-        copies.append(
-            pltpu.make_async_copy(kvs[r], kv_ref.at[pl.ds(place, part), :], sem.at[r])
-        )
-        copies[-1].start()
+def join_kernel(a_ref, b_ref, out_ref):
+    rows = a_ref.shape[0]
+    out_ref[:rows, :] = a_ref[...]
+    out_ref[rows:, :] = b_ref[...]
+
+
+def join(a, b):
+    vmem = pl.BlockSpec(memory_space=pltpu.VMEM)
+    return pl.pallas_call(
+        join_kernel,
+        out_shape=pltpu.VMEM((2 * a.shape[0], a.shape[1]), a.dtype),
+        in_specs=[vmem, vmem],
+        out_specs=vmem,
+        compiler_params=params(2),
+        cost_estimate=COST,
+        name="join",
+    )(a, b)
+
+
+def gate_kernel(tokens, e_ref, *refs):
+    out_ref = refs[-1]
+    info = jnp.concatenate([r[:, r.shape[1] - TAIL :] for r in refs[:-1]], axis=0)
     one = (iota((tokens, TAIL), 0) == iota((tokens, TAIL), 1)).astype(BF)
-    info = dot_t(one, info_ref[...])
+    info = dot_t(one, info)
     earlier = (iota((tokens, tokens), 1) < iota((tokens, tokens), 0)).astype(BF)
     lane = iota((tokens, ROWS), 1).astype(F32)
     hits = []
     for k in range(EXPERTS):
         expert = (e_ref[0] ^ k).astype(F32)
         hits.append(jnp.where(info == expert, 1.0, 0.0))
-    moe = None
     for k in range(EXPERTS):
         blocks = [[], [], []]
         for s in range(EXPERTS):
@@ -243,8 +248,39 @@
                 g1 = info[:, 8 * s + 5 + p : 8 * s + 6 + p]
                 gate = jnp.broadcast_to(h0 * g0 + h1 * g1, (tokens, ROWS))
                 blocks[p].append(jnp.where(chosen, gate, 0.0))
-        weights = jnp.concatenate(blocks[0] + blocks[1] + blocks[2], axis=0).astype(BF)
-        term = dot(weights, outs_e[k][...])
+        out_ref[k] = jnp.concatenate(blocks[0] + blocks[1] + blocks[2], axis=0).astype(BF)
+
+def gate_matrices(place, halves, tokens):
+    vmem = pl.BlockSpec(memory_space=pltpu.VMEM)
+    return pl.pallas_call(
+        functools.partial(gate_kernel, tokens),
+        out_shape=pltpu.VMEM((EXPERTS, 3 * EXPERTS * tokens, ROWS), BF),
+        in_specs=[pl.BlockSpec(memory_space=pltpu.SMEM)] + [vmem] * len(halves),
+        out_specs=vmem,
+        compiler_params=params(4),
+        cost_estimate=LONG,
+        name="gates",
+    )(place, *halves)
+
+
+def combine_kernel(spots, tokens, e_ref, *refs):
+    outs_e, hid = refs[:EXPERTS], refs[EXPERTS : 2 * EXPERTS]
+    gates_ref, gain_ref = refs[2 * EXPERTS : 2 * EXPERTS + 2]
+    kvs = refs[2 * EXPERTS + 2 : 2 * EXPERTS + 2 + len(spots)]
+    rest = refs[2 * EXPERTS + 2 + len(spots) :]
+    own_sum, own_part = rest[:2]
+    sent = rest[2 : 1 + EXPERTS]
+    kv_ref, sem = rest[1 + EXPERTS :]
+    lat = kvs[0].shape[1]
+    part = spots[0][1]
+    copies = []
+    for i, (r, rows, first) in enumerate(spots):
+        place = pl.multiple_of((e_ref[1] ^ r) * part + first, 16)
+        copies.append(pltpu.make_async_copy(kvs[i], kv_ref.at[pl.ds(place, rows), :], sem.at[i]))
+        copies[-1].start()
+    moe = None
+    for k in range(EXPERTS):
+        term = dot(gates_ref[k], outs_e[k][...])
         moe = term if moe is None else moe + term
     total = EXPERTS * tokens
     moe = moe[:total] + moe[total : 2 * total] + moe[2 * total :]
@@ -270,15 +306,16 @@
             own_part[...] = mixed[span].astype(BF)
 
 
-def combine(place, outs_e, hid, info, gain, kvs):
-    split = len(kvs)
+def combine(place, outs_e, hid, gates, gain, kvs):
+    spots = [(r, x.shape[0], first) for r, first, x in kvs]
+    kvs = [x for _, _, x in kvs]
     tokens, quarter = hid[0].shape
-    part, lat = kvs[0].shape
+    lat = kvs[0].shape[1]
     padded = (lat // 128 + 1) * 128
     outs = [pltpu.VMEM((tokens, padded), F32), pltpu.VMEM((tokens, quarter), BF)]
     outs += [pltpu.VMEM((tokens, padded + quarter), BF)] * (EXPERTS - 1)
     return pl.pallas_call(
-        functools.partial(combine_kernel, split, tokens),
+        functools.partial(combine_kernel, spots, tokens),
         out_shape=outs,
         grid_spec=pltpu.PrefetchScalarGridSpec(
             num_scalar_prefetch=1,
@@ -286,32 +323,38 @@
             in_specs=[whole(o.shape) for o in outs_e]
             + [whole(h.shape) for h in hid]
             + [
-                whole(info.shape),
+                whole(gates.shape),
                 pl.BlockSpec((1, quarter), lambda t, e: (0, e[0])),
             ]
-            + [pl.BlockSpec(memory_space=pl.ANY)] * split,
+            + [pl.BlockSpec(memory_space=pl.ANY)] * len(kvs),
             out_specs=[whole(o.shape) for o in outs],
             scratch_shapes=[
-                pltpu.VMEM((split * part, lat), BF),
-                pltpu.SemaphoreType.DMA((split,)),
+                pltpu.VMEM((quarter, lat), BF),
+                pltpu.SemaphoreType.DMA((len(kvs),)),
             ],
         ),
         compiler_params=params(8),
         cost_estimate=COST,
         name="combine",
-    )(place, *outs_e, *hid, info, gain, *kvs)
+    )(place, *outs_e, *hid, gates, gain, *kvs)
 
 
 def cached_kernel(begin, per, length_ref, *refs):
-    q_hbm, cache_hbm, w_hbm, out_ref, stat_ref, w_ref, q_ref, cache_ref, keys_ref, sem = refs
+    q_ref, cache_ref, keys_ref, sem = refs[-4:]
+    loads = (len(refs) - 8) // 2
+    q_hbm, cache_hbm = refs[:2]
+    w_hbm = refs[2 : 2 + loads]
+    out_ref, stat_ref = refs[2 + loads : 4 + loads]
+    w_ref = refs[4 + loads : -4]
     nodes, lat, heads = q_ref.shape
     ctx = cache_ref.shape[2]
     spare = keys_ref.shape[1] - lat
     copies = [
         pltpu.make_async_copy(cache_hbm, cache_ref, sem.at[0]),
         pltpu.make_async_copy(q_hbm.at[pl.ds(begin, nodes)], q_ref, sem.at[1]),
-        pltpu.make_async_copy(w_hbm, w_ref, sem.at[2]),
     ]
+    for i in range(loads):
+        copies.append(pltpu.make_async_copy(w_hbm[i], w_ref[i], sem.at[2 + i]))
     for c in copies:
         c.start()
     unused = (iota((ctx, spare), 0) >= length_ref[0]) & (iota((ctx, spare), 1) == 0)
@@ -334,34 +377,35 @@
             span = slice(i * heads, (i + 1) * heads)
             out_ref[g * per + i] = out[:, span].T.astype(out_ref.dtype)
             stat_ref[g * per + i] = jnp.concatenate([top[:, span], total[:, span]], axis=0)
-    copies[2].wait()
-
-
-def cached_attention(lengths, q_t, cache_t, weight, first, count, per=4):
+    for c in copies[2:]:
+        c.wait()
+
+
+def cached_attention(lengths, q_t, cache_t, weights, first, count, per=4):
     tokens, lat, heads = q_t.shape
     ctx = cache_t.shape[2]
     hbm = pl.BlockSpec(memory_space=pltpu.HBM)
     vmem = pl.BlockSpec(memory_space=pltpu.VMEM)
-    given = [pltpu.with_memory_space_constraint(a, pltpu.HBM) for a in (q_t, cache_t, weight)]
+    given = [pltpu.with_memory_space_constraint(a, pltpu.HBM) for a in (q_t, cache_t, *weights)]
     return pl.pallas_call(
         functools.partial(cached_kernel, first, per),
         out_shape=[
             pltpu.VMEM((count, heads, KEY_VALUE_RANK), BF),
             pltpu.VMEM((count, 2, heads), F32),
-            pltpu.VMEM(weight.shape, weight.dtype),
-        ],
-        in_specs=[pl.BlockSpec(memory_space=pltpu.SMEM), hbm, hbm, hbm],
-        out_specs=[vmem, vmem, vmem],
+        ]
+        + [pltpu.VMEM(w.shape, w.dtype) for w in weights],
+        in_specs=[pl.BlockSpec(memory_space=pltpu.SMEM)] + [hbm] * len(given),
+        out_specs=[vmem] * len(given),
         scratch_shapes=[
             pltpu.VMEM((count, lat, heads), BF),
             pltpu.VMEM(cache_t.shape, BF),
             pltpu.VMEM((ctx, (lat // 128 + 1) * 128), BF),
-            pltpu.SemaphoreType.DMA((3,)),
+            pltpu.SemaphoreType.DMA((2 + len(weights),)),
         ],
-        compiler_params=params(14),
+        compiler_params=params(10),
         cost_estimate=pl.CostEstimate(
             flops=4 * count * heads * ctx * (lat + KEY_VALUE_RANK),
-            bytes_accessed=2 * weight.size,
+            bytes_accessed=4 * count * heads * lat,
             transcendentals=count * heads * ctx,
         ),
         name="cached",
@@ -515,7 +559,8 @@
         return have
 
     def to_line(xs):
-        return [xs[0]] + [swap(xs[k], k * split) for k in range(1, EXPERTS)]
+        got = {k: swap(xs[k], k * split) for k in (3, 2, 1)}
+        return [xs[0], got[1], got[2], got[3]]
 
     q_t = jnp.transpose(queries, (0, 2, 1))
     cache_t = jnp.transpose(cache, (0, 2, 1))
@@ -524,36 +569,53 @@
     allow = jnp.broadcast_to(reach[:, :, None], reach.shape + (heads,))
 
     packed = pack(place, hidden, ffn_gain[None], routes.T, gate_weights.T)
-    near = to_line(packed[:EXPERTS])
-    kv_far = swap(kv_down, bits[-1])
-    *first, w_out = cached_attention(lengths, after(q_t, packed[0]), cache_t, expert_down, 0, half)
-    near, kv_far, first = lax.optimization_barrier((near, kv_far, first))
-    line = jnp.concatenate(near, axis=0)
-    info = jnp.concatenate([c[:, -TAIL:] for c in near], axis=0)
-    groups = spread({0: line}, bits[:0:-1])
-    own_quarters = to_line(after(packed[EXPERTS:], near[0]))
-    *second, w_in = cached_attention(lengths, after(q_t, line), cache_t, expert_in, half, half)
-    groups, own_quarters, info, allow, turn, second = lax.optimization_barrier(
-        (groups, own_quarters, info, allow, turn, second)
+    own = packed[:EXPERTS]
+    top, low = bits[-1], bits[:-1]
+    kvs = spread({0: kv_down}, [top])
+    near = to_line(own)
+    lower = join(near[0], near[1])
+    lowers = spread({0: lower}, [top])
+    q_first = after(q_t, lower, allow, turn)
+    *first, w_in, w_out = cached_attention(
+        lengths, q_first, cache_t, [expert_in, expert_down], 0, half
     )
-    groups = spread(groups, bits[:1])
-    groups = [groups[r] for r in range(split)]
+    distant, first, kvs = lax.optimization_barrier((near[2:], first, kvs))
+    upper = join(*distant)
+    across = {top: swap(upper, top)}
+    uppers = spread({0: upper}, low[::-1])
+    own_quarters = to_line(after(packed[EXPERTS:], uppers))
+    lowers = spread(lowers, low[::-1])
+    gates = gate_matrices(place, (lower, upper), hidden.shape[0])
+    lowers, uppers, across, own_quarters, gates = lax.optimization_barrier(
+        (lowers, uppers, across, own_quarters, gates)
+    )
+    uppers = uppers | spread(across, low[::-1])
+    groups = [x for r in range(split) for x in (lowers[r], uppers[r])]
     pieces = expert_slice(place, groups, w_in, w_out)
-    kvs = {0: after(kv_down, pieces[0]), bits[-1]: kv_far}
-    kvs = spread(kvs, bits[-2::-1])
-    kvs = [kvs[r] for r in range(split)]
-
-    def gathered(keep, send):
+
+    kvs = spread(after(kvs, pieces[0]), low[::-1])
+    kvs = [(r, 0, x) for r, x in kvs.items()]
+
+    def inner(keep, send):
         terms = [keep, swap(send, bits[0])]
-        for bit in bits[1:]:
+        for bit in bits[1:-1]:
             out = sum(t[1::2].astype(F32) for t in terms).astype(BF)
             terms = [t[0::2] for t in terms] + [swap(out, bit)]
-        return [sum(t[0, k].astype(F32) for t in terms).astype(BF) for k in range(keep.shape[1])]
-
-    far, middle, close = [gathered(*p) for p in pieces]
-    close = close + middle + far
-    outs_e = to_line(close)
-    own_sum, own_part, *rows = combine(place, outs_e, own_quarters, info, attn_gain[None], kvs)
+        return [t[0] for t in terms], sum(t[1].astype(F32) for t in terms).astype(BF)
+
+    def outer(terms, got):
+        return [sum(t[k].astype(F32) for t in (*terms, got)).astype(BF) for k in range(len(got))]
+
+    kept, out = zip(*[inner(*p) for p in pieces])
+    got = [swap(x, top) for x in out]
+    far = outer(kept[0], after(got[0], out[2]))
+    middle = outer(kept[1], got[1])
+    close = outer(kept[2], got[2])
+    outs_e = to_line(close + middle + far)
+    second = cached_attention(lengths, after(q_t, close[1]), cache_t, [], half, half)
+    outs_e, second = lax.optimization_barrier((outs_e, second))
+
+    own_sum, own_part, *rows = combine(place, outs_e, own_quarters, gates, attn_gain[None], kvs)
     rows = [own_sum, own_part] + [swap(r, (k + 1) * split) for k, r in enumerate(rows)]
     return final_attention(
         place, width, rows, latent_norm_gain[None], turn, allow, q_t, first, second

time: 85.4 us -> 81.9 us (0.959)
  waiting for transfers between devices: 24.3 us -> 20.8 us
  local copies, waits for them, and re-layouts: 3.2 us -> 0.26 us
  Pallas kernels: 26.7 us -> 29.5 us
    ppermute x24 -> x27, waiting for transfers between devices: 24.3 us -> 20.8 us  [swap(): return lax.ppermute(x, 'ep', [(i, i ^ bit) for i in range(size)])]
    unnamed x17 -> x8, local copies, waits for them, and re-layouts: 2.95 us -> 0.03 us
    pallas_call x2, Pallas kernels: 11.6 us -> 13.8 us  [cached_attention(): pl.pallas_call(functools.partial(cached_kernel, first, per), out_shape=[p...]
    pallas_call x1 -> x4, Pallas kernels: 3.22 us -> 3.67 us  [the longest x1 2.58 us: combine(): pl.pallas_call(functools.partial(combine_kernel, spots, tokens), out_shap...]
    ppermute x24 -> x27, starting transfers between devices: 27 us -> 27.4 us  [swap(): return lax.ppermute(x, 'ep', [(i, i ^ bit) for i in range(size)])]
  transfers between devices with their start and end apart: 24 -> 27, of which waited for: 11 -> 11; matrix products, arithmetic and copies ran while one was open for 3% -> 3% of each run, Pallas kernels for 15% -> 23%
where the time goes in v4:
time: 81.9 us; the launch traced here: 81.7 us
  Pallas kernels  29.5 us (36%)
  starting transfers between devices  27.4 us (33%)
  waiting for transfers between devices  20.8 us (25%)
  between operations  1.72 us (2%)
  matrix products  1.43 us (2%)
    ppermute x27, starting transfers between devices, swap(): return lax.ppermute(x, 'ep', [(i, i ^ bit) for i in range(size)])  27.4 us
    ppermute x27, waiting for transfers between devices, swap(): return lax.ppermute(x, 'ep', [(i, i ^ bit) for i in range(size)])  20.8 us
    pallas_call x2, Pallas kernels, cached_attention(): pl.pallas_call(functools.partial(cached_kernel, first, per), out_shape=[p...  13.8 us
    pallas_call x1, Pallas kernels, final_attention(): pl.pallas_call(functools.partial(final_kernel, width, per), out_shape=[ja...  4.42 us
    pallas_call x1, Pallas kernels, expert_slice(): pl.pallas_call(functools.partial(expert_kernel, split), out_shape=[act] +...  4.07 us
    pallas_call x1, Pallas kernels, combine(): pl.pallas_call(functools.partial(combine_kernel, spots, tokens), out_shap...  2.58 us
    pallas_call x1, Pallas kernels, pack(): pl.pallas_call(pack_kernel, out_shape=[chunk] * EXPERTS + [part] * EXPERT...  2.09 us
  transfers between devices with their start and end apart: 27, of which 11 were waited for; matrix products, arithmetic and copies ran while one was open for 3% of the time, Pallas kernels for 23%

profile of v4, /device:TPU:0, one launch (start us, length us, event | category | flops | bytes accessed | tf_op | source)
XLA Modules:
  0.0 81.7 jit_solution(17570700290183235193)
XLA Ops:
  0.6 3.0 %collective-permute-start.6 = (bf16[448,576]{1,0:T(8,128)(2,1)}, bf16[448,576]{1,0:T(8,128)(2,1)S(1)}, u32[]{:S(2)}, u32[]{:S(2)}) collective-permute-start(bf16[448,576]{1,0:T(8,128)(2,1)} %refs_10_), channel_id=1, source_target_pairs={{0,2},{1,3},{2,0},{3,1},{4,6},{5,7},{6,4},{7,5},{8,10},{9,11},{10,... | collective-permute-start | bytes 1548296 | tf_op jit(solution)/shard_map/ppermute | solution.py:553
  3.7 2.1 %pack.1 = (bf16[8,8192]{1,0:T(8,128)(2,1)S(1)}, bf16[8,8192]{1,0:T(8,128)(2,1)S(1)}, bf16[8,8192]{1,0:T(8,128)(2,1)S(1)}, bf16[8,8192]{1,0:T(8,128)(2,1)S(1)}, b...) custom-call(s32[2]{0:T(128)S(1)} %pad_add_fusion.e_ref, ...), custom_call_target="tpu_custom_call" | custom-call | flops 1024 | bytes 1024 | tf_op jit(solution)/shard_map/pack/pallas_call | solution.py:113
  5.8 1.6 %collective-permute-start = (bf16[8,8192]{1,0:T(8,128)(2,1)S(1)}, bf16[8,8192]{1,0:T(8,128)(2,1)S(1)}, u32[]{:S(2)}, u32[]{:S(2)}) collective-permute-start(bf16[8,8192]{1,0:T(8,128)(2,1)S(1)} %get-tuple-element.63), channel_id=1, source_target_pairs={{0,4},{1,5},{2,6},{3,7},{4,0},{5,1},{6,2},{7,3},{8,12},{9,13},{10,... | collective-permute-start | bytes 393224 | tf_op jit(solution)/shard_map/ppermute | solution.py:553
  7.5 2.6 %collective-permute-start.4 = (bf16[8,8192]{1,0:T(8,128)(2,1)S(1)}, bf16[8,8192]{1,0:T(8,128)(2,1)S(1)}, u32[]{:S(2)}, u32[]{:S(2)}) collective-permute-start(bf16[8,8192]{1,0:T(8,128)(2,1)S(1)} %get-tuple-element.64), channel_id=1, source_target_pairs={{0,8},{1,9},{2,10},{3,11},{4,12},{5,13},{6,14},{7,15},{8,0},{9,1},... | collective-permute-start | bytes 393224 | tf_op jit(solution)/shard_map/ppermute | solution.py:553
  11.0 1.0 %convolution_minimum_fusion.3 = f32[16,16]{0,1:T(8,128)S(1)} fusion(s32[16]{0:T(128)} %bitcast.63), kind=kOutput, calls=%fused_computation.3 | convolution fusion | flops 50688 | bytes 1088 | tf_op jit(solution)/shard_map/dot_general | solution.py:508
  13.2 8.0 %cached.2 = (bf16[8,128,512]{2,1,0:T(8,128)(2,1)S(1)}, f32[8,2,128]{2,1,0:T(2,128)S(1)}, bf16[1,7168,1024]{2,1,0:T(8,128)(2,1)S(1)}, bf16[1,512,7168]{2,1,0:T(8,128)(2,1)S(1)}) custom-call(s32[1]{0:T(128)S(6)} %copy.17.length_ref, bf16[16,576,128]{2,1,0:T(8,128)(2,1)} %bitcast.53, bf16[1,576,1024]{2,1,0:T(8,128)(2,1)} %bitcast.58, ...), custom_call_target="tpu_custom_call" | custom-call | flops 4563402752 | bytes 2359296 | tf_op jit(solution)/shard_map/cached/pallas_call | solution.py:390
  22.5 1.7 %collective-permute-start.8 = (bf16[16,8192]{1,0:T(8,128)(2,1)S(1)}, bf16[16,8192]{1,0:T(8,128)(2,1)S(1)}, u32[]{:S(2)}, u32[]{:S(2)}) collective-permute-start(bf16[16,8192]{1,0:T(8,128)(2,1)S(1)} %join.3.refs_1_), channel_id=1, source_target_pairs={{0,2},{1,3},{2,0},{3,1},{4,6},{5,7},{6,4},{7,5},{8,10},{9,11},{10,... | collective-permute-start | bytes 786440 | tf_op jit(solution)/shard_map/ppermute | solution.py:553
  24.2 1.6 %collective-permute-start.9 = (bf16[16,1792]{1,0:T(8,128)(2,1)S(1)}, bf16[16,1792]{1,0:T(8,128)(2,1)S(1)}, u32[]{:S(2)}, u32[]{:S(2)}) collective-permute-start(bf16[16,1792]{1,0:T(8,128)(2,1)S(1)} %get-tuple-element.76), channel_id=1, source_target_pairs={{0,4},{1,5},{2,6},{3,7},{4,0},{5,1},{6,2},{7,3},{8,12},{9,13},{10,... | collective-permute-start | bytes 172040 | tf_op jit(solution)/shard_map/ppermute | solution.py:553
  25.8 2.6 %collective-permute-start.10 = (bf16[16,1792]{1,0:T(8,128)(2,1)S(1)}, bf16[16,1792]{1,0:T(8,128)(2,1)S(1)}, u32[]{:S(2)}, u32[]{:S(2)}) collective-permute-start(bf16[16,1792]{1,0:T(8,128)(2,1)S(1)} %get-tuple-element.77), channel_id=1, source_target_pairs={{0,8},{1,9},{2,10},{3,11},{4,12},{5,13},{6,14},{7,15},{8,0},{9,1},... | collective-permute-start | bytes 172040 | tf_op jit(solution)/shard_map/ppermute | solution.py:553
  28.6 1.0 %gates.1.refs_8_ = bf16[4,192,40]{2,1,0:T(8,128)(2,1)S(1)} custom-call(s32[2]{0:T(128)S(1)} %pad_add_fusion.e_ref, bf16[16,8192]{1,0:T(8,128)(2,1)S(1)} %join.2.refs_0_, bf16[16,8192]{1,0:T(8,128)(2,1)S(1)} %join.3.refs_1_), custom_call_target="tpu_custom_call" | custom-call | flops 17179869184 | bytes 16777216 | tf_op jit(solution)/shard_map/gates/pallas_call | solution.py:255
  29.7 1.5 %collective-permute-done.8.refs_5_ = bf16[16,8192]{1,0:T(8,128)(2,1)S(1)} collective-permute-done((bf16[16,8192]{1,0:T(8,128)(2,1)S(1)}, bf16[16,8192]{1,0:T(8,128)(2,1)S(1)}, u32[]{:S(2)}, u32[]{:S(2)}) %collective-permute-start.8) | collective-permute-done | bytes 262176 | tf_op jit(solution)/shard_map/ppermute | solution.py:553
  31.2 1.0 %collective-permute-done.10.refs_6_ = bf16[16,1792]{1,0:T(8,128)(2,1)S(1)} collective-permute-done((bf16[16,1792]{1,0:T(8,128)(2,1)S(1)}, bf16[16,1792]{1,0:T(8,128)(2,1)S(1)}, u32[]{:S(2)}, u32[]{:S(2)}) %collective-permute-start.10) | collective-permute-done | bytes 57376 | tf_op jit(solution)/shard_map/ppermute | solution.py:553
  32.2 2.1 %collective-permute-done.11.refs_7_ = bf16[16,1792]{1,0:T(8,128)(2,1)S(1)} collective-permute-done((bf16[16,1792]{1,0:T(8,128)(2,1)S(1)}, bf16[16,1792]{1,0:T(8,128)(2,1)S(1)}, u32[]{:S(2)}, u32[]{:S(2)}) %collective-permute-start.11) | collective-permute-done | bytes 57376 | tf_op jit(solution)/shard_map/ppermute | solution.py:553
  34.4 1.5 %collective-permute-done.12.refs_7_ = bf16[16,8192]{1,0:T(8,128)(2,1)S(1)} collective-permute-done((bf16[16,8192]{1,0:T(8,128)(2,1)S(1)}, bf16[16,8192]{1,0:T(8,128)(2,1)S(1)}, u32[]{:S(2)}, u32[]{:S(2)}) %collective-permute-start.12) | collective-permute-done | bytes 262176 | tf_op jit(solution)/shard_map/ppermute | solution.py:553
  35.9 4.1 %experts.1 = (bf16[160,512]{1,0:T(8,128)(2,1)S(1)}, bf16[2,1,40,1792]{3,2,1,0:T(8,128)(2,1)S(1)}, bf16[2,1,40,1792]{3,2,1,0:T(8,128)(2,1)S(1)}, bf16[2,1,40,1792...) custom-call(s32[2]{0:T(128)S(1)} %pad_add_fusion.e_ref, bf16[16,8192]{1,0:T(8,128)(2,1)S(1)} %join.2.refs_0_, ...), custom_call_target="tpu_custom_call" | custom-call | flops 1024 | bytes 1024 | tf_op jit(solution)/shard_map/experts/pallas_call | solution.py:184
  40.2 1.4 %experts_rest.1 = (bf16[2,2,40,1792]{3,2,1,0:T(8,128)(2,1)S(1)}, bf16[2,2,40,1792]{3,2,1,0:T(8,128)(2,1)S(1)}) custom-call(s32[2]{0:T(128)S(1)} %pad_add_fusion.e_ref, bf16[160,512]{1,0:T(8,128)(2,1)S(1)} %get-tuple-element.88.act, bf16[1,512,7168]{2,1,0:T(8,128)(2,1)S(1)} %get-tuple-element.87.refs_9_.w_out), custom_call_target="tpu_custom_call" | custom-call | flops 1024 | bytes 1024 | tf_op jit(solution)/shard_map/experts_rest/pallas_call | solution.py:194
  42.8 0.6 collective-permute-start.17
  43.4 1.6 %collective-permute-start.20 = (bf16[1,40,1792]{2,1,0:T(8,128)(2,1)S(1)}, bf16[1,40,1792]{2,1,0:T(8,128)(2,1)S(1)}, u32[]{:S(2)}, u32[]{:S(2)}) collective-permute-start(bf16[1,40,1792]{2,1,0:T(8,128)(2,1)S(1)} %fusion.6), channel_id=1, source_target_pairs={{0,2},{1,3},{2,0},{3,1},{4,6},{5,7},{6,4},{7,5},{8,10},{9,11},{10,... | collective-permute-start | bytes 430088 | tf_op jit(solution)/shard_map/ppermute | solution.py:553
  45.0 4.4 %collective-permute-done.17 = bf16[1,40,1792]{2,1,0:T(8,128)(2,1)S(1)} collective-permute-done((bf16[1,40,1792]{2,1,0:T(8,128)(2,1)S(1)}, bf16[1,40,1792]{2,1,0:T(8,128)(2,1)S(1)}, u32[]{:S(2)}, u32[]{:S(2)}) %collective-permute-start.17) | collective-permute-done | bytes 143392 | tf_op jit(solution)/shard_map/ppermute | solution.py:553
  49.5 1.4 %collective-permute-start.18 = (bf16[40,1792]{1,0:T(8,128)(2,1)S(1)}, bf16[40,1792]{1,0:T(8,128)(2,1)S(1)}, u32[]{:S(2)}, u32[]{:S(2)}) collective-permute-start(bf16[40,1792]{1,0:T(8,128)(2,1)S(1)} %fusion.2), channel_id=1, source_target_pairs={{0,8},{1,9},{2,10},{3,11},{4,12},{5,13},{6,14},{7,15},{8,0},{9,1},... | collective-permute-start | bytes 430088 | tf_op jit(solution)/shard_map/ppermute | solution.py:553
  51.0 0.6 collective-permute-start.14
  52.0 2.0 %collective-permute-start.21 = (bf16[40,1792]{1,0:T(8,128)(2,1)S(1)}, bf16[40,1792]{1,0:T(8,128)(2,1)S(1)}, u32[]{:S(2)}, u32[]{:S(2)}) collective-permute-start(bf16[40,1792]{1,0:T(8,128)(2,1)S(1)} %fusion.1), channel_id=1, source_target_pairs={{0,12},{1,13},{2,14},{3,15},{4,8},{5,9},{6,10},{7,11},{8,4},{9,5},... | collective-permute-start | bytes 430088 | tf_op jit(solution)/shard_map/ppermute | solution.py:553
  54.0 4.5 %collective-permute-done.14 = bf16[2,40,1792]{2,1,0:T(8,128)(2,1)S(1)} collective-permute-done((bf16[2,40,1792]{2,1,0:T(8,128)(2,1)S(1)}, bf16[2,40,1792]{2,1,0:T(8,128)(2,1)S(1)}, u32[]{:S(2)}, u32[]{:S(2)}) %collective-permute-start.14) | collective-permute-done | bytes 286752 | tf_op jit(solution)/shard_map/ppermute | solution.py:553
  58.6 0.9 %collective-permute-start.15 = (bf16[40,1792]{1,0:T(8,128)(2,1)S(1)}, bf16[40,1792]{1,0:T(8,128)(2,1)S(1)}, u32[]{:S(2)}, u32[]{:S(2)}) collective-permute-start(bf16[40,1792]{1,0:T(8,128)(2,1)S(1)} %get-tuple-element.121), channel_id=1, source_target_pairs={{0,4},{1,5},{2,6},{3,7},{4,0},{5,1},{6,2},{7,3},{8,12},{9,13},{10,... | collective-permute-start | bytes 430088 | tf_op jit(solution)/shard_map/ppermute | solution.py:553
  59.6 5.8 %cached.3 = (bf16[8,128,512]{2,1,0:T(8,128)(2,1)S(1)}, f32[8,2,128]{2,1,0:T(2,128)S(1)}) custom-call(s32[1]{0:T(128)S(6)} %copy.17.length_ref, bf16[16,576,128]{2,1,0:T(8,128)(2,1)} %bitcast.54, bf16[1,576,1024]{2,1,0:T(8,128)(2,1)} %bitcast.59), custom_call_target="tpu_custom_call" | custom-call | flops 4563402752 | bytes 2359296 | tf_op jit(solution)/shard_map/cached/pallas_call | solution.py:390
  65.4 2.6 %combine.1 = (f32[16,640]{1,0:T(8,128)S(1)}, bf16[16,1792]{1,0:T(8,128)(2,1)S(1)}, bf16[16,2432]{1,0:T(8,128)(2,1)S(1)}, bf16[16,2432]{1,0:T(8,128)(2,1)S(1)}, bf16[16,2432]{1,0:T(8,128)(2,1)S(1)}) custom-call(s32[2]{0:T(128)S(1)} %pad_add_fusion.e_ref, bf16[40,1792]{1,0:T(8,128)(2,1)S(1)} %get-tuple-element.99.refs_0_, ...), custom_call_target="tpu_custom_call" | custom-call | flops 1024 | bytes 1024 | tf_op jit(solution)/shard_map/combine/pallas_call | solution.py:317
  68.0 1.2 %collective-permute-start.24 = (bf16[16,2432]{1,0:T(8,128)(2,1)S(1)}, bf16[16,2432]{1,0:T(8,128)(2,1)S(1)}, u32[]{:S(2)}, u32[]{:S(2)}) collective-permute-start(bf16[16,2432]{1,0:T(8,128)(2,1)S(1)} %get-tuple-element.114), channel_id=1, source_target_pairs={{0,4},{1,5},{2,6},{3,7},{4,0},{5,1},{6,2},{7,3},{8,12},{9,13},{10,... | collective-permute-start | bytes 233480 | tf_op jit(solution)/shard_map/ppermute | solution.py:553
  69.3 1.6 %collective-permute-start.25 = (bf16[16,2432]{1,0:T(8,128)(2,1)S(1)}, bf16[16,2432]{1,0:T(8,128)(2,1)S(1)}, u32[]{:S(2)}, u32[]{:S(2)}) collective-permute-start(bf16[16,2432]{1,0:T(8,128)(2,1)S(1)} %get-tuple-element.115), channel_id=1, source_target_pairs={{0,8},{1,9},{2,10},{3,11},{4,12},{5,13},{6,14},{7,15},{8,0},{9,1},... | collective-permute-start | bytes 233480 | tf_op jit(solution)/shard_map/ppermute | solution.py:553
  70.8 1.6 %collective-permute-start.26 = (bf16[16,2432]{1,0:T(8,128)(2,1)S(1)}, bf16[16,2432]{1,0:T(8,128)(2,1)S(1)}, u32[]{:S(2)}, u32[]{:S(2)}) collective-permute-start(bf16[16,2432]{1,0:T(8,128)(2,1)S(1)} %get-tuple-element.116), channel_id=1, source_target_pairs={{0,12},{1,13},{2,14},{3,15},{4,8},{5,9},{6,10},{7,11},{8,4},{9,5},... | collective-permute-start | bytes 233480 | tf_op jit(solution)/shard_map/ppermute | solution.py:553
  72.6 2.9 %collective-permute-done.25.refs_3_ = bf16[16,2432]{1,0:T(8,128)(2,1)S(1)} collective-permute-done((bf16[16,2432]{1,0:T(8,128)(2,1)S(1)}, bf16[16,2432]{1,0:T(8,128)(2,1)S(1)}, u32[]{:S(2)}, u32[]{:S(2)}) %collective-permute-start.25) | collective-permute-done | bytes 77856 | tf_op jit(solution)/shard_map/ppermute | solution.py:553
  75.5 1.6 %collective-permute-done.26.refs_4_ = bf16[16,2432]{1,0:T(8,128)(2,1)S(1)} collective-permute-done((bf16[16,2432]{1,0:T(8,128)(2,1)S(1)}, bf16[16,2432]{1,0:T(8,128)(2,1)S(1)}, u32[]{:S(2)}, u32[]{:S(2)}) %collective-permute-start.26) | collective-permute-done | bytes 77856 | tf_op jit(solution)/shard_map/ppermute | solution.py:553
  77.1 4.4 %final.1 = (bf16[16,7168]{1,0:T(8,128)(2,1)}, bf16[16,576]{1,0:T(8,128)(2,1)}, bf16[16,128,512]{2,1,0:T(8,128)(2,1)}) custom-call(s32[2]{0:T(128)S(1)} %pad_add_fusion.e_ref, f32[16,640]{1,0:T(8,128)S(1)} %get-tuple-element.112.refs_0_, bf16[16,1792]{1,0:T(8,128)(2,1)S(1)} %get-tuple-element.113.refs_1_, ...), custom_call_target="tpu_custom_call" | custom-call | flops 1024 | bytes 1024 | tf_op jit(solution)/shard_map/final/pallas_call | solution.py:484
  (61 shorter events, 5.2 us)
Async XLA Ops:
  0.6 20.7 %collective-permute-start.6 = (bf16[448,576]{1,0:T(8,128)(2,1)}, bf16[448,576]{1,0:T(8,128)(2,1)S(1)}, u32[]{:S(2)}, u32[]{:S(2)}) collective-permute-start(bf16[448,576]{1,0:T(8,128)(2,1)} %refs_10_), channel_id=1, source_target_pairs={{0,2},{1,3},{2,0},{3,1},{4,6},{5,7},{6,4},{7,5},{8,10},{9,11},{10,... | collective-permute-start | bytes 1548296 | tf_op jit(solution)/shard_map/ppermute | solution.py:553
  5.8 6.9 %collective-permute-start = (bf16[8,8192]{1,0:T(8,128)(2,1)S(1)}, bf16[8,8192]{1,0:T(8,128)(2,1)S(1)}, u32[]{:S(2)}, u32[]{:S(2)}) collective-permute-start(bf16[8,8192]{1,0:T(8,128)(2,1)S(1)} %get-tuple-element.63), channel_id=1, source_target_pairs={{0,4},{1,5},{2,6},{3,7},{4,0},{5,1},{6,2},{7,3},{8,12},{9,13},{10,... | collective-permute-start | bytes 393224 | tf_op jit(solution)/shard_map/ppermute | solution.py:553
  7.5 13.8 %collective-permute-start.4 = (bf16[8,8192]{1,0:T(8,128)(2,1)S(1)}, bf16[8,8192]{1,0:T(8,128)(2,1)S(1)}, u32[]{:S(2)}, u32[]{:S(2)}) collective-permute-start(bf16[8,8192]{1,0:T(8,128)(2,1)S(1)} %get-tuple-element.64), channel_id=1, source_target_pairs={{0,8},{1,9},{2,10},{3,11},{4,12},{5,13},{6,14},{7,15},{8,0},{9,1},... | collective-permute-start | bytes 393224 | tf_op jit(solution)/shard_map/ppermute | solution.py:553
  10.1 11.2 %collective-permute-start.5 = (bf16[8,8192]{1,0:T(8,128)(2,1)S(1)}, bf16[8,8192]{1,0:T(8,128)(2,1)S(1)}, u32[]{:S(2)}, u32[]{:S(2)}) collective-permute-start(bf16[8,8192]{1,0:T(8,128)(2,1)S(1)} %get-tuple-element.65), channel_id=1, source_target_pairs={{0,12},{1,13},{2,14},{3,15},{4,8},{5,9},{6,10},{7,11},{8,4},{9,5},... | collective-permute-start | bytes 393224 | tf_op jit(solution)/shard_map/ppermute | solution.py:553
  12.8 9.7 %collective-permute-start.2 = (bf16[16,8192]{1,0:T(8,128)(2,1)S(1)}, bf16[16,8192]{1,0:T(8,128)(2,1)S(1)}, u32[]{:S(2)}, u32[]{:S(2)}) collective-permute-start(bf16[16,8192]{1,0:T(8,128)(2,1)S(1)} %join.2.refs_0_), channel_id=1, source_target_pairs={{0,2},{1,3},{2,0},{3,1},{4,6},{5,7},{6,4},{7,5},{8,10},{9,11},{10,... | collective-permute-start | bytes 786440 | tf_op jit(solution)/shard_map/ppermute | solution.py:553
  21.3 2.9 %collective-permute-start.7 = (bf16[16,8192]{1,0:T(8,128)(2,1)S(1)}, bf16[16,8192]{1,0:T(8,128)(2,1)S(1)}, u32[]{:S(2)}, u32[]{:S(2)}) collective-permute-start(bf16[16,8192]{1,0:T(8,128)(2,1)S(1)} %join.3.refs_1_), channel_id=1, source_target_pairs={{0,1},{1,0},{2,3},{3,2},{4,5},{5,4},{6,7},{7,6},{8,9},{9,8},{10,11... | collective-permute-start | bytes 786440 | tf_op jit(solution)/shard_map/ppermute | solution.py:553
  21.4 7.0 %collective-permute-start.1 = (bf16[16,8192]{1,0:T(8,128)(2,1)S(1)}, bf16[16,8192]{1,0:T(8,128)(2,1)S(1)}, u32[]{:S(2)}, u32[]{:S(2)}) collective-permute-start(bf16[16,8192]{1,0:T(8,128)(2,1)S(1)} %join.2.refs_0_), channel_id=1, source_target_pairs={{0,1},{1,0},{2,3},{3,2},{4,5},{5,4},{6,7},{7,6},{8,9},{9,8},{10,11... | collective-permute-start | bytes 786440 | tf_op jit(solution)/shard_map/ppermute | solution.py:553
  22.5 7.2 %collective-permute-start.3 = (bf16[16,8192]{1,0:T(8,128)(2,1)S(1)}, bf16[16,8192]{1,0:T(8,128)(2,1)S(1)}, u32[]{:S(2)}, u32[]{:S(2)}) collective-permute-start(bf16[16,8192]{1,0:T(8,128)(2,1)S(1)} %collective-permute-done.2.refs_4_), channel_id=1, source_target_pairs={{0,1},{1,0},{2,3},{3,2},{4,5},{5,4},{6,7},{7,6},{8,9},{9,8},{10,11... | collective-permute-start | bytes 786440 | tf_op jit(solution)/shard_map/ppermute | solution.py:553
  22.5 8.7 %collective-permute-start.8 = (bf16[16,8192]{1,0:T(8,128)(2,1)S(1)}, bf16[16,8192]{1,0:T(8,128)(2,1)S(1)}, u32[]{:S(2)}, u32[]{:S(2)}) collective-permute-start(bf16[16,8192]{1,0:T(8,128)(2,1)S(1)} %join.3.refs_1_), channel_id=1, source_target_pairs={{0,2},{1,3},{2,0},{3,1},{4,6},{5,7},{6,4},{7,5},{8,10},{9,11},{10,... | collective-permute-start | bytes 786440 | tf_op jit(solution)/shard_map/ppermute | solution.py:553
  24.2 7.0 %collective-permute-start.9 = (bf16[16,1792]{1,0:T(8,128)(2,1)S(1)}, bf16[16,1792]{1,0:T(8,128)(2,1)S(1)}, u32[]{:S(2)}, u32[]{:S(2)}) collective-permute-start(bf16[16,1792]{1,0:T(8,128)(2,1)S(1)} %get-tuple-element.76), channel_id=1, source_target_pairs={{0,4},{1,5},{2,6},{3,7},{4,0},{5,1},{6,2},{7,3},{8,12},{9,13},{10,... | collective-permute-start | bytes 172040 | tf_op jit(solution)/shard_map/ppermute | solution.py:553
  25.8 6.4 %collective-permute-start.10 = (bf16[16,1792]{1,0:T(8,128)(2,1)S(1)}, bf16[16,1792]{1,0:T(8,128)(2,1)S(1)}, u32[]{:S(2)}, u32[]{:S(2)}) collective-permute-start(bf16[16,1792]{1,0:T(8,128)(2,1)S(1)} %get-tuple-element.77), channel_id=1, source_target_pairs={{0,8},{1,9},{2,10},{3,11},{4,12},{5,13},{6,14},{7,15},{8,0},{9,1},... | collective-permute-start | bytes 172040 | tf_op jit(solution)/shard_map/ppermute | solution.py:553
  28.4 6.0 %collective-permute-start.11 = (bf16[16,1792]{1,0:T(8,128)(2,1)S(1)}, bf16[16,1792]{1,0:T(8,128)(2,1)S(1)}, u32[]{:S(2)}, u32[]{:S(2)}) collective-permute-start(bf16[16,1792]{1,0:T(8,128)(2,1)S(1)} %get-tuple-element.78), channel_id=1, source_target_pairs={{0,12},{1,13},{2,14},{3,15},{4,8},{5,9},{6,10},{7,11},{8,4},{9,5},... | collective-permute-start | bytes 172040 | tf_op jit(solution)/shard_map/ppermute | solution.py:553
  34.4 1.5 %collective-permute-start.12 = (bf16[16,8192]{1,0:T(8,128)(2,1)S(1)}, bf16[16,8192]{1,0:T(8,128)(2,1)S(1)}, u32[]{:S(2)}, u32[]{:S(2)}) collective-permute-start(bf16[16,8192]{1,0:T(8,128)(2,1)S(1)} %collective-permute-done.8.refs_5_), channel_id=1, source_target_pairs={{0,1},{1,0},{2,3},{3,2},{4,5},{5,4},{6,7},{7,6},{8,9},{9,8},{10,11... | collective-permute-start | bytes 786440 | tf_op jit(solution)/shard_map/ppermute | solution.py:553
  40.0 2.1 %copy-start.1 = (bf16[448,576]{1,0:T(8,128)(2,1)S(1)}, bf16[448,576]{1,0:T(8,128)(2,1)}, u32[]{:S(2)}) copy-start(bf16[448,576]{1,0:T(8,128)(2,1)} %refs_10_) | copy-start | bytes 1548292
  40.0 2.7 %collective-permute-start.16 = (bf16[2,1,40,1792]{3,2,1,0:T(8,128)(2,1)S(1)}, bf16[2,1,40,1792]{3,2,1,0:T(8,128)(2,1)S(1)}, u32[]{:S(2)}, u32[]{:S(2)}) collective-permute-start(bf16[2,1,40,1792]{3,2,1,0:T(8,128)(2,1)S(1)} %get-tuple-element.92), channel_id=1, source_target_pairs={{0,1},{1,0},{2,3},{3,2},{4,5},{5,4},{6,7},{7,6},{8,9},{9,8},{10,11... | collective-permute-start | bytes 860168 | tf_op jit(solution)/shard_map/ppermute | solution.py:553
  41.6 1.7 %collective-permute-start.19 = (bf16[2,1,40,1792]{3,2,1,0:T(8,128)(2,1)S(1)}, bf16[2,1,40,1792]{3,2,1,0:T(8,128)(2,1)S(1)}, u32[]{:S(2)}, u32[]{:S(2)}) collective-permute-start(bf16[2,1,40,1792]{3,2,1,0:T(8,128)(2,1)S(1)} %get-tuple-element.94), channel_id=1, source_target_pairs={{0,1},{1,0},{2,3},{3,2},{4,5},{5,4},{6,7},{7,6},{8,9},{9,8},{10,11... | collective-permute-start | bytes 860168 | tf_op jit(solution)/shard_map/ppermute | solution.py:553
  42.1 23.3 %collective-permute-start.22 = (bf16[448,576]{1,0:T(8,128)(2,1)S(1)}, bf16[448,576]{1,0:T(8,128)(2,1)S(1)}, u32[]{:S(2)}, u32[]{:S(2)}) collective-permute-start(bf16[448,576]{1,0:T(8,128)(2,1)S(1)} %copy-done.1), channel_id=1, source_target_pairs={{0,1},{1,0},{2,3},{3,2},{4,5},{5,4},{6,7},{7,6},{8,9},{9,8},{10,11... | collective-permute-start | bytes 1548296 | tf_op jit(solution)/shard_map/ppermute | solution.py:553
  42.2 23.2 %collective-permute-start.23 = (bf16[448,576]{1,0:T(8,128)(2,1)S(1)}, bf16[448,576]{1,0:T(8,128)(2,1)S(1)}, u32[]{:S(2)}, u32[]{:S(2)}) collective-permute-start(bf16[448,576]{1,0:T(8,128)(2,1)S(1)} %collective-permute-done.6.refs_11_), channel_id=1, source_target_pairs={{0,1},{1,0},{2,3},{3,2},{4,5},{5,4},{6,7},{7,6},{8,9},{9,8},{10,11... | collective-permute-start | bytes 1548296 | tf_op jit(solution)/shard_map/ppermute | solution.py:553
  42.6 8.3 %collective-permute-start.13 = (bf16[2,2,40,1792]{3,2,1,0:T(8,128)(2,1)S(1)}, bf16[2,2,40,1792]{3,2,1,0:T(8,128)(2,1)S(1)}, u32[]{:S(2)}, u32[]{:S(2)}) collective-permute-start(bf16[2,2,40,1792]{3,2,1,0:T(8,128)(2,1)S(1)} %get-tuple-element.90), channel_id=1, source_target_pairs={{0,1},{1,0},{2,3},{3,2},{4,5},{5,4},{6,7},{7,6},{8,9},{9,8},{10,11... | collective-permute-start | bytes 1720328 | tf_op jit(solution)/shard_map/ppermute | solution.py:553
  42.8 6.7 %collective-permute-start.17 = (bf16[1,40,1792]{2,1,0:T(8,128)(2,1)S(1)}, bf16[1,40,1792]{2,1,0:T(8,128)(2,1)S(1)}, u32[]{:S(2)}, u32[]{:S(2)}) collective-permute-start(bf16[1,40,1792]{2,1,0:T(8,128)(2,1)S(1)} %fusion.5), channel_id=1, source_target_pairs={{0,2},{1,3},{2,0},{3,1},{4,6},{5,7},{6,4},{7,5},{8,10},{9,11},{10,... | collective-permute-start | bytes 430088 | tf_op jit(solution)/shard_map/ppermute | solution.py:553
  43.4 8.5 %collective-permute-start.20 = (bf16[1,40,1792]{2,1,0:T(8,128)(2,1)S(1)}, bf16[1,40,1792]{2,1,0:T(8,128)(2,1)S(1)}, u32[]{:S(2)}, u32[]{:S(2)}) collective-permute-start(bf16[1,40,1792]{2,1,0:T(8,128)(2,1)S(1)} %fusion.6), channel_id=1, source_target_pairs={{0,2},{1,3},{2,0},{3,1},{4,6},{5,7},{6,4},{7,5},{8,10},{9,11},{10,... | collective-permute-start | bytes 430088 | tf_op jit(solution)/shard_map/ppermute | solution.py:553
  49.5 15.9 %collective-permute-start.18 = (bf16[40,1792]{1,0:T(8,128)(2,1)S(1)}, bf16[40,1792]{1,0:T(8,128)(2,1)S(1)}, u32[]{:S(2)}, u32[]{:S(2)}) collective-permute-start(bf16[40,1792]{1,0:T(8,128)(2,1)S(1)} %fusion.2), channel_id=1, source_target_pairs={{0,8},{1,9},{2,10},{3,11},{4,12},{5,13},{6,14},{7,15},{8,0},{9,1},... | collective-permute-start | bytes 430088 | tf_op jit(solution)/shard_map/ppermute | solution.py:553
  51.0 7.5 %collective-permute-start.14 = (bf16[2,40,1792]{2,1,0:T(8,128)(2,1)S(1)}, bf16[2,40,1792]{2,1,0:T(8,128)(2,1)S(1)}, u32[]{:S(2)}, u32[]{:S(2)}) collective-permute-start(bf16[2,40,1792]{2,1,0:T(8,128)(2,1)S(1)} %fusion), channel_id=1, source_target_pairs={{0,2},{1,3},{2,0},{3,1},{4,6},{5,7},{6,4},{7,5},{8,10},{9,11},{10,... | collective-permute-start | bytes 860168 | tf_op jit(solution)/shard_map/ppermute | solution.py:553
  52.0 13.4 %collective-permute-start.21 = (bf16[40,1792]{1,0:T(8,128)(2,1)S(1)}, bf16[40,1792]{1,0:T(8,128)(2,1)S(1)}, u32[]{:S(2)}, u32[]{:S(2)}) collective-permute-start(bf16[40,1792]{1,0:T(8,128)(2,1)S(1)} %fusion.1), channel_id=1, source_target_pairs={{0,12},{1,13},{2,14},{3,15},{4,8},{5,9},{6,10},{7,11},{8,4},{9,5},... | collective-permute-start | bytes 430088 | tf_op jit(solution)/shard_map/ppermute | solution.py:553
  58.6 6.8 %copy-start.2 = (f32[7168]{0:T(1024)S(1)}, f32[7168]{0:T(1024)}, u32[]{:S(2)}) copy-start(f32[7168]{0:T(1024)} %param.15) | copy-start | bytes 86020
  58.6 18.5 %copy-start = (bf16[16,128,576]{1,2,0:T(8,128)(2,1)S(1)}, bf16[16,128,576]{1,2,0:T(8,128)(2,1)}, u32[]{:S(2)}) copy-start(bf16[16,128,576]{1,2,0:T(8,128)(2,1)} %param.24) | copy-start | bytes 7077892
  58.6 18.5 %copy-start.3 = (f32[512]{0:T(512)S(1)}, f32[512]{0:T(512)}, u32[]{:S(2)}) copy-start(f32[512]{0:T(512)} %param.16) | copy-start | bytes 6148
  58.6 6.8 %collective-permute-start.15 = (bf16[40,1792]{1,0:T(8,128)(2,1)S(1)}, bf16[40,1792]{1,0:T(8,128)(2,1)S(1)}, u32[]{:S(2)}, u32[]{:S(2)}) collective-permute-start(bf16[40,1792]{1,0:T(8,128)(2,1)S(1)} %get-tuple-element.121), channel_id=1, source_target_pairs={{0,4},{1,5},{2,6},{3,7},{4,0},{5,1},{6,2},{7,3},{8,12},{9,13},{10,... | collective-permute-start | bytes 430088 | tf_op jit(solution)/shard_map/ppermute | solution.py:553
  68.0 4.6 %collective-permute-start.24 = (bf16[16,2432]{1,0:T(8,128)(2,1)S(1)}, bf16[16,2432]{1,0:T(8,128)(2,1)S(1)}, u32[]{:S(2)}, u32[]{:S(2)}) collective-permute-start(bf16[16,2432]{1,0:T(8,128)(2,1)S(1)} %get-tuple-element.114), channel_id=1, source_target_pairs={{0,4},{1,5},{2,6},{3,7},{4,0},{5,1},{6,2},{7,3},{8,12},{9,13},{10,... | collective-permute-start | bytes 233480 | tf_op jit(solution)/shard_map/ppermute | solution.py:553
  69.3 6.2 %collective-permute-start.25 = (bf16[16,2432]{1,0:T(8,128)(2,1)S(1)}, bf16[16,2432]{1,0:T(8,128)(2,1)S(1)}, u32[]{:S(2)}, u32[]{:S(2)}) collective-permute-start(bf16[16,2432]{1,0:T(8,128)(2,1)S(1)} %get-tuple-element.115), channel_id=1, source_target_pairs={{0,8},{1,9},{2,10},{3,11},{4,12},{5,13},{6,14},{7,15},{8,0},{9,1},... | collective-permute-start | bytes 233480 | tf_op jit(solution)/shard_map/ppermute | solution.py:553
  70.8 6.3 %collective-permute-start.26 = (bf16[16,2432]{1,0:T(8,128)(2,1)S(1)}, bf16[16,2432]{1,0:T(8,128)(2,1)S(1)}, u32[]{:S(2)}, u32[]{:S(2)}) collective-permute-start(bf16[16,2432]{1,0:T(8,128)(2,1)S(1)} %get-tuple-element.116), channel_id=1, source_target_pairs={{0,12},{1,13},{2,14},{3,15},{4,8},{5,9},{6,10},{7,11},{8,4},{9,5},... | collective-permute-start | bytes 233480 | tf_op jit(solution)/shard_map/ppermute | solution.py:553

commit v5 on v4

--- a/solution.py
+++ b/solution.py
@@ -381,7 +381,7 @@
         c.wait()
 
 
-def cached_attention(lengths, q_t, cache_t, weights, first, count, per=4):
+def cached_attention(lengths, q_t, cache_t, weights, first, count, per=4, cost=None):
     tokens, lat, heads = q_t.shape
     ctx = cache_t.shape[2]
     hbm = pl.BlockSpec(memory_space=pltpu.HBM)
@@ -403,7 +403,8 @@
             pltpu.SemaphoreType.DMA((2 + len(weights),)),
         ],
         compiler_params=params(10),
-        cost_estimate=pl.CostEstimate(
+        cost_estimate=cost
+        or pl.CostEstimate(
             flops=4 * count * heads * ctx * (lat + KEY_VALUE_RANK),
             bytes_accessed=4 * count * heads * lat,
             transcendentals=count * heads * ctx,
@@ -416,8 +417,11 @@
     own_sum, own_part = refs[:2]
     got = refs[2 : 1 + EXPERTS]
     gain_ref, turn_ref, allow_ref, q_ref = refs[1 + EXPERTS : 5 + EXPERTS]
-    halves = refs[5 + EXPERTS : 7 + EXPERTS], refs[7 + EXPERTS : 9 + EXPERTS]
-    part_ref, entry_ref, out_hbm, out_ref, sem = refs[9 + EXPERTS :]
+    cached = refs[5 + EXPERTS : -5]
+    part_ref, entry_ref, out_hbm, out_ref, sem = refs[-5:]
+    found = []
+    for ctx_ref, stat_ref in zip(cached[0::2], cached[1::2]):
+        found += [(ctx_ref, stat_ref, i) for i in range(ctx_ref.shape[0])]
     nodes, lat, heads = q_ref.shape
     padded = own_sum.shape[1]
     quarter = own_part.shape[1]
@@ -440,7 +444,6 @@
     keys = jnp.concatenate([head, tail], axis=1).astype(BF)[:, :lat]
     entry_ref[...] = keys
     count = keys.shape[0]
-    in_half = halves[0][0].shape[0]
     copies = []
     for g in range(nodes // per):
         span = range(g * per, (g + 1) * per)
@@ -448,11 +451,9 @@
         def side(ref):
             return jnp.concatenate([ref[i] for i in span], axis=1)
 
-        ctx_ref, stat_ref = halves[g * per // in_half]
-        begin = g * per % in_half
         scores = dot(keys, side(q_ref)) * (softmax_scale * LOG2E)
         scores = jnp.where(side(allow_ref) > 0.5, scores, -jnp.inf)
-        stats = jnp.concatenate([stat_ref[begin + i] for i in range(per)], axis=1)
+        stats = jnp.concatenate([found[i][1][found[i][2]] for i in span], axis=1)
         old = stats[0:1]
         top = jnp.maximum(old, jnp.max(scores, axis=0, keepdims=True))
         weight = jnp.exp2(scores - top)
@@ -462,7 +463,8 @@
         both = jnp.concatenate([weight * scale, share], axis=0).T
         for i in range(per):
             mine = both[i * heads : (i + 1) * heads]
-            out = ctx_ref[begin + i].astype(F32) * mine[:, count : count + 1]
+            ctx_ref, _, place = found[g * per + i]
+            out = ctx_ref[place].astype(F32) * mine[:, count : count + 1]
             out = out + dot(mine[:, :count].astype(BF), keys[:, :KEY_VALUE_RANK])
             out_ref[g * per + i] = out.astype(BF)
         here = pl.ds(g * per, per)
@@ -475,10 +477,10 @@
         c.wait()
 
 
-def final_attention(place, width, rows, gain, turn, allow, q_t, first, second, per=4):
+def final_attention(place, width, rows, gain, turn, allow, q_t, cached, per=8):
     tokens, lat, heads = q_t.shape
     vmem = pl.BlockSpec(memory_space=pltpu.VMEM)
-    given = [*rows, gain, turn, allow, q_t, *first, *second]
+    given = [*rows, gain, turn, allow, q_t, *cached]
     given = [pltpu.with_memory_space_constraint(x, pltpu.VMEM) for x in given]
     out = jax.ShapeDtypeStruct((tokens, heads, KEY_VALUE_RANK), BF)
     return pl.pallas_call(
@@ -610,15 +612,20 @@
     got = [swap(x, top) for x in out]
     far = outer(kept[0], after(got[0], out[2]))
     middle = outer(kept[1], got[1])
-    close = outer(kept[2], got[2])
+    second = cached_attention(
+        lengths, after(q_t, middle, out[2]), cache_t, [], half, half // 2, cost=LONG
+    )
+    close = outer(kept[2], after(got[2], second))
     outs_e = to_line(close + middle + far)
-    second = cached_attention(lengths, after(q_t, close[1]), cache_t, [], half, half)
-    outs_e, second = lax.optimization_barrier((outs_e, second))
+    third = cached_attention(
+        lengths, after(q_t, close[1]), cache_t, [], half + half // 2, half // 2
+    )
+    outs_e, third = lax.optimization_barrier((outs_e, third))
 
     own_sum, own_part, *rows = combine(place, outs_e, own_quarters, gates, attn_gain[None], kvs)
     rows = [own_sum, own_part] + [swap(r, (k + 1) * split) for k, r in enumerate(rows)]
     return final_attention(
-        place, width, rows, latent_norm_gain[None], turn, allow, q_t, first, second
+        place, width, rows, latent_norm_gain[None], turn, allow, q_t, [*first, *second, *third]
     )
 
 

time: 81.9 us -> 79.8 us (0.974)
  waiting for transfers between devices: 20.8 us -> 17.1 us
  Pallas kernels: 29.5 us -> 31 us
    ppermute x27, waiting for transfers between devices: 20.8 us -> 17.1 us  [swap(): return lax.ppermute(x, 'ep', [(i, i ^ bit) for i in range(size)])]
    pallas_call x2 -> x3, Pallas kernels: 13.8 us -> 15.9 us  [cached_attention(): pl.pallas_call(functools.partial(cached_kernel, first, per), out_shape=[p...]
  transfers between devices with their start and end apart: 27 -> 27, of which waited for: 11 -> 12; matrix products, arithmetic and copies ran while one was open for 3% -> 3% of each run, Pallas kernels for 23% -> 26%
where the time goes in v5:
time: 79.8 us; the launch traced here: 79.6 us
  Pallas kernels  31 us (39%)
  starting transfers between devices  27.4 us (34%)
  waiting for transfers between devices  17.1 us (21%)
  between operations  1.7 us (2%)
  matrix products  1.43 us (2%)
    ppermute x27, starting transfers between devices, swap(): return lax.ppermute(x, 'ep', [(i, i ^ bit) for i in range(size)])  27.4 us
    ppermute x27, waiting for transfers between devices, swap(): return lax.ppermute(x, 'ep', [(i, i ^ bit) for i in range(size)])  17.1 us
    pallas_call x3, Pallas kernels, cached_attention(): pl.pallas_call(functools.partial(cached_kernel, first, per), out_shape=[p...  15.9 us
    pallas_call x1, Pallas kernels, expert_slice(): pl.pallas_call(functools.partial(expert_kernel, split), out_shape=[act] +...  4.07 us
    pallas_call x1, Pallas kernels, final_attention(): pl.pallas_call(functools.partial(final_kernel, width, per), out_shape=[ja...  3.9 us
    pallas_call x1, Pallas kernels, combine(): pl.pallas_call(functools.partial(combine_kernel, spots, tokens), out_shap...  2.58 us
    pallas_call x1, Pallas kernels, pack(): pl.pallas_call(pack_kernel, out_shape=[chunk] * EXPERTS + [part] * EXPERT...  2.09 us
  transfers between devices with their start and end apart: 27, of which 12 were waited for; matrix products, arithmetic and copies ran while one was open for 3% of the time, Pallas kernels for 26%

profile of v5, /device:TPU:0, one launch (start us, length us, event | category | flops | bytes accessed | tf_op | source)
XLA Modules:
  0.0 79.6 jit_solution(4600381799995430250)
XLA Ops:
  0.6 3.0 %collective-permute-start.6 = (bf16[448,576]{1,0:T(8,128)(2,1)}, bf16[448,576]{1,0:T(8,128)(2,1)S(1)}, u32[]{:S(2)}, u32[]{:S(2)}) collective-permute-start(bf16[448,576]{1,0:T(8,128)(2,1)} %refs_10_), channel_id=1, source_target_pairs={{0,2},{1,3},{2,0},{3,1},{4,6},{5,7},{6,4},{7,5},{8,10},{9,11},{10,... | collective-permute-start | bytes 1548296 | tf_op jit(solution)/shard_map/ppermute | solution.py:555
  3.7 2.1 %pack.1 = (bf16[8,8192]{1,0:T(8,128)(2,1)S(1)}, bf16[8,8192]{1,0:T(8,128)(2,1)S(1)}, bf16[8,8192]{1,0:T(8,128)(2,1)S(1)}, bf16[8,8192]{1,0:T(8,128)(2,1)S(1)}, b...) custom-call(s32[2]{0:T(128)S(1)} %pad_add_fusion.e_ref, ...), custom_call_target="tpu_custom_call" | custom-call | flops 1024 | bytes 1024 | tf_op jit(solution)/shard_map/pack/pallas_call | solution.py:113
  5.8 1.6 %collective-permute-start = (bf16[8,8192]{1,0:T(8,128)(2,1)S(1)}, bf16[8,8192]{1,0:T(8,128)(2,1)S(1)}, u32[]{:S(2)}, u32[]{:S(2)}) collective-permute-start(bf16[8,8192]{1,0:T(8,128)(2,1)S(1)} %get-tuple-element.67), channel_id=1, source_target_pairs={{0,4},{1,5},{2,6},{3,7},{4,0},{5,1},{6,2},{7,3},{8,12},{9,13},{10,... | collective-permute-start | bytes 393224 | tf_op jit(solution)/shard_map/ppermute | solution.py:555
  7.5 2.6 %collective-permute-start.4 = (bf16[8,8192]{1,0:T(8,128)(2,1)S(1)}, bf16[8,8192]{1,0:T(8,128)(2,1)S(1)}, u32[]{:S(2)}, u32[]{:S(2)}) collective-permute-start(bf16[8,8192]{1,0:T(8,128)(2,1)S(1)} %get-tuple-element.68), channel_id=1, source_target_pairs={{0,8},{1,9},{2,10},{3,11},{4,12},{5,13},{6,14},{7,15},{8,0},{9,1},... | collective-permute-start | bytes 393224 | tf_op jit(solution)/shard_map/ppermute | solution.py:555
  11.0 1.0 %convolution_minimum_fusion.3 = f32[16,16]{0,1:T(8,128)S(1)} fusion(s32[16]{0:T(128)} %bitcast.61), kind=kOutput, calls=%fused_computation.3 | convolution fusion | flops 50688 | bytes 1088 | tf_op jit(solution)/shard_map/dot_general | solution.py:510
  13.2 8.0 %cached.3 = (bf16[8,128,512]{2,1,0:T(8,128)(2,1)S(1)}, f32[8,2,128]{2,1,0:T(2,128)S(1)}, bf16[1,7168,1024]{2,1,0:T(8,128)(2,1)S(1)}, bf16[1,512,7168]{2,1,0:T(8,128)(2,1)S(1)}) custom-call(s32[1]{0:T(128)S(6)} %copy.17.length_ref, bf16[16,576,128]{2,1,0:T(8,128)(2,1)} %bitcast.49, bf16[1,576,1024]{2,1,0:T(8,128)(2,1)} %bitcast.55, ...), custom_call_target="tpu_custom_call" | custom-call | flops 4563402752 | bytes 2359296 | tf_op jit(solution)/shard_map/cached/pallas_call | solution.py:390
  22.5 1.7 %collective-permute-start.8 = (bf16[16,8192]{1,0:T(8,128)(2,1)S(1)}, bf16[16,8192]{1,0:T(8,128)(2,1)S(1)}, u32[]{:S(2)}, u32[]{:S(2)}) collective-permute-start(bf16[16,8192]{1,0:T(8,128)(2,1)S(1)} %join.3.refs_1_), channel_id=1, source_target_pairs={{0,2},{1,3},{2,0},{3,1},{4,6},{5,7},{6,4},{7,5},{8,10},{9,11},{10,... | collective-permute-start | bytes 786440 | tf_op jit(solution)/shard_map/ppermute | solution.py:555
  24.2 1.6 %collective-permute-start.9 = (bf16[16,1792]{1,0:T(8,128)(2,1)S(1)}, bf16[16,1792]{1,0:T(8,128)(2,1)S(1)}, u32[]{:S(2)}, u32[]{:S(2)}) collective-permute-start(bf16[16,1792]{1,0:T(8,128)(2,1)S(1)} %get-tuple-element.80), channel_id=1, source_target_pairs={{0,4},{1,5},{2,6},{3,7},{4,0},{5,1},{6,2},{7,3},{8,12},{9,13},{10,... | collective-permute-start | bytes 172040 | tf_op jit(solution)/shard_map/ppermute | solution.py:555
  25.8 2.6 %collective-permute-start.10 = (bf16[16,1792]{1,0:T(8,128)(2,1)S(1)}, bf16[16,1792]{1,0:T(8,128)(2,1)S(1)}, u32[]{:S(2)}, u32[]{:S(2)}) collective-permute-start(bf16[16,1792]{1,0:T(8,128)(2,1)S(1)} %get-tuple-element.81), channel_id=1, source_target_pairs={{0,8},{1,9},{2,10},{3,11},{4,12},{5,13},{6,14},{7,15},{8,0},{9,1},... | collective-permute-start | bytes 172040 | tf_op jit(solution)/shard_map/ppermute | solution.py:555
  28.6 1.0 %gates.1.refs_8_ = bf16[4,192,40]{2,1,0:T(8,128)(2,1)S(1)} custom-call(s32[2]{0:T(128)S(1)} %pad_add_fusion.e_ref, bf16[16,8192]{1,0:T(8,128)(2,1)S(1)} %join.2.refs_0_, bf16[16,8192]{1,0:T(8,128)(2,1)S(1)} %join.3.refs_1_), custom_call_target="tpu_custom_call" | custom-call | flops 17179869184 | bytes 16777216 | tf_op jit(solution)/shard_map/gates/pallas_call | solution.py:255
  29.7 1.5 %collective-permute-done.8.refs_5_ = bf16[16,8192]{1,0:T(8,128)(2,1)S(1)} collective-permute-done((bf16[16,8192]{1,0:T(8,128)(2,1)S(1)}, bf16[16,8192]{1,0:T(8,128)(2,1)S(1)}, u32[]{:S(2)}, u32[]{:S(2)}) %collective-permute-start.8) | collective-permute-done | bytes 262176 | tf_op jit(solution)/shard_map/ppermute | solution.py:555
  31.2 1.0 %collective-permute-done.10.refs_6_ = bf16[16,1792]{1,0:T(8,128)(2,1)S(1)} collective-permute-done((bf16[16,1792]{1,0:T(8,128)(2,1)S(1)}, bf16[16,1792]{1,0:T(8,128)(2,1)S(1)}, u32[]{:S(2)}, u32[]{:S(2)}) %collective-permute-start.10) | collective-permute-done | bytes 57376 | tf_op jit(solution)/shard_map/ppermute | solution.py:555
  32.2 2.1 %collective-permute-done.11.refs_7_ = bf16[16,1792]{1,0:T(8,128)(2,1)S(1)} collective-permute-done((bf16[16,1792]{1,0:T(8,128)(2,1)S(1)}, bf16[16,1792]{1,0:T(8,128)(2,1)S(1)}, u32[]{:S(2)}, u32[]{:S(2)}) %collective-permute-start.11) | collective-permute-done | bytes 57376 | tf_op jit(solution)/shard_map/ppermute | solution.py:555
  34.4 1.5 %collective-permute-done.12.refs_7_ = bf16[16,8192]{1,0:T(8,128)(2,1)S(1)} collective-permute-done((bf16[16,8192]{1,0:T(8,128)(2,1)S(1)}, bf16[16,8192]{1,0:T(8,128)(2,1)S(1)}, u32[]{:S(2)}, u32[]{:S(2)}) %collective-permute-start.12) | collective-permute-done | bytes 262176 | tf_op jit(solution)/shard_map/ppermute | solution.py:555
  35.9 4.1 %experts.1 = (bf16[160,512]{1,0:T(8,128)(2,1)S(1)}, bf16[2,1,40,1792]{3,2,1,0:T(8,128)(2,1)S(1)}, bf16[2,1,40,1792]{3,2,1,0:T(8,128)(2,1)S(1)}, bf16[2,1,40,1792...) custom-call(s32[2]{0:T(128)S(1)} %pad_add_fusion.e_ref, bf16[16,8192]{1,0:T(8,128)(2,1)S(1)} %join.2.refs_0_, ...), custom_call_target="tpu_custom_call" | custom-call | flops 1024 | bytes 1024 | tf_op jit(solution)/shard_map/experts/pallas_call | solution.py:184
  40.2 1.4 %experts_rest.1 = (bf16[2,2,40,1792]{3,2,1,0:T(8,128)(2,1)S(1)}, bf16[2,2,40,1792]{3,2,1,0:T(8,128)(2,1)S(1)}) custom-call(s32[2]{0:T(128)S(1)} %pad_add_fusion.e_ref, bf16[160,512]{1,0:T(8,128)(2,1)S(1)} %get-tuple-element.92.act, bf16[1,512,7168]{2,1,0:T(8,128)(2,1)S(1)} %get-tuple-element.91.refs_9_.w_out), custom_call_target="tpu_custom_call" | custom-call | flops 1024 | bytes 1024 | tf_op jit(solution)/shard_map/experts_rest/pallas_call | solution.py:194
  42.8 0.6 collective-permute-start.16
  43.4 1.6 %collective-permute-start.20 = (bf16[1,40,1792]{2,1,0:T(8,128)(2,1)S(1)}, bf16[1,40,1792]{2,1,0:T(8,128)(2,1)S(1)}, u32[]{:S(2)}, u32[]{:S(2)}) collective-permute-start(bf16[1,40,1792]{2,1,0:T(8,128)(2,1)S(1)} %fusion.6), channel_id=1, source_target_pairs={{0,2},{1,3},{2,0},{3,1},{4,6},{5,7},{6,4},{7,5},{8,10},{9,11},{10,... | collective-permute-start | bytes 430088 | tf_op jit(solution)/shard_map/ppermute | solution.py:555
  45.0 4.4 %collective-permute-done.16 = bf16[1,40,1792]{2,1,0:T(8,128)(2,1)S(1)} collective-permute-done((bf16[1,40,1792]{2,1,0:T(8,128)(2,1)S(1)}, bf16[1,40,1792]{2,1,0:T(8,128)(2,1)S(1)}, u32[]{:S(2)}, u32[]{:S(2)}) %collective-permute-start.16) | collective-permute-done | bytes 143392 | tf_op jit(solution)/shard_map/ppermute | solution.py:555
  49.5 1.4 %collective-permute-start.18 = (bf16[40,1792]{1,0:T(8,128)(2,1)S(1)}, bf16[40,1792]{1,0:T(8,128)(2,1)S(1)}, u32[]{:S(2)}, u32[]{:S(2)}) collective-permute-start(bf16[40,1792]{1,0:T(8,128)(2,1)S(1)} %fusion.4), channel_id=1, source_target_pairs={{0,8},{1,9},{2,10},{3,11},{4,12},{5,13},{6,14},{7,15},{8,0},{9,1},... | collective-permute-start | bytes 430088 | tf_op jit(solution)/shard_map/ppermute | solution.py:555
  51.0 0.6 collective-permute-start.14
  52.0 2.1 %collective-permute-start.21 = (bf16[40,1792]{1,0:T(8,128)(2,1)S(1)}, bf16[40,1792]{1,0:T(8,128)(2,1)S(1)}, u32[]{:S(2)}, u32[]{:S(2)}) collective-permute-start(bf16[40,1792]{1,0:T(8,128)(2,1)S(1)} %fusion.1), channel_id=1, source_target_pairs={{0,12},{1,13},{2,14},{3,15},{4,8},{5,9},{6,10},{7,11},{8,4},{9,5},... | collective-permute-start | bytes 430088 | tf_op jit(solution)/shard_map/ppermute | solution.py:555
  54.0 4.0 %cached.4 = (bf16[4,128,512]{2,1,0:T(8,128)(2,1)S(1)}, f32[4,2,128]{2,1,0:T(2,128)S(1)}) custom-call(s32[1]{0:T(128)S(6)} %copy.17.length_ref, bf16[16,576,128]{2,1,0:T(8,128)(2,1)} %bitcast.50, bf16[1,576,1024]{2,1,0:T(8,128)(2,1)} %bitcast.56), custom_call_target="tpu_custom_call" | custom-call | flops 17179869184 | bytes 16777216 | tf_op jit(solution)/shard_map/cached/pallas_call | solution.py:390
  58.6 0.9 %collective-permute-start.17 = (bf16[40,1792]{1,0:T(8,128)(2,1)S(1)}, bf16[40,1792]{1,0:T(8,128)(2,1)S(1)}, u32[]{:S(2)}, u32[]{:S(2)}) collective-permute-start(bf16[40,1792]{1,0:T(8,128)(2,1)S(1)} %get-tuple-element.129), channel_id=1, source_target_pairs={{0,4},{1,5},{2,6},{3,7},{4,0},{5,1},{6,2},{7,3},{8,12},{9,13},{10,... | collective-permute-start | bytes 430088 | tf_op jit(solution)/shard_map/ppermute | solution.py:555
  59.5 3.8 %cached.5 = (bf16[4,128,512]{2,1,0:T(8,128)(2,1)S(1)}, f32[4,2,128]{2,1,0:T(2,128)S(1)}) custom-call(s32[1]{0:T(128)S(6)} %copy.17.length_ref, bf16[16,576,128]{2,1,0:T(8,128)(2,1)} %bitcast.51, bf16[1,576,1024]{2,1,0:T(8,128)(2,1)} %bitcast.57), custom_call_target="tpu_custom_call" | custom-call | flops 2281701376 | bytes 1179648 | tf_op jit(solution)/shard_map/cached/pallas_call | solution.py:390
  63.8 2.6 %combine.1 = (f32[16,640]{1,0:T(8,128)S(1)}, bf16[16,1792]{1,0:T(8,128)(2,1)S(1)}, bf16[16,2432]{1,0:T(8,128)(2,1)S(1)}, bf16[16,2432]{1,0:T(8,128)(2,1)S(1)}, bf16[16,2432]{1,0:T(8,128)(2,1)S(1)}) custom-call(s32[2]{0:T(128)S(1)} %pad_add_fusion.e_ref, bf16[40,1792]{1,0:T(8,128)(2,1)S(1)} %get-tuple-element.107.refs_0_, ...), custom_call_target="tpu_custom_call" | custom-call | flops 1024 | bytes 1024 | tf_op jit(solution)/shard_map/combine/pallas_call | solution.py:317
  66.4 0.9 %collective-permute-start.24 = (bf16[16,2432]{1,0:T(8,128)(2,1)S(1)}, bf16[16,2432]{1,0:T(8,128)(2,1)S(1)}, u32[]{:S(2)}, u32[]{:S(2)}) collective-permute-start(bf16[16,2432]{1,0:T(8,128)(2,1)S(1)} %get-tuple-element.122), channel_id=1, source_target_pairs={{0,4},{1,5},{2,6},{3,7},{4,0},{5,1},{6,2},{7,3},{8,12},{9,13},{10,... | collective-permute-start | bytes 233480 | tf_op jit(solution)/shard_map/ppermute | solution.py:555
  67.3 1.9 %collective-permute-start.25 = (bf16[16,2432]{1,0:T(8,128)(2,1)S(1)}, bf16[16,2432]{1,0:T(8,128)(2,1)S(1)}, u32[]{:S(2)}, u32[]{:S(2)}) collective-permute-start(bf16[16,2432]{1,0:T(8,128)(2,1)S(1)} %get-tuple-element.123), channel_id=1, source_target_pairs={{0,8},{1,9},{2,10},{3,11},{4,12},{5,13},{6,14},{7,15},{8,0},{9,1},... | collective-permute-start | bytes 233480 | tf_op jit(solution)/shard_map/ppermute | solution.py:555
  69.2 1.6 %collective-permute-start.26 = (bf16[16,2432]{1,0:T(8,128)(2,1)S(1)}, bf16[16,2432]{1,0:T(8,128)(2,1)S(1)}, u32[]{:S(2)}, u32[]{:S(2)}) collective-permute-start(bf16[16,2432]{1,0:T(8,128)(2,1)S(1)} %get-tuple-element.124), channel_id=1, source_target_pairs={{0,12},{1,13},{2,14},{3,15},{4,8},{5,9},{6,10},{7,11},{8,4},{9,5},... | collective-permute-start | bytes 233480 | tf_op jit(solution)/shard_map/ppermute | solution.py:555
  70.9 3.7 %collective-permute-done.25.refs_3_ = bf16[16,2432]{1,0:T(8,128)(2,1)S(1)} collective-permute-done((bf16[16,2432]{1,0:T(8,128)(2,1)S(1)}, bf16[16,2432]{1,0:T(8,128)(2,1)S(1)}, u32[]{:S(2)}, u32[]{:S(2)}) %collective-permute-start.25) | collective-permute-done | bytes 77856 | tf_op jit(solution)/shard_map/ppermute | solution.py:555
  74.7 0.8 %collective-permute-done.26.refs_4_ = bf16[16,2432]{1,0:T(8,128)(2,1)S(1)} collective-permute-done((bf16[16,2432]{1,0:T(8,128)(2,1)S(1)}, bf16[16,2432]{1,0:T(8,128)(2,1)S(1)}, u32[]{:S(2)}, u32[]{:S(2)}) %collective-permute-start.26) | collective-permute-done | bytes 77856 | tf_op jit(solution)/shard_map/ppermute | solution.py:555
  75.5 3.9 %final.1 = (bf16[16,7168]{1,0:T(8,128)(2,1)}, bf16[16,576]{1,0:T(8,128)(2,1)}, bf16[16,128,512]{2,1,0:T(8,128)(2,1)}) custom-call(s32[2]{0:T(128)S(1)} %pad_add_fusion.e_ref, f32[16,640]{1,0:T(8,128)S(1)} %get-tuple-element.120.refs_0_, bf16[16,1792]{1,0:T(8,128)(2,1)S(1)} %get-tuple-element.121.refs_1_, ...), custom_call_target="tpu_custom_call" | custom-call | flops 1024 | bytes 1024 | tf_op jit(solution)/shard_map/final/pallas_call | solution.py:486
  (62 shorter events, 5.9 us)
Async XLA Ops:
  0.6 20.7 %collective-permute-start.6 = (bf16[448,576]{1,0:T(8,128)(2,1)}, bf16[448,576]{1,0:T(8,128)(2,1)S(1)}, u32[]{:S(2)}, u32[]{:S(2)}) collective-permute-start(bf16[448,576]{1,0:T(8,128)(2,1)} %refs_10_), channel_id=1, source_target_pairs={{0,2},{1,3},{2,0},{3,1},{4,6},{5,7},{6,4},{7,5},{8,10},{9,11},{10,... | collective-permute-start | bytes 1548296 | tf_op jit(solution)/shard_map/ppermute | solution.py:555
  5.8 6.9 %collective-permute-start = (bf16[8,8192]{1,0:T(8,128)(2,1)S(1)}, bf16[8,8192]{1,0:T(8,128)(2,1)S(1)}, u32[]{:S(2)}, u32[]{:S(2)}) collective-permute-start(bf16[8,8192]{1,0:T(8,128)(2,1)S(1)} %get-tuple-element.67), channel_id=1, source_target_pairs={{0,4},{1,5},{2,6},{3,7},{4,0},{5,1},{6,2},{7,3},{8,12},{9,13},{10,... | collective-permute-start | bytes 393224 | tf_op jit(solution)/shard_map/ppermute | solution.py:555
  7.5 13.8 %collective-permute-start.4 = (bf16[8,8192]{1,0:T(8,128)(2,1)S(1)}, bf16[8,8192]{1,0:T(8,128)(2,1)S(1)}, u32[]{:S(2)}, u32[]{:S(2)}) collective-permute-start(bf16[8,8192]{1,0:T(8,128)(2,1)S(1)} %get-tuple-element.68), channel_id=1, source_target_pairs={{0,8},{1,9},{2,10},{3,11},{4,12},{5,13},{6,14},{7,15},{8,0},{9,1},... | collective-permute-start | bytes 393224 | tf_op jit(solution)/shard_map/ppermute | solution.py:555
  10.1 11.2 %collective-permute-start.5 = (bf16[8,8192]{1,0:T(8,128)(2,1)S(1)}, bf16[8,8192]{1,0:T(8,128)(2,1)S(1)}, u32[]{:S(2)}, u32[]{:S(2)}) collective-permute-start(bf16[8,8192]{1,0:T(8,128)(2,1)S(1)} %get-tuple-element.69), channel_id=1, source_target_pairs={{0,12},{1,13},{2,14},{3,15},{4,8},{5,9},{6,10},{7,11},{8,4},{9,5},... | collective-permute-start | bytes 393224 | tf_op jit(solution)/shard_map/ppermute | solution.py:555
  12.8 9.7 %collective-permute-start.2 = (bf16[16,8192]{1,0:T(8,128)(2,1)S(1)}, bf16[16,8192]{1,0:T(8,128)(2,1)S(1)}, u32[]{:S(2)}, u32[]{:S(2)}) collective-permute-start(bf16[16,8192]{1,0:T(8,128)(2,1)S(1)} %join.2.refs_0_), channel_id=1, source_target_pairs={{0,2},{1,3},{2,0},{3,1},{4,6},{5,7},{6,4},{7,5},{8,10},{9,11},{10,... | collective-permute-start | bytes 786440 | tf_op jit(solution)/shard_map/ppermute | solution.py:555
  21.3 2.9 %collective-permute-start.7 = (bf16[16,8192]{1,0:T(8,128)(2,1)S(1)}, bf16[16,8192]{1,0:T(8,128)(2,1)S(1)}, u32[]{:S(2)}, u32[]{:S(2)}) collective-permute-start(bf16[16,8192]{1,0:T(8,128)(2,1)S(1)} %join.3.refs_1_), channel_id=1, source_target_pairs={{0,1},{1,0},{2,3},{3,2},{4,5},{5,4},{6,7},{7,6},{8,9},{9,8},{10,11... | collective-permute-start | bytes 786440 | tf_op jit(solution)/shard_map/ppermute | solution.py:555
  21.4 7.0 %collective-permute-start.1 = (bf16[16,8192]{1,0:T(8,128)(2,1)S(1)}, bf16[16,8192]{1,0:T(8,128)(2,1)S(1)}, u32[]{:S(2)}, u32[]{:S(2)}) collective-permute-start(bf16[16,8192]{1,0:T(8,128)(2,1)S(1)} %join.2.refs_0_), channel_id=1, source_target_pairs={{0,1},{1,0},{2,3},{3,2},{4,5},{5,4},{6,7},{7,6},{8,9},{9,8},{10,11... | collective-permute-start | bytes 786440 | tf_op jit(solution)/shard_map/ppermute | solution.py:555
  22.5 7.2 %collective-permute-start.3 = (bf16[16,8192]{1,0:T(8,128)(2,1)S(1)}, bf16[16,8192]{1,0:T(8,128)(2,1)S(1)}, u32[]{:S(2)}, u32[]{:S(2)}) collective-permute-start(bf16[16,8192]{1,0:T(8,128)(2,1)S(1)} %collective-permute-done.2.refs_4_), channel_id=1, source_target_pairs={{0,1},{1,0},{2,3},{3,2},{4,5},{5,4},{6,7},{7,6},{8,9},{9,8},{10,11... | collective-permute-start | bytes 786440 | tf_op jit(solution)/shard_map/ppermute | solution.py:555
  22.5 8.7 %collective-permute-start.8 = (bf16[16,8192]{1,0:T(8,128)(2,1)S(1)}, bf16[16,8192]{1,0:T(8,128)(2,1)S(1)}, u32[]{:S(2)}, u32[]{:S(2)}) collective-permute-start(bf16[16,8192]{1,0:T(8,128)(2,1)S(1)} %join.3.refs_1_), channel_id=1, source_target_pairs={{0,2},{1,3},{2,0},{3,1},{4,6},{5,7},{6,4},{7,5},{8,10},{9,11},{10,... | collective-permute-start | bytes 786440 | tf_op jit(solution)/shard_map/ppermute | solution.py:555
  24.2 7.0 %collective-permute-start.9 = (bf16[16,1792]{1,0:T(8,128)(2,1)S(1)}, bf16[16,1792]{1,0:T(8,128)(2,1)S(1)}, u32[]{:S(2)}, u32[]{:S(2)}) collective-permute-start(bf16[16,1792]{1,0:T(8,128)(2,1)S(1)} %get-tuple-element.80), channel_id=1, source_target_pairs={{0,4},{1,5},{2,6},{3,7},{4,0},{5,1},{6,2},{7,3},{8,12},{9,13},{10,... | collective-permute-start | bytes 172040 | tf_op jit(solution)/shard_map/ppermute | solution.py:555
  25.8 6.4 %collective-permute-start.10 = (bf16[16,1792]{1,0:T(8,128)(2,1)S(1)}, bf16[16,1792]{1,0:T(8,128)(2,1)S(1)}, u32[]{:S(2)}, u32[]{:S(2)}) collective-permute-start(bf16[16,1792]{1,0:T(8,128)(2,1)S(1)} %get-tuple-element.81), channel_id=1, source_target_pairs={{0,8},{1,9},{2,10},{3,11},{4,12},{5,13},{6,14},{7,15},{8,0},{9,1},... | collective-permute-start | bytes 172040 | tf_op jit(solution)/shard_map/ppermute | solution.py:555
  28.4 6.0 %collective-permute-start.11 = (bf16[16,1792]{1,0:T(8,128)(2,1)S(1)}, bf16[16,1792]{1,0:T(8,128)(2,1)S(1)}, u32[]{:S(2)}, u32[]{:S(2)}) collective-permute-start(bf16[16,1792]{1,0:T(8,128)(2,1)S(1)} %get-tuple-element.82), channel_id=1, source_target_pairs={{0,12},{1,13},{2,14},{3,15},{4,8},{5,9},{6,10},{7,11},{8,4},{9,5},... | collective-permute-start | bytes 172040 | tf_op jit(solution)/shard_map/ppermute | solution.py:555
  34.4 1.5 %collective-permute-start.12 = (bf16[16,8192]{1,0:T(8,128)(2,1)S(1)}, bf16[16,8192]{1,0:T(8,128)(2,1)S(1)}, u32[]{:S(2)}, u32[]{:S(2)}) collective-permute-start(bf16[16,8192]{1,0:T(8,128)(2,1)S(1)} %collective-permute-done.8.refs_5_), channel_id=1, source_target_pairs={{0,1},{1,0},{2,3},{3,2},{4,5},{5,4},{6,7},{7,6},{8,9},{9,8},{10,11... | collective-permute-start | bytes 786440 | tf_op jit(solution)/shard_map/ppermute | solution.py:555
  40.0 2.1 %copy-start.1 = (bf16[448,576]{1,0:T(8,128)(2,1)S(1)}, bf16[448,576]{1,0:T(8,128)(2,1)}, u32[]{:S(2)}) copy-start(bf16[448,576]{1,0:T(8,128)(2,1)} %refs_10_) | copy-start | bytes 1548292
  40.0 2.7 %collective-permute-start.15 = (bf16[2,1,40,1792]{3,2,1,0:T(8,128)(2,1)S(1)}, bf16[2,1,40,1792]{3,2,1,0:T(8,128)(2,1)S(1)}, u32[]{:S(2)}, u32[]{:S(2)}) collective-permute-start(bf16[2,1,40,1792]{3,2,1,0:T(8,128)(2,1)S(1)} %get-tuple-element.96), channel_id=1, source_target_pairs={{0,1},{1,0},{2,3},{3,2},{4,5},{5,4},{6,7},{7,6},{8,9},{9,8},{10,11... | collective-permute-start | bytes 860168 | tf_op jit(solution)/shard_map/ppermute | solution.py:555
  41.6 1.7 %collective-permute-start.19 = (bf16[2,1,40,1792]{3,2,1,0:T(8,128)(2,1)S(1)}, bf16[2,1,40,1792]{3,2,1,0:T(8,128)(2,1)S(1)}, u32[]{:S(2)}, u32[]{:S(2)}) collective-permute-start(bf16[2,1,40,1792]{3,2,1,0:T(8,128)(2,1)S(1)} %get-tuple-element.102), channel_id=1, source_target_pairs={{0,1},{1,0},{2,3},{3,2},{4,5},{5,4},{6,7},{7,6},{8,9},{9,8},{10,11... | collective-permute-start | bytes 860168 | tf_op jit(solution)/shard_map/ppermute | solution.py:555
  42.1 21.7 %collective-permute-start.22 = (bf16[448,576]{1,0:T(8,128)(2,1)S(1)}, bf16[448,576]{1,0:T(8,128)(2,1)S(1)}, u32[]{:S(2)}, u32[]{:S(2)}) collective-permute-start(bf16[448,576]{1,0:T(8,128)(2,1)S(1)} %copy-done.1), channel_id=1, source_target_pairs={{0,1},{1,0},{2,3},{3,2},{4,5},{5,4},{6,7},{7,6},{8,9},{9,8},{10,11... | collective-permute-start | bytes 1548296 | tf_op jit(solution)/shard_map/ppermute | solution.py:555
  42.2 21.6 %collective-permute-start.23 = (bf16[448,576]{1,0:T(8,128)(2,1)S(1)}, bf16[448,576]{1,0:T(8,128)(2,1)S(1)}, u32[]{:S(2)}, u32[]{:S(2)}) collective-permute-start(bf16[448,576]{1,0:T(8,128)(2,1)S(1)} %collective-permute-done.6.refs_11_), channel_id=1, source_target_pairs={{0,1},{1,0},{2,3},{3,2},{4,5},{5,4},{6,7},{7,6},{8,9},{9,8},{10,11... | collective-permute-start | bytes 1548296 | tf_op jit(solution)/shard_map/ppermute | solution.py:555
  42.6 8.3 %collective-permute-start.13 = (bf16[2,2,40,1792]{3,2,1,0:T(8,128)(2,1)S(1)}, bf16[2,2,40,1792]{3,2,1,0:T(8,128)(2,1)S(1)}, u32[]{:S(2)}, u32[]{:S(2)}) collective-permute-start(bf16[2,2,40,1792]{3,2,1,0:T(8,128)(2,1)S(1)} %get-tuple-element.94), channel_id=1, source_target_pairs={{0,1},{1,0},{2,3},{3,2},{4,5},{5,4},{6,7},{7,6},{8,9},{9,8},{10,11... | collective-permute-start | bytes 1720328 | tf_op jit(solution)/shard_map/ppermute | solution.py:555
  42.8 6.7 %collective-permute-start.16 = (bf16[1,40,1792]{2,1,0:T(8,128)(2,1)S(1)}, bf16[1,40,1792]{2,1,0:T(8,128)(2,1)S(1)}, u32[]{:S(2)}, u32[]{:S(2)}) collective-permute-start(bf16[1,40,1792]{2,1,0:T(8,128)(2,1)S(1)} %fusion.5), channel_id=1, source_target_pairs={{0,2},{1,3},{2,0},{3,1},{4,6},{5,7},{6,4},{7,5},{8,10},{9,11},{10,... | collective-permute-start | bytes 430088 | tf_op jit(solution)/shard_map/ppermute | solution.py:555
  43.4 8.5 %collective-permute-start.20 = (bf16[1,40,1792]{2,1,0:T(8,128)(2,1)S(1)}, bf16[1,40,1792]{2,1,0:T(8,128)(2,1)S(1)}, u32[]{:S(2)}, u32[]{:S(2)}) collective-permute-start(bf16[1,40,1792]{2,1,0:T(8,128)(2,1)S(1)} %fusion.6), channel_id=1, source_target_pairs={{0,2},{1,3},{2,0},{3,1},{4,6},{5,7},{6,4},{7,5},{8,10},{9,11},{10,... | collective-permute-start | bytes 430088 | tf_op jit(solution)/shard_map/ppermute | solution.py:555
  49.5 13.9 %collective-permute-start.18 = (bf16[40,1792]{1,0:T(8,128)(2,1)S(1)}, bf16[40,1792]{1,0:T(8,128)(2,1)S(1)}, u32[]{:S(2)}, u32[]{:S(2)}) collective-permute-start(bf16[40,1792]{1,0:T(8,128)(2,1)S(1)} %fusion.4), channel_id=1, source_target_pairs={{0,8},{1,9},{2,10},{3,11},{4,12},{5,13},{6,14},{7,15},{8,0},{9,1},... | collective-permute-start | bytes 430088 | tf_op jit(solution)/shard_map/ppermute | solution.py:555
  51.0 7.5 %collective-permute-start.14 = (bf16[2,40,1792]{2,1,0:T(8,128)(2,1)S(1)}, bf16[2,40,1792]{2,1,0:T(8,128)(2,1)S(1)}, u32[]{:S(2)}, u32[]{:S(2)}) collective-permute-start(bf16[2,40,1792]{2,1,0:T(8,128)(2,1)S(1)} %fusion), channel_id=1, source_target_pairs={{0,2},{1,3},{2,0},{3,1},{4,6},{5,7},{6,4},{7,5},{8,10},{9,11},{10,... | collective-permute-start | bytes 860168 | tf_op jit(solution)/shard_map/ppermute | solution.py:555
  52.0 11.4 %collective-permute-start.21 = (bf16[40,1792]{1,0:T(8,128)(2,1)S(1)}, bf16[40,1792]{1,0:T(8,128)(2,1)S(1)}, u32[]{:S(2)}, u32[]{:S(2)}) collective-permute-start(bf16[40,1792]{1,0:T(8,128)(2,1)S(1)} %fusion.1), channel_id=1, source_target_pairs={{0,12},{1,13},{2,14},{3,15},{4,8},{5,9},{6,10},{7,11},{8,4},{9,5},... | collective-permute-start | bytes 430088 | tf_op jit(solution)/shard_map/ppermute | solution.py:555
  58.1 5.7 %copy-start.2 = (f32[7168]{0:T(1024)S(1)}, f32[7168]{0:T(1024)}, u32[]{:S(2)}) copy-start(f32[7168]{0:T(1024)} %param.15) | copy-start | bytes 86020
  58.1 17.4 %copy-start = (bf16[16,128,576]{1,2,0:T(8,128)(2,1)S(1)}, bf16[16,128,576]{1,2,0:T(8,128)(2,1)}, u32[]{:S(2)}) copy-start(bf16[16,128,576]{1,2,0:T(8,128)(2,1)} %param.24) | copy-start | bytes 7077892
  58.1 17.4 %copy-start.3 = (f32[512]{0:T(512)S(1)}, f32[512]{0:T(512)}, u32[]{:S(2)}) copy-start(f32[512]{0:T(512)} %param.16) | copy-start | bytes 6148
  58.6 5.2 %collective-permute-start.17 = (bf16[40,1792]{1,0:T(8,128)(2,1)S(1)}, bf16[40,1792]{1,0:T(8,128)(2,1)S(1)}, u32[]{:S(2)}, u32[]{:S(2)}) collective-permute-start(bf16[40,1792]{1,0:T(8,128)(2,1)S(1)} %get-tuple-element.129), channel_id=1, source_target_pairs={{0,4},{1,5},{2,6},{3,7},{4,0},{5,1},{6,2},{7,3},{8,12},{9,13},{10,... | collective-permute-start | bytes 430088 | tf_op jit(solution)/shard_map/ppermute | solution.py:555
  66.4 4.5 %collective-permute-start.24 = (bf16[16,2432]{1,0:T(8,128)(2,1)S(1)}, bf16[16,2432]{1,0:T(8,128)(2,1)S(1)}, u32[]{:S(2)}, u32[]{:S(2)}) collective-permute-start(bf16[16,2432]{1,0:T(8,128)(2,1)S(1)} %get-tuple-element.122), channel_id=1, source_target_pairs={{0,4},{1,5},{2,6},{3,7},{4,0},{5,1},{6,2},{7,3},{8,12},{9,13},{10,... | collective-permute-start | bytes 233480 | tf_op jit(solution)/shard_map/ppermute | solution.py:555
  67.3 7.4 %collective-permute-start.25 = (bf16[16,2432]{1,0:T(8,128)(2,1)S(1)}, bf16[16,2432]{1,0:T(8,128)(2,1)S(1)}, u32[]{:S(2)}, u32[]{:S(2)}) collective-permute-start(bf16[16,2432]{1,0:T(8,128)(2,1)S(1)} %get-tuple-element.123), channel_id=1, source_target_pairs={{0,8},{1,9},{2,10},{3,11},{4,12},{5,13},{6,14},{7,15},{8,0},{9,1},... | collective-permute-start | bytes 233480 | tf_op jit(solution)/shard_map/ppermute | solution.py:555
  69.2 6.3 %collective-permute-start.26 = (bf16[16,2432]{1,0:T(8,128)(2,1)S(1)}, bf16[16,2432]{1,0:T(8,128)(2,1)S(1)}, u32[]{:S(2)}, u32[]{:S(2)}) collective-permute-start(bf16[16,2432]{1,0:T(8,128)(2,1)S(1)} %get-tuple-element.124), channel_id=1, source_target_pairs={{0,12},{1,13},{2,14},{3,15},{4,8},{5,9},{6,10},{7,11},{8,4},{9,5},... | collective-permute-start | bytes 233480 | tf_op jit(solution)/shard_map/ppermute | solution.py:555

commit v6 on v5

--- a/solution.py
+++ b/solution.py
@@ -13,6 +13,7 @@
 CAP = 9
 TAIL = 128
 ROWS = 40
+SPACED = 48
 BF = jnp.bfloat16
 F32 = jnp.float32
 softmax_scale = 192.0 ** (-0.5)
@@ -223,44 +224,54 @@
 
 
 def gate_kernel(tokens, e_ref, *refs):
-    out_ref = refs[-1]
-    info = jnp.concatenate([r[:, r.shape[1] - TAIL :] for r in refs[:-1]], axis=0)
+    w_hbm, out_ref, w_ref, sem = refs[-4:]
+    load = pltpu.make_async_copy(w_hbm, w_ref, sem)
+    load.start()
+    info = jnp.concatenate([r[:, r.shape[1] - TAIL :] for r in refs[:-4]], axis=0)
     one = (iota((tokens, TAIL), 0) == iota((tokens, TAIL), 1)).astype(BF)
     info = dot_t(one, info)
     earlier = (iota((tokens, tokens), 1) < iota((tokens, tokens), 0)).astype(BF)
-    lane = iota((tokens, ROWS), 1).astype(F32)
+    lanes = EXPERTS * SPACED
+    lane = iota((tokens, lanes), 1).astype(F32)
     hits = []
     for k in range(EXPERTS):
         expert = (e_ref[0] ^ k).astype(F32)
         hits.append(jnp.where(info == expert, 1.0, 0.0))
+    blocks = [[0.0] * EXPERTS for _ in range(3)]
     for k in range(EXPERTS):
-        blocks = [[], [], []]
         for s in range(EXPERTS):
             h0 = hits[k][:, 8 * s : 8 * s + 1]
             h1 = hits[k][:, 8 * s + 1 : 8 * s + 2]
-            hit = jnp.broadcast_to(h0 + h1, (tokens, ROWS))
+            hit = jnp.broadcast_to(h0 + h1, (tokens, lanes))
             rank = dot(earlier, hit.astype(BF))
             line = s ^ k
-            want = jnp.where(rank < 8.0, rank + 8.0 * line, 32.0 + line)
+            want = SPACED * k + jnp.where(rank < 8.0, rank + 8.0 * line, 32.0 + line)
             chosen = (lane == want) & (hit > 0.5)
             for p in range(3):
                 g0 = info[:, 8 * s + 2 + p : 8 * s + 3 + p]
                 g1 = info[:, 8 * s + 5 + p : 8 * s + 6 + p]
-                gate = jnp.broadcast_to(h0 * g0 + h1 * g1, (tokens, ROWS))
-                blocks[p].append(jnp.where(chosen, gate, 0.0))
-        out_ref[k] = jnp.concatenate(blocks[0] + blocks[1] + blocks[2], axis=0).astype(BF)
-
-def gate_matrices(place, halves, tokens):
+                gate = jnp.broadcast_to(h0 * g0 + h1 * g1, (tokens, lanes))
+                blocks[p][s] = jnp.where(chosen, gate, blocks[p][s])
+    out_ref[...] = jnp.concatenate(blocks[0] + blocks[1] + blocks[2], axis=0).astype(BF)
+    load.wait()
+
+def gate_matrices(place, halves, weight, tokens):
     vmem = pl.BlockSpec(memory_space=pltpu.VMEM)
     return pl.pallas_call(
         functools.partial(gate_kernel, tokens),
-        out_shape=pltpu.VMEM((EXPERTS, 3 * EXPERTS * tokens, ROWS), BF),
-        in_specs=[pl.BlockSpec(memory_space=pltpu.SMEM)] + [vmem] * len(halves),
-        out_specs=vmem,
+        out_shape=[
+            pltpu.VMEM((3 * EXPERTS * tokens, EXPERTS * SPACED), BF),
+            pltpu.VMEM(weight.shape, weight.dtype),
+        ],
+        in_specs=[pl.BlockSpec(memory_space=pltpu.SMEM)]
+        + [vmem] * len(halves)
+        + [pl.BlockSpec(memory_space=pltpu.HBM)],
+        out_specs=[vmem] * 2,
+        scratch_shapes=[pltpu.SemaphoreType.DMA],
         compiler_params=params(4),
         cost_estimate=LONG,
         name="gates",
-    )(place, *halves)
+    )(place, *halves, pltpu.with_memory_space_constraint(weight, pltpu.HBM))
 
 
 def combine_kernel(spots, tokens, e_ref, *refs):
@@ -270,7 +281,7 @@
     rest = refs[2 * EXPERTS + 2 + len(spots) :]
     own_sum, own_part = rest[:2]
     sent = rest[2 : 1 + EXPERTS]
-    kv_ref, sem = rest[1 + EXPERTS :]
+    kv_ref, rows_ref, sem = rest[1 + EXPERTS :]
     lat = kvs[0].shape[1]
     part = spots[0][1]
     copies = []
@@ -278,10 +289,11 @@
         place = pl.multiple_of((e_ref[1] ^ r) * part + first, 16)
         copies.append(pltpu.make_async_copy(kvs[i], kv_ref.at[pl.ds(place, rows), :], sem.at[i]))
         copies[-1].start()
-    moe = None
+    gap = jnp.zeros((SPACED - ROWS, outs_e[0].shape[1]), F32)
     for k in range(EXPERTS):
-        term = dot(gates_ref[k], outs_e[k][...])
-        moe = term if moe is None else moe + term
+        spaced = jnp.concatenate([outs_e[k][...].astype(F32), gap], axis=0)
+        rows_ref[SPACED * k : SPACED * (k + 1), :] = spaced.astype(BF)
+    moe = dot(gates_ref[...], rows_ref[...])
     total = EXPERTS * tokens
     moe = moe[:total] + moe[total : 2 * total] + moe[2 * total :]
     mixed = jnp.concatenate([h[...].astype(F32) for h in hid], axis=0) + moe
@@ -330,6 +342,7 @@
             out_specs=[whole(o.shape) for o in outs],
             scratch_shapes=[
                 pltpu.VMEM((quarter, lat), BF),
+                pltpu.VMEM((EXPERTS * SPACED, quarter), BF),
                 pltpu.SemaphoreType.DMA((len(kvs),)),
             ],
         ),
@@ -578,16 +591,19 @@
     lower = join(near[0], near[1])
     lowers = spread({0: lower}, [top])
     q_first = after(q_t, lower, allow, turn)
-    *first, w_in, w_out = cached_attention(
-        lengths, q_first, cache_t, [expert_in, expert_down], 0, half
-    )
-    distant, first, kvs = lax.optimization_barrier((near[2:], first, kvs))
+    *first, w_in = cached_attention(lengths, q_first, cache_t, [expert_in], 0, half, per=8)
+    quarters = packed[EXPERTS:]
+    near_quarter = swap(quarters[1], split)
+    distant, first, kvs, near_quarter = lax.optimization_barrier(
+        (near[2:], first, kvs, near_quarter)
+    )
     upper = join(*distant)
     across = {top: swap(upper, top)}
     uppers = spread({0: upper}, low[::-1])
-    own_quarters = to_line(after(packed[EXPERTS:], uppers))
+    sent = after(quarters[2:], uppers)
+    own_quarters = [swap(sent[k - 2], k * split) for k in (3, 2)]
     lowers = spread(lowers, low[::-1])
-    gates = gate_matrices(place, (lower, upper), hidden.shape[0])
+    gates, w_out = gate_matrices(place, (lower, upper), expert_down, hidden.shape[0])
     lowers, uppers, across, own_quarters, gates = lax.optimization_barrier(
         (lowers, uppers, across, own_quarters, gates)
     )
@@ -622,6 +638,7 @@
     )
     outs_e, third = lax.optimization_barrier((outs_e, third))
 
+    own_quarters = [quarters[0], near_quarter, own_quarters[1], own_quarters[0]]
     own_sum, own_part, *rows = combine(place, outs_e, own_quarters, gates, attn_gain[None], kvs)
     rows = [own_sum, own_part] + [swap(r, (k + 1) * split) for k, r in enumerate(rows)]
     return final_attention(

time: 79.8 us -> 78.8 us (0.987)
  waiting for transfers between devices: 17.1 us -> 14.2 us
  starting transfers between devices: 27.4 us -> 29.4 us
    ppermute x27, waiting for transfers between devices: 17.1 us -> 14.2 us  [swap(): return lax.ppermute(x, 'ep', [(i, i ^ bit) for i in range(size)])]
    pallas_call x1, Pallas kernels: 1.05 us -> 3.63 us  [gate_matrices(): pl.pallas_call(functools.partial(gate_kernel, tokens), out_shape=[pltpu.V...]
    pallas_call x3, Pallas kernels: 15.9 us -> 13.8 us  [cached_attention(): pl.pallas_call(functools.partial(cached_kernel, first, per), out_shape=[p...]
    ppermute x27, starting transfers between devices: 27.4 us -> 29.4 us  [swap(): return lax.ppermute(x, 'ep', [(i, i ^ bit) for i in range(size)])]
  transfers between devices with their start and end apart: 27 -> 27, of which waited for: 12 -> 9; matrix products, arithmetic and copies ran while one was open for 3% -> 3% of each run, Pallas kernels for 26% -> 27%
where the time goes in v6:
time: 78.8 us; the launch traced here: 78.6 us
  Pallas kernels  30.9 us (39%)
  starting transfers between devices  29.4 us (37%)
  waiting for transfers between devices  14.2 us (18%)
  between operations  1.72 us (2%)
  matrix products  1.43 us (2%)
    ppermute x27, starting transfers between devices, swap(): return lax.ppermute(x, 'ep', [(i, i ^ bit) for i in range(size)])  29.4 us
    ppermute x27, waiting for transfers between devices, swap(): return lax.ppermute(x, 'ep', [(i, i ^ bit) for i in range(size)])  14.2 us
    pallas_call x3, Pallas kernels, cached_attention(): pl.pallas_call(functools.partial(cached_kernel, first, per), out_shape=[p...  13.8 us
    pallas_call x1, Pallas kernels, expert_slice(): pl.pallas_call(functools.partial(expert_kernel, split), out_shape=[act] +...  4.03 us
    pallas_call x1, Pallas kernels, final_attention(): pl.pallas_call(functools.partial(final_kernel, width, per), out_shape=[ja...  3.89 us
    pallas_call x1, Pallas kernels, gate_matrices(): pl.pallas_call(functools.partial(gate_kernel, tokens), out_shape=[pltpu.V...  3.63 us
    pallas_call x1, Pallas kernels, pack(): pl.pallas_call(pack_kernel, out_shape=[chunk] * EXPERTS + [part] * EXPERT...  2.09 us
    pallas_call x1, Pallas kernels, combine(): pl.pallas_call(functools.partial(combine_kernel, spots, tokens), out_shap...  2.02 us
  transfers between devices with their start and end apart: 27, of which 9 were waited for; matrix products, arithmetic and copies ran while one was open for 3% of the time, Pallas kernels for 27%

profile of v6, /device:TPU:0, one launch (start us, length us, event | category | flops | bytes accessed | tf_op | source)
XLA Modules:
  0.0 78.6 jit_solution(3451505961246139806)
XLA Ops:
  0.6 3.0 %collective-permute-start.6 = (bf16[448,576]{1,0:T(8,128)(2,1)}, bf16[448,576]{1,0:T(8,128)(2,1)S(1)}, u32[]{:S(2)}, u32[]{:S(2)}) collective-permute-start(bf16[448,576]{1,0:T(8,128)(2,1)} %refs_10_), channel_id=1, source_target_pairs={{0,2},{1,3},{2,0},{3,1},{4,6},{5,7},{6,4},{7,5},{8,10},{9,11},{10,... | collective-permute-start | bytes 1548296 | tf_op jit(solution)/shard_map/ppermute | solution.py:568
  3.7 2.1 %pack.1 = (bf16[8,8192]{1,0:T(8,128)(2,1)S(1)}, bf16[8,8192]{1,0:T(8,128)(2,1)S(1)}, bf16[8,8192]{1,0:T(8,128)(2,1)S(1)}, bf16[8,8192]{1,0:T(8,128)(2,1)S(1)}, b...) custom-call(s32[2]{0:T(128)S(1)} %pad_add_fusion.e_ref, ...), custom_call_target="tpu_custom_call" | custom-call | flops 1024 | bytes 1024 | tf_op jit(solution)/shard_map/pack/pallas_call | solution.py:114
  5.8 1.6 %collective-permute-start.7 = (bf16[16,1792]{1,0:T(8,128)(2,1)S(1)}, bf16[16,1792]{1,0:T(8,128)(2,1)S(1)}, u32[]{:S(2)}, u32[]{:S(2)}) collective-permute-start(bf16[16,1792]{1,0:T(8,128)(2,1)S(1)} %get-tuple-element.71), channel_id=1, source_target_pairs={{0,4},{1,5},{2,6},{3,7},{4,0},{5,1},{6,2},{7,3},{8,12},{9,13},{10,... | collective-permute-start | bytes 172040 | tf_op jit(solution)/shard_map/ppermute | solution.py:568
  7.9 2.6 %collective-permute-start.4 = (bf16[8,8192]{1,0:T(8,128)(2,1)S(1)}, bf16[8,8192]{1,0:T(8,128)(2,1)S(1)}, u32[]{:S(2)}, u32[]{:S(2)}) collective-permute-start(bf16[8,8192]{1,0:T(8,128)(2,1)S(1)} %get-tuple-element.66), channel_id=1, source_target_pairs={{0,8},{1,9},{2,10},{3,11},{4,12},{5,13},{6,14},{7,15},{8,0},{9,1},... | collective-permute-start | bytes 393224 | tf_op jit(solution)/shard_map/ppermute | solution.py:568
  10.5 1.3 %collective-permute-start.5 = (bf16[8,8192]{1,0:T(8,128)(2,1)S(1)}, bf16[8,8192]{1,0:T(8,128)(2,1)S(1)}, u32[]{:S(2)}, u32[]{:S(2)}) collective-permute-start(bf16[8,8192]{1,0:T(8,128)(2,1)S(1)} %get-tuple-element.67), channel_id=1, source_target_pairs={{0,12},{1,13},{2,14},{3,15},{4,8},{5,9},{6,10},{7,11},{8,4},{9,5},... | collective-permute-start | bytes 393224 | tf_op jit(solution)/shard_map/ppermute | solution.py:568
  12.5 1.0 %convolution_minimum_fusion.3 = f32[16,16]{0,1:T(8,128)S(1)} fusion(s32[16]{0:T(128)} %bitcast.61), kind=kOutput, calls=%fused_computation.3 | convolution fusion | flops 50688 | bytes 1088 | tf_op jit(solution)/shard_map/dot_general | solution.py:523
  14.3 1.1 %collective-permute-done.b_ref = bf16[8,8192]{1,0:T(8,128)(2,1)S(1)} collective-permute-done((bf16[8,8192]{1,0:T(8,128)(2,1)S(1)}, bf16[8,8192]{1,0:T(8,128)(2,1)S(1)}, u32[]{:S(2)}, u32[]{:S(2)}) %collective-permute-start) | collective-permute-done | bytes 131104 | tf_op jit(solution)/shard_map/ppermute | solution.py:568
  15.9 5.9 %cached.3 = (bf16[8,128,512]{2,1,0:T(8,128)(2,1)S(1)}, f32[8,2,128]{2,1,0:T(2,128)S(1)}, bf16[1,7168,1024]{2,1,0:T(8,128)(2,1)S(1)}) custom-call(s32[1]{0:T(128)S(6)} %copy.17.length_ref, bf16[16,576,128]{2,1,0:T(8,128)(2,1)} %bitcast.49, bf16[1,576,1024]{2,1,0:T(8,128)(2,1)} %bitcast.55, bf16[1,7168,1024]{2,1,0:T(8,128)(2,1)} %refs_2_.2), custom_call_target="tpu_custom_call" | custom-call | flops 4563402752 | bytes 2359296 | tf_op jit(solution)/shard_map/cached/pallas_call | solution.py:403
  22.0 0.5 collective-permute-start.1
  22.9 1.4 %collective-permute-start.9 = (bf16[16,8192]{1,0:T(8,128)(2,1)S(1)}, bf16[16,8192]{1,0:T(8,128)(2,1)S(1)}, u32[]{:S(2)}, u32[]{:S(2)}) collective-permute-start(bf16[16,8192]{1,0:T(8,128)(2,1)S(1)} %join.3.refs_1_), channel_id=1, source_target_pairs={{0,2},{1,3},{2,0},{3,1},{4,6},{5,7},{6,4},{7,5},{8,10},{9,11},{10,... | collective-permute-start | bytes 786440 | tf_op jit(solution)/shard_map/ppermute | solution.py:568
  24.3 3.5 %collective-permute-start.10 = (bf16[16,1792]{1,0:T(8,128)(2,1)S(1)}, bf16[16,1792]{1,0:T(8,128)(2,1)S(1)}, u32[]{:S(2)}, u32[]{:S(2)}) collective-permute-start(bf16[16,1792]{1,0:T(8,128)(2,1)S(1)} %get-tuple-element.76), channel_id=1, source_target_pairs={{0,12},{1,13},{2,14},{3,15},{4,8},{5,9},{6,10},{7,11},{8,4},{9,5},... | collective-permute-start | bytes 172040 | tf_op jit(solution)/shard_map/ppermute | solution.py:568
  27.8 3.6 %gates.1 = (bf16[192,192]{1,0:T(8,128)(2,1)S(1)}, bf16[1,512,7168]{2,1,0:T(8,128)(2,1)S(1)}) custom-call(s32[2]{0:T(128)S(1)} %pad_add_fusion.e_ref, bf16[16,8192]{1,0:T(8,128)(2,1)S(1)} %join.2.refs_0_, bf16[16,8192]{1,0:T(8,128)(2,1)S(1)} %join.3.refs_1_, bf16[1,512,7168]{2,1,0:T(8,128)(2,1)} %refs_2_.3), custom_call_target="tpu_custom_call" | custom-call | flops 17179869184 | bytes 16777216 | tf_op jit(solution)/shard_map/gates/pallas_call | solution.py:260
  31.6 1.5 %collective-permute-done.11.refs_6_ = bf16[16,1792]{1,0:T(8,128)(2,1)S(1)} collective-permute-done((bf16[16,1792]{1,0:T(8,128)(2,1)S(1)}, bf16[16,1792]{1,0:T(8,128)(2,1)S(1)}, u32[]{:S(2)}, u32[]{:S(2)}) %collective-permute-start.11) | collective-permute-done | bytes 57376 | tf_op jit(solution)/shard_map/ppermute | solution.py:568
  33.1 1.5 %collective-permute-done.12.refs_7_ = bf16[16,8192]{1,0:T(8,128)(2,1)S(1)} collective-permute-done((bf16[16,8192]{1,0:T(8,128)(2,1)S(1)}, bf16[16,8192]{1,0:T(8,128)(2,1)S(1)}, u32[]{:S(2)}, u32[]{:S(2)}) %collective-permute-start.12) | collective-permute-done | bytes 262176 | tf_op jit(solution)/shard_map/ppermute | solution.py:568
  34.6 4.0 %experts.1 = (bf16[160,512]{1,0:T(8,128)(2,1)S(1)}, bf16[2,1,40,1792]{3,2,1,0:T(8,128)(2,1)S(1)}, bf16[2,1,40,1792]{3,2,1,0:T(8,128)(2,1)S(1)}, bf16[2,1,40,1792...) custom-call(s32[2]{0:T(128)S(1)} %pad_add_fusion.e_ref, bf16[16,8192]{1,0:T(8,128)(2,1)S(1)} %join.2.refs_0_, ...), custom_call_target="tpu_custom_call" | custom-call | flops 1024 | bytes 1024 | tf_op jit(solution)/shard_map/experts/pallas_call | solution.py:185
  38.9 1.4 %experts_rest.1 = (bf16[2,2,40,1792]{3,2,1,0:T(8,128)(2,1)S(1)}, bf16[2,2,40,1792]{3,2,1,0:T(8,128)(2,1)S(1)}) custom-call(s32[2]{0:T(128)S(1)} %pad_add_fusion.e_ref, bf16[160,512]{1,0:T(8,128)(2,1)S(1)} %get-tuple-element.88.act, bf16[1,512,7168]{2,1,0:T(8,128)(2,1)S(1)} %get-tuple-element.87.refs_9_.w_out), custom_call_target="tpu_custom_call" | custom-call | flops 1024 | bytes 1024 | tf_op jit(solution)/shard_map/experts_rest/pallas_call | solution.py:195
  41.5 0.7 collective-permute-start.16
  42.2 1.5 %collective-permute-start.20 = (bf16[1,40,1792]{2,1,0:T(8,128)(2,1)S(1)}, bf16[1,40,1792]{2,1,0:T(8,128)(2,1)S(1)}, u32[]{:S(2)}, u32[]{:S(2)}) collective-permute-start(bf16[1,40,1792]{2,1,0:T(8,128)(2,1)S(1)} %fusion.6), channel_id=1, source_target_pairs={{0,2},{1,3},{2,0},{3,1},{4,6},{5,7},{6,4},{7,5},{8,10},{9,11},{10,... | collective-permute-start | bytes 430088 | tf_op jit(solution)/shard_map/ppermute | solution.py:568
  43.7 4.4 %collective-permute-done.16 = bf16[1,40,1792]{2,1,0:T(8,128)(2,1)S(1)} collective-permute-done((bf16[1,40,1792]{2,1,0:T(8,128)(2,1)S(1)}, bf16[1,40,1792]{2,1,0:T(8,128)(2,1)S(1)}, u32[]{:S(2)}, u32[]{:S(2)}) %collective-permute-start.16) | collective-permute-done | bytes 143392 | tf_op jit(solution)/shard_map/ppermute | solution.py:568
  48.2 1.5 %collective-permute-start.18 = (bf16[40,1792]{1,0:T(8,128)(2,1)S(1)}, bf16[40,1792]{1,0:T(8,128)(2,1)S(1)}, u32[]{:S(2)}, u32[]{:S(2)}) collective-permute-start(bf16[40,1792]{1,0:T(8,128)(2,1)S(1)} %fusion.4), channel_id=1, source_target_pairs={{0,8},{1,9},{2,10},{3,11},{4,12},{5,13},{6,14},{7,15},{8,0},{9,1},... | collective-permute-start | bytes 430088 | tf_op jit(solution)/shard_map/ppermute | solution.py:568
  49.7 1.1 %collective-permute-start.14 = (bf16[2,40,1792]{2,1,0:T(8,128)(2,1)S(1)}, bf16[2,40,1792]{2,1,0:T(8,128)(2,1)S(1)}, u32[]{:S(2)}, u32[]{:S(2)}) collective-permute-start(bf16[2,40,1792]{2,1,0:T(8,128)(2,1)S(1)} %fusion), channel_id=1, source_target_pairs={{0,2},{1,3},{2,0},{3,1},{4,6},{5,7},{6,4},{7,5},{8,10},{9,11},{10,... | collective-permute-start | bytes 860168 | tf_op jit(solution)/shard_map/ppermute | solution.py:568
  50.9 2.9 %collective-permute-start.21 = (bf16[40,1792]{1,0:T(8,128)(2,1)S(1)}, bf16[40,1792]{1,0:T(8,128)(2,1)S(1)}, u32[]{:S(2)}, u32[]{:S(2)}) collective-permute-start(bf16[40,1792]{1,0:T(8,128)(2,1)S(1)} %fusion.1), channel_id=1, source_target_pairs={{0,12},{1,13},{2,14},{3,15},{4,8},{5,9},{6,10},{7,11},{8,4},{9,5},... | collective-permute-start | bytes 430088 | tf_op jit(solution)/shard_map/ppermute | solution.py:568
  53.8 4.0 %cached.4 = (bf16[4,128,512]{2,1,0:T(8,128)(2,1)S(1)}, f32[4,2,128]{2,1,0:T(2,128)S(1)}) custom-call(s32[1]{0:T(128)S(6)} %copy.17.length_ref, bf16[16,576,128]{2,1,0:T(8,128)(2,1)} %bitcast.50, bf16[1,576,1024]{2,1,0:T(8,128)(2,1)} %bitcast.56), custom_call_target="tpu_custom_call" | custom-call | flops 17179869184 | bytes 16777216 | tf_op jit(solution)/shard_map/cached/pallas_call | solution.py:403
  57.9 1.1 %collective-permute-start.17 = (bf16[40,1792]{1,0:T(8,128)(2,1)S(1)}, bf16[40,1792]{1,0:T(8,128)(2,1)S(1)}, u32[]{:S(2)}, u32[]{:S(2)}) collective-permute-start(bf16[40,1792]{1,0:T(8,128)(2,1)S(1)} %get-tuple-element.125), channel_id=1, source_target_pairs={{0,4},{1,5},{2,6},{3,7},{4,0},{5,1},{6,2},{7,3},{8,12},{9,13},{10,... | collective-permute-start | bytes 430088 | tf_op jit(solution)/shard_map/ppermute | solution.py:568
  59.0 3.8 %cached.5 = (bf16[4,128,512]{2,1,0:T(8,128)(2,1)S(1)}, f32[4,2,128]{2,1,0:T(2,128)S(1)}) custom-call(s32[1]{0:T(128)S(6)} %copy.17.length_ref, bf16[16,576,128]{2,1,0:T(8,128)(2,1)} %bitcast.51, bf16[1,576,1024]{2,1,0:T(8,128)(2,1)} %bitcast.57), custom_call_target="tpu_custom_call" | custom-call | flops 2281701376 | bytes 1179648 | tf_op jit(solution)/shard_map/cached/pallas_call | solution.py:403
  63.1 2.0 %combine.1 = (f32[16,640]{1,0:T(8,128)S(1)}, bf16[16,1792]{1,0:T(8,128)(2,1)S(1)}, bf16[16,2432]{1,0:T(8,128)(2,1)S(1)}, bf16[16,2432]{1,0:T(8,128)(2,1)S(1)}, bf16[16,2432]{1,0:T(8,128)(2,1)S(1)}) custom-call(s32[2]{0:T(128)S(1)} %pad_add_fusion.e_ref, bf16[40,1792]{1,0:T(8,128)(2,1)S(1)} %get-tuple-element.103.refs_0_, ...), custom_call_target="tpu_custom_call" | custom-call | flops 1024 | bytes 1024 | tf_op jit(solution)/shard_map/combine/pallas_call | solution.py:329
  65.1 1.1 %collective-permute-start.24 = (bf16[16,2432]{1,0:T(8,128)(2,1)S(1)}, bf16[16,2432]{1,0:T(8,128)(2,1)S(1)}, u32[]{:S(2)}, u32[]{:S(2)}) collective-permute-start(bf16[16,2432]{1,0:T(8,128)(2,1)S(1)} %get-tuple-element.118), channel_id=1, source_target_pairs={{0,4},{1,5},{2,6},{3,7},{4,0},{5,1},{6,2},{7,3},{8,12},{9,13},{10,... | collective-permute-start | bytes 233480 | tf_op jit(solution)/shard_map/ppermute | solution.py:568
  66.2 1.7 %collective-permute-start.25 = (bf16[16,2432]{1,0:T(8,128)(2,1)S(1)}, bf16[16,2432]{1,0:T(8,128)(2,1)S(1)}, u32[]{:S(2)}, u32[]{:S(2)}) collective-permute-start(bf16[16,2432]{1,0:T(8,128)(2,1)S(1)} %get-tuple-element.119), channel_id=1, source_target_pairs={{0,8},{1,9},{2,10},{3,11},{4,12},{5,13},{6,14},{7,15},{8,0},{9,1},... | collective-permute-start | bytes 233480 | tf_op jit(solution)/shard_map/ppermute | solution.py:568
  68.0 1.6 %collective-permute-start.26 = (bf16[16,2432]{1,0:T(8,128)(2,1)S(1)}, bf16[16,2432]{1,0:T(8,128)(2,1)S(1)}, u32[]{:S(2)}, u32[]{:S(2)}) collective-permute-start(bf16[16,2432]{1,0:T(8,128)(2,1)S(1)} %get-tuple-element.120), channel_id=1, source_target_pairs={{0,12},{1,13},{2,14},{3,15},{4,8},{5,9},{6,10},{7,11},{8,4},{9,5},... | collective-permute-start | bytes 233480 | tf_op jit(solution)/shard_map/ppermute | solution.py:568
  69.6 0.5 collective-permute-done.24.refs_2_
  70.1 4.4 %collective-permute-done.25.refs_3_ = bf16[16,2432]{1,0:T(8,128)(2,1)S(1)} collective-permute-done((bf16[16,2432]{1,0:T(8,128)(2,1)S(1)}, bf16[16,2432]{1,0:T(8,128)(2,1)S(1)}, u32[]{:S(2)}, u32[]{:S(2)}) %collective-permute-start.25) | collective-permute-done | bytes 77856 | tf_op jit(solution)/shard_map/ppermute | solution.py:568
  74.5 3.9 %final.1 = (bf16[16,7168]{1,0:T(8,128)(2,1)}, bf16[16,576]{1,0:T(8,128)(2,1)}, bf16[16,128,512]{2,1,0:T(8,128)(2,1)}) custom-call(s32[2]{0:T(128)S(1)} %pad_add_fusion.e_ref, f32[16,640]{1,0:T(8,128)S(1)} %get-tuple-element.116.refs_0_, bf16[16,1792]{1,0:T(8,128)(2,1)S(1)} %get-tuple-element.117.refs_1_, ...), custom_call_target="tpu_custom_call" | custom-call | flops 1024 | bytes 1024 | tf_op jit(solution)/shard_map/final/pallas_call | solution.py:499
  (62 shorter events, 4.3 us)
Async XLA Ops:
  0.6 21.3 %collective-permute-start.6 = (bf16[448,576]{1,0:T(8,128)(2,1)}, bf16[448,576]{1,0:T(8,128)(2,1)S(1)}, u32[]{:S(2)}, u32[]{:S(2)}) collective-permute-start(bf16[448,576]{1,0:T(8,128)(2,1)} %refs_10_), channel_id=1, source_target_pairs={{0,2},{1,3},{2,0},{3,1},{4,6},{5,7},{6,4},{7,5},{8,10},{9,11},{10,... | collective-permute-start | bytes 1548296 | tf_op jit(solution)/shard_map/ppermute | solution.py:568
  5.8 16.1 %collective-permute-start.7 = (bf16[16,1792]{1,0:T(8,128)(2,1)S(1)}, bf16[16,1792]{1,0:T(8,128)(2,1)S(1)}, u32[]{:S(2)}, u32[]{:S(2)}) collective-permute-start(bf16[16,1792]{1,0:T(8,128)(2,1)S(1)} %get-tuple-element.71), channel_id=1, source_target_pairs={{0,4},{1,5},{2,6},{3,7},{4,0},{5,1},{6,2},{7,3},{8,12},{9,13},{10,... | collective-permute-start | bytes 172040 | tf_op jit(solution)/shard_map/ppermute | solution.py:568
  7.5 8.0 %collective-permute-start = (bf16[8,8192]{1,0:T(8,128)(2,1)S(1)}, bf16[8,8192]{1,0:T(8,128)(2,1)S(1)}, u32[]{:S(2)}, u32[]{:S(2)}) collective-permute-start(bf16[8,8192]{1,0:T(8,128)(2,1)S(1)} %get-tuple-element.65), channel_id=1, source_target_pairs={{0,4},{1,5},{2,6},{3,7},{4,0},{5,1},{6,2},{7,3},{8,12},{9,13},{10,... | collective-permute-start | bytes 393224 | tf_op jit(solution)/shard_map/ppermute | solution.py:568
  7.9 14.0 %collective-permute-start.4 = (bf16[8,8192]{1,0:T(8,128)(2,1)S(1)}, bf16[8,8192]{1,0:T(8,128)(2,1)S(1)}, u32[]{:S(2)}, u32[]{:S(2)}) collective-permute-start(bf16[8,8192]{1,0:T(8,128)(2,1)S(1)} %get-tuple-element.66), channel_id=1, source_target_pairs={{0,8},{1,9},{2,10},{3,11},{4,12},{5,13},{6,14},{7,15},{8,0},{9,1},... | collective-permute-start | bytes 393224 | tf_op jit(solution)/shard_map/ppermute | solution.py:568
  10.5 11.4 %collective-permute-start.5 = (bf16[8,8192]{1,0:T(8,128)(2,1)S(1)}, bf16[8,8192]{1,0:T(8,128)(2,1)S(1)}, u32[]{:S(2)}, u32[]{:S(2)}) collective-permute-start(bf16[8,8192]{1,0:T(8,128)(2,1)S(1)} %get-tuple-element.67), channel_id=1, source_target_pairs={{0,12},{1,13},{2,14},{3,15},{4,8},{5,9},{6,10},{7,11},{8,4},{9,5},... | collective-permute-start | bytes 393224 | tf_op jit(solution)/shard_map/ppermute | solution.py:568
  15.5 7.4 %collective-permute-start.2 = (bf16[16,8192]{1,0:T(8,128)(2,1)S(1)}, bf16[16,8192]{1,0:T(8,128)(2,1)S(1)}, u32[]{:S(2)}, u32[]{:S(2)}) collective-permute-start(bf16[16,8192]{1,0:T(8,128)(2,1)S(1)} %join.2.refs_0_), channel_id=1, source_target_pairs={{0,2},{1,3},{2,0},{3,1},{4,6},{5,7},{6,4},{7,5},{8,10},{9,11},{10,... | collective-permute-start | bytes 786440 | tf_op jit(solution)/shard_map/ppermute | solution.py:568
  22.0 2.4 %collective-permute-start.8 = (bf16[16,8192]{1,0:T(8,128)(2,1)S(1)}, bf16[16,8192]{1,0:T(8,128)(2,1)S(1)}, u32[]{:S(2)}, u32[]{:S(2)}) collective-permute-start(bf16[16,8192]{1,0:T(8,128)(2,1)S(1)} %join.3.refs_1_), channel_id=1, source_target_pairs={{0,1},{1,0},{2,3},{3,2},{4,5},{5,4},{6,7},{7,6},{8,9},{9,8},{10,11... | collective-permute-start | bytes 786440 | tf_op jit(solution)/shard_map/ppermute | solution.py:568
  22.0 9.4 %collective-permute-start.1 = (bf16[16,8192]{1,0:T(8,128)(2,1)S(1)}, bf16[16,8192]{1,0:T(8,128)(2,1)S(1)}, u32[]{:S(2)}, u32[]{:S(2)}) collective-permute-start(bf16[16,8192]{1,0:T(8,128)(2,1)S(1)} %join.2.refs_0_), channel_id=1, source_target_pairs={{0,1},{1,0},{2,3},{3,2},{4,5},{5,4},{6,7},{7,6},{8,9},{9,8},{10,11... | collective-permute-start | bytes 786440 | tf_op jit(solution)/shard_map/ppermute | solution.py:568
  22.9 8.6 %collective-permute-start.3 = (bf16[16,8192]{1,0:T(8,128)(2,1)S(1)}, bf16[16,8192]{1,0:T(8,128)(2,1)S(1)}, u32[]{:S(2)}, u32[]{:S(2)}) collective-permute-start(bf16[16,8192]{1,0:T(8,128)(2,1)S(1)} %collective-permute-done.2.refs_4_), channel_id=1, source_target_pairs={{0,1},{1,0},{2,3},{3,2},{4,5},{5,4},{6,7},{7,6},{8,9},{9,8},{10,11... | collective-permute-start | bytes 786440 | tf_op jit(solution)/shard_map/ppermute | solution.py:568
  22.9 8.7 %collective-permute-start.9 = (bf16[16,8192]{1,0:T(8,128)(2,1)S(1)}, bf16[16,8192]{1,0:T(8,128)(2,1)S(1)}, u32[]{:S(2)}, u32[]{:S(2)}) collective-permute-start(bf16[16,8192]{1,0:T(8,128)(2,1)S(1)} %join.3.refs_1_), channel_id=1, source_target_pairs={{0,2},{1,3},{2,0},{3,1},{4,6},{5,7},{6,4},{7,5},{8,10},{9,11},{10,... | collective-permute-start | bytes 786440 | tf_op jit(solution)/shard_map/ppermute | solution.py:568
  24.3 7.3 %collective-permute-start.10 = (bf16[16,1792]{1,0:T(8,128)(2,1)S(1)}, bf16[16,1792]{1,0:T(8,128)(2,1)S(1)}, u32[]{:S(2)}, u32[]{:S(2)}) collective-permute-start(bf16[16,1792]{1,0:T(8,128)(2,1)S(1)} %get-tuple-element.76), channel_id=1, source_target_pairs={{0,12},{1,13},{2,14},{3,15},{4,8},{5,9},{6,10},{7,11},{8,4},{9,5},... | collective-permute-start | bytes 172040 | tf_op jit(solution)/shard_map/ppermute | solution.py:568
  27.8 5.3 %collective-permute-start.11 = (bf16[16,1792]{1,0:T(8,128)(2,1)S(1)}, bf16[16,1792]{1,0:T(8,128)(2,1)S(1)}, u32[]{:S(2)}, u32[]{:S(2)}) collective-permute-start(bf16[16,1792]{1,0:T(8,128)(2,1)S(1)} %get-tuple-element.77), channel_id=1, source_target_pairs={{0,8},{1,9},{2,10},{3,11},{4,12},{5,13},{6,14},{7,15},{8,0},{9,1},... | collective-permute-start | bytes 172040 | tf_op jit(solution)/shard_map/ppermute | solution.py:568
  33.1 1.5 %collective-permute-start.12 = (bf16[16,8192]{1,0:T(8,128)(2,1)S(1)}, bf16[16,8192]{1,0:T(8,128)(2,1)S(1)}, u32[]{:S(2)}, u32[]{:S(2)}) collective-permute-start(bf16[16,8192]{1,0:T(8,128)(2,1)S(1)} %collective-permute-done.9.refs_5_), channel_id=1, source_target_pairs={{0,1},{1,0},{2,3},{3,2},{4,5},{5,4},{6,7},{7,6},{8,9},{9,8},{10,11... | collective-permute-start | bytes 786440 | tf_op jit(solution)/shard_map/ppermute | solution.py:568
  38.7 2.1 %copy-start.1 = (bf16[448,576]{1,0:T(8,128)(2,1)S(1)}, bf16[448,576]{1,0:T(8,128)(2,1)}, u32[]{:S(2)}) copy-start(bf16[448,576]{1,0:T(8,128)(2,1)} %refs_10_) | copy-start | bytes 1548292
  38.7 2.7 %collective-permute-start.15 = (bf16[2,1,40,1792]{3,2,1,0:T(8,128)(2,1)S(1)}, bf16[2,1,40,1792]{3,2,1,0:T(8,128)(2,1)S(1)}, u32[]{:S(2)}, u32[]{:S(2)}) collective-permute-start(bf16[2,1,40,1792]{3,2,1,0:T(8,128)(2,1)S(1)} %get-tuple-element.92), channel_id=1, source_target_pairs={{0,1},{1,0},{2,3},{3,2},{4,5},{5,4},{6,7},{7,6},{8,9},{9,8},{10,11... | collective-permute-start | bytes 860168 | tf_op jit(solution)/shard_map/ppermute | solution.py:568
  40.3 1.8 %collective-permute-start.19 = (bf16[2,1,40,1792]{3,2,1,0:T(8,128)(2,1)S(1)}, bf16[2,1,40,1792]{3,2,1,0:T(8,128)(2,1)S(1)}, u32[]{:S(2)}, u32[]{:S(2)}) collective-permute-start(bf16[2,1,40,1792]{3,2,1,0:T(8,128)(2,1)S(1)} %get-tuple-element.98), channel_id=1, source_target_pairs={{0,1},{1,0},{2,3},{3,2},{4,5},{5,4},{6,7},{7,6},{8,9},{9,8},{10,11... | collective-permute-start | bytes 860168 | tf_op jit(solution)/shard_map/ppermute | solution.py:568
  40.8 22.3 %collective-permute-start.22 = (bf16[448,576]{1,0:T(8,128)(2,1)S(1)}, bf16[448,576]{1,0:T(8,128)(2,1)S(1)}, u32[]{:S(2)}, u32[]{:S(2)}) collective-permute-start(bf16[448,576]{1,0:T(8,128)(2,1)S(1)} %copy-done.1), channel_id=1, source_target_pairs={{0,1},{1,0},{2,3},{3,2},{4,5},{5,4},{6,7},{7,6},{8,9},{9,8},{10,11... | collective-permute-start | bytes 1548296 | tf_op jit(solution)/shard_map/ppermute | solution.py:568
  40.9 22.2 %collective-permute-start.23 = (bf16[448,576]{1,0:T(8,128)(2,1)S(1)}, bf16[448,576]{1,0:T(8,128)(2,1)S(1)}, u32[]{:S(2)}, u32[]{:S(2)}) collective-permute-start(bf16[448,576]{1,0:T(8,128)(2,1)S(1)} %collective-permute-done.6.refs_11_), channel_id=1, source_target_pairs={{0,1},{1,0},{2,3},{3,2},{4,5},{5,4},{6,7},{7,6},{8,9},{9,8},{10,11... | collective-permute-start | bytes 1548296 | tf_op jit(solution)/shard_map/ppermute | solution.py:568
  41.3 8.4 %collective-permute-start.13 = (bf16[2,2,40,1792]{3,2,1,0:T(8,128)(2,1)S(1)}, bf16[2,2,40,1792]{3,2,1,0:T(8,128)(2,1)S(1)}, u32[]{:S(2)}, u32[]{:S(2)}) collective-permute-start(bf16[2,2,40,1792]{3,2,1,0:T(8,128)(2,1)S(1)} %get-tuple-element.90), channel_id=1, source_target_pairs={{0,1},{1,0},{2,3},{3,2},{4,5},{5,4},{6,7},{7,6},{8,9},{9,8},{10,11... | collective-permute-start | bytes 1720328 | tf_op jit(solution)/shard_map/ppermute | solution.py:568
  41.5 6.7 %collective-permute-start.16 = (bf16[1,40,1792]{2,1,0:T(8,128)(2,1)S(1)}, bf16[1,40,1792]{2,1,0:T(8,128)(2,1)S(1)}, u32[]{:S(2)}, u32[]{:S(2)}) collective-permute-start(bf16[1,40,1792]{2,1,0:T(8,128)(2,1)S(1)} %fusion.5), channel_id=1, source_target_pairs={{0,2},{1,3},{2,0},{3,1},{4,6},{5,7},{6,4},{7,5},{8,10},{9,11},{10,... | collective-permute-start | bytes 430088 | tf_op jit(solution)/shard_map/ppermute | solution.py:568
  42.2 8.6 %collective-permute-start.20 = (bf16[1,40,1792]{2,1,0:T(8,128)(2,1)S(1)}, bf16[1,40,1792]{2,1,0:T(8,128)(2,1)S(1)}, u32[]{:S(2)}, u32[]{:S(2)}) collective-permute-start(bf16[1,40,1792]{2,1,0:T(8,128)(2,1)S(1)} %fusion.6), channel_id=1, source_target_pairs={{0,2},{1,3},{2,0},{3,1},{4,6},{5,7},{6,4},{7,5},{8,10},{9,11},{10,... | collective-permute-start | bytes 430088 | tf_op jit(solution)/shard_map/ppermute | solution.py:568
  48.2 14.7 %collective-permute-start.18 = (bf16[40,1792]{1,0:T(8,128)(2,1)S(1)}, bf16[40,1792]{1,0:T(8,128)(2,1)S(1)}, u32[]{:S(2)}, u32[]{:S(2)}) collective-permute-start(bf16[40,1792]{1,0:T(8,128)(2,1)S(1)} %fusion.4), channel_id=1, source_target_pairs={{0,8},{1,9},{2,10},{3,11},{4,12},{5,13},{6,14},{7,15},{8,0},{9,1},... | collective-permute-start | bytes 430088 | tf_op jit(solution)/shard_map/ppermute | solution.py:568
  49.7 8.1 %collective-permute-start.14 = (bf16[2,40,1792]{2,1,0:T(8,128)(2,1)S(1)}, bf16[2,40,1792]{2,1,0:T(8,128)(2,1)S(1)}, u32[]{:S(2)}, u32[]{:S(2)}) collective-permute-start(bf16[2,40,1792]{2,1,0:T(8,128)(2,1)S(1)} %fusion), channel_id=1, source_target_pairs={{0,2},{1,3},{2,0},{3,1},{4,6},{5,7},{6,4},{7,5},{8,10},{9,11},{10,... | collective-permute-start | bytes 860168 | tf_op jit(solution)/shard_map/ppermute | solution.py:568
  50.9 12.0 %collective-permute-start.21 = (bf16[40,1792]{1,0:T(8,128)(2,1)S(1)}, bf16[40,1792]{1,0:T(8,128)(2,1)S(1)}, u32[]{:S(2)}, u32[]{:S(2)}) collective-permute-start(bf16[40,1792]{1,0:T(8,128)(2,1)S(1)} %fusion.1), channel_id=1, source_target_pairs={{0,12},{1,13},{2,14},{3,15},{4,8},{5,9},{6,10},{7,11},{8,4},{9,5},... | collective-permute-start | bytes 430088 | tf_op jit(solution)/shard_map/ppermute | solution.py:568
  57.8 5.3 %copy-start.2 = (f32[7168]{0:T(1024)S(1)}, f32[7168]{0:T(1024)}, u32[]{:S(2)}) copy-start(f32[7168]{0:T(1024)} %param.15) | copy-start | bytes 86020
  57.8 16.7 %copy-start = (bf16[16,128,576]{1,2,0:T(8,128)(2,1)S(1)}, bf16[16,128,576]{1,2,0:T(8,128)(2,1)}, u32[]{:S(2)}) copy-start(bf16[16,128,576]{1,2,0:T(8,128)(2,1)} %param.24) | copy-start | bytes 7077892
  57.8 16.7 %copy-start.3 = (f32[512]{0:T(512)S(1)}, f32[512]{0:T(512)}, u32[]{:S(2)}) copy-start(f32[512]{0:T(512)} %param.16) | copy-start | bytes 6148
  57.9 5.2 %collective-permute-start.17 = (bf16[40,1792]{1,0:T(8,128)(2,1)S(1)}, bf16[40,1792]{1,0:T(8,128)(2,1)S(1)}, u32[]{:S(2)}, u32[]{:S(2)}) collective-permute-start(bf16[40,1792]{1,0:T(8,128)(2,1)S(1)} %get-tuple-element.125), channel_id=1, source_target_pairs={{0,4},{1,5},{2,6},{3,7},{4,0},{5,1},{6,2},{7,3},{8,12},{9,13},{10,... | collective-permute-start | bytes 430088 | tf_op jit(solution)/shard_map/ppermute | solution.py:568
  65.1 5.0 %collective-permute-start.24 = (bf16[16,2432]{1,0:T(8,128)(2,1)S(1)}, bf16[16,2432]{1,0:T(8,128)(2,1)S(1)}, u32[]{:S(2)}, u32[]{:S(2)}) collective-permute-start(bf16[16,2432]{1,0:T(8,128)(2,1)S(1)} %get-tuple-element.118), channel_id=1, source_target_pairs={{0,4},{1,5},{2,6},{3,7},{4,0},{5,1},{6,2},{7,3},{8,12},{9,13},{10,... | collective-permute-start | bytes 233480 | tf_op jit(solution)/shard_map/ppermute | solution.py:568
  66.2 8.3 %collective-permute-start.25 = (bf16[16,2432]{1,0:T(8,128)(2,1)S(1)}, bf16[16,2432]{1,0:T(8,128)(2,1)S(1)}, u32[]{:S(2)}, u32[]{:S(2)}) collective-permute-start(bf16[16,2432]{1,0:T(8,128)(2,1)S(1)} %get-tuple-element.119), channel_id=1, source_target_pairs={{0,8},{1,9},{2,10},{3,11},{4,12},{5,13},{6,14},{7,15},{8,0},{9,1},... | collective-permute-start | bytes 233480 | tf_op jit(solution)/shard_map/ppermute | solution.py:568
  68.0 6.5 %collective-permute-start.26 = (bf16[16,2432]{1,0:T(8,128)(2,1)S(1)}, bf16[16,2432]{1,0:T(8,128)(2,1)S(1)}, u32[]{:S(2)}, u32[]{:S(2)}) collective-permute-start(bf16[16,2432]{1,0:T(8,128)(2,1)S(1)} %get-tuple-element.120), channel_id=1, source_target_pairs={{0,12},{1,13},{2,14},{3,15},{4,8},{5,9},{6,10},{7,11},{8,4},{9,5},... | collective-permute-start | bytes 233480 | tf_op jit(solution)/shard_map/ppermute | solution.py:568

commit v7 on v6

--- a/solution.py
+++ b/solution.py
@@ -164,11 +164,11 @@
         up = dot(x[...], w_in[0, :, hid + i * step : hid + (i + 1) * step])
         act[:, i * step : (i + 1) * step] = (gate / (1.0 + jnp.exp(-gate)) * up).astype(BF)
     down(split, e_ref, act, w_out, pieces[0], pieces[1], 3)
-    down(split, e_ref, act, w_out, pieces[2], pieces[3], 2)
-
-
-def expert_rest_kernel(split, e_ref, act, w_out, keep, send):
-    down(split, e_ref, act, w_out, keep, send, 0)
+
+
+def expert_rest_kernel(split, e_ref, act, w_out, *pieces):
+    down(split, e_ref, act, w_out, pieces[0], pieces[1], 2)
+    down(split, e_ref, act, w_out, pieces[2], pieces[3], 0)
 
 
 def expert_slice(e, groups, w_in, w_out):
@@ -182,11 +182,12 @@
     act = jax.ShapeDtypeStruct((rows, hid), BF)
     vmem = pl.BlockSpec(memory_space=pltpu.VMEM)
     smem = pl.BlockSpec(memory_space=pltpu.SMEM)
+    single_shape = single
     act, *single = pl.pallas_call(
         functools.partial(expert_kernel, split),
-        out_shape=[act] + [single] * 4,
+        out_shape=[act] + [single] * 2,
         in_specs=[smem] + [vmem] * (2 * split + 2),
-        out_specs=[vmem] * 5,
+        out_specs=[vmem] * 3,
         scratch_shapes=[pltpu.VMEM((rows, width), BF)],
         compiler_params=params(10),
         cost_estimate=COST,
@@ -194,14 +195,14 @@
     )(e, *groups, w_in, w_out)
     rest = pl.pallas_call(
         functools.partial(expert_rest_kernel, split),
-        out_shape=[half, half],
+        out_shape=[single_shape, single_shape, half, half],
         in_specs=[smem] + [vmem] * 2,
-        out_specs=[vmem] * 2,
+        out_specs=[vmem] * 4,
         compiler_params=params(6),
         cost_estimate=COST,
         name="experts_rest",
     )(e, act, w_out)
-    return single[:2], single[2:], rest
+    return single, rest[:2], rest[2:]
 
 
 def join_kernel(a_ref, b_ref, out_ref):

time: 78.8 us -> 78.5 us (level)
  transfers between devices with their start and end apart: 27 -> 27, of which waited for: 9 -> 11; matrix products, arithmetic and copies ran while one was open for 3% -> 3% of each run, Pallas kernels for 27% -> 25%
where the time goes in v7:
time: 78.5 us; the launch traced here: 78.2 us
  Pallas kernels  30.9 us (39%)
  starting transfers between devices  28.8 us (37%)
  waiting for transfers between devices  14.5 us (18%)
  between operations  1.72 us (2%)
  matrix products  1.43 us (2%)
    ppermute x27, starting transfers between devices, swap(): return lax.ppermute(x, 'ep', [(i, i ^ bit) for i in range(size)])  28.8 us
    ppermute x27, waiting for transfers between devices, swap(): return lax.ppermute(x, 'ep', [(i, i ^ bit) for i in range(size)])  14.5 us
    pallas_call x3, Pallas kernels, cached_attention(): pl.pallas_call(functools.partial(cached_kernel, first, per), out_shape=[p...  13.8 us
    pallas_call x1, Pallas kernels, final_attention(): pl.pallas_call(functools.partial(final_kernel, width, per), out_shape=[ja...  3.88 us
    pallas_call x1, Pallas kernels, expert_slice(): pl.pallas_call(functools.partial(expert_kernel, split), out_shape=[act] +...  3.68 us
    pallas_call x1, Pallas kernels, gate_matrices(): pl.pallas_call(functools.partial(gate_kernel, tokens), out_shape=[pltpu.V...  3.63 us
    pallas_call x1, Pallas kernels, pack(): pl.pallas_call(pack_kernel, out_shape=[chunk] * EXPERTS + [part] * EXPERT...  2.09 us
    pallas_call x1, Pallas kernels, combine(): pl.pallas_call(functools.partial(combine_kernel, spots, tokens), out_shap...  2.01 us
  transfers between devices with their start and end apart: 27, of which 11 were waited for; matrix products, arithmetic and copies ran while one was open for 3% of the time, Pallas kernels for 25%

profile of v7, /device:TPU:0, one launch (start us, length us, event | category | flops | bytes accessed | tf_op | source)
XLA Modules:
  0.0 78.2 jit_solution(18377318020310218137)
XLA Ops:
  0.6 3.0 %collective-permute-start.6 = (bf16[448,576]{1,0:T(8,128)(2,1)}, bf16[448,576]{1,0:T(8,128)(2,1)S(1)}, u32[]{:S(2)}, u32[]{:S(2)}) collective-permute-start(bf16[448,576]{1,0:T(8,128)(2,1)} %refs_10_), channel_id=1, source_target_pairs={{0,2},{1,3},{2,0},{3,1},{4,6},{5,7},{6,4},{7,5},{8,10},{9,11},{10,... | collective-permute-start | bytes 1548296 | tf_op jit(solution)/shard_map/ppermute | solution.py:569
  3.7 2.1 %pack.1 = (bf16[8,8192]{1,0:T(8,128)(2,1)S(1)}, bf16[8,8192]{1,0:T(8,128)(2,1)S(1)}, bf16[8,8192]{1,0:T(8,128)(2,1)S(1)}, bf16[8,8192]{1,0:T(8,128)(2,1)S(1)}, b...) custom-call(s32[2]{0:T(128)S(1)} %pad_add_fusion.e_ref, ...), custom_call_target="tpu_custom_call" | custom-call | flops 1024 | bytes 1024 | tf_op jit(solution)/shard_map/pack/pallas_call | solution.py:114
  5.8 1.6 %collective-permute-start.7 = (bf16[16,1792]{1,0:T(8,128)(2,1)S(1)}, bf16[16,1792]{1,0:T(8,128)(2,1)S(1)}, u32[]{:S(2)}, u32[]{:S(2)}) collective-permute-start(bf16[16,1792]{1,0:T(8,128)(2,1)S(1)} %get-tuple-element.71), channel_id=1, source_target_pairs={{0,4},{1,5},{2,6},{3,7},{4,0},{5,1},{6,2},{7,3},{8,12},{9,13},{10,... | collective-permute-start | bytes 172040 | tf_op jit(solution)/shard_map/ppermute | solution.py:569
  7.9 2.6 %collective-permute-start.4 = (bf16[8,8192]{1,0:T(8,128)(2,1)S(1)}, bf16[8,8192]{1,0:T(8,128)(2,1)S(1)}, u32[]{:S(2)}, u32[]{:S(2)}) collective-permute-start(bf16[8,8192]{1,0:T(8,128)(2,1)S(1)} %get-tuple-element.66), channel_id=1, source_target_pairs={{0,8},{1,9},{2,10},{3,11},{4,12},{5,13},{6,14},{7,15},{8,0},{9,1},... | collective-permute-start | bytes 393224 | tf_op jit(solution)/shard_map/ppermute | solution.py:569
  10.5 1.3 %collective-permute-start.5 = (bf16[8,8192]{1,0:T(8,128)(2,1)S(1)}, bf16[8,8192]{1,0:T(8,128)(2,1)S(1)}, u32[]{:S(2)}, u32[]{:S(2)}) collective-permute-start(bf16[8,8192]{1,0:T(8,128)(2,1)S(1)} %get-tuple-element.67), channel_id=1, source_target_pairs={{0,12},{1,13},{2,14},{3,15},{4,8},{5,9},{6,10},{7,11},{8,4},{9,5},... | collective-permute-start | bytes 393224 | tf_op jit(solution)/shard_map/ppermute | solution.py:569
  12.5 1.0 %convolution_minimum_fusion.3 = f32[16,16]{0,1:T(8,128)S(1)} fusion(s32[16]{0:T(128)} %bitcast.61), kind=kOutput, calls=%fused_computation.3 | convolution fusion | flops 50688 | bytes 1088 | tf_op jit(solution)/shard_map/dot_general | solution.py:524
  14.3 1.1 %collective-permute-done.b_ref = bf16[8,8192]{1,0:T(8,128)(2,1)S(1)} collective-permute-done((bf16[8,8192]{1,0:T(8,128)(2,1)S(1)}, bf16[8,8192]{1,0:T(8,128)(2,1)S(1)}, u32[]{:S(2)}, u32[]{:S(2)}) %collective-permute-start) | collective-permute-done | bytes 131104 | tf_op jit(solution)/shard_map/ppermute | solution.py:569
  15.9 5.9 %cached.3 = (bf16[8,128,512]{2,1,0:T(8,128)(2,1)S(1)}, f32[8,2,128]{2,1,0:T(2,128)S(1)}, bf16[1,7168,1024]{2,1,0:T(8,128)(2,1)S(1)}) custom-call(s32[1]{0:T(128)S(6)} %copy.17.length_ref, bf16[16,576,128]{2,1,0:T(8,128)(2,1)} %bitcast.49, bf16[1,576,1024]{2,1,0:T(8,128)(2,1)} %bitcast.55, bf16[1,7168,1024]{2,1,0:T(8,128)(2,1)} %refs_2_.2), custom_call_target="tpu_custom_call" | custom-call | flops 4563402752 | bytes 2359296 | tf_op jit(solution)/shard_map/cached/pallas_call | solution.py:404
  22.9 1.4 %collective-permute-start.9 = (bf16[16,8192]{1,0:T(8,128)(2,1)S(1)}, bf16[16,8192]{1,0:T(8,128)(2,1)S(1)}, u32[]{:S(2)}, u32[]{:S(2)}) collective-permute-start(bf16[16,8192]{1,0:T(8,128)(2,1)S(1)} %join.3.refs_1_), channel_id=1, source_target_pairs={{0,2},{1,3},{2,0},{3,1},{4,6},{5,7},{6,4},{7,5},{8,10},{9,11},{10,... | collective-permute-start | bytes 786440 | tf_op jit(solution)/shard_map/ppermute | solution.py:569
  24.3 3.5 %collective-permute-start.10 = (bf16[16,1792]{1,0:T(8,128)(2,1)S(1)}, bf16[16,1792]{1,0:T(8,128)(2,1)S(1)}, u32[]{:S(2)}, u32[]{:S(2)}) collective-permute-start(bf16[16,1792]{1,0:T(8,128)(2,1)S(1)} %get-tuple-element.76), channel_id=1, source_target_pairs={{0,12},{1,13},{2,14},{3,15},{4,8},{5,9},{6,10},{7,11},{8,4},{9,5},... | collective-permute-start | bytes 172040 | tf_op jit(solution)/shard_map/ppermute | solution.py:569
  27.8 3.6 %gates.1 = (bf16[192,192]{1,0:T(8,128)(2,1)S(1)}, bf16[1,512,7168]{2,1,0:T(8,128)(2,1)S(1)}) custom-call(s32[2]{0:T(128)S(1)} %pad_add_fusion.e_ref, bf16[16,8192]{1,0:T(8,128)(2,1)S(1)} %join.2.refs_0_, bf16[16,8192]{1,0:T(8,128)(2,1)S(1)} %join.3.refs_1_, bf16[1,512,7168]{2,1,0:T(8,128)(2,1)} %refs_2_.3), custom_call_target="tpu_custom_call" | custom-call | flops 17179869184 | bytes 16777216 | tf_op jit(solution)/shard_map/gates/pallas_call | solution.py:261
  31.6 1.5 %collective-permute-done.11.refs_6_ = bf16[16,1792]{1,0:T(8,128)(2,1)S(1)} collective-permute-done((bf16[16,1792]{1,0:T(8,128)(2,1)S(1)}, bf16[16,1792]{1,0:T(8,128)(2,1)S(1)}, u32[]{:S(2)}, u32[]{:S(2)}) %collective-permute-start.11) | collective-permute-done | bytes 57376 | tf_op jit(solution)/shard_map/ppermute | solution.py:569
  33.1 1.5 %collective-permute-done.12.refs_7_ = bf16[16,8192]{1,0:T(8,128)(2,1)S(1)} collective-permute-done((bf16[16,8192]{1,0:T(8,128)(2,1)S(1)}, bf16[16,8192]{1,0:T(8,128)(2,1)S(1)}, u32[]{:S(2)}, u32[]{:S(2)}) %collective-permute-start.12) | collective-permute-done | bytes 262176 | tf_op jit(solution)/shard_map/ppermute | solution.py:569
  34.6 3.7 %experts.1 = (bf16[160,512]{1,0:T(8,128)(2,1)S(1)}, bf16[2,1,40,1792]{3,2,1,0:T(8,128)(2,1)S(1)}, bf16[2,1,40,1792]{3,2,1,0:T(8,128)(2,1)S(1)}) custom-call(s32[2]{0:T(128)S(1)} %pad_add_fusion.e_ref, bf16[16,8192]{1,0:T(8,128)(2,1)S(1)} %join.2.refs_0_, bf16[16,8192]{1,0:T(8,128)(2,1)S(1)} %join.3.refs_1_, ...), custom_call_target="tpu_custom_call" | custom-call | flops 1024 | bytes 1024 | tf_op jit(solution)/shard_map/experts/pallas_call | solution.py:186
  38.3 1.8 %experts_rest.1 = (bf16[2,1,40,1792]{3,2,1,0:T(8,128)(2,1)S(1)}, bf16[2,1,40,1792]{3,2,1,0:T(8,128)(2,1)S(1)}, bf16[2,2,40,1792]{3,2,1,0:T(8,128)(2,1)S(1)}, bf16[2,2,40,1792]{3,2,1,0:T(8,128)(2,1)S(1)}) custom-call(s32[2]{0:T(128)S(1)} %pad_add_fusion.e_ref, bf16[160,512]{1,0:T(8,128)(2,1)S(1)} %get-tuple-element.88.act, ...), custom_call_target="tpu_custom_call" | custom-call | flops 1024 | bytes 1024 | tf_op jit(solution)/shard_map/experts_rest/pallas_call | solution.py:196
  41.8 0.7 collective-permute-start.16
  42.5 1.5 %collective-permute-start.20 = (bf16[1,40,1792]{2,1,0:T(8,128)(2,1)S(1)}, bf16[1,40,1792]{2,1,0:T(8,128)(2,1)S(1)}, u32[]{:S(2)}, u32[]{:S(2)}) collective-permute-start(bf16[1,40,1792]{2,1,0:T(8,128)(2,1)S(1)} %fusion.6), channel_id=1, source_target_pairs={{0,2},{1,3},{2,0},{3,1},{4,6},{5,7},{6,4},{7,5},{8,10},{9,11},{10,... | collective-permute-start | bytes 430088 | tf_op jit(solution)/shard_map/ppermute | solution.py:569
  44.0 4.5 %collective-permute-done.16 = bf16[1,40,1792]{2,1,0:T(8,128)(2,1)S(1)} collective-permute-done((bf16[1,40,1792]{2,1,0:T(8,128)(2,1)S(1)}, bf16[1,40,1792]{2,1,0:T(8,128)(2,1)S(1)}, u32[]{:S(2)}, u32[]{:S(2)}) %collective-permute-start.16) | collective-permute-done | bytes 143392 | tf_op jit(solution)/shard_map/ppermute | solution.py:569
  48.5 1.4 %collective-permute-start.18 = (bf16[40,1792]{1,0:T(8,128)(2,1)S(1)}, bf16[40,1792]{1,0:T(8,128)(2,1)S(1)}, u32[]{:S(2)}, u32[]{:S(2)}) collective-permute-start(bf16[40,1792]{1,0:T(8,128)(2,1)S(1)} %fusion.4), channel_id=1, source_target_pairs={{0,8},{1,9},{2,10},{3,11},{4,12},{5,13},{6,14},{7,15},{8,0},{9,1},... | collective-permute-start | bytes 430088 | tf_op jit(solution)/shard_map/ppermute | solution.py:569
  50.1 1.1 %collective-permute-start.14 = (bf16[2,40,1792]{2,1,0:T(8,128)(2,1)S(1)}, bf16[2,40,1792]{2,1,0:T(8,128)(2,1)S(1)}, u32[]{:S(2)}, u32[]{:S(2)}) collective-permute-start(bf16[2,40,1792]{2,1,0:T(8,128)(2,1)S(1)} %fusion), channel_id=1, source_target_pairs={{0,2},{1,3},{2,0},{3,1},{4,6},{5,7},{6,4},{7,5},{8,10},{9,11},{10,... | collective-permute-start | bytes 860168 | tf_op jit(solution)/shard_map/ppermute | solution.py:569
  51.2 2.9 %collective-permute-start.21 = (bf16[40,1792]{1,0:T(8,128)(2,1)S(1)}, bf16[40,1792]{1,0:T(8,128)(2,1)S(1)}, u32[]{:S(2)}, u32[]{:S(2)}) collective-permute-start(bf16[40,1792]{1,0:T(8,128)(2,1)S(1)} %fusion.1), channel_id=1, source_target_pairs={{0,12},{1,13},{2,14},{3,15},{4,8},{5,9},{6,10},{7,11},{8,4},{9,5},... | collective-permute-start | bytes 430088 | tf_op jit(solution)/shard_map/ppermute | solution.py:569
  54.1 4.0 %cached.4 = (bf16[4,128,512]{2,1,0:T(8,128)(2,1)S(1)}, f32[4,2,128]{2,1,0:T(2,128)S(1)}) custom-call(s32[1]{0:T(128)S(6)} %copy.17.length_ref, bf16[16,576,128]{2,1,0:T(8,128)(2,1)} %bitcast.50, bf16[1,576,1024]{2,1,0:T(8,128)(2,1)} %bitcast.56), custom_call_target="tpu_custom_call" | custom-call | flops 17179869184 | bytes 16777216 | tf_op jit(solution)/shard_map/cached/pallas_call | solution.py:404
  58.3 0.6 collective-permute-start.17
  58.9 3.8 %cached.5 = (bf16[4,128,512]{2,1,0:T(8,128)(2,1)S(1)}, f32[4,2,128]{2,1,0:T(2,128)S(1)}) custom-call(s32[1]{0:T(128)S(6)} %copy.17.length_ref, bf16[16,576,128]{2,1,0:T(8,128)(2,1)} %bitcast.51, bf16[1,576,1024]{2,1,0:T(8,128)(2,1)} %bitcast.57), custom_call_target="tpu_custom_call" | custom-call | flops 2281701376 | bytes 1179648 | tf_op jit(solution)/shard_map/cached/pallas_call | solution.py:404
  62.7 0.7 collective-permute-done.17.refs_1_
  63.5 2.0 %combine.1 = (f32[16,640]{1,0:T(8,128)S(1)}, bf16[16,1792]{1,0:T(8,128)(2,1)S(1)}, bf16[16,2432]{1,0:T(8,128)(2,1)S(1)}, bf16[16,2432]{1,0:T(8,128)(2,1)S(1)}, bf16[16,2432]{1,0:T(8,128)(2,1)S(1)}) custom-call(s32[2]{0:T(128)S(1)} %pad_add_fusion.e_ref, bf16[40,1792]{1,0:T(8,128)(2,1)S(1)} %get-tuple-element.103.refs_0_, ...), custom_call_target="tpu_custom_call" | custom-call | flops 1024 | bytes 1024 | tf_op jit(solution)/shard_map/combine/pallas_call | solution.py:330
  65.5 0.9 %collective-permute-start.24 = (bf16[16,2432]{1,0:T(8,128)(2,1)S(1)}, bf16[16,2432]{1,0:T(8,128)(2,1)S(1)}, u32[]{:S(2)}, u32[]{:S(2)}) collective-permute-start(bf16[16,2432]{1,0:T(8,128)(2,1)S(1)} %get-tuple-element.118), channel_id=1, source_target_pairs={{0,4},{1,5},{2,6},{3,7},{4,0},{5,1},{6,2},{7,3},{8,12},{9,13},{10,... | collective-permute-start | bytes 233480 | tf_op jit(solution)/shard_map/ppermute | solution.py:569
  66.4 1.5 %collective-permute-start.25 = (bf16[16,2432]{1,0:T(8,128)(2,1)S(1)}, bf16[16,2432]{1,0:T(8,128)(2,1)S(1)}, u32[]{:S(2)}, u32[]{:S(2)}) collective-permute-start(bf16[16,2432]{1,0:T(8,128)(2,1)S(1)} %get-tuple-element.119), channel_id=1, source_target_pairs={{0,8},{1,9},{2,10},{3,11},{4,12},{5,13},{6,14},{7,15},{8,0},{9,1},... | collective-permute-start | bytes 233480 | tf_op jit(solution)/shard_map/ppermute | solution.py:569
  67.9 2.1 %collective-permute-start.26 = (bf16[16,2432]{1,0:T(8,128)(2,1)S(1)}, bf16[16,2432]{1,0:T(8,128)(2,1)S(1)}, u32[]{:S(2)}, u32[]{:S(2)}) collective-permute-start(bf16[16,2432]{1,0:T(8,128)(2,1)S(1)} %get-tuple-element.120), channel_id=1, source_target_pairs={{0,12},{1,13},{2,14},{3,15},{4,8},{5,9},{6,10},{7,11},{8,4},{9,5},... | collective-permute-start | bytes 233480 | tf_op jit(solution)/shard_map/ppermute | solution.py:569
  70.3 3.0 %collective-permute-done.25.refs_3_ = bf16[16,2432]{1,0:T(8,128)(2,1)S(1)} collective-permute-done((bf16[16,2432]{1,0:T(8,128)(2,1)S(1)}, bf16[16,2432]{1,0:T(8,128)(2,1)S(1)}, u32[]{:S(2)}, u32[]{:S(2)}) %collective-permute-start.25) | collective-permute-done | bytes 77856 | tf_op jit(solution)/shard_map/ppermute | solution.py:569
  73.3 0.9 %collective-permute-done.26.refs_4_ = bf16[16,2432]{1,0:T(8,128)(2,1)S(1)} collective-permute-done((bf16[16,2432]{1,0:T(8,128)(2,1)S(1)}, bf16[16,2432]{1,0:T(8,128)(2,1)S(1)}, u32[]{:S(2)}, u32[]{:S(2)}) %collective-permute-start.26) | collective-permute-done | bytes 77856 | tf_op jit(solution)/shard_map/ppermute | solution.py:569
  74.2 3.9 %final.1 = (bf16[16,7168]{1,0:T(8,128)(2,1)}, bf16[16,576]{1,0:T(8,128)(2,1)}, bf16[16,128,512]{2,1,0:T(8,128)(2,1)}) custom-call(s32[2]{0:T(128)S(1)} %pad_add_fusion.e_ref, f32[16,640]{1,0:T(8,128)S(1)} %get-tuple-element.116.refs_0_, bf16[16,1792]{1,0:T(8,128)(2,1)S(1)} %get-tuple-element.117.refs_1_, ...), custom_call_target="tpu_custom_call" | custom-call | flops 1024 | bytes 1024 | tf_op jit(solution)/shard_map/final/pallas_call | solution.py:500
  (62 shorter events, 5.3 us)
Async XLA Ops:
  0.6 21.3 %collective-permute-start.6 = (bf16[448,576]{1,0:T(8,128)(2,1)}, bf16[448,576]{1,0:T(8,128)(2,1)S(1)}, u32[]{:S(2)}, u32[]{:S(2)}) collective-permute-start(bf16[448,576]{1,0:T(8,128)(2,1)} %refs_10_), channel_id=1, source_target_pairs={{0,2},{1,3},{2,0},{3,1},{4,6},{5,7},{6,4},{7,5},{8,10},{9,11},{10,... | collective-permute-start | bytes 1548296 | tf_op jit(solution)/shard_map/ppermute | solution.py:569
  5.8 16.1 %collective-permute-start.7 = (bf16[16,1792]{1,0:T(8,128)(2,1)S(1)}, bf16[16,1792]{1,0:T(8,128)(2,1)S(1)}, u32[]{:S(2)}, u32[]{:S(2)}) collective-permute-start(bf16[16,1792]{1,0:T(8,128)(2,1)S(1)} %get-tuple-element.71), channel_id=1, source_target_pairs={{0,4},{1,5},{2,6},{3,7},{4,0},{5,1},{6,2},{7,3},{8,12},{9,13},{10,... | collective-permute-start | bytes 172040 | tf_op jit(solution)/shard_map/ppermute | solution.py:569
  7.5 8.0 %collective-permute-start = (bf16[8,8192]{1,0:T(8,128)(2,1)S(1)}, bf16[8,8192]{1,0:T(8,128)(2,1)S(1)}, u32[]{:S(2)}, u32[]{:S(2)}) collective-permute-start(bf16[8,8192]{1,0:T(8,128)(2,1)S(1)} %get-tuple-element.65), channel_id=1, source_target_pairs={{0,4},{1,5},{2,6},{3,7},{4,0},{5,1},{6,2},{7,3},{8,12},{9,13},{10,... | collective-permute-start | bytes 393224 | tf_op jit(solution)/shard_map/ppermute | solution.py:569
  7.9 14.0 %collective-permute-start.4 = (bf16[8,8192]{1,0:T(8,128)(2,1)S(1)}, bf16[8,8192]{1,0:T(8,128)(2,1)S(1)}, u32[]{:S(2)}, u32[]{:S(2)}) collective-permute-start(bf16[8,8192]{1,0:T(8,128)(2,1)S(1)} %get-tuple-element.66), channel_id=1, source_target_pairs={{0,8},{1,9},{2,10},{3,11},{4,12},{5,13},{6,14},{7,15},{8,0},{9,1},... | collective-permute-start | bytes 393224 | tf_op jit(solution)/shard_map/ppermute | solution.py:569
  10.5 11.4 %collective-permute-start.5 = (bf16[8,8192]{1,0:T(8,128)(2,1)S(1)}, bf16[8,8192]{1,0:T(8,128)(2,1)S(1)}, u32[]{:S(2)}, u32[]{:S(2)}) collective-permute-start(bf16[8,8192]{1,0:T(8,128)(2,1)S(1)} %get-tuple-element.67), channel_id=1, source_target_pairs={{0,12},{1,13},{2,14},{3,15},{4,8},{5,9},{6,10},{7,11},{8,4},{9,5},... | collective-permute-start | bytes 393224 | tf_op jit(solution)/shard_map/ppermute | solution.py:569
  15.5 7.4 %collective-permute-start.2 = (bf16[16,8192]{1,0:T(8,128)(2,1)S(1)}, bf16[16,8192]{1,0:T(8,128)(2,1)S(1)}, u32[]{:S(2)}, u32[]{:S(2)}) collective-permute-start(bf16[16,8192]{1,0:T(8,128)(2,1)S(1)} %join.2.refs_0_), channel_id=1, source_target_pairs={{0,2},{1,3},{2,0},{3,1},{4,6},{5,7},{6,4},{7,5},{8,10},{9,11},{10,... | collective-permute-start | bytes 786440 | tf_op jit(solution)/shard_map/ppermute | solution.py:569
  22.0 2.4 %collective-permute-start.8 = (bf16[16,8192]{1,0:T(8,128)(2,1)S(1)}, bf16[16,8192]{1,0:T(8,128)(2,1)S(1)}, u32[]{:S(2)}, u32[]{:S(2)}) collective-permute-start(bf16[16,8192]{1,0:T(8,128)(2,1)S(1)} %join.3.refs_1_), channel_id=1, source_target_pairs={{0,1},{1,0},{2,3},{3,2},{4,5},{5,4},{6,7},{7,6},{8,9},{9,8},{10,11... | collective-permute-start | bytes 786440 | tf_op jit(solution)/shard_map/ppermute | solution.py:569
  22.0 9.4 %collective-permute-start.1 = (bf16[16,8192]{1,0:T(8,128)(2,1)S(1)}, bf16[16,8192]{1,0:T(8,128)(2,1)S(1)}, u32[]{:S(2)}, u32[]{:S(2)}) collective-permute-start(bf16[16,8192]{1,0:T(8,128)(2,1)S(1)} %join.2.refs_0_), channel_id=1, source_target_pairs={{0,1},{1,0},{2,3},{3,2},{4,5},{5,4},{6,7},{7,6},{8,9},{9,8},{10,11... | collective-permute-start | bytes 786440 | tf_op jit(solution)/shard_map/ppermute | solution.py:569
  22.9 8.6 %collective-permute-start.3 = (bf16[16,8192]{1,0:T(8,128)(2,1)S(1)}, bf16[16,8192]{1,0:T(8,128)(2,1)S(1)}, u32[]{:S(2)}, u32[]{:S(2)}) collective-permute-start(bf16[16,8192]{1,0:T(8,128)(2,1)S(1)} %collective-permute-done.2.refs_4_), channel_id=1, source_target_pairs={{0,1},{1,0},{2,3},{3,2},{4,5},{5,4},{6,7},{7,6},{8,9},{9,8},{10,11... | collective-permute-start | bytes 786440 | tf_op jit(solution)/shard_map/ppermute | solution.py:569
  22.9 8.7 %collective-permute-start.9 = (bf16[16,8192]{1,0:T(8,128)(2,1)S(1)}, bf16[16,8192]{1,0:T(8,128)(2,1)S(1)}, u32[]{:S(2)}, u32[]{:S(2)}) collective-permute-start(bf16[16,8192]{1,0:T(8,128)(2,1)S(1)} %join.3.refs_1_), channel_id=1, source_target_pairs={{0,2},{1,3},{2,0},{3,1},{4,6},{5,7},{6,4},{7,5},{8,10},{9,11},{10,... | collective-permute-start | bytes 786440 | tf_op jit(solution)/shard_map/ppermute | solution.py:569
  24.3 7.3 %collective-permute-start.10 = (bf16[16,1792]{1,0:T(8,128)(2,1)S(1)}, bf16[16,1792]{1,0:T(8,128)(2,1)S(1)}, u32[]{:S(2)}, u32[]{:S(2)}) collective-permute-start(bf16[16,1792]{1,0:T(8,128)(2,1)S(1)} %get-tuple-element.76), channel_id=1, source_target_pairs={{0,12},{1,13},{2,14},{3,15},{4,8},{5,9},{6,10},{7,11},{8,4},{9,5},... | collective-permute-start | bytes 172040 | tf_op jit(solution)/shard_map/ppermute | solution.py:569
  27.8 5.3 %collective-permute-start.11 = (bf16[16,1792]{1,0:T(8,128)(2,1)S(1)}, bf16[16,1792]{1,0:T(8,128)(2,1)S(1)}, u32[]{:S(2)}, u32[]{:S(2)}) collective-permute-start(bf16[16,1792]{1,0:T(8,128)(2,1)S(1)} %get-tuple-element.77), channel_id=1, source_target_pairs={{0,8},{1,9},{2,10},{3,11},{4,12},{5,13},{6,14},{7,15},{8,0},{9,1},... | collective-permute-start | bytes 172040 | tf_op jit(solution)/shard_map/ppermute | solution.py:569
  33.1 1.5 %collective-permute-start.12 = (bf16[16,8192]{1,0:T(8,128)(2,1)S(1)}, bf16[16,8192]{1,0:T(8,128)(2,1)S(1)}, u32[]{:S(2)}, u32[]{:S(2)}) collective-permute-start(bf16[16,8192]{1,0:T(8,128)(2,1)S(1)} %collective-permute-done.9.refs_5_), channel_id=1, source_target_pairs={{0,1},{1,0},{2,3},{3,2},{4,5},{5,4},{6,7},{7,6},{8,9},{9,8},{10,11... | collective-permute-start | bytes 786440 | tf_op jit(solution)/shard_map/ppermute | solution.py:569
  38.3 2.4 %copy-start.1 = (bf16[448,576]{1,0:T(8,128)(2,1)S(1)}, bf16[448,576]{1,0:T(8,128)(2,1)}, u32[]{:S(2)}) copy-start(bf16[448,576]{1,0:T(8,128)(2,1)} %refs_10_) | copy-start | bytes 1548292
  40.1 1.6 %collective-permute-start.15 = (bf16[2,1,40,1792]{3,2,1,0:T(8,128)(2,1)S(1)}, bf16[2,1,40,1792]{3,2,1,0:T(8,128)(2,1)S(1)}, u32[]{:S(2)}, u32[]{:S(2)}) collective-permute-start(bf16[2,1,40,1792]{3,2,1,0:T(8,128)(2,1)S(1)} %get-tuple-element.92), channel_id=1, source_target_pairs={{0,1},{1,0},{2,3},{3,2},{4,5},{5,4},{6,7},{7,6},{8,9},{9,8},{10,11... | collective-permute-start | bytes 860168 | tf_op jit(solution)/shard_map/ppermute | solution.py:569
  40.3 2.1 %collective-permute-start.19 = (bf16[2,1,40,1792]{3,2,1,0:T(8,128)(2,1)S(1)}, bf16[2,1,40,1792]{3,2,1,0:T(8,128)(2,1)S(1)}, u32[]{:S(2)}, u32[]{:S(2)}) collective-permute-start(bf16[2,1,40,1792]{3,2,1,0:T(8,128)(2,1)S(1)} %get-tuple-element.98), channel_id=1, source_target_pairs={{0,1},{1,0},{2,3},{3,2},{4,5},{5,4},{6,7},{7,6},{8,9},{9,8},{10,11... | collective-permute-start | bytes 860168 | tf_op jit(solution)/shard_map/ppermute | solution.py:569
  40.7 22.8 %collective-permute-start.22 = (bf16[448,576]{1,0:T(8,128)(2,1)S(1)}, bf16[448,576]{1,0:T(8,128)(2,1)S(1)}, u32[]{:S(2)}, u32[]{:S(2)}) collective-permute-start(bf16[448,576]{1,0:T(8,128)(2,1)S(1)} %copy-done.1), channel_id=1, source_target_pairs={{0,1},{1,0},{2,3},{3,2},{4,5},{5,4},{6,7},{7,6},{8,9},{9,8},{10,11... | collective-permute-start | bytes 1548296 | tf_op jit(solution)/shard_map/ppermute | solution.py:569
  40.8 22.6 %collective-permute-start.23 = (bf16[448,576]{1,0:T(8,128)(2,1)S(1)}, bf16[448,576]{1,0:T(8,128)(2,1)S(1)}, u32[]{:S(2)}, u32[]{:S(2)}) collective-permute-start(bf16[448,576]{1,0:T(8,128)(2,1)S(1)} %collective-permute-done.6.refs_11_), channel_id=1, source_target_pairs={{0,1},{1,0},{2,3},{3,2},{4,5},{5,4},{6,7},{7,6},{8,9},{9,8},{10,11... | collective-permute-start | bytes 1548296 | tf_op jit(solution)/shard_map/ppermute | solution.py:569
  41.2 8.8 %collective-permute-start.13 = (bf16[2,2,40,1792]{3,2,1,0:T(8,128)(2,1)S(1)}, bf16[2,2,40,1792]{3,2,1,0:T(8,128)(2,1)S(1)}, u32[]{:S(2)}, u32[]{:S(2)}) collective-permute-start(bf16[2,2,40,1792]{3,2,1,0:T(8,128)(2,1)S(1)} %get-tuple-element.90), channel_id=1, source_target_pairs={{0,1},{1,0},{2,3},{3,2},{4,5},{5,4},{6,7},{7,6},{8,9},{9,8},{10,11... | collective-permute-start | bytes 1720328 | tf_op jit(solution)/shard_map/ppermute | solution.py:569
  41.8 6.7 %collective-permute-start.16 = (bf16[1,40,1792]{2,1,0:T(8,128)(2,1)S(1)}, bf16[1,40,1792]{2,1,0:T(8,128)(2,1)S(1)}, u32[]{:S(2)}, u32[]{:S(2)}) collective-permute-start(bf16[1,40,1792]{2,1,0:T(8,128)(2,1)S(1)} %fusion.5), channel_id=1, source_target_pairs={{0,2},{1,3},{2,0},{3,1},{4,6},{5,7},{6,4},{7,5},{8,10},{9,11},{10,... | collective-permute-start | bytes 430088 | tf_op jit(solution)/shard_map/ppermute | solution.py:569
  42.5 8.7 %collective-permute-start.20 = (bf16[1,40,1792]{2,1,0:T(8,128)(2,1)S(1)}, bf16[1,40,1792]{2,1,0:T(8,128)(2,1)S(1)}, u32[]{:S(2)}, u32[]{:S(2)}) collective-permute-start(bf16[1,40,1792]{2,1,0:T(8,128)(2,1)S(1)} %fusion.6), channel_id=1, source_target_pairs={{0,2},{1,3},{2,0},{3,1},{4,6},{5,7},{6,4},{7,5},{8,10},{9,11},{10,... | collective-permute-start | bytes 430088 | tf_op jit(solution)/shard_map/ppermute | solution.py:569
  48.5 14.2 %collective-permute-start.18 = (bf16[40,1792]{1,0:T(8,128)(2,1)S(1)}, bf16[40,1792]{1,0:T(8,128)(2,1)S(1)}, u32[]{:S(2)}, u32[]{:S(2)}) collective-permute-start(bf16[40,1792]{1,0:T(8,128)(2,1)S(1)} %fusion.4), channel_id=1, source_target_pairs={{0,8},{1,9},{2,10},{3,11},{4,12},{5,13},{6,14},{7,15},{8,0},{9,1},... | collective-permute-start | bytes 430088 | tf_op jit(solution)/shard_map/ppermute | solution.py:569
  50.1 8.1 %collective-permute-start.14 = (bf16[2,40,1792]{2,1,0:T(8,128)(2,1)S(1)}, bf16[2,40,1792]{2,1,0:T(8,128)(2,1)S(1)}, u32[]{:S(2)}, u32[]{:S(2)}) collective-permute-start(bf16[2,40,1792]{2,1,0:T(8,128)(2,1)S(1)} %fusion), channel_id=1, source_target_pairs={{0,2},{1,3},{2,0},{3,1},{4,6},{5,7},{6,4},{7,5},{8,10},{9,11},{10,... | collective-permute-start | bytes 860168 | tf_op jit(solution)/shard_map/ppermute | solution.py:569
  51.2 11.5 %collective-permute-start.21 = (bf16[40,1792]{1,0:T(8,128)(2,1)S(1)}, bf16[40,1792]{1,0:T(8,128)(2,1)S(1)}, u32[]{:S(2)}, u32[]{:S(2)}) collective-permute-start(bf16[40,1792]{1,0:T(8,128)(2,1)S(1)} %fusion.1), channel_id=1, source_target_pairs={{0,12},{1,13},{2,14},{3,15},{4,8},{5,9},{6,10},{7,11},{8,4},{9,5},... | collective-permute-start | bytes 430088 | tf_op jit(solution)/shard_map/ppermute | solution.py:569
  58.1 5.3 %copy-start.2 = (f32[7168]{0:T(1024)S(1)}, f32[7168]{0:T(1024)}, u32[]{:S(2)}) copy-start(f32[7168]{0:T(1024)} %param.15) | copy-start | bytes 86020
  58.1 16.0 %copy-start = (bf16[16,128,576]{1,2,0:T(8,128)(2,1)S(1)}, bf16[16,128,576]{1,2,0:T(8,128)(2,1)}, u32[]{:S(2)}) copy-start(bf16[16,128,576]{1,2,0:T(8,128)(2,1)} %param.24) | copy-start | bytes 7077892
  58.2 16.0 %copy-start.3 = (f32[512]{0:T(512)S(1)}, f32[512]{0:T(512)}, u32[]{:S(2)}) copy-start(f32[512]{0:T(512)} %param.16) | copy-start | bytes 6148
  58.3 5.2 %collective-permute-start.17 = (bf16[40,1792]{1,0:T(8,128)(2,1)S(1)}, bf16[40,1792]{1,0:T(8,128)(2,1)S(1)}, u32[]{:S(2)}, u32[]{:S(2)}) collective-permute-start(bf16[40,1792]{1,0:T(8,128)(2,1)S(1)} %get-tuple-element.125), channel_id=1, source_target_pairs={{0,4},{1,5},{2,6},{3,7},{4,0},{5,1},{6,2},{7,3},{8,12},{9,13},{10,... | collective-permute-start | bytes 430088 | tf_op jit(solution)/shard_map/ppermute | solution.py:569
  65.5 4.8 %collective-permute-start.24 = (bf16[16,2432]{1,0:T(8,128)(2,1)S(1)}, bf16[16,2432]{1,0:T(8,128)(2,1)S(1)}, u32[]{:S(2)}, u32[]{:S(2)}) collective-permute-start(bf16[16,2432]{1,0:T(8,128)(2,1)S(1)} %get-tuple-element.118), channel_id=1, source_target_pairs={{0,4},{1,5},{2,6},{3,7},{4,0},{5,1},{6,2},{7,3},{8,12},{9,13},{10,... | collective-permute-start | bytes 233480 | tf_op jit(solution)/shard_map/ppermute | solution.py:569
  66.4 6.9 %collective-permute-start.25 = (bf16[16,2432]{1,0:T(8,128)(2,1)S(1)}, bf16[16,2432]{1,0:T(8,128)(2,1)S(1)}, u32[]{:S(2)}, u32[]{:S(2)}) collective-permute-start(bf16[16,2432]{1,0:T(8,128)(2,1)S(1)} %get-tuple-element.119), channel_id=1, source_target_pairs={{0,8},{1,9},{2,10},{3,11},{4,12},{5,13},{6,14},{7,15},{8,0},{9,1},... | collective-permute-start | bytes 233480 | tf_op jit(solution)/shard_map/ppermute | solution.py:569
  67.9 6.3 %collective-permute-start.26 = (bf16[16,2432]{1,0:T(8,128)(2,1)S(1)}, bf16[16,2432]{1,0:T(8,128)(2,1)S(1)}, u32[]{:S(2)}, u32[]{:S(2)}) collective-permute-start(bf16[16,2432]{1,0:T(8,128)(2,1)S(1)} %get-tuple-element.120), channel_id=1, source_target_pairs={{0,12},{1,13},{2,14},{3,15},{4,8},{5,9},{6,10},{7,11},{8,4},{9,5},... | collective-permute-start | bytes 233480 | tf_op jit(solution)/shard_map/ppermute | solution.py:569

commit v8 on v6

--- a/solution.py
+++ b/solution.py
@@ -430,8 +430,8 @@
     own_sum, own_part = refs[:2]
     got = refs[2 : 1 + EXPERTS]
     gain_ref, turn_ref, allow_ref, q_ref = refs[1 + EXPERTS : 5 + EXPERTS]
-    cached = refs[5 + EXPERTS : -5]
-    part_ref, entry_ref, out_hbm, out_ref, sem = refs[-5:]
+    cached = refs[5 + EXPERTS : -7]
+    part_hbm, entry_hbm, out_hbm, part_ref, entry_ref, out_ref, sem = refs[-7:]
     found = []
     for ctx_ref, stat_ref in zip(cached[0::2], cached[1::2]):
         found += [(ctx_ref, stat_ref, i) for i in range(ctx_ref.shape[0])]
@@ -456,8 +456,16 @@
     )
     keys = jnp.concatenate([head, tail], axis=1).astype(BF)[:, :lat]
     entry_ref[...] = keys
+    for k in range(EXPERTS):
+        start = pl.multiple_of((e_ref[0] ^ k) * quarter, 128)
+        part_ref[:, pl.ds(start, quarter)] = got[k - 1][:, padded:] if k else own_part[...]
+    copies = [
+        pltpu.make_async_copy(part_ref, part_hbm, sem.at[0]),
+        pltpu.make_async_copy(entry_ref, entry_hbm, sem.at[1]),
+    ]
+    for c in copies:
+        c.start()
     count = keys.shape[0]
-    copies = []
     for g in range(nodes // per):
         span = range(g * per, (g + 1) * per)
 
@@ -480,12 +488,13 @@
             out = ctx_ref[place].astype(F32) * mine[:, count : count + 1]
             out = out + dot(mine[:, :count].astype(BF), keys[:, :KEY_VALUE_RANK])
             out_ref[g * per + i] = out.astype(BF)
-        here = pl.ds(g * per, per)
-        copies.append(pltpu.make_async_copy(out_ref.at[here], out_hbm.at[here], sem.at[g]))
-        copies[-1].start()
-    for k in range(EXPERTS):
-        start = pl.multiple_of((e_ref[0] ^ k) * quarter, 128)
-        part_ref[:, pl.ds(start, quarter)] = got[k - 1][:, padded:] if k else own_part[...]
+            if i % 2:
+                here = pl.ds(g * per + i - 1, 2)
+                number = len(copies)
+                copies.append(
+                    pltpu.make_async_copy(out_ref.at[here], out_hbm.at[here], sem.at[number])
+                )
+                copies[-1].start()
     for c in copies:
         c.wait()
 
@@ -504,10 +513,12 @@
             out,
         ],
         in_specs=[pl.BlockSpec(memory_space=pltpu.SMEM)] + [vmem] * len(given),
-        out_specs=[vmem, vmem, pl.BlockSpec(memory_space=pltpu.HBM)],
+        out_specs=[pl.BlockSpec(memory_space=pltpu.HBM)] * 3,
         scratch_shapes=[
+            pltpu.VMEM((tokens, width), BF),
+            pltpu.VMEM((tokens, lat), BF),
             pltpu.VMEM(out.shape, BF),
-            pltpu.SemaphoreType.DMA((tokens // per,)),
+            pltpu.SemaphoreType.DMA((2 + tokens // 2,)),
         ],
         compiler_params=params(12),
         cost_estimate=COST,

time: 78.8 us -> 78 us (0.990)
  Pallas kernels: 30.9 us -> 30.1 us
where the time goes in v8:
time: 78 us; the launch traced here: 77.8 us
  Pallas kernels  30.1 us (39%)
  starting transfers between devices  29.4 us (38%)
  waiting for transfers between devices  14.2 us (18%)
  between operations  1.72 us (2%)
  matrix products  1.43 us (2%)
    ppermute x27, starting transfers between devices, swap(): return lax.ppermute(x, 'ep', [(i, i ^ bit) for i in range(size)])  29.4 us
    ppermute x27, waiting for transfers between devices, swap(): return lax.ppermute(x, 'ep', [(i, i ^ bit) for i in range(size)])  14.2 us
    pallas_call x3, Pallas kernels, cached_attention(): pl.pallas_call(functools.partial(cached_kernel, first, per), out_shape=[p...  13.8 us
    pallas_call x1, Pallas kernels, expert_slice(): pl.pallas_call(functools.partial(expert_kernel, split), out_shape=[act] +...  4.03 us
    pallas_call x1, Pallas kernels, gate_matrices(): pl.pallas_call(functools.partial(gate_kernel, tokens), out_shape=[pltpu.V...  3.63 us
    pallas_call x1, Pallas kernels, final_attention(): pl.pallas_call(functools.partial(final_kernel, width, per), out_shape=[ja...  3.1 us
    pallas_call x1, Pallas kernels, pack(): pl.pallas_call(pack_kernel, out_shape=[chunk] * EXPERTS + [part] * EXPERT...  2.09 us
    pallas_call x1, Pallas kernels, combine(): pl.pallas_call(functools.partial(combine_kernel, spots, tokens), out_shap...  2.02 us
  transfers between devices with their start and end apart: 27, of which 9 were waited for; matrix products, arithmetic and copies ran while one was open for 3% of the time, Pallas kernels for 27%

profile of v8, /device:TPU:0, one launch (start us, length us, event | category | flops | bytes accessed | tf_op | source)
XLA Modules:
  0.0 77.8 jit_solution(66226347787245568)
XLA Ops:
  0.6 3.0 %collective-permute-start.6 = (bf16[448,576]{1,0:T(8,128)(2,1)}, bf16[448,576]{1,0:T(8,128)(2,1)S(1)}, u32[]{:S(2)}, u32[]{:S(2)}) collective-permute-start(bf16[448,576]{1,0:T(8,128)(2,1)} %refs_10_), channel_id=1, source_target_pairs={{0,2},{1,3},{2,0},{3,1},{4,6},{5,7},{6,4},{7,5},{8,10},{9,11},{10,... | collective-permute-start | bytes 1548296 | tf_op jit(solution)/shard_map/ppermute | solution.py:579
  3.7 2.1 %pack.1 = (bf16[8,8192]{1,0:T(8,128)(2,1)S(1)}, bf16[8,8192]{1,0:T(8,128)(2,1)S(1)}, bf16[8,8192]{1,0:T(8,128)(2,1)S(1)}, bf16[8,8192]{1,0:T(8,128)(2,1)S(1)}, b...) custom-call(s32[2]{0:T(128)S(1)} %pad_add_fusion.e_ref, ...), custom_call_target="tpu_custom_call" | custom-call | flops 1024 | bytes 1024 | tf_op jit(solution)/shard_map/pack/pallas_call | solution.py:114
  5.8 1.6 %collective-permute-start.7 = (bf16[16,1792]{1,0:T(8,128)(2,1)S(1)}, bf16[16,1792]{1,0:T(8,128)(2,1)S(1)}, u32[]{:S(2)}, u32[]{:S(2)}) collective-permute-start(bf16[16,1792]{1,0:T(8,128)(2,1)S(1)} %get-tuple-element.71), channel_id=1, source_target_pairs={{0,4},{1,5},{2,6},{3,7},{4,0},{5,1},{6,2},{7,3},{8,12},{9,13},{10,... | collective-permute-start | bytes 172040 | tf_op jit(solution)/shard_map/ppermute | solution.py:579
  7.9 2.6 %collective-permute-start.4 = (bf16[8,8192]{1,0:T(8,128)(2,1)S(1)}, bf16[8,8192]{1,0:T(8,128)(2,1)S(1)}, u32[]{:S(2)}, u32[]{:S(2)}) collective-permute-start(bf16[8,8192]{1,0:T(8,128)(2,1)S(1)} %get-tuple-element.66), channel_id=1, source_target_pairs={{0,8},{1,9},{2,10},{3,11},{4,12},{5,13},{6,14},{7,15},{8,0},{9,1},... | collective-permute-start | bytes 393224 | tf_op jit(solution)/shard_map/ppermute | solution.py:579
  10.5 1.3 %collective-permute-start.5 = (bf16[8,8192]{1,0:T(8,128)(2,1)S(1)}, bf16[8,8192]{1,0:T(8,128)(2,1)S(1)}, u32[]{:S(2)}, u32[]{:S(2)}) collective-permute-start(bf16[8,8192]{1,0:T(8,128)(2,1)S(1)} %get-tuple-element.67), channel_id=1, source_target_pairs={{0,12},{1,13},{2,14},{3,15},{4,8},{5,9},{6,10},{7,11},{8,4},{9,5},... | collective-permute-start | bytes 393224 | tf_op jit(solution)/shard_map/ppermute | solution.py:579
  12.5 1.0 %convolution_minimum_fusion.3 = f32[16,16]{0,1:T(8,128)S(1)} fusion(s32[16]{0:T(128)} %bitcast.61), kind=kOutput, calls=%fused_computation.3 | convolution fusion | flops 50688 | bytes 1088 | tf_op jit(solution)/shard_map/dot_general | solution.py:534
  14.3 1.1 %collective-permute-done.b_ref = bf16[8,8192]{1,0:T(8,128)(2,1)S(1)} collective-permute-done((bf16[8,8192]{1,0:T(8,128)(2,1)S(1)}, bf16[8,8192]{1,0:T(8,128)(2,1)S(1)}, u32[]{:S(2)}, u32[]{:S(2)}) %collective-permute-start) | collective-permute-done | bytes 131104 | tf_op jit(solution)/shard_map/ppermute | solution.py:579
  15.9 5.9 %cached.3 = (bf16[8,128,512]{2,1,0:T(8,128)(2,1)S(1)}, f32[8,2,128]{2,1,0:T(2,128)S(1)}, bf16[1,7168,1024]{2,1,0:T(8,128)(2,1)S(1)}) custom-call(s32[1]{0:T(128)S(6)} %copy.17.length_ref, bf16[16,576,128]{2,1,0:T(8,128)(2,1)} %bitcast.49, bf16[1,576,1024]{2,1,0:T(8,128)(2,1)} %bitcast.55, bf16[1,7168,1024]{2,1,0:T(8,128)(2,1)} %refs_2_.2), custom_call_target="tpu_custom_call" | custom-call | flops 4563402752 | bytes 2359296 | tf_op jit(solution)/shard_map/cached/pallas_call | solution.py:403
  22.0 0.5 collective-permute-start.1
  22.9 1.4 %collective-permute-start.9 = (bf16[16,8192]{1,0:T(8,128)(2,1)S(1)}, bf16[16,8192]{1,0:T(8,128)(2,1)S(1)}, u32[]{:S(2)}, u32[]{:S(2)}) collective-permute-start(bf16[16,8192]{1,0:T(8,128)(2,1)S(1)} %join.3.refs_1_), channel_id=1, source_target_pairs={{0,2},{1,3},{2,0},{3,1},{4,6},{5,7},{6,4},{7,5},{8,10},{9,11},{10,... | collective-permute-start | bytes 786440 | tf_op jit(solution)/shard_map/ppermute | solution.py:579
  24.3 3.5 %collective-permute-start.10 = (bf16[16,1792]{1,0:T(8,128)(2,1)S(1)}, bf16[16,1792]{1,0:T(8,128)(2,1)S(1)}, u32[]{:S(2)}, u32[]{:S(2)}) collective-permute-start(bf16[16,1792]{1,0:T(8,128)(2,1)S(1)} %get-tuple-element.76), channel_id=1, source_target_pairs={{0,12},{1,13},{2,14},{3,15},{4,8},{5,9},{6,10},{7,11},{8,4},{9,5},... | collective-permute-start | bytes 172040 | tf_op jit(solution)/shard_map/ppermute | solution.py:579
  27.8 3.6 %gates.1 = (bf16[192,192]{1,0:T(8,128)(2,1)S(1)}, bf16[1,512,7168]{2,1,0:T(8,128)(2,1)S(1)}) custom-call(s32[2]{0:T(128)S(1)} %pad_add_fusion.e_ref, bf16[16,8192]{1,0:T(8,128)(2,1)S(1)} %join.2.refs_0_, bf16[16,8192]{1,0:T(8,128)(2,1)S(1)} %join.3.refs_1_, bf16[1,512,7168]{2,1,0:T(8,128)(2,1)} %refs_2_.3), custom_call_target="tpu_custom_call" | custom-call | flops 17179869184 | bytes 16777216 | tf_op jit(solution)/shard_map/gates/pallas_call | solution.py:260
  31.6 1.5 %collective-permute-done.11.refs_6_ = bf16[16,1792]{1,0:T(8,128)(2,1)S(1)} collective-permute-done((bf16[16,1792]{1,0:T(8,128)(2,1)S(1)}, bf16[16,1792]{1,0:T(8,128)(2,1)S(1)}, u32[]{:S(2)}, u32[]{:S(2)}) %collective-permute-start.11) | collective-permute-done | bytes 57376 | tf_op jit(solution)/shard_map/ppermute | solution.py:579
  33.1 1.5 %collective-permute-done.12.refs_7_ = bf16[16,8192]{1,0:T(8,128)(2,1)S(1)} collective-permute-done((bf16[16,8192]{1,0:T(8,128)(2,1)S(1)}, bf16[16,8192]{1,0:T(8,128)(2,1)S(1)}, u32[]{:S(2)}, u32[]{:S(2)}) %collective-permute-start.12) | collective-permute-done | bytes 262176 | tf_op jit(solution)/shard_map/ppermute | solution.py:579
  34.6 4.0 %experts.1 = (bf16[160,512]{1,0:T(8,128)(2,1)S(1)}, bf16[2,1,40,1792]{3,2,1,0:T(8,128)(2,1)S(1)}, bf16[2,1,40,1792]{3,2,1,0:T(8,128)(2,1)S(1)}, bf16[2,1,40,1792...) custom-call(s32[2]{0:T(128)S(1)} %pad_add_fusion.e_ref, bf16[16,8192]{1,0:T(8,128)(2,1)S(1)} %join.2.refs_0_, ...), custom_call_target="tpu_custom_call" | custom-call | flops 1024 | bytes 1024 | tf_op jit(solution)/shard_map/experts/pallas_call | solution.py:185
  38.9 1.4 %experts_rest.1 = (bf16[2,2,40,1792]{3,2,1,0:T(8,128)(2,1)S(1)}, bf16[2,2,40,1792]{3,2,1,0:T(8,128)(2,1)S(1)}) custom-call(s32[2]{0:T(128)S(1)} %pad_add_fusion.e_ref, bf16[160,512]{1,0:T(8,128)(2,1)S(1)} %get-tuple-element.88.act, bf16[1,512,7168]{2,1,0:T(8,128)(2,1)S(1)} %get-tuple-element.87.refs_9_.w_out), custom_call_target="tpu_custom_call" | custom-call | flops 1024 | bytes 1024 | tf_op jit(solution)/shard_map/experts_rest/pallas_call | solution.py:195
  41.5 0.7 collective-permute-start.16
  42.2 1.5 %collective-permute-start.20 = (bf16[1,40,1792]{2,1,0:T(8,128)(2,1)S(1)}, bf16[1,40,1792]{2,1,0:T(8,128)(2,1)S(1)}, u32[]{:S(2)}, u32[]{:S(2)}) collective-permute-start(bf16[1,40,1792]{2,1,0:T(8,128)(2,1)S(1)} %fusion.6), channel_id=1, source_target_pairs={{0,2},{1,3},{2,0},{3,1},{4,6},{5,7},{6,4},{7,5},{8,10},{9,11},{10,... | collective-permute-start | bytes 430088 | tf_op jit(solution)/shard_map/ppermute | solution.py:579
  43.7 4.4 %collective-permute-done.16 = bf16[1,40,1792]{2,1,0:T(8,128)(2,1)S(1)} collective-permute-done((bf16[1,40,1792]{2,1,0:T(8,128)(2,1)S(1)}, bf16[1,40,1792]{2,1,0:T(8,128)(2,1)S(1)}, u32[]{:S(2)}, u32[]{:S(2)}) %collective-permute-start.16) | collective-permute-done | bytes 143392 | tf_op jit(solution)/shard_map/ppermute | solution.py:579
  48.2 1.5 %collective-permute-start.18 = (bf16[40,1792]{1,0:T(8,128)(2,1)S(1)}, bf16[40,1792]{1,0:T(8,128)(2,1)S(1)}, u32[]{:S(2)}, u32[]{:S(2)}) collective-permute-start(bf16[40,1792]{1,0:T(8,128)(2,1)S(1)} %fusion.4), channel_id=1, source_target_pairs={{0,8},{1,9},{2,10},{3,11},{4,12},{5,13},{6,14},{7,15},{8,0},{9,1},... | collective-permute-start | bytes 430088 | tf_op jit(solution)/shard_map/ppermute | solution.py:579
  49.7 1.1 %collective-permute-start.14 = (bf16[2,40,1792]{2,1,0:T(8,128)(2,1)S(1)}, bf16[2,40,1792]{2,1,0:T(8,128)(2,1)S(1)}, u32[]{:S(2)}, u32[]{:S(2)}) collective-permute-start(bf16[2,40,1792]{2,1,0:T(8,128)(2,1)S(1)} %fusion), channel_id=1, source_target_pairs={{0,2},{1,3},{2,0},{3,1},{4,6},{5,7},{6,4},{7,5},{8,10},{9,11},{10,... | collective-permute-start | bytes 860168 | tf_op jit(solution)/shard_map/ppermute | solution.py:579
  50.9 2.9 %collective-permute-start.21 = (bf16[40,1792]{1,0:T(8,128)(2,1)S(1)}, bf16[40,1792]{1,0:T(8,128)(2,1)S(1)}, u32[]{:S(2)}, u32[]{:S(2)}) collective-permute-start(bf16[40,1792]{1,0:T(8,128)(2,1)S(1)} %fusion.1), channel_id=1, source_target_pairs={{0,12},{1,13},{2,14},{3,15},{4,8},{5,9},{6,10},{7,11},{8,4},{9,5},... | collective-permute-start | bytes 430088 | tf_op jit(solution)/shard_map/ppermute | solution.py:579
  53.8 4.0 %cached.4 = (bf16[4,128,512]{2,1,0:T(8,128)(2,1)S(1)}, f32[4,2,128]{2,1,0:T(2,128)S(1)}) custom-call(s32[1]{0:T(128)S(6)} %copy.17.length_ref, bf16[16,576,128]{2,1,0:T(8,128)(2,1)} %bitcast.50, bf16[1,576,1024]{2,1,0:T(8,128)(2,1)} %bitcast.56), custom_call_target="tpu_custom_call" | custom-call | flops 17179869184 | bytes 16777216 | tf_op jit(solution)/shard_map/cached/pallas_call | solution.py:403
  57.9 1.1 %collective-permute-start.17 = (bf16[40,1792]{1,0:T(8,128)(2,1)S(1)}, bf16[40,1792]{1,0:T(8,128)(2,1)S(1)}, u32[]{:S(2)}, u32[]{:S(2)}) collective-permute-start(bf16[40,1792]{1,0:T(8,128)(2,1)S(1)} %get-tuple-element.125), channel_id=1, source_target_pairs={{0,4},{1,5},{2,6},{3,7},{4,0},{5,1},{6,2},{7,3},{8,12},{9,13},{10,... | collective-permute-start | bytes 430088 | tf_op jit(solution)/shard_map/ppermute | solution.py:579
  59.0 3.8 %cached.5 = (bf16[4,128,512]{2,1,0:T(8,128)(2,1)S(1)}, f32[4,2,128]{2,1,0:T(2,128)S(1)}) custom-call(s32[1]{0:T(128)S(6)} %copy.17.length_ref, bf16[16,576,128]{2,1,0:T(8,128)(2,1)} %bitcast.51, bf16[1,576,1024]{2,1,0:T(8,128)(2,1)} %bitcast.57), custom_call_target="tpu_custom_call" | custom-call | flops 2281701376 | bytes 1179648 | tf_op jit(solution)/shard_map/cached/pallas_call | solution.py:403
  63.1 2.0 %combine.1 = (f32[16,640]{1,0:T(8,128)S(1)}, bf16[16,1792]{1,0:T(8,128)(2,1)S(1)}, bf16[16,2432]{1,0:T(8,128)(2,1)S(1)}, bf16[16,2432]{1,0:T(8,128)(2,1)S(1)}, bf16[16,2432]{1,0:T(8,128)(2,1)S(1)}) custom-call(s32[2]{0:T(128)S(1)} %pad_add_fusion.e_ref, bf16[40,1792]{1,0:T(8,128)(2,1)S(1)} %get-tuple-element.103.refs_0_, ...), custom_call_target="tpu_custom_call" | custom-call | flops 1024 | bytes 1024 | tf_op jit(solution)/shard_map/combine/pallas_call | solution.py:329
  65.1 1.1 %collective-permute-start.24 = (bf16[16,2432]{1,0:T(8,128)(2,1)S(1)}, bf16[16,2432]{1,0:T(8,128)(2,1)S(1)}, u32[]{:S(2)}, u32[]{:S(2)}) collective-permute-start(bf16[16,2432]{1,0:T(8,128)(2,1)S(1)} %get-tuple-element.118), channel_id=1, source_target_pairs={{0,4},{1,5},{2,6},{3,7},{4,0},{5,1},{6,2},{7,3},{8,12},{9,13},{10,... | collective-permute-start | bytes 233480 | tf_op jit(solution)/shard_map/ppermute | solution.py:579
  66.2 1.7 %collective-permute-start.25 = (bf16[16,2432]{1,0:T(8,128)(2,1)S(1)}, bf16[16,2432]{1,0:T(8,128)(2,1)S(1)}, u32[]{:S(2)}, u32[]{:S(2)}) collective-permute-start(bf16[16,2432]{1,0:T(8,128)(2,1)S(1)} %get-tuple-element.119), channel_id=1, source_target_pairs={{0,8},{1,9},{2,10},{3,11},{4,12},{5,13},{6,14},{7,15},{8,0},{9,1},... | collective-permute-start | bytes 233480 | tf_op jit(solution)/shard_map/ppermute | solution.py:579
  68.0 1.6 %collective-permute-start.26 = (bf16[16,2432]{1,0:T(8,128)(2,1)S(1)}, bf16[16,2432]{1,0:T(8,128)(2,1)S(1)}, u32[]{:S(2)}, u32[]{:S(2)}) collective-permute-start(bf16[16,2432]{1,0:T(8,128)(2,1)S(1)} %get-tuple-element.120), channel_id=1, source_target_pairs={{0,12},{1,13},{2,14},{3,15},{4,8},{5,9},{6,10},{7,11},{8,4},{9,5},... | collective-permute-start | bytes 233480 | tf_op jit(solution)/shard_map/ppermute | solution.py:579
  69.6 0.5 collective-permute-done.24.refs_2_
  70.1 4.4 %collective-permute-done.25.refs_3_ = bf16[16,2432]{1,0:T(8,128)(2,1)S(1)} collective-permute-done((bf16[16,2432]{1,0:T(8,128)(2,1)S(1)}, bf16[16,2432]{1,0:T(8,128)(2,1)S(1)}, u32[]{:S(2)}, u32[]{:S(2)}) %collective-permute-start.25) | collective-permute-done | bytes 77856 | tf_op jit(solution)/shard_map/ppermute | solution.py:579
  74.5 3.1 %final.1 = (bf16[16,7168]{1,0:T(8,128)(2,1)}, bf16[16,576]{1,0:T(8,128)(2,1)}, bf16[16,128,512]{2,1,0:T(8,128)(2,1)}) custom-call(s32[2]{0:T(128)S(1)} %pad_add_fusion.e_ref, f32[16,640]{1,0:T(8,128)S(1)} %get-tuple-element.116.refs_0_, bf16[16,1792]{1,0:T(8,128)(2,1)S(1)} %get-tuple-element.117.refs_1_, ...), custom_call_target="tpu_custom_call" | custom-call | flops 1024 | bytes 1024 | tf_op jit(solution)/shard_map/final/pallas_call | solution.py:508
  (62 shorter events, 4.3 us)
Async XLA Ops:
  0.6 21.3 %collective-permute-start.6 = (bf16[448,576]{1,0:T(8,128)(2,1)}, bf16[448,576]{1,0:T(8,128)(2,1)S(1)}, u32[]{:S(2)}, u32[]{:S(2)}) collective-permute-start(bf16[448,576]{1,0:T(8,128)(2,1)} %refs_10_), channel_id=1, source_target_pairs={{0,2},{1,3},{2,0},{3,1},{4,6},{5,7},{6,4},{7,5},{8,10},{9,11},{10,... | collective-permute-start | bytes 1548296 | tf_op jit(solution)/shard_map/ppermute | solution.py:579
  5.8 16.1 %collective-permute-start.7 = (bf16[16,1792]{1,0:T(8,128)(2,1)S(1)}, bf16[16,1792]{1,0:T(8,128)(2,1)S(1)}, u32[]{:S(2)}, u32[]{:S(2)}) collective-permute-start(bf16[16,1792]{1,0:T(8,128)(2,1)S(1)} %get-tuple-element.71), channel_id=1, source_target_pairs={{0,4},{1,5},{2,6},{3,7},{4,0},{5,1},{6,2},{7,3},{8,12},{9,13},{10,... | collective-permute-start | bytes 172040 | tf_op jit(solution)/shard_map/ppermute | solution.py:579
  7.5 8.0 %collective-permute-start = (bf16[8,8192]{1,0:T(8,128)(2,1)S(1)}, bf16[8,8192]{1,0:T(8,128)(2,1)S(1)}, u32[]{:S(2)}, u32[]{:S(2)}) collective-permute-start(bf16[8,8192]{1,0:T(8,128)(2,1)S(1)} %get-tuple-element.65), channel_id=1, source_target_pairs={{0,4},{1,5},{2,6},{3,7},{4,0},{5,1},{6,2},{7,3},{8,12},{9,13},{10,... | collective-permute-start | bytes 393224 | tf_op jit(solution)/shard_map/ppermute | solution.py:579
  7.9 14.0 %collective-permute-start.4 = (bf16[8,8192]{1,0:T(8,128)(2,1)S(1)}, bf16[8,8192]{1,0:T(8,128)(2,1)S(1)}, u32[]{:S(2)}, u32[]{:S(2)}) collective-permute-start(bf16[8,8192]{1,0:T(8,128)(2,1)S(1)} %get-tuple-element.66), channel_id=1, source_target_pairs={{0,8},{1,9},{2,10},{3,11},{4,12},{5,13},{6,14},{7,15},{8,0},{9,1},... | collective-permute-start | bytes 393224 | tf_op jit(solution)/shard_map/ppermute | solution.py:579
  10.5 11.4 %collective-permute-start.5 = (bf16[8,8192]{1,0:T(8,128)(2,1)S(1)}, bf16[8,8192]{1,0:T(8,128)(2,1)S(1)}, u32[]{:S(2)}, u32[]{:S(2)}) collective-permute-start(bf16[8,8192]{1,0:T(8,128)(2,1)S(1)} %get-tuple-element.67), channel_id=1, source_target_pairs={{0,12},{1,13},{2,14},{3,15},{4,8},{5,9},{6,10},{7,11},{8,4},{9,5},... | collective-permute-start | bytes 393224 | tf_op jit(solution)/shard_map/ppermute | solution.py:579
  15.5 7.4 %collective-permute-start.2 = (bf16[16,8192]{1,0:T(8,128)(2,1)S(1)}, bf16[16,8192]{1,0:T(8,128)(2,1)S(1)}, u32[]{:S(2)}, u32[]{:S(2)}) collective-permute-start(bf16[16,8192]{1,0:T(8,128)(2,1)S(1)} %join.2.refs_0_), channel_id=1, source_target_pairs={{0,2},{1,3},{2,0},{3,1},{4,6},{5,7},{6,4},{7,5},{8,10},{9,11},{10,... | collective-permute-start | bytes 786440 | tf_op jit(solution)/shard_map/ppermute | solution.py:579
  22.0 2.4 %collective-permute-start.8 = (bf16[16,8192]{1,0:T(8,128)(2,1)S(1)}, bf16[16,8192]{1,0:T(8,128)(2,1)S(1)}, u32[]{:S(2)}, u32[]{:S(2)}) collective-permute-start(bf16[16,8192]{1,0:T(8,128)(2,1)S(1)} %join.3.refs_1_), channel_id=1, source_target_pairs={{0,1},{1,0},{2,3},{3,2},{4,5},{5,4},{6,7},{7,6},{8,9},{9,8},{10,11... | collective-permute-start | bytes 786440 | tf_op jit(solution)/shard_map/ppermute | solution.py:579
  22.0 9.4 %collective-permute-start.1 = (bf16[16,8192]{1,0:T(8,128)(2,1)S(1)}, bf16[16,8192]{1,0:T(8,128)(2,1)S(1)}, u32[]{:S(2)}, u32[]{:S(2)}) collective-permute-start(bf16[16,8192]{1,0:T(8,128)(2,1)S(1)} %join.2.refs_0_), channel_id=1, source_target_pairs={{0,1},{1,0},{2,3},{3,2},{4,5},{5,4},{6,7},{7,6},{8,9},{9,8},{10,11... | collective-permute-start | bytes 786440 | tf_op jit(solution)/shard_map/ppermute | solution.py:579
  22.9 8.6 %collective-permute-start.3 = (bf16[16,8192]{1,0:T(8,128)(2,1)S(1)}, bf16[16,8192]{1,0:T(8,128)(2,1)S(1)}, u32[]{:S(2)}, u32[]{:S(2)}) collective-permute-start(bf16[16,8192]{1,0:T(8,128)(2,1)S(1)} %collective-permute-done.2.refs_4_), channel_id=1, source_target_pairs={{0,1},{1,0},{2,3},{3,2},{4,5},{5,4},{6,7},{7,6},{8,9},{9,8},{10,11... | collective-permute-start | bytes 786440 | tf_op jit(solution)/shard_map/ppermute | solution.py:579
  22.9 8.7 %collective-permute-start.9 = (bf16[16,8192]{1,0:T(8,128)(2,1)S(1)}, bf16[16,8192]{1,0:T(8,128)(2,1)S(1)}, u32[]{:S(2)}, u32[]{:S(2)}) collective-permute-start(bf16[16,8192]{1,0:T(8,128)(2,1)S(1)} %join.3.refs_1_), channel_id=1, source_target_pairs={{0,2},{1,3},{2,0},{3,1},{4,6},{5,7},{6,4},{7,5},{8,10},{9,11},{10,... | collective-permute-start | bytes 786440 | tf_op jit(solution)/shard_map/ppermute | solution.py:579
  24.3 7.3 %collective-permute-start.10 = (bf16[16,1792]{1,0:T(8,128)(2,1)S(1)}, bf16[16,1792]{1,0:T(8,128)(2,1)S(1)}, u32[]{:S(2)}, u32[]{:S(2)}) collective-permute-start(bf16[16,1792]{1,0:T(8,128)(2,1)S(1)} %get-tuple-element.76), channel_id=1, source_target_pairs={{0,12},{1,13},{2,14},{3,15},{4,8},{5,9},{6,10},{7,11},{8,4},{9,5},... | collective-permute-start | bytes 172040 | tf_op jit(solution)/shard_map/ppermute | solution.py:579
  27.8 5.3 %collective-permute-start.11 = (bf16[16,1792]{1,0:T(8,128)(2,1)S(1)}, bf16[16,1792]{1,0:T(8,128)(2,1)S(1)}, u32[]{:S(2)}, u32[]{:S(2)}) collective-permute-start(bf16[16,1792]{1,0:T(8,128)(2,1)S(1)} %get-tuple-element.77), channel_id=1, source_target_pairs={{0,8},{1,9},{2,10},{3,11},{4,12},{5,13},{6,14},{7,15},{8,0},{9,1},... | collective-permute-start | bytes 172040 | tf_op jit(solution)/shard_map/ppermute | solution.py:579
  33.1 1.5 %collective-permute-start.12 = (bf16[16,8192]{1,0:T(8,128)(2,1)S(1)}, bf16[16,8192]{1,0:T(8,128)(2,1)S(1)}, u32[]{:S(2)}, u32[]{:S(2)}) collective-permute-start(bf16[16,8192]{1,0:T(8,128)(2,1)S(1)} %collective-permute-done.9.refs_5_), channel_id=1, source_target_pairs={{0,1},{1,0},{2,3},{3,2},{4,5},{5,4},{6,7},{7,6},{8,9},{9,8},{10,11... | collective-permute-start | bytes 786440 | tf_op jit(solution)/shard_map/ppermute | solution.py:579
  38.7 2.1 %copy-start.1 = (bf16[448,576]{1,0:T(8,128)(2,1)S(1)}, bf16[448,576]{1,0:T(8,128)(2,1)}, u32[]{:S(2)}) copy-start(bf16[448,576]{1,0:T(8,128)(2,1)} %refs_10_) | copy-start | bytes 1548292
  38.7 2.7 %collective-permute-start.15 = (bf16[2,1,40,1792]{3,2,1,0:T(8,128)(2,1)S(1)}, bf16[2,1,40,1792]{3,2,1,0:T(8,128)(2,1)S(1)}, u32[]{:S(2)}, u32[]{:S(2)}) collective-permute-start(bf16[2,1,40,1792]{3,2,1,0:T(8,128)(2,1)S(1)} %get-tuple-element.92), channel_id=1, source_target_pairs={{0,1},{1,0},{2,3},{3,2},{4,5},{5,4},{6,7},{7,6},{8,9},{9,8},{10,11... | collective-permute-start | bytes 860168 | tf_op jit(solution)/shard_map/ppermute | solution.py:579
  40.3 1.8 %collective-permute-start.19 = (bf16[2,1,40,1792]{3,2,1,0:T(8,128)(2,1)S(1)}, bf16[2,1,40,1792]{3,2,1,0:T(8,128)(2,1)S(1)}, u32[]{:S(2)}, u32[]{:S(2)}) collective-permute-start(bf16[2,1,40,1792]{3,2,1,0:T(8,128)(2,1)S(1)} %get-tuple-element.98), channel_id=1, source_target_pairs={{0,1},{1,0},{2,3},{3,2},{4,5},{5,4},{6,7},{7,6},{8,9},{9,8},{10,11... | collective-permute-start | bytes 860168 | tf_op jit(solution)/shard_map/ppermute | solution.py:579
  40.8 22.3 %collective-permute-start.22 = (bf16[448,576]{1,0:T(8,128)(2,1)S(1)}, bf16[448,576]{1,0:T(8,128)(2,1)S(1)}, u32[]{:S(2)}, u32[]{:S(2)}) collective-permute-start(bf16[448,576]{1,0:T(8,128)(2,1)S(1)} %copy-done.1), channel_id=1, source_target_pairs={{0,1},{1,0},{2,3},{3,2},{4,5},{5,4},{6,7},{7,6},{8,9},{9,8},{10,11... | collective-permute-start | bytes 1548296 | tf_op jit(solution)/shard_map/ppermute | solution.py:579
  40.9 22.2 %collective-permute-start.23 = (bf16[448,576]{1,0:T(8,128)(2,1)S(1)}, bf16[448,576]{1,0:T(8,128)(2,1)S(1)}, u32[]{:S(2)}, u32[]{:S(2)}) collective-permute-start(bf16[448,576]{1,0:T(8,128)(2,1)S(1)} %collective-permute-done.6.refs_11_), channel_id=1, source_target_pairs={{0,1},{1,0},{2,3},{3,2},{4,5},{5,4},{6,7},{7,6},{8,9},{9,8},{10,11... | collective-permute-start | bytes 1548296 | tf_op jit(solution)/shard_map/ppermute | solution.py:579
  41.3 8.4 %collective-permute-start.13 = (bf16[2,2,40,1792]{3,2,1,0:T(8,128)(2,1)S(1)}, bf16[2,2,40,1792]{3,2,1,0:T(8,128)(2,1)S(1)}, u32[]{:S(2)}, u32[]{:S(2)}) collective-permute-start(bf16[2,2,40,1792]{3,2,1,0:T(8,128)(2,1)S(1)} %get-tuple-element.90), channel_id=1, source_target_pairs={{0,1},{1,0},{2,3},{3,2},{4,5},{5,4},{6,7},{7,6},{8,9},{9,8},{10,11... | collective-permute-start | bytes 1720328 | tf_op jit(solution)/shard_map/ppermute | solution.py:579
  41.5 6.7 %collective-permute-start.16 = (bf16[1,40,1792]{2,1,0:T(8,128)(2,1)S(1)}, bf16[1,40,1792]{2,1,0:T(8,128)(2,1)S(1)}, u32[]{:S(2)}, u32[]{:S(2)}) collective-permute-start(bf16[1,40,1792]{2,1,0:T(8,128)(2,1)S(1)} %fusion.5), channel_id=1, source_target_pairs={{0,2},{1,3},{2,0},{3,1},{4,6},{5,7},{6,4},{7,5},{8,10},{9,11},{10,... | collective-permute-start | bytes 430088 | tf_op jit(solution)/shard_map/ppermute | solution.py:579
  42.2 8.6 %collective-permute-start.20 = (bf16[1,40,1792]{2,1,0:T(8,128)(2,1)S(1)}, bf16[1,40,1792]{2,1,0:T(8,128)(2,1)S(1)}, u32[]{:S(2)}, u32[]{:S(2)}) collective-permute-start(bf16[1,40,1792]{2,1,0:T(8,128)(2,1)S(1)} %fusion.6), channel_id=1, source_target_pairs={{0,2},{1,3},{2,0},{3,1},{4,6},{5,7},{6,4},{7,5},{8,10},{9,11},{10,... | collective-permute-start | bytes 430088 | tf_op jit(solution)/shard_map/ppermute | solution.py:579
  48.2 14.7 %collective-permute-start.18 = (bf16[40,1792]{1,0:T(8,128)(2,1)S(1)}, bf16[40,1792]{1,0:T(8,128)(2,1)S(1)}, u32[]{:S(2)}, u32[]{:S(2)}) collective-permute-start(bf16[40,1792]{1,0:T(8,128)(2,1)S(1)} %fusion.4), channel_id=1, source_target_pairs={{0,8},{1,9},{2,10},{3,11},{4,12},{5,13},{6,14},{7,15},{8,0},{9,1},... | collective-permute-start | bytes 430088 | tf_op jit(solution)/shard_map/ppermute | solution.py:579
  49.7 8.1 %collective-permute-start.14 = (bf16[2,40,1792]{2,1,0:T(8,128)(2,1)S(1)}, bf16[2,40,1792]{2,1,0:T(8,128)(2,1)S(1)}, u32[]{:S(2)}, u32[]{:S(2)}) collective-permute-start(bf16[2,40,1792]{2,1,0:T(8,128)(2,1)S(1)} %fusion), channel_id=1, source_target_pairs={{0,2},{1,3},{2,0},{3,1},{4,6},{5,7},{6,4},{7,5},{8,10},{9,11},{10,... | collective-permute-start | bytes 860168 | tf_op jit(solution)/shard_map/ppermute | solution.py:579
  50.9 12.0 %collective-permute-start.21 = (bf16[40,1792]{1,0:T(8,128)(2,1)S(1)}, bf16[40,1792]{1,0:T(8,128)(2,1)S(1)}, u32[]{:S(2)}, u32[]{:S(2)}) collective-permute-start(bf16[40,1792]{1,0:T(8,128)(2,1)S(1)} %fusion.1), channel_id=1, source_target_pairs={{0,12},{1,13},{2,14},{3,15},{4,8},{5,9},{6,10},{7,11},{8,4},{9,5},... | collective-permute-start | bytes 430088 | tf_op jit(solution)/shard_map/ppermute | solution.py:579
  57.8 5.3 %copy-start.2 = (f32[7168]{0:T(1024)S(1)}, f32[7168]{0:T(1024)}, u32[]{:S(2)}) copy-start(f32[7168]{0:T(1024)} %param.15) | copy-start | bytes 86020
  57.8 16.7 %copy-start = (bf16[16,128,576]{1,2,0:T(8,128)(2,1)S(1)}, bf16[16,128,576]{1,2,0:T(8,128)(2,1)}, u32[]{:S(2)}) copy-start(bf16[16,128,576]{1,2,0:T(8,128)(2,1)} %param.24) | copy-start | bytes 7077892
  57.8 16.7 %copy-start.3 = (f32[512]{0:T(512)S(1)}, f32[512]{0:T(512)}, u32[]{:S(2)}) copy-start(f32[512]{0:T(512)} %param.16) | copy-start | bytes 6148
  57.9 5.2 %collective-permute-start.17 = (bf16[40,1792]{1,0:T(8,128)(2,1)S(1)}, bf16[40,1792]{1,0:T(8,128)(2,1)S(1)}, u32[]{:S(2)}, u32[]{:S(2)}) collective-permute-start(bf16[40,1792]{1,0:T(8,128)(2,1)S(1)} %get-tuple-element.125), channel_id=1, source_target_pairs={{0,4},{1,5},{2,6},{3,7},{4,0},{5,1},{6,2},{7,3},{8,12},{9,13},{10,... | collective-permute-start | bytes 430088 | tf_op jit(solution)/shard_map/ppermute | solution.py:579
  65.1 5.0 %collective-permute-start.24 = (bf16[16,2432]{1,0:T(8,128)(2,1)S(1)}, bf16[16,2432]{1,0:T(8,128)(2,1)S(1)}, u32[]{:S(2)}, u32[]{:S(2)}) collective-permute-start(bf16[16,2432]{1,0:T(8,128)(2,1)S(1)} %get-tuple-element.118), channel_id=1, source_target_pairs={{0,4},{1,5},{2,6},{3,7},{4,0},{5,1},{6,2},{7,3},{8,12},{9,13},{10,... | collective-permute-start | bytes 233480 | tf_op jit(solution)/shard_map/ppermute | solution.py:579
  66.2 8.3 %collective-permute-start.25 = (bf16[16,2432]{1,0:T(8,128)(2,1)S(1)}, bf16[16,2432]{1,0:T(8,128)(2,1)S(1)}, u32[]{:S(2)}, u32[]{:S(2)}) collective-permute-start(bf16[16,2432]{1,0:T(8,128)(2,1)S(1)} %get-tuple-element.119), channel_id=1, source_target_pairs={{0,8},{1,9},{2,10},{3,11},{4,12},{5,13},{6,14},{7,15},{8,0},{9,1},... | collective-permute-start | bytes 233480 | tf_op jit(solution)/shard_map/ppermute | solution.py:579
  68.0 6.5 %collective-permute-start.26 = (bf16[16,2432]{1,0:T(8,128)(2,1)S(1)}, bf16[16,2432]{1,0:T(8,128)(2,1)S(1)}, u32[]{:S(2)}, u32[]{:S(2)}) collective-permute-start(bf16[16,2432]{1,0:T(8,128)(2,1)S(1)} %get-tuple-element.120), channel_id=1, source_target_pairs={{0,12},{1,13},{2,14},{3,15},{4,8},{5,9},{6,10},{7,11},{8,4},{9,5},... | collective-permute-start | bytes 233480 | tf_op jit(solution)/shard_map/ppermute | solution.py:579
